TPU v7x, 256 devices: a whole 4x4x8 slice. The times are simulated.
256 devices in a mesh: gx: 16 (over z, core), gy: 4 (over y), gz: 4 (over x).
Axes of the slice: x: 4, y: 4, z: 8, core: 2. Of those that a mesh axis runs over, the one named last changes fastest.
Arguments:
- facies: int32 [32, 256, 512], P('gz', 'gx', 'gy'), may hold values from 0 to 7
- boundary: int32 [32, 256, 512], P('gz', 'gx', 'gy'), may hold values from 0 to 2, as said below
- horizontal_conductivity: float32 [8], replicated, may hold values from 0.2 to 5
- vertical_conductivity: float32 [8], replicated, may hold values from 0.1 to 2
- source: float32 [32, 256, 512], P('gz', 'gx', 'gy'), may hold values from -20 to 20
- density: float32 [32, 256, 512], P('gz', 'gx', 'gy'), may hold values from 0 to 4
Outputs:
- pressure: float32 [32, 256, 512], P('gz', 'gx', 'gy')
- residual: float32 [32, 256, 512], P('gz', 'gx', 'gy')
Inputs may be any that keep to these rules, and one draw needn't show every extreme that they name: 0 inland, 1 sea boundary, 2 river boundary; boundary cells are few.
All inputs are finite; a program needn't handle non-finite values.
Results may differ from a plain program's by a relative error of at most 0.0003.
Values sent between devices are 32-bit elements; how exact they have to be, the bound alone decides.
No kernel may reach another device: no remote copies, remote signals or barrier semaphores. Data moves between devices by JAX's collectives and lax.ppermute only.
A program may use at most 256 MiB of HBM per device.

v0:
```python
import jax
import jax.numpy as jnp
from jax import lax
from jax.experimental import pallas as pl
from jax.experimental.pallas import tpu as pltpu
from jax.sharding import PartitionSpec as P

COARSE_SWEEPS = 8
W = 2.0 / 3.0
F32 = jnp.float32
UX, UY, UZ, RD, C, V = range(6)
SINK = RD
H = 5
Z0 = 8 + 2 * H

VMEM = pl.BlockSpec(memory_space=pltpu.VMEM)
SMEM = pl.BlockSpec(memory_space=pltpu.SMEM)


def call(kernel, outs, *args, scratch=(), smem=0):
    specs = [SMEM] * smem + [VMEM] * (len(args) - smem)
    return pl.pallas_call(
        kernel,
        out_shape=[jax.ShapeDtypeStruct(s, F32) for s in outs],
        in_specs=specs,
        out_specs=[VMEM] * len(outs),
        scratch_shapes=[pltpu.VMEM(s, F32) for s in scratch],
        compiler_params=pltpu.CompilerParams(vmem_limit_bytes=50 * 2**20),
    )(*args)


def iota(shape, dim):
    return lax.broadcasted_iota(jnp.int32, shape, dim)


def dot(a, b):
    return lax.dot_general(
        a, b, (((1,), (0,)), ((), ())), precision=lax.Precision.HIGHEST, preferred_element_type=F32
    )


def dot_nt(a, b):
    return lax.dot_general(
        a, b, (((1,), (1,)), ((), ())), precision=lax.Precision.HIGHEST, preferred_element_type=F32
    )


def onehot(cond):
    return jnp.where(cond, 1.0, 0.0).astype(F32)


def up(a, dim):
    return pltpu.roll(a, a.shape[dim] - 1, dim)


def down(a, dim):
    return pltpu.roll(a, 1, dim)


def each(start, stop, body):
    def step(z, carry):
        body(z)
        return carry

    lax.fori_loop(start, stop, step, 0)


def wrap(z, n):
    return lax.rem(z + n, n)


def around(a, field, z, zm, zp):
    v = field(z)
    ux, uy = a[UX, z], a[UY, z]
    out = ux * up(v, 0) + down(ux * v, 0)
    out = out + (uy * up(v, 1) + down(uy * v, 1))
    return v, out + (a[UZ, z] * field(zp) + a[UZ, zm] * field(zm))


def smoothed(a, field, z, zm, zp):
    v, beside = around(a, field, z, zm, zp)
    return v * (1.0 / 3.0) + a[C, z] + a[RD, z] * beside


def finish(a, d, r, z, zm):
    ux, uy = a[UX, z], a[UY, z]
    diag = a[SINK, z] + a[UZ, z] + a[UZ, zm] + ux + down(ux, 0) + uy + down(uy, 1)
    d[z] = diag
    rd = jnp.where(diag > 0.0, W / jnp.where(diag > 0.0, diag, 1.0), 0.0)
    a[RD, z] = rd
    if r is not None:
        a[C, z] = rd * r[z]


def circ(n):
    return lambda z: (z, wrap(z - 1, n), wrap(z + 1, n))


def pre(a, d, r, res, n):
    c3 = circ(n)
    each(0, n, lambda z: finish(a, d, r, z, wrap(z - 1, n)))

    def one(z):
        a[V, z] = smoothed(a, lambda k: a[C, k], *c3(z))

    each(0, n, one)
    if res is not None:

        def two(z):
            v, beside = around(a, lambda k: a[V, k], *c3(z))
            res[z] = d[z] * (1.5 * a[C, z] - v) + beside

        each(0, n, two)


def pair_rows(t, n):
    return t[pl.ds(0, n, stride=2), :] + t[pl.ds(1, n, stride=2), :]


def halve(a, sink, r, t, store, n, rows):
    odd_row = iota((rows, 128), 0) % 2 == 1
    odd_lane = iota((rows, 128), 1) % 2 == 1

    def body(z):
        lo, hi = 2 * z, 2 * z + 1
        parts = (
            jnp.where(odd_row, a[UX, lo] + a[UX, hi], 0.0),
            jnp.where(odd_lane, a[UY, lo] + a[UY, hi], 0.0),
            a[UZ, hi],
            sink[lo] + sink[hi],
            r[lo] + r[hi],
        )
        for k, part in enumerate(parts):
            t[k] = part
        for k in range(5):
            store(k, z, pair_rows(t.at[k], rows // 2))

    each(0, n // 2, body)


def stretch(e, q, p):
    return dot(dot(q, e), p)


def pack_z(f, b, s, d, lo, hi):
    for k, ref in enumerate((f, b, s, d)):
        lo[k] = ref[0:H].astype(F32)
        hi[k] = ref[8 - H : 8].astype(F32)


def pack_x(f, b, s, d, above, below, lo, hi):
    for out, row in ((lo, 0), (hi, 8)):
        for k, ref in enumerate((f, b, s, d)):
            out[k, 0:H] = below[k, :, row : row + 8]
            out[k, H : H + 8] = ref[:, row : row + 8].astype(F32)
            out[k, H + 8 : Z0] = above[k, :, row : row + 8]


ROWS0 = 4 * Z0 * 32


def pack_y(xl, xh, rl, rh, lo, hi):
    whole = jnp.concatenate([xl[...], xh[...], rl[...], rh[...]], axis=2).reshape(ROWS0, 128)
    i, j = iota((16, 128), 0), iota((16, 128), 1)
    edges = dot_nt(onehot(j == jnp.where(i < 8, i, 112 + i)), whole)
    lo[...] = edges[0:8]
    hi[...] = edges[8:16]


def level0(pos, hc, vc, xl, xh, rl, rh, yl, yh, a, packed, raw, hs, vs, dd, res, sk, t, m):
    gx, gy, gz = pos[0], pos[1], pos[2]
    i, j = iota((16, 128), 0), iota((16, 128), 1)
    place = onehot(j == jnp.where(i < 8, i, 112 + i))
    sides = jnp.concatenate([yl[...], yh[...]], axis=0)
    beyond = dot(jnp.transpose(sides), place).reshape(4, Z0, 32, 128)
    raw[:, :, :, 128:256] = beyond
    for row, ref in ((0, xl), (8, xh), (16, rl), (24, rh)):
        raw[:, :, row : row + 8, 0:128] = ref[...]

    row, lane = iota((32, 256), 0), iota((32, 256), 1)
    x = gx * 16 + jnp.where(row < 24, row, row - 32)
    y = gy * 128 + jnp.where(lane < 192, lane, lane - 256)
    inside = (x >= 0) & (x < 256) & (y >= 0) & (y < 512)
    own = (jnp.where(row < 24, 1, 0) * jnp.where(lane < 192, 1, 0)) > 0
    del own

    def materials(z):
        zg = gz * 8 + z - H
        here = inside & ((zg >= 0) & (zg < 32))
        kind = raw[0, z]
        h = jnp.full((32, 256), hc[0], F32)
        v = jnp.full((32, 256), vc[0], F32)
        for n in range(1, 8):
            is_n = kind == float(n)
            h = jnp.where(is_n, hc[n], h)
            v = jnp.where(is_n, vc[n], v)
        hs[z] = jnp.where(here, h, 0.0)
        vs[z] = jnp.where(here, v, 0.0)

    each(0, Z0, materials)

    def harmonic(c, n):
        s = c + n
        return 2.0 * c * n / jnp.where(s > 0.0, s, 1.0)

    def couple(z):
        h = hs[z]
        a[UX, z] = harmonic(h, up(h, 0))
        a[UY, z] = harmonic(h, up(h, 1))
        a[UZ, z] = harmonic(vs[z], vs[z + 1])

    each(0, Z0 - 1, couple)

    odd_row, odd_lane = row % 2 == 1, lane % 2 == 1

    def setup(z):
        h, v = hs[z], vs[z]
        sink = jnp.where(raw[1, z] == 1.0, 2.0 * v, jnp.where(raw[1, z] == 2.0, 0.5 * h, 0.0))
        ux, uy, uz, lz = a[UX, z], a[UY, z], a[UZ, z], a[UZ, z - 1]
        lx, ly = down(ux, 0), down(uy, 1)
        diag = sink + lz + uz + lx + ux + ly + uy
        dens = raw[3, z]
        b = raw[2, z] + 0.5 * uz * (dens + raw[3, z + 1]) - 0.5 * lz * (raw[3, z - 1] + dens)
        rd = jnp.where(diag > 0.0, W / jnp.where(diag > 0.0, diag, 1.0), 0.0)
        a[RD, z] = rd
        a[C, z] = rd * b
        dd[z] = diag
        sk[z] = sink
        outer = sink + jnp.where(odd_row, ux, lx) + jnp.where(odd_lane, uy, ly)
        hs[z] = outer + jnp.where((z - H) % 2 == 1, uz, lz)

    each(1, Z0 - 1, setup)

    def first(z):
        a[V, z] = smoothed(a, lambda k: a[C, k], z, z - 1, z + 1)

    each(2, Z0 - 2, first)

    def residual(z):
        v, beside = around(a, lambda k: a[V, k], z, z - 1, z + 1)
        res[z - H] = (dd[z] * (1.5 * a[C, z] - v) + beside)[0:16, 0:128]

    each(H, H + 8, residual)

    o_row = iota((16, 128), 0) % 2 == 1
    o_lane = iota((16, 128), 1) % 2 == 1

    def coarsen(z):
        lo, hi = H + 2 * z, H + 2 * z + 1

        def both(ref):
            return ref[lo, 0:16, 0:128] + ref[hi, 0:16, 0:128]

        parts = (
            jnp.where(o_row, both(a.at[UX]), 0.0),
            jnp.where(o_lane, both(a.at[UY]), 0.0),
            a[UZ, hi, 0:16, 0:128],
            both(sk),
            res[2 * z] + res[2 * z + 1],
            both(hs),
        )
        for k, part in enumerate(parts):
            t[k] = part
        for k in range(6):
            m[lax.div(z, 2), k, lax.rem(z, 2)] = pair_rows(t.at[k], 8)

    each(0, 4, coarsen)
    i, j = iota((128, 128), 0), iota((128, 128), 1)
    out = dot(m[0].reshape(96, 128), onehot(j == i // 2))
    out = out + dot(m[1].reshape(96, 128), onehot(j == 64 + i // 2))
    out = out.reshape(6, 2, 8, 128)
    packed[0:4] = out[0:4]
    packed[4] = W * out[4] / out[5]


def pack_x1(own, b1, b2, b3, full, lo, hi):
    for n, ref in enumerate((own, b1, b2, b3)):
        full[:, 2 * n : 2 * n + 2] = ref[...]
        first, second = ref[:, 0], ref[:, 1]
        lo[:, n] = jnp.concatenate([first[:, 0:4], second[:, 0:4]], axis=1)
        hi[:, n] = jnp.concatenate([first[:, 4:8], second[:, 4:8]], axis=1)


def pack_y1(own, r1, l1, r2, l2, whole, lo, hi):
    whole[:, :, 0:8] = own[...]
    whole[:, :, 8:16] = r1[...]
    whole[:, :, 24:32] = l1[...]
    for n in range(4):
        for s in range(2):
            part = slice(4 * s, 4 * s + 4)
            whole[:, 2 * n + s, 16:24] = jnp.concatenate([r2[:, n, part], l2[:, n, part]], axis=1)
    i, j = iota((64, 128), 0), iota((64, 128), 1)
    half, k = (i // 16) % 2, i % 16
    lane = jnp.where(i < 32, k, 48 + k) + 64 * half
    edges = dot_nt(onehot(j == lane), whole[...].reshape(1280, 128))
    lo[...] = edges[0:32]
    hi[...] = edges[32:64]


def sums(n, width):
    i, j = iota((128, 128), 0), iota((128, 128), 1)
    return onehot((i < n) & (j % width == i // 2))


def level12(pos, whole, yl, yh, a, b, sent, d1, r1, t1, m1, d2, r2, s1, s2, q2, m2):
    gx, gy, gz = pos[0], pos[1], pos[2]
    sides = jnp.transpose(jnp.concatenate([yl[...], yh[...]], axis=0))
    i, j = iota((64, 128), 0), iota((64, 128), 1)
    side, half, k = i // 32, (i // 16) % 2, i % 16
    to = jnp.where(side == 0, 64 + k, 112 + k)
    row, lane = iota((32, 128), 0), iota((32, 128), 1)
    x = gx * 8 + jnp.where(row < 20, row, row - 32)
    y = gy * 64 + jnp.where(lane < 96, lane, lane - 128)
    inside = (x >= 0) & (x < 128) & (y >= 0) & (y < 256)
    for part in range(2):
        beyond = dot(sides, onehot((half == part) & (j == to))).reshape(5, 8, 32, 128)
        for n in range(4):
            for s in range(2):
                for k5 in range(5):
                    v = whole[k5, 2 * n + s]
                    if part:
                        v = pltpu.roll(v, 64, 1)
                    v = jnp.where(lane < 64, v, beyond[k5, 2 * n + s])
                    v = jnp.where(inside, v, 0.0)
                    z = 4 * n + 2 * part + s
                    a[k5, z] = v
                    if k5 == SINK:
                        s1[z] = v
    pre(a, d1, None, r1, 16)

    def keep1(k, z, value):
        m1[k, z] = value

    halve(a, s1, r1, t1, keep1, 16, 32)
    out = dot(m1[...].reshape(640, 128), sums(128, 64)).reshape(5, 8, 16, 128)
    b[0:4] = out[0:4]
    s2[...] = out[3]
    q2[...] = out[4]
    pre(b, d2, q2, r2, 8)

    def keep2(k, z, value):
        m2[z, k] = value[0:2]

    m2[...] = jnp.zeros((4, 8, 2, 128), F32)
    halve(b, s2, r2, t1.at[:, 0:16], keep2, 8, 16)
    i, j = iota((128, 128), 0), iota((128, 128), 1)
    total = jnp.zeros((8, 128), F32)
    for z in range(4):
        zg = lax.rem(z + gz, 4)
        for s in range(2):
            to = (zg * 2 + s) * 16 + i // 2
            total = total + dot(m2[z, :, s], onehot((i < 32) & (j == to)))
    sent[...] = jnp.broadcast_to(total[None], (64, 8, 128))


def finish_up(a, n):
    c3 = circ(n)

    def run(src, dst):
        def body(z):
            dst[z] = smoothed(a, lambda k: src[k], *c3(z))

        each(0, n, body)

    return run


def solve(
    pos, got, a0, a1, a2, pressure, left,
    a3, a4, a5, d3, d4, d5, r3, r4, s3, s4, t3, m3, m4, e1, e2, e3, e4, e5, w0,
):
    gx, gy, gz = pos[0], pos[1], pos[2]
    lane = iota((16, 128), 1)
    for k in range(5):
        rows = [got[pl.ds(g * 128 + k, 16, stride=8), :] for g in range(4)]
        for z in range(4):
            for s in range(2):
                at = (z * 2 + s) * 16
                value = jnp.zeros((16, 128), F32)
                for g in range(4):
                    shift = (16 * g - at) % 128
                    moved = pltpu.roll(rows[g], shift, 1) if shift else rows[g]
                    value = jnp.where(lane // 16 == g, moved, value)
                value = value + pltpu.roll(value, 64, 1)
                if k < 4:
                    a3[k, z, pl.ds(s, 16, stride=2), :] = value
                else:
                    r3[z, pl.ds(s, 16, stride=2), :] = value
    s3[...] = a3[SINK]
    pre(a3, d3, r3, e3, 4)

    def keep3(k, z, value):
        m3[k, z] = value

    halve(a3, s3, e3, t3, keep3, 4, 32)
    out = dot(m3[...].reshape(160, 128), sums(64, 32)).reshape(5, 2, 16, 128)
    a4[0:4] = out[0:4]
    s4[...] = out[3]
    r4[...] = out[4]
    pre(a4, d4, r4, e4, 2)

    def keep4(k, z, value):
        m4[k, z] = value

    halve(a4, s4, e4, t3.at[:, 0:16], keep4, 2, 16)
    out = dot(m4[...].reshape(40, 128), sums(32, 16)).reshape(5, 8, 128)
    ux, uy, uz, sink, r = out[0], out[1], out[2], out[3], out[4]
    diag = sink + uz + uz + ux + down(ux, 0) + uy + down(uy, 1)
    rd = W / diag
    c = rd * r
    v = c
    for _ in range(COARSE_SWEEPS - 1):
        beside = ux * up(v, 0) + down(ux * v, 0) + (uy * up(v, 1) + down(uy * v, 1))
        beside = beside + (uz * v + uz * v)
        v = v * (1.0 / 3.0) + c + rd * beside

    def double(rows):
        i, j = iota((rows, rows // 2), 0), iota((rows, rows // 2), 1)
        return onehot(j == i // 2)

    def lanes(width):
        i, j = iota((128, 128), 0), iota((128, 128), 1)
        return onehot((i < width // 2) & (i == (j % width) // 2))

    e = stretch(v, double(16), lanes(32))
    for z in range(2):
        a4[V, z] = a4[V, z] + e
    run = finish_up(a4, 2)
    run(a4.at[V], e4)
    run(e4, r4)
    q, p = double(32), lanes(64)
    for z in range(2):
        e = stretch(r4[z], q, p)
        a3[V, 2 * z] = a3[V, 2 * z] + e
        a3[V, 2 * z + 1] = a3[V, 2 * z + 1] + e
    run = finish_up(a3, 4)
    run(a3.at[V], e3)
    run(e3, r3)
    i, j = iota((128, 128), 0), iota((128, 128), 1)
    jj = j % 64
    at = jnp.where(jj < 40, jj // 2, jj // 2 - 32) + 16 * gy
    p = onehot((i < 64) & (i == lax.rem(at + 64, 64)))
    i, j = iota((16, 32), 0), iota((16, 32), 1)
    at = jnp.where(i < 10, i // 2, i // 2 - 8) + 2 * gx
    q = onehot(j == lax.rem(at + 32, 32))
    for z in range(4):
        e = stretch(r3[lax.rem(z + gz, 4)], q, p)
        e2[2 * z] = a2[V, 2 * z] + e
        e2[2 * z + 1] = a2[V, 2 * z + 1] + e
    run = finish_up(a2, 8)
    run(e2, e5)
    run(e5, e2)
    i, j = iota((128, 128), 0), iota((128, 128), 1)
    q, p = double(32), onehot((i < 64) & (i == j // 2))
    for z in range(8):
        e = stretch(e2[z], q, p)
        e1[0, 2 * z] = a1[V, 2 * z] + e
        e1[0, 2 * z + 1] = a1[V, 2 * z + 1] + e
    run = finish_up(a1, 16)
    run(e1.at[0], e1.at[1])
    run(e1.at[1], e1.at[0])
    i, j = iota((32, 32), 0), iota((32, 32), 1)
    q = onehot(j == jnp.where(i < 24, i // 2, i // 2 + 16))
    i, j = iota((128, 256), 0), iota((128, 256), 1)
    p = onehot(i == j // 2)
    for zc in range(-2, 6):
        e = stretch(e1[0, zc % 16], q, p)
        for z in (2 * zc, 2 * zc + 1):
            if -3 <= z <= 10:
                w0[0, z + H] = a0[V, z + H] + e

    def sweep0(src, dst):
        def body(z):
            w0[dst, z] = smoothed(a0, lambda k: w0[src, k], z, z - 1, z + 1)

        return body

    each(3, Z0 - 3, sweep0(0, 1))
    each(4, Z0 - 4, sweep0(1, 0))

    def last(z):
        v, beside = around(a0, lambda k: w0[0, k], z, z - 1, z + 1)
        r = W / a0[RD, z] * (1.5 * a0[C, z] - v) + beside
        pressure[z - H] = v[0:16, 0:128]
        left[z - H] = r[0:16, 0:128]

    each(H, H + 8, last)


def shift(value, axis, by):
    count = lax.axis_size(axis)
    return lax.ppermute(value, axis, [((i + by) % count, i) for i in range(count)])


def local(facies, boundary, hc, vc, source, density):
    pos = jnp.stack([lax.axis_index(n) for n in ("gx", "gy", "gz")]).astype(jnp.int32)
    raw = (facies, boundary, source, density)
    lo, hi = call(pack_z, [(4, H, 16, 128)] * 2, *raw)
    above, below = shift(lo, "gz", 1), shift(hi, "gz", -1)
    xl, xh = call(pack_x, [(4, Z0, 8, 128)] * 2, *raw, above, below)
    rl, rh = shift(xl, "gx", 1), shift(xh, "gx", -1)
    lo, hi = call(pack_y, [(8, ROWS0)] * 2, xl, xh, rl, rh)
    yl, yh = shift(lo, "gy", 1), shift(hi, "gy", -1)
    a0, packed = call(
        level0,
        [(6, Z0, 32, 256), (5, 2, 8, 128)],
        pos, hc, vc, xl, xh, rl, rh, yl, yh,
        smem=3,
        scratch=[
            (4, Z0, 32, 256), (Z0, 32, 256), (Z0, 32, 256), (Z0, 32, 256), (8, 16, 128),
            (Z0, 32, 256), (6, 16, 128), (2, 6, 2, 8, 128),
        ],
    )
    blocks = [shift(packed, "gz", n) for n in (1, 2, 3)]
    full, lo, hi = call(
        pack_x1, [(5, 8, 8, 128), (5, 4, 8, 128), (5, 4, 8, 128)], packed, *blocks
    )
    r1, l1 = shift(full, "gx", 1), shift(full, "gx", -1)
    r2, l2 = shift(lo, "gx", 2), shift(hi, "gx", -2)
    whole, lo, hi = call(
        pack_y1, [(5, 8, 32, 128), (32, 1280), (32, 1280)], full, r1, l1, r2, l2
    )
    yl, yh = shift(lo, "gy", 1), shift(hi, "gy", -1)
    a1, a2, sent = call(
        level12,
        [(6, 16, 32, 128), (6, 8, 16, 128), (64, 8, 128)],
        pos, whole, yl, yh,
        smem=1,
        scratch=[
            (16, 32, 128), (16, 32, 128), (5, 32, 128), (5, 8, 16, 128),
            (8, 16, 128), (8, 16, 128), (16, 32, 128), (8, 16, 128), (8, 16, 128), (4, 8, 2, 128),
        ],
    )
    got = lax.all_to_all(sent, ("gy", "gx"), 0, 0)
    return tuple(
        call(
            solve,
            [(8, 16, 128), (8, 16, 128)],
            pos, got.reshape(512, 128), a0, a1, a2,
            smem=1,
            scratch=[
                (6, 4, 32, 128), (6, 2, 16, 128), (6, 1, 8, 128),
                (4, 32, 128), (2, 16, 128), (1, 8, 128),
                (4, 32, 128), (2, 16, 128), (4, 32, 128), (2, 16, 128),
                (5, 32, 128), (5, 2, 16, 128), (5, 1, 8, 128),
                (2, 16, 32, 128), (8, 16, 128), (4, 32, 128), (2, 16, 128), (8, 16, 128),
                (2, Z0, 32, 256),
            ],
        )
    )


def solution(mesh):
    split = P("gz", "gx", "gy")
    return jax.shard_map(
        local,
        mesh=mesh,
        in_specs=(split, split, P(), P(), split, split),
        out_specs=(split, split),
        check_vma=False,
    )
```

profile of v0, /device:TPU:1, one launch (start us, length us, event | category | flops | bytes accessed | tf_op | source)
XLA Modules:
  0.0 114.0 jit_solution(13790978221832690150)
XLA Ops:
  0.6 0.8 copy-done
  1.5 0.8 copy-done.1
  2.3 0.8 copy-done.2
  3.2 0.8 copy-done.3
  4.0 3.4 %collective-permute-start = (f32[4,5,16,128]{3,2,1,0:T(8,128)S(1)}, f32[4,5,16,128]{3,2,1,0:T(8,128)S(1)}, u32[]{:S(2)}, u32[]{:S(2)}) collective-permute-start(f32[4,5,16,128]{3,2,1,0:T(8,128)S(1)} %get-tuple-element.19), channel_id=1, source_target_pairs={{1,0},{2,1},{3,2},{0,3},{5,4},{6,5},{7,6},{4,7},{9,8},{10,9},{11,1... | collective-permute-start | bytes 491528 | tf_op jit(solution)/shard_map/ppermute | solution.py:492
  7.4 2.9 %collective-permute-done.above = f32[4,5,16,128]{3,2,1,0:T(8,128)S(1)} collective-permute-done((f32[4,5,16,128]{3,2,1,0:T(8,128)S(1)}, f32[4,5,16,128]{3,2,1,0:T(8,128)S(1)}, u32[]{:S(2)}, u32[]{:S(2)}) %collective-permute-start) | collective-permute-done | bytes 163872 | tf_op jit(solution)/shard_map/ppermute | solution.py:492
  10.3 3.1 %collective-permute-done.1.below = f32[4,5,16,128]{3,2,1,0:T(8,128)S(1)} collective-permute-done((f32[4,5,16,128]{3,2,1,0:T(8,128)S(1)}, f32[4,5,16,128]{3,2,1,0:T(8,128)S(1)}, u32[]{:S(2)}, u32[]{:S(2)}) %collective-permute-start.1) | collective-permute-done | bytes 163872 | tf_op jit(solution)/shard_map/ppermute | solution.py:492
  13.4 1.9 %collective-permute-start.2 = (f32[4,18,8,128]{3,2,1,0:T(8,128)S(1)}, f32[4,18,8,128]{3,2,1,0:T(8,128)S(1)}, u32[]{:S(2)}, u32[]{:S(2)}) collective-permute-start(f32[4,18,8,128]{3,2,1,0:T(8,128)S(1)} %get-tuple-element.21.xl), channel_id=1, source_target_pairs={{16,0},{32,16},{48,32},{64,48},{80,64},{96,80},{112,96},{128,112},... | collective-permute-start | bytes 884744 | tf_op jit(solution)/shard_map/ppermute | solution.py:492
  15.3 1.5 %collective-permute-start.3 = (f32[4,18,8,128]{3,2,1,0:T(8,128)S(1)}, f32[4,18,8,128]{3,2,1,0:T(8,128)S(1)}, u32[]{:S(2)}, u32[]{:S(2)}) collective-permute-start(f32[4,18,8,128]{3,2,1,0:T(8,128)S(1)} %get-tuple-element.22.xh), channel_id=1, source_target_pairs={{240,0},{0,16},{16,32},{32,48},{48,64},{64,80},{80,96},{96,112},{1... | collective-permute-start | bytes 884744 | tf_op jit(solution)/shard_map/ppermute | solution.py:492
  16.8 4.4 %collective-permute-done.2.rl = f32[4,18,8,128]{3,2,1,0:T(8,128)S(1)} collective-permute-done((f32[4,18,8,128]{3,2,1,0:T(8,128)S(1)}, f32[4,18,8,128]{3,2,1,0:T(8,128)S(1)}, u32[]{:S(2)}, u32[]{:S(2)}) %collective-permute-start.2) | collective-permute-done | bytes 294944 | tf_op jit(solution)/shard_map/ppermute | solution.py:492
  21.2 1.0 shard_map.79
  22.3 2.7 %collective-permute-start.4 = (f32[8,2304]{1,0:T(8,128)S(1)}, f32[8,2304]{1,0:T(8,128)S(1)}, u32[]{:S(2)}, u32[]{:S(2)}) collective-permute-start(f32[8,2304]{1,0:T(8,128)S(1)} %get-tuple-element.23), channel_id=1, source_target_pairs={{4,0},{8,4},{12,8},{0,12},{5,1},{9,5},{13,9},{1,13},{6,2},{10,6},{... | collective-permute-start | bytes 221192 | tf_op jit(solution)/shard_map/ppermute | solution.py:492
  25.1 1.3 %collective-permute-done.4.yl = f32[8,2304]{1,0:T(8,128)S(1)} collective-permute-done((f32[8,2304]{1,0:T(8,128)S(1)}, f32[8,2304]{1,0:T(8,128)S(1)}, u32[]{:S(2)}, u32[]{:S(2)}) %collective-permute-start.4) | collective-permute-done | bytes 73760 | tf_op jit(solution)/shard_map/ppermute | solution.py:492
  26.4 3.0 %collective-permute-done.5.yh = f32[8,2304]{1,0:T(8,128)S(1)} collective-permute-done((f32[8,2304]{1,0:T(8,128)S(1)}, f32[8,2304]{1,0:T(8,128)S(1)}, u32[]{:S(2)}, u32[]{:S(2)}) %collective-permute-start.5) | collective-permute-done | bytes 73760 | tf_op jit(solution)/shard_map/ppermute | solution.py:492
  29.4 0.7 copy-done.4
  30.1 0.7 copy-done.5
  30.7 9.3 %shard_map.80 = (f32[6,18,32,256]{3,2,1,0:T(8,128)}, f32[5,2,8,128]{3,2,1,0:T(8,128)S(1)}) custom-call(s32[3]{0:T(128)S(1)} %pad_add_fusion.pos, f32[8]{0:T(128)S(1)} %copy-done.4, f32[8]{0:T(128)S(1)} %copy-done.5, f32[4,18,8,128]{3,2,1,0:T(8,128)S(1)} %get-tuple-element.21.xl, f32[4,18,8,128]{3,2,1,0:T(8,128)S(1)} %get-tuple-element.22.xh, ...), custom_call_target="tpu_custom_call" | custom-call | tf_op jit(solution)/shard_map/pallas_call | solution.py:22
  40.0 1.2 %collective-permute-start.7 = (f32[5,2,8,128]{3,2,1,0:T(8,128)S(1)}, f32[5,2,8,128]{3,2,1,0:T(8,128)S(1)}, u32[]{:S(2)}, u32[]{:S(2)}) collective-permute-start(f32[5,2,8,128]{3,2,1,0:T(8,128)S(1)} %get-tuple-element.25.own), channel_id=1, source_target_pairs={{2,0},{3,1},{0,2},{1,3},{6,4},{7,5},{4,6},{5,7},{10,8},{11,9},{8,1... | collective-permute-start | bytes 122888 | tf_op jit(solution)/shard_map/ppermute | solution.py:492
  41.2 1.5 %collective-permute-start.6 = (f32[5,2,8,128]{3,2,1,0:T(8,128)S(1)}, f32[5,2,8,128]{3,2,1,0:T(8,128)S(1)}, u32[]{:S(2)}, u32[]{:S(2)}) collective-permute-start(f32[5,2,8,128]{3,2,1,0:T(8,128)S(1)} %get-tuple-element.25.own), channel_id=1, source_target_pairs={{1,0},{2,1},{3,2},{0,3},{5,4},{6,5},{7,6},{4,7},{9,8},{10,9},{11,1... | collective-permute-start | bytes 122888 | tf_op jit(solution)/shard_map/ppermute | solution.py:492
  42.7 1.8 %collective-permute-done.8.b3 = f32[5,2,8,128]{3,2,1,0:T(8,128)S(1)} collective-permute-done((f32[5,2,8,128]{3,2,1,0:T(8,128)S(1)}, f32[5,2,8,128]{3,2,1,0:T(8,128)S(1)}, u32[]{:S(2)}, u32[]{:S(2)}) %collective-permute-start.8) | collective-permute-done | bytes 40992 | tf_op jit(solution)/shard_map/ppermute | solution.py:492
  45.1 4.6 %collective-permute-start.10 = (f32[5,8,8,128]{3,2,1,0:T(8,128)S(1)}, f32[5,8,8,128]{3,2,1,0:T(8,128)S(1)}, u32[]{:S(2)}, u32[]{:S(2)}) collective-permute-start(f32[5,8,8,128]{3,2,1,0:T(8,128)S(1)} %get-tuple-element.26.own), channel_id=1, source_target_pairs={{240,0},{0,16},{16,32},{32,48},{48,64},{64,80},{80,96},{96,112},{1... | collective-permute-start | bytes 491528 | tf_op jit(solution)/shard_map/ppermute | solution.py:492
  49.8 3.8 %collective-permute-start.9 = (f32[5,8,8,128]{3,2,1,0:T(8,128)S(1)}, f32[5,8,8,128]{3,2,1,0:T(8,128)S(1)}, u32[]{:S(2)}, u32[]{:S(2)}) collective-permute-start(f32[5,8,8,128]{3,2,1,0:T(8,128)S(1)} %get-tuple-element.26.own), channel_id=1, source_target_pairs={{16,0},{32,16},{48,32},{64,48},{80,64},{96,80},{112,96},{128,112},... | collective-permute-start | bytes 491528 | tf_op jit(solution)/shard_map/ppermute | solution.py:492
  53.5 2.6 %collective-permute-start.11 = (f32[5,4,8,128]{3,2,1,0:T(8,128)S(1)}, f32[5,4,8,128]{3,2,1,0:T(8,128)S(1)}, u32[]{:S(2)}, u32[]{:S(2)}) collective-permute-start(f32[5,4,8,128]{3,2,1,0:T(8,128)S(1)} %get-tuple-element.27), channel_id=1, source_target_pairs={{32,0},{48,16},{64,32},{80,48},{96,64},{112,80},{128,96},{144,112}... | collective-permute-start | bytes 245768 | tf_op jit(solution)/shard_map/ppermute | solution.py:492
  56.1 1.8 %collective-permute-done.11.r2 = f32[5,4,8,128]{3,2,1,0:T(8,128)S(1)} collective-permute-done((f32[5,4,8,128]{3,2,1,0:T(8,128)S(1)}, f32[5,4,8,128]{3,2,1,0:T(8,128)S(1)}, u32[]{:S(2)}, u32[]{:S(2)}) %collective-permute-start.11) | collective-permute-done | bytes 81952 | tf_op jit(solution)/shard_map/ppermute | solution.py:492
  57.9 3.1 %collective-permute-done.12.l2 = f32[5,4,8,128]{3,2,1,0:T(8,128)S(1)} collective-permute-done((f32[5,4,8,128]{3,2,1,0:T(8,128)S(1)}, f32[5,4,8,128]{3,2,1,0:T(8,128)S(1)}, u32[]{:S(2)}, u32[]{:S(2)}) %collective-permute-start.12) | collective-permute-done | bytes 81952 | tf_op jit(solution)/shard_map/ppermute | solution.py:492
  61.0 0.8 shard_map.82
  61.9 1.5 %collective-permute-start.14 = (f32[32,1280]{1,0:T(8,128)S(1)}, f32[32,1280]{1,0:T(8,128)S(1)}, u32[]{:S(2)}, u32[]{:S(2)}) collective-permute-start(f32[32,1280]{1,0:T(8,128)S(1)} %get-tuple-element.31), channel_id=1, source_target_pairs={{12,0},{0,4},{4,8},{8,12},{13,1},{1,5},{5,9},{9,13},{14,2},{2,6},{... | collective-permute-start | bytes 491528 | tf_op jit(solution)/shard_map/ppermute | solution.py:492
  63.4 3.0 %collective-permute-done.13.yl = f32[32,1280]{1,0:T(8,128)S(1)} collective-permute-done((f32[32,1280]{1,0:T(8,128)S(1)}, f32[32,1280]{1,0:T(8,128)S(1)}, u32[]{:S(2)}, u32[]{:S(2)}) %collective-permute-start.13) | collective-permute-done | bytes 163872 | tf_op jit(solution)/shard_map/ppermute | solution.py:492
  66.4 1.5 %collective-permute-done.14.yh = f32[32,1280]{1,0:T(8,128)S(1)} collective-permute-done((f32[32,1280]{1,0:T(8,128)S(1)}, f32[32,1280]{1,0:T(8,128)S(1)}, u32[]{:S(2)}, u32[]{:S(2)}) %collective-permute-start.14) | collective-permute-done | bytes 163872 | tf_op jit(solution)/shard_map/ppermute | solution.py:492
  67.9 9.0 %shard_map.83 = (f32[6,16,32,128]{3,2,1,0:T(8,128)S(1)}, f32[6,8,16,128]{3,2,1,0:T(8,128)S(1)}, f32[64,8,128]{2,1,0:T(8,128)S(1)}) custom-call(s32[3]{0:T(128)S(1)} %pad_add_fusion.pos, f32[5,8,32,128]{3,2,1,0:T(8,128)S(1)} %get-tuple-element.29.whole, f32[32,1280]{1,0:T(8,128)S(1)} %collective-permute-done.13.yl, f32[32,1280]{1,0:T(8,128)S(1)} %collective-permute-done.14.yh), custom_call_target="tpu_custom_call" | custom-call | tf_op jit(solution)/shard_map/pallas_call | solution.py:22
  76.9 18.9 %all_to_all.5 = f32[64,8,128]{2,1,0:T(8,128)S(1)} all-to-all(f32[64,8,128]{2,1,0:T(8,128)S(1)} %get-tuple-element.32), channel_id=1, replica_groups=mesh['gx'=16,'gy'=4,'gz'=4] {'gy','gx'}, dimensions={0} | all-to-all | bytes 524288 | tf_op jit(solution)/shard_map/all_to_all | solution.py:534
  95.7 18.3 %shard_map.84 = (f32[8,16,128]{2,1,0:T(8,128)}, f32[8,16,128]{2,1,0:T(8,128)}) custom-call(s32[3]{0:T(128)S(1)} %pad_add_fusion.pos, f32[512,128]{1,0:T(8,128)S(1)} %bitcast.4, f32[6,18,32,256]{3,2,1,0:T(8,128)} %get-tuple-element.33.a0, f32[6,16,32,128]{3,2,1,0:T(8,128)S(1)} %get-tuple-element.34.a1, f32[6,8,16,128]{3,2,1,0:T(8,128)S(1)} %get-tuple-element.35.a2), custom_call_target="tpu_custom_call" | custom-call | tf_op jit(solution)/shard_map/pallas_call | solution.py:22
  (20 shorter events, 0.8 us)
Async XLA Ops:
  0.6 0.8 copy-start
  1.5 0.8 copy-start.1
  2.3 0.8 copy-start.2
  3.2 0.8 copy-start.3
  4.0 6.3 %collective-permute-start = (f32[4,5,16,128]{3,2,1,0:T(8,128)S(1)}, f32[4,5,16,128]{3,2,1,0:T(8,128)S(1)}, u32[]{:S(2)}, u32[]{:S(2)}) collective-permute-start(f32[4,5,16,128]{3,2,1,0:T(8,128)S(1)} %get-tuple-element.19), channel_id=1, source_target_pairs={{1,0},{2,1},{3,2},{0,3},{5,4},{6,5},{7,6},{4,7},{9,8},{10,9},{11,1... | collective-permute-start | bytes 491528 | tf_op jit(solution)/shard_map/ppermute | solution.py:492
  7.4 6.0 %collective-permute-start.1 = (f32[4,5,16,128]{3,2,1,0:T(8,128)S(1)}, f32[4,5,16,128]{3,2,1,0:T(8,128)S(1)}, u32[]{:S(2)}, u32[]{:S(2)}) collective-permute-start(f32[4,5,16,128]{3,2,1,0:T(8,128)S(1)} %get-tuple-element.20), channel_id=1, source_target_pairs={{3,0},{0,1},{1,2},{2,3},{7,4},{4,5},{5,6},{6,7},{11,8},{8,9},{9,10... | collective-permute-start | bytes 491528 | tf_op jit(solution)/shard_map/ppermute | solution.py:492
  13.4 7.8 %collective-permute-start.2 = (f32[4,18,8,128]{3,2,1,0:T(8,128)S(1)}, f32[4,18,8,128]{3,2,1,0:T(8,128)S(1)}, u32[]{:S(2)}, u32[]{:S(2)}) collective-permute-start(f32[4,18,8,128]{3,2,1,0:T(8,128)S(1)} %get-tuple-element.21.xl), channel_id=1, source_target_pairs={{16,0},{32,16},{48,32},{64,48},{80,64},{96,80},{112,96},{128,112},... | collective-permute-start | bytes 884744 | tf_op jit(solution)/shard_map/ppermute | solution.py:492
  15.3 5.9 %collective-permute-start.3 = (f32[4,18,8,128]{3,2,1,0:T(8,128)S(1)}, f32[4,18,8,128]{3,2,1,0:T(8,128)S(1)}, u32[]{:S(2)}, u32[]{:S(2)}) collective-permute-start(f32[4,18,8,128]{3,2,1,0:T(8,128)S(1)} %get-tuple-element.22.xh), channel_id=1, source_target_pairs={{240,0},{0,16},{16,32},{32,48},{48,64},{64,80},{80,96},{96,112},{1... | collective-permute-start | bytes 884744 | tf_op jit(solution)/shard_map/ppermute | solution.py:492
  22.3 4.2 %collective-permute-start.4 = (f32[8,2304]{1,0:T(8,128)S(1)}, f32[8,2304]{1,0:T(8,128)S(1)}, u32[]{:S(2)}, u32[]{:S(2)}) collective-permute-start(f32[8,2304]{1,0:T(8,128)S(1)} %get-tuple-element.23), channel_id=1, source_target_pairs={{4,0},{8,4},{12,8},{0,12},{5,1},{9,5},{13,9},{1,13},{6,2},{10,6},{... | collective-permute-start | bytes 221192 | tf_op jit(solution)/shard_map/ppermute | solution.py:492
  25.0 4.4 %collective-permute-start.5 = (f32[8,2304]{1,0:T(8,128)S(1)}, f32[8,2304]{1,0:T(8,128)S(1)}, u32[]{:S(2)}, u32[]{:S(2)}) collective-permute-start(f32[8,2304]{1,0:T(8,128)S(1)} %get-tuple-element.24), channel_id=1, source_target_pairs={{12,0},{0,4},{4,8},{8,12},{13,1},{1,5},{5,9},{9,13},{14,2},{2,6},{... | collective-permute-start | bytes 221192 | tf_op jit(solution)/shard_map/ppermute | solution.py:492
  29.4 0.7 copy-start.4
  30.1 0.7 copy-start.5
  40.0 4.5 %collective-permute-start.8 = (f32[5,2,8,128]{3,2,1,0:T(8,128)S(1)}, f32[5,2,8,128]{3,2,1,0:T(8,128)S(1)}, u32[]{:S(2)}, u32[]{:S(2)}) collective-permute-start(f32[5,2,8,128]{3,2,1,0:T(8,128)S(1)} %get-tuple-element.25.own), channel_id=1, source_target_pairs={{3,0},{0,1},{1,2},{2,3},{7,4},{4,5},{5,6},{6,7},{11,8},{8,9},{9,10... | collective-permute-start | bytes 122888 | tf_op jit(solution)/shard_map/ppermute | solution.py:492
  40.0 4.5 %collective-permute-start.7 = (f32[5,2,8,128]{3,2,1,0:T(8,128)S(1)}, f32[5,2,8,128]{3,2,1,0:T(8,128)S(1)}, u32[]{:S(2)}, u32[]{:S(2)}) collective-permute-start(f32[5,2,8,128]{3,2,1,0:T(8,128)S(1)} %get-tuple-element.25.own), channel_id=1, source_target_pairs={{2,0},{3,1},{0,2},{1,3},{6,4},{7,5},{4,6},{5,7},{10,8},{11,9},{8,1... | collective-permute-start | bytes 122888 | tf_op jit(solution)/shard_map/ppermute | solution.py:492
  41.2 3.9 %collective-permute-start.6 = (f32[5,2,8,128]{3,2,1,0:T(8,128)S(1)}, f32[5,2,8,128]{3,2,1,0:T(8,128)S(1)}, u32[]{:S(2)}, u32[]{:S(2)}) collective-permute-start(f32[5,2,8,128]{3,2,1,0:T(8,128)S(1)} %get-tuple-element.25.own), channel_id=1, source_target_pairs={{1,0},{2,1},{3,2},{0,3},{5,4},{6,5},{7,6},{4,7},{9,8},{10,9},{11,1... | collective-permute-start | bytes 122888 | tf_op jit(solution)/shard_map/ppermute | solution.py:492
  45.1 15.9 %collective-permute-start.10 = (f32[5,8,8,128]{3,2,1,0:T(8,128)S(1)}, f32[5,8,8,128]{3,2,1,0:T(8,128)S(1)}, u32[]{:S(2)}, u32[]{:S(2)}) collective-permute-start(f32[5,8,8,128]{3,2,1,0:T(8,128)S(1)} %get-tuple-element.26.own), channel_id=1, source_target_pairs={{240,0},{0,16},{16,32},{32,48},{48,64},{64,80},{80,96},{96,112},{1... | collective-permute-start | bytes 491528 | tf_op jit(solution)/shard_map/ppermute | solution.py:492
  49.8 11.2 %collective-permute-start.9 = (f32[5,8,8,128]{3,2,1,0:T(8,128)S(1)}, f32[5,8,8,128]{3,2,1,0:T(8,128)S(1)}, u32[]{:S(2)}, u32[]{:S(2)}) collective-permute-start(f32[5,8,8,128]{3,2,1,0:T(8,128)S(1)} %get-tuple-element.26.own), channel_id=1, source_target_pairs={{16,0},{32,16},{48,32},{64,48},{80,64},{96,80},{112,96},{128,112},... | collective-permute-start | bytes 491528 | tf_op jit(solution)/shard_map/ppermute | solution.py:492
  53.5 4.4 %collective-permute-start.11 = (f32[5,4,8,128]{3,2,1,0:T(8,128)S(1)}, f32[5,4,8,128]{3,2,1,0:T(8,128)S(1)}, u32[]{:S(2)}, u32[]{:S(2)}) collective-permute-start(f32[5,4,8,128]{3,2,1,0:T(8,128)S(1)} %get-tuple-element.27), channel_id=1, source_target_pairs={{32,0},{48,16},{64,32},{80,48},{96,64},{112,80},{128,96},{144,112}... | collective-permute-start | bytes 245768 | tf_op jit(solution)/shard_map/ppermute | solution.py:492
  56.1 4.9 %collective-permute-start.12 = (f32[5,4,8,128]{3,2,1,0:T(8,128)S(1)}, f32[5,4,8,128]{3,2,1,0:T(8,128)S(1)}, u32[]{:S(2)}, u32[]{:S(2)}) collective-permute-start(f32[5,4,8,128]{3,2,1,0:T(8,128)S(1)} %get-tuple-element.28), channel_id=1, source_target_pairs={{224,0},{240,16},{0,32},{16,48},{32,64},{48,80},{64,96},{80,112},{... | collective-permute-start | bytes 245768 | tf_op jit(solution)/shard_map/ppermute | solution.py:492
  61.8 4.6 %collective-permute-start.13 = (f32[32,1280]{1,0:T(8,128)S(1)}, f32[32,1280]{1,0:T(8,128)S(1)}, u32[]{:S(2)}, u32[]{:S(2)}) collective-permute-start(f32[32,1280]{1,0:T(8,128)S(1)} %get-tuple-element.30), channel_id=1, source_target_pairs={{4,0},{8,4},{12,8},{0,12},{5,1},{9,5},{13,9},{1,13},{6,2},{10,6},{... | collective-permute-start | bytes 491528 | tf_op jit(solution)/shard_map/ppermute | solution.py:492
  61.9 6.0 %collective-permute-start.14 = (f32[32,1280]{1,0:T(8,128)S(1)}, f32[32,1280]{1,0:T(8,128)S(1)}, u32[]{:S(2)}, u32[]{:S(2)}) collective-permute-start(f32[32,1280]{1,0:T(8,128)S(1)} %get-tuple-element.31), channel_id=1, source_target_pairs={{12,0},{0,4},{4,8},{8,12},{13,1},{1,5},{5,9},{9,13},{14,2},{2,6},{... | collective-permute-start | bytes 491528 | tf_op jit(solution)/shard_map/ppermute | solution.py:492
where the time goes:
time: 114 us
  Pallas kernels  38.5 us (34%)
  waiting for transfers between devices  26.5 us (23%)
  starting transfers between devices  24.8 us (22%)
  blocking collectives  18.9 us (17%)
  local copies, waits for them, and re-layouts  4.66 us (4%)
    pallas_call x8, Pallas kernels, call(): pl.pallas_call(kernel, out_shape=[jax.ShapeDtypeStruct(s, F32) for s in o...  38.5 us
    ppermute x15, waiting for transfers between devices, shift(): lax.ppermute(value, axis, [((i + by) % count, i) for i in range(count)])  26.5 us
    ppermute x15, starting transfers between devices, shift(): lax.ppermute(value, axis, [((i + by) % count, i) for i in range(count)])  24.8 us
    all_to_all x1, blocking collectives, local(): got = lax.all_to_all(sent, ('gy', 'gx'), 0, 0)  18.9 us
    unnamed x12, local copies, waits for them, and re-layouts  4.66 us
  transfers between devices with their start and end apart: 15, of which 11 were waited for; matrix products, arithmetic and copies ran while one was open for 0% of the time, Pallas kernels for 0%

commit v1 on v0

v1 whole, which is shorter than its diff:
```python
import jax
import jax.numpy as jnp
from jax import lax
from jax.experimental import pallas as pl
from jax.experimental.pallas import tpu as pltpu
from jax.sharding import PartitionSpec as P

COARSE_SWEEPS = 8
W = 2.0 / 3.0
F32 = jnp.float32
UX, UY, UZ, RD, C, V = range(6)
SINK = RD
H = 5
Z0 = 8 + 2 * H

VMEM = pl.BlockSpec(memory_space=pltpu.VMEM)
SMEM = pl.BlockSpec(memory_space=pltpu.SMEM)
ANY = pl.BlockSpec(memory_space=pl.ANY)


def call(kernel, outs, *args, scratch=(), spaces=None):
    return pl.pallas_call(
        kernel,
        out_shape=[jax.ShapeDtypeStruct(s, F32) for s in outs],
        in_specs=spaces or [VMEM] * len(args),
        out_specs=[VMEM] * len(outs),
        scratch_shapes=[pltpu.VMEM(s, F32) if isinstance(s, tuple) else s for s in scratch],
        compiler_params=pltpu.CompilerParams(vmem_limit_bytes=24 * 2**20),
    )(*args)


def iota(shape, dim):
    return lax.broadcasted_iota(jnp.int32, shape, dim)


def up(a, dim):
    return pltpu.roll(a, a.shape[dim] - 1, dim)


def down(a, dim):
    return pltpu.roll(a, 1, dim)


def turn(a, by):
    by %= 128
    return pltpu.roll(a, by, a.ndim - 1) if by else a


def pick(a, index):
    return jnp.take_along_axis(a, index, axis=1, mode="promise_in_bounds")


def fold_lanes(a):
    return pick(a + up(a, 1), (2 * iota(a.shape, 1)) % 128)


def spread_lanes(a, first=0):
    return pick(a, first + iota(a.shape, 1) // 2)


def each(start, stop, body, unroll=1):
    if unroll >= stop - start:
        for z in range(start, stop):
            body(z)
        return

    def step(z, carry):
        body(z)
        return carry

    lax.fori_loop(start, stop, step, 0, unroll=unroll)


def wrap(z, n):
    return z % n if isinstance(z, int) else lax.rem(z + n, n)


def around(a, field, z, zm, zp):
    v = field(z)
    ux, uy = a[UX, z], a[UY, z]
    out = ux * up(v, 0) + down(ux * v, 0)
    out = out + (uy * up(v, 1) + down(uy * v, 1))
    return v, out + (a[UZ, z] * field(zp) + a[UZ, zm] * field(zm))


def smoothed(a, field, z, zm, zp):
    v, beside = around(a, field, z, zm, zp)
    return v * (1.0 / 3.0) + a[C, z] + a[RD, z] * beside


def finish(a, d, r, z, zm):
    ux, uy = a[UX, z], a[UY, z]
    diag = a[SINK, z] + a[UZ, z] + a[UZ, zm] + ux + down(ux, 0) + uy + down(uy, 1)
    d[z] = diag
    rd = jnp.where(diag > 0.0, W / jnp.where(diag > 0.0, diag, 1.0), 0.0)
    a[RD, z] = rd
    if r is not None:
        a[C, z] = rd * r[z]


def circ(n):
    return lambda z: (z, wrap(z - 1, n), wrap(z + 1, n))


def pre(a, d, r, res, n, unroll):
    c3 = circ(n)
    each(0, n, lambda z: finish(a, d, r, z, wrap(z - 1, n)), unroll)

    def one(z):
        a[V, z] = smoothed(a, lambda k: a[C, k], *c3(z))

    each(0, n, one, unroll)

    def two(z):
        v, beside = around(a, lambda k: a[V, k], *c3(z))
        res[z] = d[z] * (1.5 * a[C, z] - v) + beside

    each(0, n, two, unroll)


def halve(a, sink, r, t, store, n, rows):
    odd_row = iota((rows, 128), 0) % 2 == 1
    odd_lane = iota((rows, 128), 1) % 2 == 1

    def body(z):
        lo, hi = 2 * z, 2 * z + 1
        parts = (
            jnp.where(odd_row, a[UX, lo] + a[UX, hi], 0.0),
            jnp.where(odd_lane, a[UY, lo] + a[UY, hi], 0.0),
            a[UZ, hi],
            sink[lo] + sink[hi],
            r[lo] + r[hi],
        )
        for k, part in enumerate(parts):
            t[k, z] = part
        for k in range(5):
            store(k, z, fold_rows(t.at[k, z], rows // 2))

    each(0, n // 2, body, n)


def fold_rows(t, n):
    return t[pl.ds(0, n, stride=2), :] + t[pl.ds(1, n, stride=2), :]


def spread_rows(t, value):
    n = value.shape[0]
    t[pl.ds(0, n, stride=2), :] = value
    t[pl.ds(1, n, stride=2), :] = value
    return t[...]


def pack_z(f, b, s, d, lo, hi, own, fi, bi, sems):
    copies = [
        pltpu.make_async_copy(f, fi, sems.at[0]),
        pltpu.make_async_copy(b, bi, sems.at[1]),
        pltpu.make_async_copy(s, own.at[2], sems.at[2]),
        pltpu.make_async_copy(d, own.at[3], sems.at[3]),
    ]
    for copy in copies:
        copy.start()
    for k, copy in enumerate(copies):
        copy.wait()
        if k < 2:
            own[k] = (fi, bi)[k][...].astype(F32)
        lo[k] = own[k, 0:H]
        hi[k] = own[k, 8 - H : 8]


def pack_x(own, above, below, lo, hi):
    for out, row in ((lo, 0), (hi, 8)):
        out[:, 0:H] = below[:, :, row : row + 8]
        out[:, H : H + 8] = own[:, :, row : row + 8]
        out[:, H + 8 : Z0] = above[:, :, row : row + 8]


GROUPS0 = 4 * Z0 // 4


def pack_y(xl, xh, rl, rh, lo, hi):
    block = iota((8, 128), 1) // 8
    for g in range(GROUPS0):
        left = right = None
        for n in range(4):
            k, z = divmod(4 * g + n, Z0)
            for tile, ref in enumerate((xl, xh, rl, rh)):
                at = 4 * n + tile
                v = ref[k, z]
                a, b = turn(v, 8 * at), turn(v, 8 * at + 8)
                left = a if at == 0 else jnp.where(block == at, a, left)
                right = b if at == 0 else jnp.where(block == at, b, right)
        lo[g] = left
        hi[g] = right


def level0(pos, tables, xl, xh, rl, rh, yl, yh, a, packed, raw, hs, vs, dd, res, sk, t, m):
    gx, gy, gz = pos[0], pos[1], pos[2]
    lane8 = iota((8, 128), 1)
    for g in range(GROUPS0):
        right, left = yl[g], yh[g]
        for n in range(4):
            k, z = divmod(4 * g + n, Z0)
            for tile in range(4):
                at = 8 * (4 * n + tile)
                raw[k, z, 8 * tile : 8 * tile + 8, 128:256] = jnp.where(
                    lane8 < 8,
                    turn(right, -at),
                    jnp.where(lane8 >= 120, turn(left, 120 - at), 0.0),
                )
    for row, ref in ((0, xl), (8, xh), (16, rl), (24, rh)):
        raw[:, :, row : row + 8, 0:128] = ref[...]

    row, lane = iota((32, 256), 0), iota((32, 256), 1)
    x = gx * 16 + jnp.where(row < 24, row, row - 32)
    y = gy * 128 + jnp.where(lane < 192, lane, lane - 256)
    inside = (x >= 0) & (x < 256) & (y >= 0) & (y < 512)

    def materials(z):
        zg = gz * 8 + z - H
        here = inside & ((zg >= 0) & (zg < 32))
        kind = raw[0, z]
        h = jnp.full((32, 256), tables[0], F32)
        v = jnp.full((32, 256), tables[8], F32)
        for n in range(1, 8):
            is_n = kind == float(n)
            h = jnp.where(is_n, tables[n], h)
            v = jnp.where(is_n, tables[8 + n], v)
        hs[z] = jnp.where(here, h, 0.0)
        vs[z] = jnp.where(here, v, 0.0)

    each(0, Z0, materials, 2)

    def harmonic(c, n):
        s = c + n
        return 2.0 * c * n / jnp.where(s > 0.0, s, 1.0)

    def couple(z):
        h = hs[z]
        a[UX, z] = harmonic(h, up(h, 0))
        a[UY, z] = harmonic(h, up(h, 1))
        a[UZ, z] = harmonic(vs[z], vs[z + 1])

    each(0, Z0 - 1, couple, 2)

    odd_row, odd_lane = row % 2 == 1, lane % 2 == 1

    def setup(z):
        h, v = hs[z], vs[z]
        sink = jnp.where(raw[1, z] == 1.0, 2.0 * v, jnp.where(raw[1, z] == 2.0, 0.5 * h, 0.0))
        ux, uy, uz, lz = a[UX, z], a[UY, z], a[UZ, z], a[UZ, z - 1]
        lx, ly = down(ux, 0), down(uy, 1)
        diag = sink + lz + uz + lx + ux + ly + uy
        dens = raw[3, z]
        b = raw[2, z] + 0.5 * uz * (dens + raw[3, z + 1]) - 0.5 * lz * (raw[3, z - 1] + dens)
        rd = jnp.where(diag > 0.0, W / jnp.where(diag > 0.0, diag, 1.0), 0.0)
        a[RD, z] = rd
        a[C, z] = rd * b
        dd[z] = diag
        sk[z] = sink
        outer = sink + jnp.where(odd_row, ux, lx) + jnp.where(odd_lane, uy, ly)
        hs[z] = outer + jnp.where((z - H) % 2 == 1, uz, lz)

    each(1, Z0 - 1, setup, 2)

    def first(z):
        a[V, z] = smoothed(a, lambda k: a[C, k], z, z - 1, z + 1)

    each(2, Z0 - 2, first, 2)

    def residual(z):
        v, beside = around(a, lambda k: a[V, k], z, z - 1, z + 1)
        res[z - H] = (dd[z] * (1.5 * a[C, z] - v) + beside)[0:16, 0:128]

    each(H, H + 8, residual, 2)

    o_row = iota((16, 128), 0) % 2 == 1
    o_lane = iota((16, 128), 1) % 2 == 1

    def coarsen(z):
        lo, hi = H + 2 * z, H + 2 * z + 1

        def both(ref):
            return ref[lo, 0:16, 0:128] + ref[hi, 0:16, 0:128]

        parts = (
            jnp.where(o_row, both(a.at[UX]), 0.0),
            jnp.where(o_lane, both(a.at[UY]), 0.0),
            a[UZ, hi, 0:16, 0:128],
            both(sk),
            res[2 * z] + res[2 * z + 1],
            both(hs),
        )
        for k, part in enumerate(parts):
            t[k, z] = part
        for k in range(6):
            m[k, z] = fold_rows(t.at[k, z], 8)

    each(0, 4, coarsen, 4)
    lower = lane8 < 64
    for s in range(2):
        parts = [jnp.where(lower, fold_lanes(m[k, s]), fold_lanes(m[k, 2 + s])) for k in range(6)]
        for k in range(4):
            packed[k, s] = parts[k]
        packed[4, s] = W * parts[4] / parts[5]


def pack_x1(own, b1, b2, b3, full, lo, hi):
    for n, ref in enumerate((own, b1, b2, b3)):
        full[:, 2 * n : 2 * n + 2] = ref[...]
        first, second = ref[:, 0], ref[:, 1]
        lo[:, n] = jnp.concatenate([first[:, 0:4], second[:, 0:4]], axis=1)
        hi[:, n] = jnp.concatenate([first[:, 4:8], second[:, 4:8]], axis=1)


def pack_y1(own, r1, l1, r2, l2, whole, lo, hi):
    whole[:, :, 0:8] = own[...]
    whole[:, :, 8:16] = r1[...]
    whole[:, :, 24:32] = l1[...]
    for n in range(4):
        for s in range(2):
            part = slice(4 * s, 4 * s + 4)
            whole[:, 2 * n + s, 16:24] = jnp.concatenate([r2[:, n, part], l2[:, n, part]], axis=1)
    block = (iota((8, 128), 1) // 16) % 4
    for k in range(5):
        for n in range(8):
            left = right = None
            for tile in range(4):
                v = whole[k, n, 8 * tile : 8 * tile + 8]
                a, b = turn(v, 16 * tile), turn(v, 16 * tile + 80)
                left = a if tile == 0 else jnp.where(block == tile, a, left)
                right = b if tile == 0 else jnp.where(block == tile, b, right)
            lo[k, n] = left
            hi[k, n] = right


def level12(pos, whole, yl, yh, a, b, sent, d1, r1, t1, m1, d2, r2, s1, s2, q2):
    gx, gy, gz = pos[0], pos[1], pos[2]
    row, lane = iota((8, 128), 0), iota((8, 128), 1)
    y = gy * 64 + jnp.where(lane < 96, lane, lane - 128)
    in_y = (y >= 0) & (y < 256)
    for tile in range(4):
        x = gx * 8 + jnp.where(8 * tile + row < 20, 8 * tile + row, 8 * tile + row - 32)
        inside = in_y & (x >= 0) & (x < 128)
        rows = slice(8 * tile, 8 * tile + 8)
        for k in range(5):
            for n in range(8):
                v, right, left = whole[k, n, rows], yl[k, n], yh[k, n]
                for part in range(2):
                    own = turn(v, 64 * part)
                    beyond = jnp.where(
                        lane < 80,
                        turn(right, 64 - 64 * part - 16 * tile),
                        jnp.where(lane >= 112, turn(left, 112 - 64 * part - 16 * tile), 0.0),
                    )
                    value = jnp.where(inside, jnp.where(lane < 64, own, beyond), 0.0)
                    z = 4 * (n // 2) + 2 * part + n % 2
                    a[k, z, rows] = value
                    if k == SINK:
                        s1[z, rows] = value
    pre(a, d1, None, r1, 16, 4)

    def keep1(k, z, value):
        value = fold_lanes(value)
        if k < 4:
            b[k, z] = value
        if k == SINK:
            s2[z] = value
        if k == 4:
            q2[z] = value

    halve(a, s1, r1, t1, keep1, 16, 32)
    pre(b, d2, q2, r2, 8, 8)

    def keep2(k, z, value):
        m1[z, 0, k : k + 1] = value[0:1]
        m1[z, 1, k : k + 1] = value[1:2]

    m1[...] = jnp.zeros((4, 2, 8, 128), F32)
    halve(b, s2, r2, t1.at[:, :, 0:16], keep2, 8, 16)
    total = jnp.zeros((8, 128), F32)
    for z in range(4):
        zg = lax.rem(z + gz, 4)
        for s in range(2):
            v = m1[z, s]
            v = pick(v + up(v, 1), 2 * (lane % 16))
            total = jnp.where(lane // 16 == 2 * zg + s, v, total)
    sent[...] = jnp.broadcast_to(total[None], (64, 8, 128))


def sweep(a, src, dst, n, unroll):
    c3 = circ(n)

    def body(z):
        dst[z] = smoothed(a, lambda k: src[k], *c3(z))

    each(0, n, body, unroll)


def solve(
    pos, got, a0, a1, a2, pressure, left,
    a3, a4, d3, d4, r3, r4, s3, s4, t3, q5, e1, e2, e3, e4, f2, g4, g3, g2, g1, g0, b3, w0,
):
    gx, gy, gz = pos[0], pos[1], pos[2]
    lane = iota((16, 128), 1)
    for k in range(5):
        rows = [got[pl.ds(g * 128 + k, 16, stride=8), :] for g in range(4)]
        for z in range(4):
            for s in range(2):
                at = (z * 2 + s) * 16
                value = turn(rows[0], -at)
                for g in range(1, 4):
                    value = jnp.where(lane // 16 == g, turn(rows[g], 16 * g - at), value)
                value = jnp.where(lane < 64, value, turn(value, 64))
                if k < 4:
                    a3[k, z, pl.ds(s, 16, stride=2), :] = value
                else:
                    r3[z, pl.ds(s, 16, stride=2), :] = value
    s3[...] = a3[SINK]
    pre(a3, d3, r3, e3, 4, 4)

    def keep3(k, z, value):
        value = fold_lanes(value)
        if k < 4:
            a4[k, z] = value
        if k == SINK:
            s4[z] = value
        if k == 4:
            r4[z] = value

    halve(a3, s3, e3, t3, keep3, 4, 32)
    pre(a4, d4, r4, e4, 2, 2)

    def keep4(k, z, value):
        q5[k] = fold_lanes(value)

    halve(a4, s4, e4, t3.at[:, :, 0:16], keep4, 2, 16)
    ux, uy, uz, sink, r = q5[0], q5[1], q5[2], q5[3], q5[4]
    lx, ly = down(ux, 0), down(uy, 1)
    diag = sink + uz + uz + ux + lx + uy + ly
    rd = W / diag
    c = rd * r
    ux, lx, uy, ly = rd * ux, rd * lx, rd * uy, rd * ly
    v = c
    for _ in range(COARSE_SWEEPS - 1):
        beside = (ux * up(v, 0) + lx * down(v, 0)) + (uy * up(v, 1) + ly * down(v, 1))
        v = (v * (1.0 / 3.0) + c) + beside

    e = spread_rows(g4, spread_lanes(v))
    for z in range(2):
        a4[V, z] = a4[V, z] + e
    sweep(a4, a4.at[V], e4, 2, 2)
    sweep(a4, e4, r4, 2, 2)
    for z in range(2):
        e = spread_rows(g3.at[z], spread_lanes(r4[z]))
        a3[V, 2 * z] = a3[V, 2 * z] + e
        a3[V, 2 * z + 1] = a3[V, 2 * z + 1] + e
    sweep(a3, a3.at[V], e3, 4, 4)
    sweep(a3, e3, r3, 4, 4)
    b3[:, 8:40] = r3[...]
    b3[:, 0:8] = r3[:, 24:32]
    b3[:, 40:48] = r3[:, 0:8]
    lane = iota((8, 128), 1) % 64
    index = jnp.where(lane < 40, lane // 2, lane // 2 - 32) + 16 * gy
    index = lax.rem(index + 64, 64)
    for z in range(4):
        e = b3[lax.rem(z + gz, 4), pl.ds(2 * gx + 5, 8), :]
        e = pick(pltpu.roll(e, 5, 0), index)
        e = spread_rows(g2.at[z], e)
        e2[2 * z] = a2[V, 2 * z] + e
        e2[2 * z + 1] = a2[V, 2 * z + 1] + e
    sweep(a2, e2, f2, 8, 8)
    sweep(a2, f2, e2, 8, 8)
    for z in range(8):
        e = spread_rows(g1.at[z], spread_lanes(e2[z]))
        e1[0, 2 * z] = a1[V, 2 * z] + e
        e1[0, 2 * z + 1] = a1[V, 2 * z + 1] + e
    sweep(a1, e1.at[0], e1.at[1], 16, 4)
    sweep(a1, e1.at[1], e1.at[0], 16, 4)
    upper = iota((8, 128), 0) < 4
    for zc in range(-2, 6):
        v = e1[0, zc % 16]
        v = jnp.concatenate([v[0:8], jnp.where(upper, v[8:16], v[24:32])], axis=0)
        for half in range(2):
            e = spread_rows(g0.at[half, zc + 2], spread_lanes(v, 64 * half))
            lanes = slice(128 * half, 128 * half + 128)
            for z in (2 * zc, 2 * zc + 1):
                if -3 <= z <= 10:
                    w0[0, z + H, :, lanes] = a0[V, z + H, :, lanes] + e

    def sweep0(src, dst):
        def body(z):
            w0[dst, z] = smoothed(a0, lambda k: w0[src, k], z, z - 1, z + 1)

        return body

    each(3, Z0 - 3, sweep0(0, 1), 2)
    each(4, Z0 - 4, sweep0(1, 0), 2)

    def last(z):
        v, beside = around(a0, lambda k: w0[0, k], z, z - 1, z + 1)
        r = W / a0[RD, z] * (1.5 * a0[C, z] - v) + beside
        pressure[z - H] = v[0:16, 0:128]
        left[z - H] = r[0:16, 0:128]

    each(H, H + 8, last, 2)


def shift(value, axis, by):
    count = lax.axis_size(axis)
    return lax.ppermute(value, axis, [((i + by) % count, i) for i in range(count)])


def local(facies, boundary, hc, vc, source, density):
    pos = jnp.stack([lax.axis_index(n) for n in ("gx", "gy", "gz")]).astype(jnp.int32)
    tables = jnp.concatenate([hc, vc])
    lo, hi, own = call(
        pack_z,
        [(4, H, 16, 128)] * 2 + [(4, 8, 16, 128)],
        facies, boundary, source, density,
        spaces=[ANY] * 4,
        scratch=[
            pltpu.VMEM((8, 16, 128), jnp.int32), pltpu.VMEM((8, 16, 128), jnp.int32),
            pltpu.SemaphoreType.DMA((4,)),
        ],
    )
    above, below = shift(lo, "gz", 1), shift(hi, "gz", -1)
    xl, xh = call(pack_x, [(4, Z0, 8, 128)] * 2, own, above, below)
    rl, rh = shift(xl, "gx", 1), shift(xh, "gx", -1)
    lo, hi = call(pack_y, [(GROUPS0, 8, 128)] * 2, xl, xh, rl, rh)
    yl, yh = shift(lo, "gy", 1), shift(hi, "gy", -1)
    a0, packed = call(
        level0,
        [(6, Z0, 32, 256), (5, 2, 8, 128)],
        pos, tables, xl, xh, rl, rh, yl, yh,
        spaces=[SMEM] * 2 + [VMEM] * 6,
        scratch=[
            (4, Z0, 32, 256), (Z0, 32, 256), (Z0, 32, 256), (Z0, 32, 256), (8, 16, 128),
            (Z0, 32, 256), (6, 4, 16, 128), (6, 4, 8, 128),
        ],
    )
    blocks = [shift(packed, "gz", n) for n in (1, 2, 3)]
    full, lo, hi = call(
        pack_x1, [(5, 8, 8, 128), (5, 4, 8, 128), (5, 4, 8, 128)], packed, *blocks
    )
    r1, l1 = shift(full, "gx", 1), shift(full, "gx", -1)
    r2, l2 = shift(lo, "gx", 2), shift(hi, "gx", -2)
    whole, lo, hi = call(
        pack_y1, [(5, 8, 32, 128), (5, 8, 8, 128), (5, 8, 8, 128)], full, r1, l1, r2, l2
    )
    yl, yh = shift(lo, "gy", 1), shift(hi, "gy", -1)
    a1, a2, sent = call(
        level12,
        [(6, 16, 32, 128), (6, 8, 16, 128), (64, 8, 128)],
        pos, whole, yl, yh,
        spaces=[SMEM] + [VMEM] * 3,
        scratch=[
            (16, 32, 128), (16, 32, 128), (5, 8, 32, 128), (4, 2, 8, 128),
            (8, 16, 128), (8, 16, 128), (16, 32, 128), (8, 16, 128), (8, 16, 128),
        ],
    )
    got = lax.all_to_all(sent, ("gy", "gx"), 0, 0)
    return tuple(
        call(
            solve,
            [(8, 16, 128), (8, 16, 128)],
            pos, got.reshape(512, 128), a0, a1, a2,
            spaces=[SMEM] + [VMEM] * 4,
            scratch=[
                (6, 4, 32, 128), (6, 2, 16, 128),
                (4, 32, 128), (2, 16, 128),
                (4, 32, 128), (2, 16, 128), (4, 32, 128), (2, 16, 128),
                (5, 2, 32, 128), (5, 8, 128),
                (2, 16, 32, 128), (8, 16, 128), (4, 32, 128), (2, 16, 128), (8, 16, 128),
                (16, 128), (2, 32, 128), (4, 16, 128), (8, 32, 128), (2, 8, 32, 128),
                (4, 48, 128), (2, Z0, 32, 256),
            ],
        )
    )


def solution(mesh):
    split = P("gz", "gx", "gy")
    return jax.shard_map(
        local,
        mesh=mesh,
        in_specs=(split, split, P(), P(), split, split),
        out_specs=(split, split),
        check_vma=False,
    )
```

time: 114 us -> 91.1 us (0.80)
  Pallas kernels: 38.5 us -> 16.4 us
  local copies, waits for them, and re-layouts: 4.66 us -> 3.35 us
    pallas_call x8, Pallas kernels: 38.5 us -> 16.4 us  [call(): pl.pallas_call(kernel, out_shape=[jax.ShapeDtypeStruct(s, F32) for s in o...]
    unnamed x12 -> x8, local copies, waits for them, and re-layouts: 4.66 us -> 3.35 us
  transfers between devices with their start and end apart: 15 -> 15, of which waited for: 11 -> 12; matrix products, arithmetic and copies ran while one was open for 0% -> 1% of each run, Pallas kernels for 0% -> 0%
where the time goes in v1:
time: 91.1 us; the launch traced here: 90.8 us
  waiting for transfers between devices  25.5 us (28%)
  starting transfers between devices  24.9 us (27%)
  blocking collectives  19.1 us (21%)
  Pallas kernels  16.4 us (18%)
  local copies, waits for them, and re-layouts  3.35 us (4%)
    ppermute x15, waiting for transfers between devices, shift(): lax.ppermute(value, axis, [((i + by) % count, i) for i in range(count)])  25.5 us
    ppermute x15, starting transfers between devices, shift(): lax.ppermute(value, axis, [((i + by) % count, i) for i in range(count)])  24.9 us
    all_to_all x1, blocking collectives, local(): got = lax.all_to_all(sent, ('gy', 'gx'), 0, 0)  19.1 us
    pallas_call x8, Pallas kernels, call(): pl.pallas_call(kernel, out_shape=[jax.ShapeDtypeStruct(s, F32) for s in o...  16.4 us
    unnamed x8, local copies, waits for them, and re-layouts  3.35 us
  transfers between devices with their start and end apart: 15, of which 12 were waited for; matrix products, arithmetic and copies ran while one was open for 1% of the time, Pallas kernels for 0%

profile of v1, /device:TPU:1, one launch (start us, length us, event | category | flops | bytes accessed | tf_op | source)
XLA Modules:
  0.0 90.8 jit_solution(13272849706607812241)
XLA Ops:
  0.6 0.8 copy-done
  1.5 0.8 copy-done.1
  2.3 0.8 copy-done.2
  3.2 0.8 copy-done.3
  4.4 3.4 %collective-permute-start = (f32[4,5,16,128]{3,2,1,0:T(8,128)S(1)}, f32[4,5,16,128]{3,2,1,0:T(8,128)S(1)}, u32[]{:S(2)}, u32[]{:S(2)}) collective-permute-start(f32[4,5,16,128]{3,2,1,0:T(8,128)S(1)} %get-tuple-element.21), channel_id=1, source_target_pairs={{1,0},{2,1},{3,2},{0,3},{5,4},{6,5},{7,6},{4,7},{9,8},{10,9},{11,1... | collective-permute-start | bytes 491528 | tf_op jit(solution)/shard_map/ppermute | solution.py:510
  7.8 2.9 %collective-permute-done.above = f32[4,5,16,128]{3,2,1,0:T(8,128)S(1)} collective-permute-done((f32[4,5,16,128]{3,2,1,0:T(8,128)S(1)}, f32[4,5,16,128]{3,2,1,0:T(8,128)S(1)}, u32[]{:S(2)}, u32[]{:S(2)}) %collective-permute-start) | collective-permute-done | bytes 163872 | tf_op jit(solution)/shard_map/ppermute | solution.py:510
  10.6 3.1 %collective-permute-done.1.below = f32[4,5,16,128]{3,2,1,0:T(8,128)S(1)} collective-permute-done((f32[4,5,16,128]{3,2,1,0:T(8,128)S(1)}, f32[4,5,16,128]{3,2,1,0:T(8,128)S(1)}, u32[]{:S(2)}, u32[]{:S(2)}) %collective-permute-start.1) | collective-permute-done | bytes 163872 | tf_op jit(solution)/shard_map/ppermute | solution.py:510
  13.8 1.9 %collective-permute-start.2 = (f32[4,18,8,128]{3,2,1,0:T(8,128)S(1)}, f32[4,18,8,128]{3,2,1,0:T(8,128)S(1)}, u32[]{:S(2)}, u32[]{:S(2)}) collective-permute-start(f32[4,18,8,128]{3,2,1,0:T(8,128)S(1)} %get-tuple-element.23.xl), channel_id=1, source_target_pairs={{16,0},{32,16},{48,32},{64,48},{80,64},{96,80},{112,96},{128,112},... | collective-permute-start | bytes 884744 | tf_op jit(solution)/shard_map/ppermute | solution.py:510
  15.6 1.5 %collective-permute-start.3 = (f32[4,18,8,128]{3,2,1,0:T(8,128)S(1)}, f32[4,18,8,128]{3,2,1,0:T(8,128)S(1)}, u32[]{:S(2)}, u32[]{:S(2)}) collective-permute-start(f32[4,18,8,128]{3,2,1,0:T(8,128)S(1)} %get-tuple-element.24.xh), channel_id=1, source_target_pairs={{240,0},{0,16},{16,32},{32,48},{48,64},{64,80},{80,96},{96,112},{1... | collective-permute-start | bytes 884744 | tf_op jit(solution)/shard_map/ppermute | solution.py:510
  17.2 0.7 pad_maximum_fusion.tables
  17.9 3.6 %collective-permute-done.2.rl = f32[4,18,8,128]{3,2,1,0:T(8,128)S(1)} collective-permute-done((f32[4,18,8,128]{3,2,1,0:T(8,128)S(1)}, f32[4,18,8,128]{3,2,1,0:T(8,128)S(1)}, u32[]{:S(2)}, u32[]{:S(2)}) %collective-permute-start.2) | collective-permute-done | bytes 294944 | tf_op jit(solution)/shard_map/ppermute | solution.py:510
  21.6 0.6 shard_map.79
  22.2 2.8 %collective-permute-start.4 = (f32[18,8,128]{2,1,0:T(8,128)S(1)}, f32[18,8,128]{2,1,0:T(8,128)S(1)}, u32[]{:S(2)}, u32[]{:S(2)}) collective-permute-start(f32[18,8,128]{2,1,0:T(8,128)S(1)} %get-tuple-element.25), channel_id=1, source_target_pairs={{4,0},{8,4},{12,8},{0,12},{5,1},{9,5},{13,9},{1,13},{6,2},{10,6},{... | collective-permute-start | bytes 221192 | tf_op jit(solution)/shard_map/ppermute | solution.py:510
  25.1 1.3 %collective-permute-done.4.yl = f32[18,8,128]{2,1,0:T(8,128)S(1)} collective-permute-done((f32[18,8,128]{2,1,0:T(8,128)S(1)}, f32[18,8,128]{2,1,0:T(8,128)S(1)}, u32[]{:S(2)}, u32[]{:S(2)}) %collective-permute-start.4) | collective-permute-done | bytes 73760 | tf_op jit(solution)/shard_map/ppermute | solution.py:510
  26.4 3.0 %collective-permute-done.5.yh = f32[18,8,128]{2,1,0:T(8,128)S(1)} collective-permute-done((f32[18,8,128]{2,1,0:T(8,128)S(1)}, f32[18,8,128]{2,1,0:T(8,128)S(1)}, u32[]{:S(2)}, u32[]{:S(2)}) %collective-permute-start.5) | collective-permute-done | bytes 73760 | tf_op jit(solution)/shard_map/ppermute | solution.py:510
  29.4 5.1 %shard_map.80 = (f32[6,18,32,256]{3,2,1,0:T(8,128)S(1)}, f32[5,2,8,128]{3,2,1,0:T(8,128)S(1)}) custom-call(s32[3]{0:T(128)S(1)} %pad_add_fusion.pos, f32[16]{0:T(128)S(1)} %pad_maximum_fusion.tables, f32[4,18,8,128]{3,2,1,0:T(8,128)S(1)} %get-tuple-element.23.xl, f32[4,18,8,128]{3,2,1,0:T(8,128)S(1)} %get-tuple-element.24.xh, ...), custom_call_target="tpu_custom_call" | custom-call | tf_op jit(solution)/shard_map/pallas_call | solution.py:22
  34.7 1.2 %collective-permute-start.7 = (f32[5,2,8,128]{3,2,1,0:T(8,128)S(1)}, f32[5,2,8,128]{3,2,1,0:T(8,128)S(1)}, u32[]{:S(2)}, u32[]{:S(2)}) collective-permute-start(f32[5,2,8,128]{3,2,1,0:T(8,128)S(1)} %get-tuple-element.27.own), channel_id=1, source_target_pairs={{2,0},{3,1},{0,2},{1,3},{6,4},{7,5},{4,6},{5,7},{10,8},{11,9},{8,1... | collective-permute-start | bytes 122888 | tf_op jit(solution)/shard_map/ppermute | solution.py:510
  35.8 1.5 %collective-permute-start.6 = (f32[5,2,8,128]{3,2,1,0:T(8,128)S(1)}, f32[5,2,8,128]{3,2,1,0:T(8,128)S(1)}, u32[]{:S(2)}, u32[]{:S(2)}) collective-permute-start(f32[5,2,8,128]{3,2,1,0:T(8,128)S(1)} %get-tuple-element.27.own), channel_id=1, source_target_pairs={{1,0},{2,1},{3,2},{0,3},{5,4},{6,5},{7,6},{4,7},{9,8},{10,9},{11,1... | collective-permute-start | bytes 122888 | tf_op jit(solution)/shard_map/ppermute | solution.py:510
  37.3 1.4 %collective-permute-done.8.b3 = f32[5,2,8,128]{3,2,1,0:T(8,128)S(1)} collective-permute-done((f32[5,2,8,128]{3,2,1,0:T(8,128)S(1)}, f32[5,2,8,128]{3,2,1,0:T(8,128)S(1)}, u32[]{:S(2)}, u32[]{:S(2)}) %collective-permute-start.8) | collective-permute-done | bytes 40992 | tf_op jit(solution)/shard_map/ppermute | solution.py:510
  38.7 0.4 collective-permute-done.7.b2
  39.2 0.6 collective-permute-done.6.b1
  39.8 4.6 %collective-permute-start.10 = (f32[5,8,8,128]{3,2,1,0:T(8,128)S(1)}, f32[5,8,8,128]{3,2,1,0:T(8,128)S(1)}, u32[]{:S(2)}, u32[]{:S(2)}) collective-permute-start(f32[5,8,8,128]{3,2,1,0:T(8,128)S(1)} %get-tuple-element.28.own), channel_id=1, source_target_pairs={{240,0},{0,16},{16,32},{32,48},{48,64},{64,80},{80,96},{96,112},{1... | collective-permute-start | bytes 491528 | tf_op jit(solution)/shard_map/ppermute | solution.py:510
  44.4 3.8 %collective-permute-start.9 = (f32[5,8,8,128]{3,2,1,0:T(8,128)S(1)}, f32[5,8,8,128]{3,2,1,0:T(8,128)S(1)}, u32[]{:S(2)}, u32[]{:S(2)}) collective-permute-start(f32[5,8,8,128]{3,2,1,0:T(8,128)S(1)} %get-tuple-element.28.own), channel_id=1, source_target_pairs={{16,0},{32,16},{48,32},{64,48},{80,64},{96,80},{112,96},{128,112},... | collective-permute-start | bytes 491528 | tf_op jit(solution)/shard_map/ppermute | solution.py:510
  48.2 2.6 %collective-permute-start.11 = (f32[5,4,8,128]{3,2,1,0:T(8,128)S(1)}, f32[5,4,8,128]{3,2,1,0:T(8,128)S(1)}, u32[]{:S(2)}, u32[]{:S(2)}) collective-permute-start(f32[5,4,8,128]{3,2,1,0:T(8,128)S(1)} %get-tuple-element.29), channel_id=1, source_target_pairs={{32,0},{48,16},{64,32},{80,48},{96,64},{112,80},{128,96},{144,112}... | collective-permute-start | bytes 245768 | tf_op jit(solution)/shard_map/ppermute | solution.py:510
  50.8 1.8 %collective-permute-done.11.r2 = f32[5,4,8,128]{3,2,1,0:T(8,128)S(1)} collective-permute-done((f32[5,4,8,128]{3,2,1,0:T(8,128)S(1)}, f32[5,4,8,128]{3,2,1,0:T(8,128)S(1)}, u32[]{:S(2)}, u32[]{:S(2)}) %collective-permute-start.11) | collective-permute-done | bytes 81952 | tf_op jit(solution)/shard_map/ppermute | solution.py:510
  52.6 3.1 %collective-permute-done.12.l2 = f32[5,4,8,128]{3,2,1,0:T(8,128)S(1)} collective-permute-done((f32[5,4,8,128]{3,2,1,0:T(8,128)S(1)}, f32[5,4,8,128]{3,2,1,0:T(8,128)S(1)}, u32[]{:S(2)}, u32[]{:S(2)}) %collective-permute-start.12) | collective-permute-done | bytes 81952 | tf_op jit(solution)/shard_map/ppermute | solution.py:510
  56.1 1.5 %collective-permute-start.14 = (f32[5,8,8,128]{3,2,1,0:T(8,128)S(1)}, f32[5,8,8,128]{3,2,1,0:T(8,128)S(1)}, u32[]{:S(2)}, u32[]{:S(2)}) collective-permute-start(f32[5,8,8,128]{3,2,1,0:T(8,128)S(1)} %get-tuple-element.33), channel_id=1, source_target_pairs={{12,0},{0,4},{4,8},{8,12},{13,1},{1,5},{5,9},{9,13},{14,2},{2,6},{... | collective-permute-start | bytes 491528 | tf_op jit(solution)/shard_map/ppermute | solution.py:510
  57.5 3.0 %collective-permute-done.13.yl = f32[5,8,8,128]{3,2,1,0:T(8,128)S(1)} collective-permute-done((f32[5,8,8,128]{3,2,1,0:T(8,128)S(1)}, f32[5,8,8,128]{3,2,1,0:T(8,128)S(1)}, u32[]{:S(2)}, u32[]{:S(2)}) %collective-permute-start.13) | collective-permute-done | bytes 163872 | tf_op jit(solution)/shard_map/ppermute | solution.py:510
  60.5 1.3 %collective-permute-done.14.yh = f32[5,8,8,128]{3,2,1,0:T(8,128)S(1)} collective-permute-done((f32[5,8,8,128]{3,2,1,0:T(8,128)S(1)}, f32[5,8,8,128]{3,2,1,0:T(8,128)S(1)}, u32[]{:S(2)}, u32[]{:S(2)}) %collective-permute-start.14) | collective-permute-done | bytes 163872 | tf_op jit(solution)/shard_map/ppermute | solution.py:510
  61.9 3.5 %shard_map.83 = (f32[6,16,32,128]{3,2,1,0:T(8,128)S(1)}, f32[6,8,16,128]{3,2,1,0:T(8,128)S(1)}, f32[64,8,128]{2,1,0:T(8,128)S(1)}) custom-call(s32[3]{0:T(128)S(1)} %pad_add_fusion.pos, f32[5,8,32,128]{3,2,1,0:T(8,128)S(1)} %get-tuple-element.31.whole, f32[5,8,8,128]{3,2,1,0:T(8,128)S(1)} %collective-permute-done.13.yl, ...), custom_call_target="tpu_custom_call" | custom-call | tf_op jit(solution)/shard_map/pallas_call | solution.py:22
  65.4 19.1 %all_to_all.5 = f32[64,8,128]{2,1,0:T(8,128)S(1)} all-to-all(f32[64,8,128]{2,1,0:T(8,128)S(1)} %get-tuple-element.34), channel_id=1, replica_groups=mesh['gx'=16,'gy'=4,'gz'=4] {'gy','gx'}, dimensions={0} | all-to-all | bytes 524288 | tf_op jit(solution)/shard_map/all_to_all | solution.py:561
  84.4 6.4 %shard_map.84 = (f32[8,16,128]{2,1,0:T(8,128)}, f32[8,16,128]{2,1,0:T(8,128)}) custom-call(s32[3]{0:T(128)S(1)} %pad_add_fusion.pos, f32[512,128]{1,0:T(8,128)S(1)} %bitcast.4, f32[6,18,32,256]{3,2,1,0:T(8,128)S(1)} %get-tuple-element.35.a0, f32[6,16,32,128]{3,2,1,0:T(8,128)S(1)} %get-tuple-element.36.a1, f32[6,8,16,128]{3,2,1,0:T(8,128)S(1)} %get-tuple-element.37.a2), custom_call_target="tpu_custom_call" | custom-call | tf_op jit(solution)/shard_map/pallas_call | solution.py:22
  (17 shorter events, 1.0 us)
Async XLA Ops:
  0.6 0.8 copy-start
  1.5 0.8 copy-start.1
  2.3 0.8 copy-start.2
  3.2 0.8 copy-start.3
  4.4 6.3 %collective-permute-start = (f32[4,5,16,128]{3,2,1,0:T(8,128)S(1)}, f32[4,5,16,128]{3,2,1,0:T(8,128)S(1)}, u32[]{:S(2)}, u32[]{:S(2)}) collective-permute-start(f32[4,5,16,128]{3,2,1,0:T(8,128)S(1)} %get-tuple-element.21), channel_id=1, source_target_pairs={{1,0},{2,1},{3,2},{0,3},{5,4},{6,5},{7,6},{4,7},{9,8},{10,9},{11,1... | collective-permute-start | bytes 491528 | tf_op jit(solution)/shard_map/ppermute | solution.py:510
  7.8 6.0 %collective-permute-start.1 = (f32[4,5,16,128]{3,2,1,0:T(8,128)S(1)}, f32[4,5,16,128]{3,2,1,0:T(8,128)S(1)}, u32[]{:S(2)}, u32[]{:S(2)}) collective-permute-start(f32[4,5,16,128]{3,2,1,0:T(8,128)S(1)} %get-tuple-element.22), channel_id=1, source_target_pairs={{3,0},{0,1},{1,2},{2,3},{7,4},{4,5},{5,6},{6,7},{11,8},{8,9},{9,10... | collective-permute-start | bytes 491528 | tf_op jit(solution)/shard_map/ppermute | solution.py:510
  13.8 7.8 %collective-permute-start.2 = (f32[4,18,8,128]{3,2,1,0:T(8,128)S(1)}, f32[4,18,8,128]{3,2,1,0:T(8,128)S(1)}, u32[]{:S(2)}, u32[]{:S(2)}) collective-permute-start(f32[4,18,8,128]{3,2,1,0:T(8,128)S(1)} %get-tuple-element.23.xl), channel_id=1, source_target_pairs={{16,0},{32,16},{48,32},{64,48},{80,64},{96,80},{112,96},{128,112},... | collective-permute-start | bytes 884744 | tf_op jit(solution)/shard_map/ppermute | solution.py:510
  15.6 5.9 %collective-permute-start.3 = (f32[4,18,8,128]{3,2,1,0:T(8,128)S(1)}, f32[4,18,8,128]{3,2,1,0:T(8,128)S(1)}, u32[]{:S(2)}, u32[]{:S(2)}) collective-permute-start(f32[4,18,8,128]{3,2,1,0:T(8,128)S(1)} %get-tuple-element.24.xh), channel_id=1, source_target_pairs={{240,0},{0,16},{16,32},{32,48},{48,64},{64,80},{80,96},{96,112},{1... | collective-permute-start | bytes 884744 | tf_op jit(solution)/shard_map/ppermute | solution.py:510
  22.2 4.2 %collective-permute-start.4 = (f32[18,8,128]{2,1,0:T(8,128)S(1)}, f32[18,8,128]{2,1,0:T(8,128)S(1)}, u32[]{:S(2)}, u32[]{:S(2)}) collective-permute-start(f32[18,8,128]{2,1,0:T(8,128)S(1)} %get-tuple-element.25), channel_id=1, source_target_pairs={{4,0},{8,4},{12,8},{0,12},{5,1},{9,5},{13,9},{1,13},{6,2},{10,6},{... | collective-permute-start | bytes 221192 | tf_op jit(solution)/shard_map/ppermute | solution.py:510
  25.0 4.4 %collective-permute-start.5 = (f32[18,8,128]{2,1,0:T(8,128)S(1)}, f32[18,8,128]{2,1,0:T(8,128)S(1)}, u32[]{:S(2)}, u32[]{:S(2)}) collective-permute-start(f32[18,8,128]{2,1,0:T(8,128)S(1)} %get-tuple-element.26), channel_id=1, source_target_pairs={{12,0},{0,4},{4,8},{8,12},{13,1},{1,5},{5,9},{9,13},{14,2},{2,6},{... | collective-permute-start | bytes 221192 | tf_op jit(solution)/shard_map/ppermute | solution.py:510
  34.6 4.2 %collective-permute-start.8 = (f32[5,2,8,128]{3,2,1,0:T(8,128)S(1)}, f32[5,2,8,128]{3,2,1,0:T(8,128)S(1)}, u32[]{:S(2)}, u32[]{:S(2)}) collective-permute-start(f32[5,2,8,128]{3,2,1,0:T(8,128)S(1)} %get-tuple-element.27.own), channel_id=1, source_target_pairs={{3,0},{0,1},{1,2},{2,3},{7,4},{4,5},{5,6},{6,7},{11,8},{8,9},{9,10... | collective-permute-start | bytes 122888 | tf_op jit(solution)/shard_map/ppermute | solution.py:510
  34.7 4.5 %collective-permute-start.7 = (f32[5,2,8,128]{3,2,1,0:T(8,128)S(1)}, f32[5,2,8,128]{3,2,1,0:T(8,128)S(1)}, u32[]{:S(2)}, u32[]{:S(2)}) collective-permute-start(f32[5,2,8,128]{3,2,1,0:T(8,128)S(1)} %get-tuple-element.27.own), channel_id=1, source_target_pairs={{2,0},{3,1},{0,2},{1,3},{6,4},{7,5},{4,6},{5,7},{10,8},{11,9},{8,1... | collective-permute-start | bytes 122888 | tf_op jit(solution)/shard_map/ppermute | solution.py:510
  35.8 3.9 %collective-permute-start.6 = (f32[5,2,8,128]{3,2,1,0:T(8,128)S(1)}, f32[5,2,8,128]{3,2,1,0:T(8,128)S(1)}, u32[]{:S(2)}, u32[]{:S(2)}) collective-permute-start(f32[5,2,8,128]{3,2,1,0:T(8,128)S(1)} %get-tuple-element.27.own), channel_id=1, source_target_pairs={{1,0},{2,1},{3,2},{0,3},{5,4},{6,5},{7,6},{4,7},{9,8},{10,9},{11,1... | collective-permute-start | bytes 122888 | tf_op jit(solution)/shard_map/ppermute | solution.py:510
  39.8 15.9 %collective-permute-start.10 = (f32[5,8,8,128]{3,2,1,0:T(8,128)S(1)}, f32[5,8,8,128]{3,2,1,0:T(8,128)S(1)}, u32[]{:S(2)}, u32[]{:S(2)}) collective-permute-start(f32[5,8,8,128]{3,2,1,0:T(8,128)S(1)} %get-tuple-element.28.own), channel_id=1, source_target_pairs={{240,0},{0,16},{16,32},{32,48},{48,64},{64,80},{80,96},{96,112},{1... | collective-permute-start | bytes 491528 | tf_op jit(solution)/shard_map/ppermute | solution.py:510
  44.4 11.2 %collective-permute-start.9 = (f32[5,8,8,128]{3,2,1,0:T(8,128)S(1)}, f32[5,8,8,128]{3,2,1,0:T(8,128)S(1)}, u32[]{:S(2)}, u32[]{:S(2)}) collective-permute-start(f32[5,8,8,128]{3,2,1,0:T(8,128)S(1)} %get-tuple-element.28.own), channel_id=1, source_target_pairs={{16,0},{32,16},{48,32},{64,48},{80,64},{96,80},{112,96},{128,112},... | collective-permute-start | bytes 491528 | tf_op jit(solution)/shard_map/ppermute | solution.py:510
  48.2 4.4 %collective-permute-start.11 = (f32[5,4,8,128]{3,2,1,0:T(8,128)S(1)}, f32[5,4,8,128]{3,2,1,0:T(8,128)S(1)}, u32[]{:S(2)}, u32[]{:S(2)}) collective-permute-start(f32[5,4,8,128]{3,2,1,0:T(8,128)S(1)} %get-tuple-element.29), channel_id=1, source_target_pairs={{32,0},{48,16},{64,32},{80,48},{96,64},{112,80},{128,96},{144,112}... | collective-permute-start | bytes 245768 | tf_op jit(solution)/shard_map/ppermute | solution.py:510
  50.8 4.9 %collective-permute-start.12 = (f32[5,4,8,128]{3,2,1,0:T(8,128)S(1)}, f32[5,4,8,128]{3,2,1,0:T(8,128)S(1)}, u32[]{:S(2)}, u32[]{:S(2)}) collective-permute-start(f32[5,4,8,128]{3,2,1,0:T(8,128)S(1)} %get-tuple-element.30), channel_id=1, source_target_pairs={{224,0},{240,16},{0,32},{16,48},{32,64},{48,80},{64,96},{80,112},{... | collective-permute-start | bytes 245768 | tf_op jit(solution)/shard_map/ppermute | solution.py:510
  56.0 4.6 %collective-permute-start.13 = (f32[5,8,8,128]{3,2,1,0:T(8,128)S(1)}, f32[5,8,8,128]{3,2,1,0:T(8,128)S(1)}, u32[]{:S(2)}, u32[]{:S(2)}) collective-permute-start(f32[5,8,8,128]{3,2,1,0:T(8,128)S(1)} %get-tuple-element.32), channel_id=1, source_target_pairs={{4,0},{8,4},{12,8},{0,12},{5,1},{9,5},{13,9},{1,13},{6,2},{10,6},{... | collective-permute-start | bytes 491528 | tf_op jit(solution)/shard_map/ppermute | solution.py:510
  56.1 5.8 %collective-permute-start.14 = (f32[5,8,8,128]{3,2,1,0:T(8,128)S(1)}, f32[5,8,8,128]{3,2,1,0:T(8,128)S(1)}, u32[]{:S(2)}, u32[]{:S(2)}) collective-permute-start(f32[5,8,8,128]{3,2,1,0:T(8,128)S(1)} %get-tuple-element.33), channel_id=1, source_target_pairs={{12,0},{0,4},{4,8},{8,12},{13,1},{1,5},{5,9},{9,13},{14,2},{2,6},{... | collective-permute-start | bytes 491528 | tf_op jit(solution)/shard_map/ppermute | solution.py:510

commit v2 on v1

--- a/solution.py
+++ b/solution.py
@@ -15,7 +15,7 @@
 
 VMEM = pl.BlockSpec(memory_space=pltpu.VMEM)
 SMEM = pl.BlockSpec(memory_space=pltpu.SMEM)
-ANY = pl.BlockSpec(memory_space=pl.ANY)
+HBM = pl.BlockSpec(memory_space=pltpu.HBM)
 
 
 def call(kernel, outs, *args, scratch=(), spaces=None):
@@ -167,45 +167,80 @@
         hi[k] = own[k, 8 - H : 8]
 
 
-def pack_x(own, above, below, lo, hi):
-    for out, row in ((lo, 0), (hi, 8)):
+FACIES, BOUNDARY, SOURCE, DENSITY = range(4)
+XTILES = 2 * Z0 + 3
+
+
+def pack_x(own, above, below, xl, xh, lo, hi):
+    for out, row in ((xl, 0), (xh, 8)):
         out[:, 0:H] = below[:, :, row : row + 8]
         out[:, H : H + 8] = own[:, :, row : row + 8]
         out[:, H + 8 : Z0] = above[:, :, row : row + 8]
-
-
-GROUPS0 = 4 * Z0 // 4
-
-
-def pack_y(xl, xh, rl, rh, lo, hi):
-    block = iota((8, 128), 1) // 8
-    for g in range(GROUPS0):
-        left = right = None
-        for n in range(4):
-            k, z = divmod(4 * g + n, Z0)
+    first = iota((8, 128), 0) < 4
+    lo[XTILES - 1] = hi[XTILES - 1] = jnp.zeros((8, 128), F32)
+    for z in range(Z0):
+        fifth = 2 * Z0 + z // 8, slice(z % 8, z % 8 + 1)
+        f, b, s, d = (xl[k, z] for k in range(4))
+        lo[2 * z] = jnp.where(first, b, pltpu.roll(s, 4, 0))
+        lo[2 * z + 1] = jnp.where(first, d, pltpu.roll(f, 4, 0))
+        lo[fifth] = f[4:5]
+        f, b, s, d = (xh[k, z] for k in range(4))
+        hi[2 * z] = jnp.where(first, pltpu.roll(b, 4, 0), s)
+        hi[2 * z + 1] = jnp.where(first, pltpu.roll(d, 4, 0), f)
+        hi[fifth] = f[3:4]
+
+
+SMALL = 7
+YTILES = SMALL + 5
+
+
+def block_of(k, z, tile):
+    if k == FACIES:
+        return SMALL + z // 4, 8 * (4 * (z % 4) + tile), 8
+    layer = (k - 1) * Z0 + z
+    return layer // 8, 4 * (4 * (layer % 8) + tile), 4
+
+
+def pack_y(xl, xh, ml, mh, rl, rh, lo, hi):
+    row, lane = iota((8, 128), 0), iota((8, 128), 1)
+    for z in range(Z0):
+        fifth = 2 * Z0 + z // 8, slice(z % 8, z % 8 + 1)
+        bs, df = ml[2 * z], ml[2 * z + 1]
+        rl[BOUNDARY, z] = bs
+        rl[SOURCE, z] = pltpu.roll(bs, 4, 0)
+        rl[DENSITY, z] = df
+        rl[FACIES, z] = jnp.where(row == 4, ml[fifth], pltpu.roll(df, 4, 0))
+        bs, df = mh[2 * z], mh[2 * z + 1]
+        rh[BOUNDARY, z] = pltpu.roll(bs, 4, 0)
+        rh[SOURCE, z] = bs
+        rh[DENSITY, z] = pltpu.roll(df, 4, 0)
+        rh[FACIES, z] = jnp.where(row == 3, mh[fifth], df)
+    left, right = [None] * YTILES, [None] * YTILES
+    for k in range(4):
+        for z in range(Z0):
             for tile, ref in enumerate((xl, xh, rl, rh)):
-                at = 4 * n + tile
+                g, at, width = block_of(k, z, tile)
                 v = ref[k, z]
-                a, b = turn(v, 8 * at), turn(v, 8 * at + 8)
-                left = a if at == 0 else jnp.where(block == at, a, left)
-                right = b if at == 0 else jnp.where(block == at, b, right)
-        lo[g] = left
-        hi[g] = right
+                here = lane // width == at // width
+                a, b = turn(v, at), turn(v, at + width)
+                left[g] = a if at == 0 else jnp.where(here, a, left[g])
+                right[g] = b if at == 0 else jnp.where(here, b, right[g])
+    for g in range(YTILES):
+        lo[g] = left[g]
+        hi[g] = right[g]
 
 
 def level0(pos, tables, xl, xh, rl, rh, yl, yh, a, packed, raw, hs, vs, dd, res, sk, t, m):
     gx, gy, gz = pos[0], pos[1], pos[2]
     lane8 = iota((8, 128), 1)
-    for g in range(GROUPS0):
-        right, left = yl[g], yh[g]
-        for n in range(4):
-            k, z = divmod(4 * g + n, Z0)
+    for k in range(4):
+        for z in range(Z0):
             for tile in range(4):
-                at = 8 * (4 * n + tile)
+                g, at, width = block_of(k, z, tile)
                 raw[k, z, 8 * tile : 8 * tile + 8, 128:256] = jnp.where(
-                    lane8 < 8,
-                    turn(right, -at),
-                    jnp.where(lane8 >= 120, turn(left, 120 - at), 0.0),
+                    lane8 < width,
+                    turn(yl[g], -at),
+                    jnp.where(lane8 >= 128 - width, turn(yh[g], -at - width), 0.0),
                 )
     for row, ref in ((0, xl), (8, xh), (16, rl), (24, rh)):
         raw[:, :, row : row + 8, 0:128] = ref[...]
@@ -320,17 +355,17 @@
         for s in range(2):
             part = slice(4 * s, 4 * s + 4)
             whole[:, 2 * n + s, 16:24] = jnp.concatenate([r2[:, n, part], l2[:, n, part]], axis=1)
-    block = (iota((8, 128), 1) // 16) % 4
-    for k in range(5):
-        for n in range(8):
-            left = right = None
-            for tile in range(4):
-                v = whole[k, n, 8 * tile : 8 * tile + 8]
-                a, b = turn(v, 16 * tile), turn(v, 16 * tile + 80)
-                left = a if tile == 0 else jnp.where(block == tile, a, left)
-                right = b if tile == 0 else jnp.where(block == tile, b, right)
-            lo[k, n] = left
-            hi[k, n] = right
+    block = (iota((8, 128), 1) % 64) // 12
+    for g in range(32):
+        left = right = None
+        for at in range(5):
+            layer, tile = divmod(5 * g + at, 4)
+            v = whole[layer // 8, layer % 8, 8 * tile : 8 * tile + 8]
+            a, b = turn(v, 12 * at), turn(v, 12 * at - 52)
+            left = a if at == 0 else jnp.where(block == at, a, left)
+            right = b if at == 0 else jnp.where(block == at, b, right)
+        lo[g] = left
+        hi[g] = right
 
 
 def level12(pos, whole, yl, yh, a, b, sent, d1, r1, t1, m1, d2, r2, s1, s2, q2):
@@ -344,13 +379,14 @@
         rows = slice(8 * tile, 8 * tile + 8)
         for k in range(5):
             for n in range(8):
-                v, right, left = whole[k, n, rows], yl[k, n], yh[k, n]
+                g, at = divmod(4 * (8 * k + n) + tile, 5)
+                v, right, left = whole[k, n, rows], yl[g], yh[g]
                 for part in range(2):
                     own = turn(v, 64 * part)
                     beyond = jnp.where(
-                        lane < 80,
-                        turn(right, 64 - 64 * part - 16 * tile),
-                        jnp.where(lane >= 112, turn(left, 112 - 64 * part - 16 * tile), 0.0),
+                        lane < 76,
+                        turn(right, 64 - 64 * part - 12 * at),
+                        jnp.where(lane >= 116, turn(left, 116 - 64 * part - 12 * at), 0.0),
                     )
                     value = jnp.where(inside, jnp.where(lane < 64, own, beyond), 0.0)
                     z = 4 * (n // 2) + 2 * part + n % 2
@@ -384,7 +420,8 @@
             v = m1[z, s]
             v = pick(v + up(v, 1), 2 * (lane % 16))
             total = jnp.where(lane // 16 == 2 * zg + s, v, total)
-    sent[...] = jnp.broadcast_to(total[None], (64, 8, 128))
+    for k in range(5):
+        sent[:, :, 128 * k : 128 * k + 128] = jnp.broadcast_to(total[k : k + 1][None], (64, 1, 128))
 
 
 def sweep(a, src, dst, n, unroll):
@@ -403,7 +440,7 @@
     gx, gy, gz = pos[0], pos[1], pos[2]
     lane = iota((16, 128), 1)
     for k in range(5):
-        rows = [got[pl.ds(g * 128 + k, 16, stride=8), :] for g in range(4)]
+        rows = [got[16 * g : 16 * g + 16, 0, 128 * k : 128 * k + 128] for g in range(4)]
         for z in range(4):
             for s in range(2):
                 at = (z * 2 + s) * 16
@@ -517,16 +554,20 @@
         pack_z,
         [(4, H, 16, 128)] * 2 + [(4, 8, 16, 128)],
         facies, boundary, source, density,
-        spaces=[ANY] * 4,
+        spaces=[HBM] * 4,
         scratch=[
             pltpu.VMEM((8, 16, 128), jnp.int32), pltpu.VMEM((8, 16, 128), jnp.int32),
             pltpu.SemaphoreType.DMA((4,)),
         ],
     )
     above, below = shift(lo, "gz", 1), shift(hi, "gz", -1)
-    xl, xh = call(pack_x, [(4, Z0, 8, 128)] * 2, own, above, below)
-    rl, rh = shift(xl, "gx", 1), shift(xh, "gx", -1)
-    lo, hi = call(pack_y, [(GROUPS0, 8, 128)] * 2, xl, xh, rl, rh)
+    xl, xh, lo, hi = call(
+        pack_x, [(4, Z0, 8, 128)] * 2 + [(XTILES, 8, 128)] * 2, own, above, below
+    )
+    ml, mh = shift(lo, "gx", 1), shift(hi, "gx", -1)
+    rl, rh, lo, hi = call(
+        pack_y, [(4, Z0, 8, 128)] * 2 + [(YTILES, 8, 128)] * 2, xl, xh, ml, mh
+    )
     yl, yh = shift(lo, "gy", 1), shift(hi, "gy", -1)
     a0, packed = call(
         level0,
@@ -545,12 +586,12 @@
     r1, l1 = shift(full, "gx", 1), shift(full, "gx", -1)
     r2, l2 = shift(lo, "gx", 2), shift(hi, "gx", -2)
     whole, lo, hi = call(
-        pack_y1, [(5, 8, 32, 128), (5, 8, 8, 128), (5, 8, 8, 128)], full, r1, l1, r2, l2
+        pack_y1, [(5, 8, 32, 128), (32, 8, 128), (32, 8, 128)], full, r1, l1, r2, l2
     )
     yl, yh = shift(lo, "gy", 1), shift(hi, "gy", -1)
     a1, a2, sent = call(
         level12,
-        [(6, 16, 32, 128), (6, 8, 16, 128), (64, 8, 128)],
+        [(6, 16, 32, 128), (6, 8, 16, 128), (64, 1, 640)],
         pos, whole, yl, yh,
         spaces=[SMEM] + [VMEM] * 3,
         scratch=[
@@ -563,7 +604,7 @@
         call(
             solve,
             [(8, 16, 128), (8, 16, 128)],
-            pos, got.reshape(512, 128), a0, a1, a2,
+            pos, got, a0, a1, a2,
             spaces=[SMEM] + [VMEM] * 4,
             scratch=[
                 (6, 4, 32, 128), (6, 2, 16, 128),

time: 91.1 us -> 87.8 us (0.964)
  waiting for transfers between devices: 25.5 us -> 23.8 us
  blocking collectives: 19.1 us -> 17.7 us
    ppermute x15, waiting for transfers between devices: 25.5 us -> 23.8 us  [shift(): lax.ppermute(value, axis, [((i + by) % count, i) for i in range(count)])]
    all_to_all x1, blocking collectives: 19.1 us -> 17.7 us  [local(): got = lax.all_to_all(sent, ('gy', 'gx'), 0, 0)]
  transfers between devices with their start and end apart: 15 -> 15, of which waited for: 12 -> 13; matrix products, arithmetic and copies ran while one was open for 1% -> 1% of each run, Pallas kernels for 0% -> 0%
where the time goes in v2:
time: 87.8 us; the launch traced here: 87.5 us
  starting transfers between devices  24.4 us (28%)
  waiting for transfers between devices  23.8 us (27%)
  blocking collectives  17.7 us (20%)
  Pallas kernels  16.7 us (19%)
  local copies, waits for them, and re-layouts  3.35 us (4%)
    ppermute x15, starting transfers between devices, shift(): lax.ppermute(value, axis, [((i + by) % count, i) for i in range(count)])  24.4 us
    ppermute x15, waiting for transfers between devices, shift(): lax.ppermute(value, axis, [((i + by) % count, i) for i in range(count)])  23.8 us
    all_to_all x1, blocking collectives, local(): got = lax.all_to_all(sent, ('gy', 'gx'), 0, 0)  17.7 us
    pallas_call x8, Pallas kernels, call(): pl.pallas_call(kernel, out_shape=[jax.ShapeDtypeStruct(s, F32) for s in o...  16.7 us
    unnamed x8, local copies, waits for them, and re-layouts  3.35 us
  transfers between devices with their start and end apart: 15, of which 13 were waited for; matrix products, arithmetic and copies ran while one was open for 1% of the time, Pallas kernels for 0%

profile of v2, /device:TPU:1, one launch (start us, length us, event | category | flops | bytes accessed | tf_op | source)
XLA Modules:
  0.0 87.5 jit_solution(2021429893337768810)
XLA Ops:
  0.6 0.8 copy-done
  1.5 0.8 copy-done.1
  2.3 0.8 copy-done.2
  3.2 0.8 copy-done.3
  4.4 3.4 %collective-permute-start = (f32[4,5,16,128]{3,2,1,0:T(8,128)S(1)}, f32[4,5,16,128]{3,2,1,0:T(8,128)S(1)}, u32[]{:S(2)}, u32[]{:S(2)}) collective-permute-start(f32[4,5,16,128]{3,2,1,0:T(8,128)S(1)} %get-tuple-element.25), channel_id=1, source_target_pairs={{1,0},{2,1},{3,2},{0,3},{5,4},{6,5},{7,6},{4,7},{9,8},{10,9},{11,1... | collective-permute-start | bytes 491528 | tf_op jit(solution)/shard_map/ppermute | solution.py:547
  7.8 2.9 %collective-permute-done.above = f32[4,5,16,128]{3,2,1,0:T(8,128)S(1)} collective-permute-done((f32[4,5,16,128]{3,2,1,0:T(8,128)S(1)}, f32[4,5,16,128]{3,2,1,0:T(8,128)S(1)}, u32[]{:S(2)}, u32[]{:S(2)}) %collective-permute-start) | collective-permute-done | bytes 163872 | tf_op jit(solution)/shard_map/ppermute | solution.py:547
  10.6 3.1 %collective-permute-done.1.below = f32[4,5,16,128]{3,2,1,0:T(8,128)S(1)} collective-permute-done((f32[4,5,16,128]{3,2,1,0:T(8,128)S(1)}, f32[4,5,16,128]{3,2,1,0:T(8,128)S(1)}, u32[]{:S(2)}, u32[]{:S(2)}) %collective-permute-start.1) | collective-permute-done | bytes 163872 | tf_op jit(solution)/shard_map/ppermute | solution.py:547
  13.8 1.9 %collective-permute-start.2 = (f32[39,8,128]{2,1,0:T(8,128)S(1)}, f32[39,8,128]{2,1,0:T(8,128)S(1)}, u32[]{:S(2)}, u32[]{:S(2)}) collective-permute-start(f32[39,8,128]{2,1,0:T(8,128)S(1)} %get-tuple-element.29), channel_id=1, source_target_pairs={{16,0},{32,16},{48,32},{64,48},{80,64},{96,80},{112,96},{128,112},... | collective-permute-start | bytes 479240 | tf_op jit(solution)/shard_map/ppermute | solution.py:547
  15.7 1.5 %collective-permute-start.3 = (f32[39,8,128]{2,1,0:T(8,128)S(1)}, f32[39,8,128]{2,1,0:T(8,128)S(1)}, u32[]{:S(2)}, u32[]{:S(2)}) collective-permute-start(f32[39,8,128]{2,1,0:T(8,128)S(1)} %get-tuple-element.30), channel_id=1, source_target_pairs={{240,0},{0,16},{16,32},{32,48},{48,64},{64,80},{80,96},{96,112},{1... | collective-permute-start | bytes 479240 | tf_op jit(solution)/shard_map/ppermute | solution.py:547
  17.2 0.7 pad_maximum_fusion.tables
  18.0 2.2 %collective-permute-done.2.ml = f32[39,8,128]{2,1,0:T(8,128)S(1)} collective-permute-done((f32[39,8,128]{2,1,0:T(8,128)S(1)}, f32[39,8,128]{2,1,0:T(8,128)S(1)}, u32[]{:S(2)}, u32[]{:S(2)}) %collective-permute-start.2) | collective-permute-done | bytes 159776 | tf_op jit(solution)/shard_map/ppermute | solution.py:547
  20.2 0.5 collective-permute-done.3.mh
  20.7 0.7 shard_map.79
  21.3 2.8 %collective-permute-start.4 = (f32[12,8,128]{2,1,0:T(8,128)S(1)}, f32[12,8,128]{2,1,0:T(8,128)S(1)}, u32[]{:S(2)}, u32[]{:S(2)}) collective-permute-start(f32[12,8,128]{2,1,0:T(8,128)S(1)} %get-tuple-element.33), channel_id=1, source_target_pairs={{4,0},{8,4},{12,8},{0,12},{5,1},{9,5},{13,9},{1,13},{6,2},{10,6},{... | collective-permute-start | bytes 147464 | tf_op jit(solution)/shard_map/ppermute | solution.py:547
  24.2 1.1 %collective-permute-done.4.yl = f32[12,8,128]{2,1,0:T(8,128)S(1)} collective-permute-done((f32[12,8,128]{2,1,0:T(8,128)S(1)}, f32[12,8,128]{2,1,0:T(8,128)S(1)}, u32[]{:S(2)}, u32[]{:S(2)}) %collective-permute-start.4) | collective-permute-done | bytes 49184 | tf_op jit(solution)/shard_map/ppermute | solution.py:547
  25.3 3.0 %collective-permute-done.5.yh = f32[12,8,128]{2,1,0:T(8,128)S(1)} collective-permute-done((f32[12,8,128]{2,1,0:T(8,128)S(1)}, f32[12,8,128]{2,1,0:T(8,128)S(1)}, u32[]{:S(2)}, u32[]{:S(2)}) %collective-permute-start.5) | collective-permute-done | bytes 49184 | tf_op jit(solution)/shard_map/ppermute | solution.py:547
  28.3 5.2 %shard_map.80 = (f32[6,18,32,256]{3,2,1,0:T(8,128)S(1)}, f32[5,2,8,128]{3,2,1,0:T(8,128)S(1)}) custom-call(s32[3]{0:T(128)S(1)} %pad_add_fusion.pos, f32[16]{0:T(128)S(1)} %pad_maximum_fusion.tables, f32[4,18,8,128]{3,2,1,0:T(8,128)S(1)} %get-tuple-element.27.xl, f32[4,18,8,128]{3,2,1,0:T(8,128)S(1)} %get-tuple-element.28.xh, ...), custom_call_target="tpu_custom_call" | custom-call | tf_op jit(solution)/shard_map/pallas_call | solution.py:22
  33.6 1.5 %collective-permute-start.7 = (f32[5,2,8,128]{3,2,1,0:T(8,128)S(1)}, f32[5,2,8,128]{3,2,1,0:T(8,128)S(1)}, u32[]{:S(2)}, u32[]{:S(2)}) collective-permute-start(f32[5,2,8,128]{3,2,1,0:T(8,128)S(1)} %get-tuple-element.35.own), channel_id=1, source_target_pairs={{2,0},{3,1},{0,2},{1,3},{6,4},{7,5},{4,6},{5,7},{10,8},{11,9},{8,1... | collective-permute-start | bytes 122888 | tf_op jit(solution)/shard_map/ppermute | solution.py:547
  35.1 1.2 %collective-permute-start.6 = (f32[5,2,8,128]{3,2,1,0:T(8,128)S(1)}, f32[5,2,8,128]{3,2,1,0:T(8,128)S(1)}, u32[]{:S(2)}, u32[]{:S(2)}) collective-permute-start(f32[5,2,8,128]{3,2,1,0:T(8,128)S(1)} %get-tuple-element.35.own), channel_id=1, source_target_pairs={{1,0},{2,1},{3,2},{0,3},{5,4},{6,5},{7,6},{4,7},{9,8},{10,9},{11,1... | collective-permute-start | bytes 122888 | tf_op jit(solution)/shard_map/ppermute | solution.py:547
  36.2 1.4 %collective-permute-done.8.b3 = f32[5,2,8,128]{3,2,1,0:T(8,128)S(1)} collective-permute-done((f32[5,2,8,128]{3,2,1,0:T(8,128)S(1)}, f32[5,2,8,128]{3,2,1,0:T(8,128)S(1)}, u32[]{:S(2)}, u32[]{:S(2)}) %collective-permute-start.8) | collective-permute-done | bytes 40992 | tf_op jit(solution)/shard_map/ppermute | solution.py:547
  38.0 0.6 collective-permute-done.6.b1
  38.7 4.1 %collective-permute-start.10 = (f32[5,8,8,128]{3,2,1,0:T(8,128)S(1)}, f32[5,8,8,128]{3,2,1,0:T(8,128)S(1)}, u32[]{:S(2)}, u32[]{:S(2)}) collective-permute-start(f32[5,8,8,128]{3,2,1,0:T(8,128)S(1)} %get-tuple-element.36.own), channel_id=1, source_target_pairs={{240,0},{0,16},{16,32},{32,48},{48,64},{64,80},{80,96},{96,112},{1... | collective-permute-start | bytes 491528 | tf_op jit(solution)/shard_map/ppermute | solution.py:547
  42.8 3.8 %collective-permute-start.9 = (f32[5,8,8,128]{3,2,1,0:T(8,128)S(1)}, f32[5,8,8,128]{3,2,1,0:T(8,128)S(1)}, u32[]{:S(2)}, u32[]{:S(2)}) collective-permute-start(f32[5,8,8,128]{3,2,1,0:T(8,128)S(1)} %get-tuple-element.36.own), channel_id=1, source_target_pairs={{16,0},{32,16},{48,32},{64,48},{80,64},{96,80},{112,96},{128,112},... | collective-permute-start | bytes 491528 | tf_op jit(solution)/shard_map/ppermute | solution.py:547
  46.6 2.6 %collective-permute-start.11 = (f32[5,4,8,128]{3,2,1,0:T(8,128)S(1)}, f32[5,4,8,128]{3,2,1,0:T(8,128)S(1)}, u32[]{:S(2)}, u32[]{:S(2)}) collective-permute-start(f32[5,4,8,128]{3,2,1,0:T(8,128)S(1)} %get-tuple-element.37), channel_id=1, source_target_pairs={{32,0},{48,16},{64,32},{80,48},{96,64},{112,80},{128,96},{144,112}... | collective-permute-start | bytes 245768 | tf_op jit(solution)/shard_map/ppermute | solution.py:547
  49.2 1.8 %collective-permute-done.11.r2 = f32[5,4,8,128]{3,2,1,0:T(8,128)S(1)} collective-permute-done((f32[5,4,8,128]{3,2,1,0:T(8,128)S(1)}, f32[5,4,8,128]{3,2,1,0:T(8,128)S(1)}, u32[]{:S(2)}, u32[]{:S(2)}) %collective-permute-start.11) | collective-permute-done | bytes 81952 | tf_op jit(solution)/shard_map/ppermute | solution.py:547
  50.9 3.1 %collective-permute-done.12.l2 = f32[5,4,8,128]{3,2,1,0:T(8,128)S(1)} collective-permute-done((f32[5,4,8,128]{3,2,1,0:T(8,128)S(1)}, f32[5,4,8,128]{3,2,1,0:T(8,128)S(1)}, u32[]{:S(2)}, u32[]{:S(2)}) %collective-permute-start.12) | collective-permute-done | bytes 81952 | tf_op jit(solution)/shard_map/ppermute | solution.py:547
  54.5 1.5 %collective-permute-start.14 = (f32[32,8,128]{2,1,0:T(8,128)S(1)}, f32[32,8,128]{2,1,0:T(8,128)S(1)}, u32[]{:S(2)}, u32[]{:S(2)}) collective-permute-start(f32[32,8,128]{2,1,0:T(8,128)S(1)} %get-tuple-element.41), channel_id=1, source_target_pairs={{12,0},{0,4},{4,8},{8,12},{13,1},{1,5},{5,9},{9,13},{14,2},{2,6},{... | collective-permute-start | bytes 393224 | tf_op jit(solution)/shard_map/ppermute | solution.py:547
  56.0 2.4 %collective-permute-done.13.yl = f32[32,8,128]{2,1,0:T(8,128)S(1)} collective-permute-done((f32[32,8,128]{2,1,0:T(8,128)S(1)}, f32[32,8,128]{2,1,0:T(8,128)S(1)}, u32[]{:S(2)}, u32[]{:S(2)}) %collective-permute-start.13) | collective-permute-done | bytes 131104 | tf_op jit(solution)/shard_map/ppermute | solution.py:547
  58.3 1.5 %collective-permute-done.14.yh = f32[32,8,128]{2,1,0:T(8,128)S(1)} collective-permute-done((f32[32,8,128]{2,1,0:T(8,128)S(1)}, f32[32,8,128]{2,1,0:T(8,128)S(1)}, u32[]{:S(2)}, u32[]{:S(2)}) %collective-permute-start.14) | collective-permute-done | bytes 131104 | tf_op jit(solution)/shard_map/ppermute | solution.py:547
  59.8 3.6 %shard_map.83 = (f32[6,16,32,128]{3,2,1,0:T(8,128)S(1)}, f32[6,8,16,128]{3,2,1,0:T(8,128)S(1)}, f32[64,1,640]{2,1,0:T(1,128)S(1)}) custom-call(s32[3]{0:T(128)S(1)} %pad_add_fusion.pos, f32[5,8,32,128]{3,2,1,0:T(8,128)S(1)} %get-tuple-element.39.whole, f32[32,8,128]{2,1,0:T(8,128)S(1)} %collective-permute-done.13.yl, ...), custom_call_target="tpu_custom_call" | custom-call | tf_op jit(solution)/shard_map/pallas_call | solution.py:22
  63.4 17.7 %all_to_all.5.got = f32[64,1,640]{2,1,0:T(1,128)S(1)} all-to-all(f32[64,1,640]{2,1,0:T(1,128)S(1)} %get-tuple-element.42), channel_id=1, replica_groups=mesh['gx'=16,'gy'=4,'gz'=4] {'gy','gx'}, dimensions={0} | all-to-all | bytes 327680 | tf_op jit(solution)/shard_map/all_to_all | solution.py:602
  81.1 6.4 %shard_map.84 = (f32[8,16,128]{2,1,0:T(8,128)}, f32[8,16,128]{2,1,0:T(8,128)}) custom-call(s32[3]{0:T(128)S(1)} %pad_add_fusion.pos, f32[64,1,640]{2,1,0:T(1,128)S(1)} %all_to_all.5.got, f32[6,18,32,256]{3,2,1,0:T(8,128)S(1)} %get-tuple-element.43.a0, f32[6,16,32,128]{3,2,1,0:T(8,128)S(1)} %get-tuple-element.44.a1, f32[6,8,16,128]{3,2,1,0:T(8,128)S(1)} %get-tuple-element.45.a2), custom_call_target="tpu_custom_call" | custom-call | tf_op jit(solution)/shard_map/pallas_call | solution.py:22
  (17 shorter events, 1.5 us)
Async XLA Ops:
  0.6 0.8 copy-start
  1.5 0.8 copy-start.1
  2.3 0.8 copy-start.2
  3.2 0.8 copy-start.3
  4.4 6.3 %collective-permute-start = (f32[4,5,16,128]{3,2,1,0:T(8,128)S(1)}, f32[4,5,16,128]{3,2,1,0:T(8,128)S(1)}, u32[]{:S(2)}, u32[]{:S(2)}) collective-permute-start(f32[4,5,16,128]{3,2,1,0:T(8,128)S(1)} %get-tuple-element.25), channel_id=1, source_target_pairs={{1,0},{2,1},{3,2},{0,3},{5,4},{6,5},{7,6},{4,7},{9,8},{10,9},{11,1... | collective-permute-start | bytes 491528 | tf_op jit(solution)/shard_map/ppermute | solution.py:547
  7.8 6.0 %collective-permute-start.1 = (f32[4,5,16,128]{3,2,1,0:T(8,128)S(1)}, f32[4,5,16,128]{3,2,1,0:T(8,128)S(1)}, u32[]{:S(2)}, u32[]{:S(2)}) collective-permute-start(f32[4,5,16,128]{3,2,1,0:T(8,128)S(1)} %get-tuple-element.26), channel_id=1, source_target_pairs={{3,0},{0,1},{1,2},{2,3},{7,4},{4,5},{5,6},{6,7},{11,8},{8,9},{9,10... | collective-permute-start | bytes 491528 | tf_op jit(solution)/shard_map/ppermute | solution.py:547
  13.8 6.4 %collective-permute-start.2 = (f32[39,8,128]{2,1,0:T(8,128)S(1)}, f32[39,8,128]{2,1,0:T(8,128)S(1)}, u32[]{:S(2)}, u32[]{:S(2)}) collective-permute-start(f32[39,8,128]{2,1,0:T(8,128)S(1)} %get-tuple-element.29), channel_id=1, source_target_pairs={{16,0},{32,16},{48,32},{64,48},{80,64},{96,80},{112,96},{128,112},... | collective-permute-start | bytes 479240 | tf_op jit(solution)/shard_map/ppermute | solution.py:547
  15.7 5.0 %collective-permute-start.3 = (f32[39,8,128]{2,1,0:T(8,128)S(1)}, f32[39,8,128]{2,1,0:T(8,128)S(1)}, u32[]{:S(2)}, u32[]{:S(2)}) collective-permute-start(f32[39,8,128]{2,1,0:T(8,128)S(1)} %get-tuple-element.30), channel_id=1, source_target_pairs={{240,0},{0,16},{16,32},{32,48},{48,64},{64,80},{80,96},{96,112},{1... | collective-permute-start | bytes 479240 | tf_op jit(solution)/shard_map/ppermute | solution.py:547
  21.3 4.0 %collective-permute-start.4 = (f32[12,8,128]{2,1,0:T(8,128)S(1)}, f32[12,8,128]{2,1,0:T(8,128)S(1)}, u32[]{:S(2)}, u32[]{:S(2)}) collective-permute-start(f32[12,8,128]{2,1,0:T(8,128)S(1)} %get-tuple-element.33), channel_id=1, source_target_pairs={{4,0},{8,4},{12,8},{0,12},{5,1},{9,5},{13,9},{1,13},{6,2},{10,6},{... | collective-permute-start | bytes 147464 | tf_op jit(solution)/shard_map/ppermute | solution.py:547
  24.1 4.2 %collective-permute-start.5 = (f32[12,8,128]{2,1,0:T(8,128)S(1)}, f32[12,8,128]{2,1,0:T(8,128)S(1)}, u32[]{:S(2)}, u32[]{:S(2)}) collective-permute-start(f32[12,8,128]{2,1,0:T(8,128)S(1)} %get-tuple-element.34), channel_id=1, source_target_pairs={{12,0},{0,4},{4,8},{8,12},{13,1},{1,5},{5,9},{9,13},{14,2},{2,6},{... | collective-permute-start | bytes 147464 | tf_op jit(solution)/shard_map/ppermute | solution.py:547
  33.5 4.2 %collective-permute-start.8 = (f32[5,2,8,128]{3,2,1,0:T(8,128)S(1)}, f32[5,2,8,128]{3,2,1,0:T(8,128)S(1)}, u32[]{:S(2)}, u32[]{:S(2)}) collective-permute-start(f32[5,2,8,128]{3,2,1,0:T(8,128)S(1)} %get-tuple-element.35.own), channel_id=1, source_target_pairs={{3,0},{0,1},{1,2},{2,3},{7,4},{4,5},{5,6},{6,7},{11,8},{8,9},{9,10... | collective-permute-start | bytes 122888 | tf_op jit(solution)/shard_map/ppermute | solution.py:547
  33.6 4.5 %collective-permute-start.7 = (f32[5,2,8,128]{3,2,1,0:T(8,128)S(1)}, f32[5,2,8,128]{3,2,1,0:T(8,128)S(1)}, u32[]{:S(2)}, u32[]{:S(2)}) collective-permute-start(f32[5,2,8,128]{3,2,1,0:T(8,128)S(1)} %get-tuple-element.35.own), channel_id=1, source_target_pairs={{2,0},{3,1},{0,2},{1,3},{6,4},{7,5},{4,6},{5,7},{10,8},{11,9},{8,1... | collective-permute-start | bytes 122888 | tf_op jit(solution)/shard_map/ppermute | solution.py:547
  35.1 3.6 %collective-permute-start.6 = (f32[5,2,8,128]{3,2,1,0:T(8,128)S(1)}, f32[5,2,8,128]{3,2,1,0:T(8,128)S(1)}, u32[]{:S(2)}, u32[]{:S(2)}) collective-permute-start(f32[5,2,8,128]{3,2,1,0:T(8,128)S(1)} %get-tuple-element.35.own), channel_id=1, source_target_pairs={{1,0},{2,1},{3,2},{0,3},{5,4},{6,5},{7,6},{4,7},{9,8},{10,9},{11,1... | collective-permute-start | bytes 122888 | tf_op jit(solution)/shard_map/ppermute | solution.py:547
  38.7 15.4 %collective-permute-start.10 = (f32[5,8,8,128]{3,2,1,0:T(8,128)S(1)}, f32[5,8,8,128]{3,2,1,0:T(8,128)S(1)}, u32[]{:S(2)}, u32[]{:S(2)}) collective-permute-start(f32[5,8,8,128]{3,2,1,0:T(8,128)S(1)} %get-tuple-element.36.own), channel_id=1, source_target_pairs={{240,0},{0,16},{16,32},{32,48},{48,64},{64,80},{80,96},{96,112},{1... | collective-permute-start | bytes 491528 | tf_op jit(solution)/shard_map/ppermute | solution.py:547
  42.8 11.2 %collective-permute-start.9 = (f32[5,8,8,128]{3,2,1,0:T(8,128)S(1)}, f32[5,8,8,128]{3,2,1,0:T(8,128)S(1)}, u32[]{:S(2)}, u32[]{:S(2)}) collective-permute-start(f32[5,8,8,128]{3,2,1,0:T(8,128)S(1)} %get-tuple-element.36.own), channel_id=1, source_target_pairs={{16,0},{32,16},{48,32},{64,48},{80,64},{96,80},{112,96},{128,112},... | collective-permute-start | bytes 491528 | tf_op jit(solution)/shard_map/ppermute | solution.py:547
  46.6 4.4 %collective-permute-start.11 = (f32[5,4,8,128]{3,2,1,0:T(8,128)S(1)}, f32[5,4,8,128]{3,2,1,0:T(8,128)S(1)}, u32[]{:S(2)}, u32[]{:S(2)}) collective-permute-start(f32[5,4,8,128]{3,2,1,0:T(8,128)S(1)} %get-tuple-element.37), channel_id=1, source_target_pairs={{32,0},{48,16},{64,32},{80,48},{96,64},{112,80},{128,96},{144,112}... | collective-permute-start | bytes 245768 | tf_op jit(solution)/shard_map/ppermute | solution.py:547
  49.2 4.9 %collective-permute-start.12 = (f32[5,4,8,128]{3,2,1,0:T(8,128)S(1)}, f32[5,4,8,128]{3,2,1,0:T(8,128)S(1)}, u32[]{:S(2)}, u32[]{:S(2)}) collective-permute-start(f32[5,4,8,128]{3,2,1,0:T(8,128)S(1)} %get-tuple-element.38), channel_id=1, source_target_pairs={{224,0},{240,16},{0,32},{16,48},{32,64},{48,80},{64,96},{80,112},{... | collective-permute-start | bytes 245768 | tf_op jit(solution)/shard_map/ppermute | solution.py:547
  54.4 3.9 %collective-permute-start.13 = (f32[32,8,128]{2,1,0:T(8,128)S(1)}, f32[32,8,128]{2,1,0:T(8,128)S(1)}, u32[]{:S(2)}, u32[]{:S(2)}) collective-permute-start(f32[32,8,128]{2,1,0:T(8,128)S(1)} %get-tuple-element.40), channel_id=1, source_target_pairs={{4,0},{8,4},{12,8},{0,12},{5,1},{9,5},{13,9},{1,13},{6,2},{10,6},{... | collective-permute-start | bytes 393224 | tf_op jit(solution)/shard_map/ppermute | solution.py:547
  54.5 5.3 %collective-permute-start.14 = (f32[32,8,128]{2,1,0:T(8,128)S(1)}, f32[32,8,128]{2,1,0:T(8,128)S(1)}, u32[]{:S(2)}, u32[]{:S(2)}) collective-permute-start(f32[32,8,128]{2,1,0:T(8,128)S(1)} %get-tuple-element.41), channel_id=1, source_target_pairs={{12,0},{0,4},{4,8},{8,12},{13,1},{1,5},{5,9},{9,13},{14,2},{2,6},{... | collective-permute-start | bytes 393224 | tf_op jit(solution)/shard_map/ppermute | solution.py:547

commit v3 on v2

--- a/solution.py
+++ b/solution.py
@@ -18,14 +18,14 @@
 HBM = pl.BlockSpec(memory_space=pltpu.HBM)
 
 
-def call(kernel, outs, *args, scratch=(), spaces=None):
+def call(kernel, outs, *args, scratch=(), spaces=None, limit=24):
     return pl.pallas_call(
         kernel,
         out_shape=[jax.ShapeDtypeStruct(s, F32) for s in outs],
         in_specs=spaces or [VMEM] * len(args),
         out_specs=[VMEM] * len(outs),
         scratch_shapes=[pltpu.VMEM(s, F32) if isinstance(s, tuple) else s for s in scratch],
-        compiler_params=pltpu.CompilerParams(vmem_limit_bytes=24 * 2**20),
+        compiler_params=pltpu.CompilerParams(vmem_limit_bytes=limit * 2**20),
     )(*args)
 
 
@@ -555,6 +555,7 @@
         [(4, H, 16, 128)] * 2 + [(4, 8, 16, 128)],
         facies, boundary, source, density,
         spaces=[HBM] * 4,
+        limit=60,
         scratch=[
             pltpu.VMEM((8, 16, 128), jnp.int32), pltpu.VMEM((8, 16, 128), jnp.int32),
             pltpu.SemaphoreType.DMA((4,)),

time: 87.8 us -> 86.9 us (0.990)
  local copies, waits for them, and re-layouts: 3.35 us -> 0.95 us
  Pallas kernels: 16.7 us -> 18.1 us
    unnamed x8 -> x2, local copies, waits for them, and re-layouts: 3.35 us -> 0.95 us
    pallas_call x8, Pallas kernels: 16.7 us -> 18.1 us  [call(): pl.pallas_call(kernel, out_shape=[jax.ShapeDtypeStruct(s, F32) for s in o...]
where the time goes in v3:
time: 86.9 us; the launch traced here: 86.7 us
  starting transfers between devices  24.4 us (28%)
  waiting for transfers between devices  24 us (28%)
  Pallas kernels  18.1 us (21%)
  blocking collectives  17.7 us (20%)
  local copies, waits for them, and re-layouts  0.95 us (1%)
    ppermute x15, starting transfers between devices, shift(): lax.ppermute(value, axis, [((i + by) % count, i) for i in range(count)])  24.4 us
    ppermute x15, waiting for transfers between devices, shift(): lax.ppermute(value, axis, [((i + by) % count, i) for i in range(count)])  24 us
    pallas_call x8, Pallas kernels, call(): pl.pallas_call(kernel, out_shape=[jax.ShapeDtypeStruct(s, F32) for s in o...  18.1 us
    all_to_all x1, blocking collectives, local(): got = lax.all_to_all(sent, ('gy', 'gx'), 0, 0)  17.7 us
  transfers between devices with their start and end apart: 15, of which 13 were waited for; matrix products, arithmetic and copies ran while one was open for 1% of the time, Pallas kernels for 0%

profile of v3, /device:TPU:1, one launch (start us, length us, event | category | flops | bytes accessed | tf_op | source)
XLA Modules:
  0.0 86.7 jit_solution(13329286713479771631)
XLA Ops:
  0.6 1.8 %shard_map.77 = (f32[4,5,16,128]{3,2,1,0:T(8,128)}, f32[4,5,16,128]{3,2,1,0:T(8,128)}, f32[4,8,16,128]{3,2,1,0:T(8,128)}) custom-call(s32[8,16,128]{2,1,0:T(8,128)} %f.1, s32[8,16,128]{2,1,0:T(8,128)} %b.1, f32[8,16,128]{2,1,0:T(8,128)} %s.1, f32[8,16,128]{2,1,0:T(8,128)} %d.1), custom_call_target="tpu_custom_call" | custom-call | tf_op jit(solution)/shard_map/pallas_call | solution.py:22
  2.4 3.4 %collective-permute-start = (f32[4,5,16,128]{3,2,1,0:T(8,128)}, f32[4,5,16,128]{3,2,1,0:T(8,128)S(1)}, u32[]{:S(2)}, u32[]{:S(2)}) collective-permute-start(f32[4,5,16,128]{3,2,1,0:T(8,128)} %get-tuple-element.25), channel_id=1, source_target_pairs={{1,0},{2,1},{3,2},{0,3},{5,4},{6,5},{7,6},{4,7},{9,8},{10,9},{11,1... | collective-permute-start | bytes 491528 | tf_op jit(solution)/shard_map/ppermute | solution.py:547
  5.8 3.2 %collective-permute-done.above = f32[4,5,16,128]{3,2,1,0:T(8,128)S(1)} collective-permute-done((f32[4,5,16,128]{3,2,1,0:T(8,128)}, f32[4,5,16,128]{3,2,1,0:T(8,128)S(1)}, u32[]{:S(2)}, u32[]{:S(2)}) %collective-permute-start) | collective-permute-done | bytes 163872 | tf_op jit(solution)/shard_map/ppermute | solution.py:547
  9.0 3.0 %collective-permute-done.1.below = f32[4,5,16,128]{3,2,1,0:T(8,128)S(1)} collective-permute-done((f32[4,5,16,128]{3,2,1,0:T(8,128)}, f32[4,5,16,128]{3,2,1,0:T(8,128)S(1)}, u32[]{:S(2)}, u32[]{:S(2)}) %collective-permute-start.1) | collective-permute-done | bytes 163872 | tf_op jit(solution)/shard_map/ppermute | solution.py:547
  12.0 0.9 %copy-done = f32[4,8,16,128]{3,2,1,0:T(8,128)S(1)} copy-done((f32[4,8,16,128]{3,2,1,0:T(8,128)S(1)}, f32[4,8,16,128]{3,2,1,0:T(8,128)}, u32[]{:S(2)}) %copy-start) | copy-done | bytes 262168
  13.0 1.9 %collective-permute-start.2 = (f32[39,8,128]{2,1,0:T(8,128)S(1)}, f32[39,8,128]{2,1,0:T(8,128)S(1)}, u32[]{:S(2)}, u32[]{:S(2)}) collective-permute-start(f32[39,8,128]{2,1,0:T(8,128)S(1)} %get-tuple-element.29), channel_id=1, source_target_pairs={{16,0},{32,16},{48,32},{64,48},{80,64},{96,80},{112,96},{128,112},... | collective-permute-start | bytes 479240 | tf_op jit(solution)/shard_map/ppermute | solution.py:547
  14.9 1.5 %collective-permute-start.3 = (f32[39,8,128]{2,1,0:T(8,128)S(1)}, f32[39,8,128]{2,1,0:T(8,128)S(1)}, u32[]{:S(2)}, u32[]{:S(2)}) collective-permute-start(f32[39,8,128]{2,1,0:T(8,128)S(1)} %get-tuple-element.30), channel_id=1, source_target_pairs={{240,0},{0,16},{16,32},{32,48},{48,64},{64,80},{80,96},{96,112},{1... | collective-permute-start | bytes 479240 | tf_op jit(solution)/shard_map/ppermute | solution.py:547
  16.4 0.7 pad_maximum_fusion.tables
  17.2 2.2 %collective-permute-done.2.ml = f32[39,8,128]{2,1,0:T(8,128)S(1)} collective-permute-done((f32[39,8,128]{2,1,0:T(8,128)S(1)}, f32[39,8,128]{2,1,0:T(8,128)S(1)}, u32[]{:S(2)}, u32[]{:S(2)}) %collective-permute-start.2) | collective-permute-done | bytes 159776 | tf_op jit(solution)/shard_map/ppermute | solution.py:547
  19.4 0.5 collective-permute-done.3.mh
  19.9 0.7 shard_map.79
  20.5 2.8 %collective-permute-start.4 = (f32[12,8,128]{2,1,0:T(8,128)S(1)}, f32[12,8,128]{2,1,0:T(8,128)S(1)}, u32[]{:S(2)}, u32[]{:S(2)}) collective-permute-start(f32[12,8,128]{2,1,0:T(8,128)S(1)} %get-tuple-element.33), channel_id=1, source_target_pairs={{4,0},{8,4},{12,8},{0,12},{5,1},{9,5},{13,9},{1,13},{6,2},{10,6},{... | collective-permute-start | bytes 147464 | tf_op jit(solution)/shard_map/ppermute | solution.py:547
  23.4 1.1 %collective-permute-done.4.yl = f32[12,8,128]{2,1,0:T(8,128)S(1)} collective-permute-done((f32[12,8,128]{2,1,0:T(8,128)S(1)}, f32[12,8,128]{2,1,0:T(8,128)S(1)}, u32[]{:S(2)}, u32[]{:S(2)}) %collective-permute-start.4) | collective-permute-done | bytes 49184 | tf_op jit(solution)/shard_map/ppermute | solution.py:547
  24.5 3.0 %collective-permute-done.5.yh = f32[12,8,128]{2,1,0:T(8,128)S(1)} collective-permute-done((f32[12,8,128]{2,1,0:T(8,128)S(1)}, f32[12,8,128]{2,1,0:T(8,128)S(1)}, u32[]{:S(2)}, u32[]{:S(2)}) %collective-permute-start.5) | collective-permute-done | bytes 49184 | tf_op jit(solution)/shard_map/ppermute | solution.py:547
  27.5 5.2 %shard_map.80 = (f32[6,18,32,256]{3,2,1,0:T(8,128)S(1)}, f32[5,2,8,128]{3,2,1,0:T(8,128)S(1)}) custom-call(s32[3]{0:T(128)S(1)} %pad_add_fusion.pos, f32[16]{0:T(128)S(1)} %pad_maximum_fusion.tables, f32[4,18,8,128]{3,2,1,0:T(8,128)S(1)} %get-tuple-element.27.xl, f32[4,18,8,128]{3,2,1,0:T(8,128)S(1)} %get-tuple-element.28.xh, ...), custom_call_target="tpu_custom_call" | custom-call | tf_op jit(solution)/shard_map/pallas_call | solution.py:22
  32.8 1.5 %collective-permute-start.7 = (f32[5,2,8,128]{3,2,1,0:T(8,128)S(1)}, f32[5,2,8,128]{3,2,1,0:T(8,128)S(1)}, u32[]{:S(2)}, u32[]{:S(2)}) collective-permute-start(f32[5,2,8,128]{3,2,1,0:T(8,128)S(1)} %get-tuple-element.35.own), channel_id=1, source_target_pairs={{2,0},{3,1},{0,2},{1,3},{6,4},{7,5},{4,6},{5,7},{10,8},{11,9},{8,1... | collective-permute-start | bytes 122888 | tf_op jit(solution)/shard_map/ppermute | solution.py:547
  34.3 1.2 %collective-permute-start.6 = (f32[5,2,8,128]{3,2,1,0:T(8,128)S(1)}, f32[5,2,8,128]{3,2,1,0:T(8,128)S(1)}, u32[]{:S(2)}, u32[]{:S(2)}) collective-permute-start(f32[5,2,8,128]{3,2,1,0:T(8,128)S(1)} %get-tuple-element.35.own), channel_id=1, source_target_pairs={{1,0},{2,1},{3,2},{0,3},{5,4},{6,5},{7,6},{4,7},{9,8},{10,9},{11,1... | collective-permute-start | bytes 122888 | tf_op jit(solution)/shard_map/ppermute | solution.py:547
  35.4 1.4 %collective-permute-done.8.b3 = f32[5,2,8,128]{3,2,1,0:T(8,128)S(1)} collective-permute-done((f32[5,2,8,128]{3,2,1,0:T(8,128)S(1)}, f32[5,2,8,128]{3,2,1,0:T(8,128)S(1)}, u32[]{:S(2)}, u32[]{:S(2)}) %collective-permute-start.8) | collective-permute-done | bytes 40992 | tf_op jit(solution)/shard_map/ppermute | solution.py:547
  36.8 0.4 collective-permute-done.7.b2
  37.3 0.6 collective-permute-done.6.b1
  37.9 4.1 %collective-permute-start.10 = (f32[5,8,8,128]{3,2,1,0:T(8,128)S(1)}, f32[5,8,8,128]{3,2,1,0:T(8,128)S(1)}, u32[]{:S(2)}, u32[]{:S(2)}) collective-permute-start(f32[5,8,8,128]{3,2,1,0:T(8,128)S(1)} %get-tuple-element.36.own), channel_id=1, source_target_pairs={{240,0},{0,16},{16,32},{32,48},{48,64},{64,80},{80,96},{96,112},{1... | collective-permute-start | bytes 491528 | tf_op jit(solution)/shard_map/ppermute | solution.py:547
  42.0 3.8 %collective-permute-start.9 = (f32[5,8,8,128]{3,2,1,0:T(8,128)S(1)}, f32[5,8,8,128]{3,2,1,0:T(8,128)S(1)}, u32[]{:S(2)}, u32[]{:S(2)}) collective-permute-start(f32[5,8,8,128]{3,2,1,0:T(8,128)S(1)} %get-tuple-element.36.own), channel_id=1, source_target_pairs={{16,0},{32,16},{48,32},{64,48},{80,64},{96,80},{112,96},{128,112},... | collective-permute-start | bytes 491528 | tf_op jit(solution)/shard_map/ppermute | solution.py:547
  45.8 2.6 %collective-permute-start.11 = (f32[5,4,8,128]{3,2,1,0:T(8,128)S(1)}, f32[5,4,8,128]{3,2,1,0:T(8,128)S(1)}, u32[]{:S(2)}, u32[]{:S(2)}) collective-permute-start(f32[5,4,8,128]{3,2,1,0:T(8,128)S(1)} %get-tuple-element.37), channel_id=1, source_target_pairs={{32,0},{48,16},{64,32},{80,48},{96,64},{112,80},{128,96},{144,112}... | collective-permute-start | bytes 245768 | tf_op jit(solution)/shard_map/ppermute | solution.py:547
  48.4 1.8 %collective-permute-done.11.r2 = f32[5,4,8,128]{3,2,1,0:T(8,128)S(1)} collective-permute-done((f32[5,4,8,128]{3,2,1,0:T(8,128)S(1)}, f32[5,4,8,128]{3,2,1,0:T(8,128)S(1)}, u32[]{:S(2)}, u32[]{:S(2)}) %collective-permute-start.11) | collective-permute-done | bytes 81952 | tf_op jit(solution)/shard_map/ppermute | solution.py:547
  50.2 3.1 %collective-permute-done.12.l2 = f32[5,4,8,128]{3,2,1,0:T(8,128)S(1)} collective-permute-done((f32[5,4,8,128]{3,2,1,0:T(8,128)S(1)}, f32[5,4,8,128]{3,2,1,0:T(8,128)S(1)}, u32[]{:S(2)}, u32[]{:S(2)}) %collective-permute-start.12) | collective-permute-done | bytes 81952 | tf_op jit(solution)/shard_map/ppermute | solution.py:547
  53.2 0.4 shard_map.82
  53.7 1.5 %collective-permute-start.14 = (f32[32,8,128]{2,1,0:T(8,128)S(1)}, f32[32,8,128]{2,1,0:T(8,128)S(1)}, u32[]{:S(2)}, u32[]{:S(2)}) collective-permute-start(f32[32,8,128]{2,1,0:T(8,128)S(1)} %get-tuple-element.41), channel_id=1, source_target_pairs={{12,0},{0,4},{4,8},{8,12},{13,1},{1,5},{5,9},{9,13},{14,2},{2,6},{... | collective-permute-start | bytes 393224 | tf_op jit(solution)/shard_map/ppermute | solution.py:547
  55.2 2.4 %collective-permute-done.13.yl = f32[32,8,128]{2,1,0:T(8,128)S(1)} collective-permute-done((f32[32,8,128]{2,1,0:T(8,128)S(1)}, f32[32,8,128]{2,1,0:T(8,128)S(1)}, u32[]{:S(2)}, u32[]{:S(2)}) %collective-permute-start.13) | collective-permute-done | bytes 131104 | tf_op jit(solution)/shard_map/ppermute | solution.py:547
  57.5 1.5 %collective-permute-done.14.yh = f32[32,8,128]{2,1,0:T(8,128)S(1)} collective-permute-done((f32[32,8,128]{2,1,0:T(8,128)S(1)}, f32[32,8,128]{2,1,0:T(8,128)S(1)}, u32[]{:S(2)}, u32[]{:S(2)}) %collective-permute-start.14) | collective-permute-done | bytes 131104 | tf_op jit(solution)/shard_map/ppermute | solution.py:547
  59.0 3.6 %shard_map.83 = (f32[6,16,32,128]{3,2,1,0:T(8,128)S(1)}, f32[6,8,16,128]{3,2,1,0:T(8,128)S(1)}, f32[64,1,640]{2,1,0:T(1,128)S(1)}) custom-call(s32[3]{0:T(128)S(1)} %pad_add_fusion.pos, f32[5,8,32,128]{3,2,1,0:T(8,128)S(1)} %get-tuple-element.39.whole, f32[32,8,128]{2,1,0:T(8,128)S(1)} %collective-permute-done.13.yl, ...), custom_call_target="tpu_custom_call" | custom-call | tf_op jit(solution)/shard_map/pallas_call | solution.py:22
  62.6 17.7 %all_to_all.5.got = f32[64,1,640]{2,1,0:T(1,128)S(1)} all-to-all(f32[64,1,640]{2,1,0:T(1,128)S(1)} %get-tuple-element.42), channel_id=1, replica_groups=mesh['gx'=16,'gy'=4,'gz'=4] {'gy','gx'}, dimensions={0} | all-to-all | bytes 327680 | tf_op jit(solution)/shard_map/all_to_all | solution.py:603
  80.3 6.4 %shard_map.84 = (f32[8,16,128]{2,1,0:T(8,128)}, f32[8,16,128]{2,1,0:T(8,128)}) custom-call(s32[3]{0:T(128)S(1)} %pad_add_fusion.pos, f32[64,1,640]{2,1,0:T(1,128)S(1)} %all_to_all.5.got, f32[6,18,32,256]{3,2,1,0:T(8,128)S(1)} %get-tuple-element.43.a0, f32[6,16,32,128]{3,2,1,0:T(8,128)S(1)} %get-tuple-element.44.a1, f32[6,8,16,128]{3,2,1,0:T(8,128)S(1)} %get-tuple-element.45.a2), custom_call_target="tpu_custom_call" | custom-call | tf_op jit(solution)/shard_map/pallas_call | solution.py:22
  (11 shorter events, 0.3 us)
Async XLA Ops:
  2.4 6.6 %collective-permute-start = (f32[4,5,16,128]{3,2,1,0:T(8,128)}, f32[4,5,16,128]{3,2,1,0:T(8,128)S(1)}, u32[]{:S(2)}, u32[]{:S(2)}) collective-permute-start(f32[4,5,16,128]{3,2,1,0:T(8,128)} %get-tuple-element.25), channel_id=1, source_target_pairs={{1,0},{2,1},{3,2},{0,3},{5,4},{6,5},{7,6},{4,7},{9,8},{10,9},{11,1... | collective-permute-start | bytes 491528 | tf_op jit(solution)/shard_map/ppermute | solution.py:547
  5.8 6.2 %collective-permute-start.1 = (f32[4,5,16,128]{3,2,1,0:T(8,128)}, f32[4,5,16,128]{3,2,1,0:T(8,128)S(1)}, u32[]{:S(2)}, u32[]{:S(2)}) collective-permute-start(f32[4,5,16,128]{3,2,1,0:T(8,128)} %get-tuple-element.26), channel_id=1, source_target_pairs={{3,0},{0,1},{1,2},{2,3},{7,4},{4,5},{5,6},{6,7},{11,8},{8,9},{9,10... | collective-permute-start | bytes 491528 | tf_op jit(solution)/shard_map/ppermute | solution.py:547
  12.0 1.0 %copy-start = (f32[4,8,16,128]{3,2,1,0:T(8,128)S(1)}, f32[4,8,16,128]{3,2,1,0:T(8,128)}, u32[]{:S(2)}) copy-start(f32[4,8,16,128]{3,2,1,0:T(8,128)} %get-tuple-element.24.own) | copy-start | bytes 786436
  13.0 6.4 %collective-permute-start.2 = (f32[39,8,128]{2,1,0:T(8,128)S(1)}, f32[39,8,128]{2,1,0:T(8,128)S(1)}, u32[]{:S(2)}, u32[]{:S(2)}) collective-permute-start(f32[39,8,128]{2,1,0:T(8,128)S(1)} %get-tuple-element.29), channel_id=1, source_target_pairs={{16,0},{32,16},{48,32},{64,48},{80,64},{96,80},{112,96},{128,112},... | collective-permute-start | bytes 479240 | tf_op jit(solution)/shard_map/ppermute | solution.py:547
  14.9 5.0 %collective-permute-start.3 = (f32[39,8,128]{2,1,0:T(8,128)S(1)}, f32[39,8,128]{2,1,0:T(8,128)S(1)}, u32[]{:S(2)}, u32[]{:S(2)}) collective-permute-start(f32[39,8,128]{2,1,0:T(8,128)S(1)} %get-tuple-element.30), channel_id=1, source_target_pairs={{240,0},{0,16},{16,32},{32,48},{48,64},{64,80},{80,96},{96,112},{1... | collective-permute-start | bytes 479240 | tf_op jit(solution)/shard_map/ppermute | solution.py:547
  20.5 4.0 %collective-permute-start.4 = (f32[12,8,128]{2,1,0:T(8,128)S(1)}, f32[12,8,128]{2,1,0:T(8,128)S(1)}, u32[]{:S(2)}, u32[]{:S(2)}) collective-permute-start(f32[12,8,128]{2,1,0:T(8,128)S(1)} %get-tuple-element.33), channel_id=1, source_target_pairs={{4,0},{8,4},{12,8},{0,12},{5,1},{9,5},{13,9},{1,13},{6,2},{10,6},{... | collective-permute-start | bytes 147464 | tf_op jit(solution)/shard_map/ppermute | solution.py:547
  23.3 4.2 %collective-permute-start.5 = (f32[12,8,128]{2,1,0:T(8,128)S(1)}, f32[12,8,128]{2,1,0:T(8,128)S(1)}, u32[]{:S(2)}, u32[]{:S(2)}) collective-permute-start(f32[12,8,128]{2,1,0:T(8,128)S(1)} %get-tuple-element.34), channel_id=1, source_target_pairs={{12,0},{0,4},{4,8},{8,12},{13,1},{1,5},{5,9},{9,13},{14,2},{2,6},{... | collective-permute-start | bytes 147464 | tf_op jit(solution)/shard_map/ppermute | solution.py:547
  32.7 4.2 %collective-permute-start.8 = (f32[5,2,8,128]{3,2,1,0:T(8,128)S(1)}, f32[5,2,8,128]{3,2,1,0:T(8,128)S(1)}, u32[]{:S(2)}, u32[]{:S(2)}) collective-permute-start(f32[5,2,8,128]{3,2,1,0:T(8,128)S(1)} %get-tuple-element.35.own), channel_id=1, source_target_pairs={{3,0},{0,1},{1,2},{2,3},{7,4},{4,5},{5,6},{6,7},{11,8},{8,9},{9,10... | collective-permute-start | bytes 122888 | tf_op jit(solution)/shard_map/ppermute | solution.py:547
  32.8 4.5 %collective-permute-start.7 = (f32[5,2,8,128]{3,2,1,0:T(8,128)S(1)}, f32[5,2,8,128]{3,2,1,0:T(8,128)S(1)}, u32[]{:S(2)}, u32[]{:S(2)}) collective-permute-start(f32[5,2,8,128]{3,2,1,0:T(8,128)S(1)} %get-tuple-element.35.own), channel_id=1, source_target_pairs={{2,0},{3,1},{0,2},{1,3},{6,4},{7,5},{4,6},{5,7},{10,8},{11,9},{8,1... | collective-permute-start | bytes 122888 | tf_op jit(solution)/shard_map/ppermute | solution.py:547
  34.3 3.6 %collective-permute-start.6 = (f32[5,2,8,128]{3,2,1,0:T(8,128)S(1)}, f32[5,2,8,128]{3,2,1,0:T(8,128)S(1)}, u32[]{:S(2)}, u32[]{:S(2)}) collective-permute-start(f32[5,2,8,128]{3,2,1,0:T(8,128)S(1)} %get-tuple-element.35.own), channel_id=1, source_target_pairs={{1,0},{2,1},{3,2},{0,3},{5,4},{6,5},{7,6},{4,7},{9,8},{10,9},{11,1... | collective-permute-start | bytes 122888 | tf_op jit(solution)/shard_map/ppermute | solution.py:547
  37.9 15.4 %collective-permute-start.10 = (f32[5,8,8,128]{3,2,1,0:T(8,128)S(1)}, f32[5,8,8,128]{3,2,1,0:T(8,128)S(1)}, u32[]{:S(2)}, u32[]{:S(2)}) collective-permute-start(f32[5,8,8,128]{3,2,1,0:T(8,128)S(1)} %get-tuple-element.36.own), channel_id=1, source_target_pairs={{240,0},{0,16},{16,32},{32,48},{48,64},{64,80},{80,96},{96,112},{1... | collective-permute-start | bytes 491528 | tf_op jit(solution)/shard_map/ppermute | solution.py:547
  42.0 11.2 %collective-permute-start.9 = (f32[5,8,8,128]{3,2,1,0:T(8,128)S(1)}, f32[5,8,8,128]{3,2,1,0:T(8,128)S(1)}, u32[]{:S(2)}, u32[]{:S(2)}) collective-permute-start(f32[5,8,8,128]{3,2,1,0:T(8,128)S(1)} %get-tuple-element.36.own), channel_id=1, source_target_pairs={{16,0},{32,16},{48,32},{64,48},{80,64},{96,80},{112,96},{128,112},... | collective-permute-start | bytes 491528 | tf_op jit(solution)/shard_map/ppermute | solution.py:547
  45.8 4.4 %collective-permute-start.11 = (f32[5,4,8,128]{3,2,1,0:T(8,128)S(1)}, f32[5,4,8,128]{3,2,1,0:T(8,128)S(1)}, u32[]{:S(2)}, u32[]{:S(2)}) collective-permute-start(f32[5,4,8,128]{3,2,1,0:T(8,128)S(1)} %get-tuple-element.37), channel_id=1, source_target_pairs={{32,0},{48,16},{64,32},{80,48},{96,64},{112,80},{128,96},{144,112}... | collective-permute-start | bytes 245768 | tf_op jit(solution)/shard_map/ppermute | solution.py:547
  48.4 4.9 %collective-permute-start.12 = (f32[5,4,8,128]{3,2,1,0:T(8,128)S(1)}, f32[5,4,8,128]{3,2,1,0:T(8,128)S(1)}, u32[]{:S(2)}, u32[]{:S(2)}) collective-permute-start(f32[5,4,8,128]{3,2,1,0:T(8,128)S(1)} %get-tuple-element.38), channel_id=1, source_target_pairs={{224,0},{240,16},{0,32},{16,48},{32,64},{48,80},{64,96},{80,112},{... | collective-permute-start | bytes 245768 | tf_op jit(solution)/shard_map/ppermute | solution.py:547
  53.6 3.9 %collective-permute-start.13 = (f32[32,8,128]{2,1,0:T(8,128)S(1)}, f32[32,8,128]{2,1,0:T(8,128)S(1)}, u32[]{:S(2)}, u32[]{:S(2)}) collective-permute-start(f32[32,8,128]{2,1,0:T(8,128)S(1)} %get-tuple-element.40), channel_id=1, source_target_pairs={{4,0},{8,4},{12,8},{0,12},{5,1},{9,5},{13,9},{1,13},{6,2},{10,6},{... | collective-permute-start | bytes 393224 | tf_op jit(solution)/shard_map/ppermute | solution.py:547
  53.7 5.3 %collective-permute-start.14 = (f32[32,8,128]{2,1,0:T(8,128)S(1)}, f32[32,8,128]{2,1,0:T(8,128)S(1)}, u32[]{:S(2)}, u32[]{:S(2)}) collective-permute-start(f32[32,8,128]{2,1,0:T(8,128)S(1)} %get-tuple-element.41), channel_id=1, source_target_pairs={{12,0},{0,4},{4,8},{8,12},{13,1},{1,5},{5,9},{9,13},{14,2},{2,6},{... | collective-permute-start | bytes 393224 | tf_op jit(solution)/shard_map/ppermute | solution.py:547

commit v4 on v3

--- a/solution.py
+++ b/solution.py
@@ -58,21 +58,13 @@
     return pick(a, first + iota(a.shape, 1) // 2)
 
 
-def each(start, stop, body, unroll=1):
-    if unroll >= stop - start:
-        for z in range(start, stop):
-            body(z)
-        return
-
-    def step(z, carry):
+def each(start, stop, body):
+    for z in range(start, stop):
         body(z)
-        return carry
-
-    lax.fori_loop(start, stop, step, 0, unroll=unroll)
 
 
 def wrap(z, n):
-    return z % n if isinstance(z, int) else lax.rem(z + n, n)
+    return z % n
 
 
 def around(a, field, z, zm, zp):
@@ -102,20 +94,20 @@
     return lambda z: (z, wrap(z - 1, n), wrap(z + 1, n))
 
 
-def pre(a, d, r, res, n, unroll):
+def pre(a, d, r, res, n):
     c3 = circ(n)
-    each(0, n, lambda z: finish(a, d, r, z, wrap(z - 1, n)), unroll)
+    each(0, n, lambda z: finish(a, d, r, z, wrap(z - 1, n)))
 
     def one(z):
         a[V, z] = smoothed(a, lambda k: a[C, k], *c3(z))
 
-    each(0, n, one, unroll)
+    each(0, n, one)
 
     def two(z):
         v, beside = around(a, lambda k: a[V, k], *c3(z))
         res[z] = d[z] * (1.5 * a[C, z] - v) + beside
 
-    each(0, n, two, unroll)
+    each(0, n, two)
 
 
 def halve(a, sink, r, t, store, n, rows):
@@ -136,7 +128,7 @@
         for k in range(5):
             store(k, z, fold_rows(t.at[k, z], rows // 2))
 
-    each(0, n // 2, body, n)
+    each(0, n // 2, body)
 
 
 def fold_rows(t, n):
@@ -150,21 +142,27 @@
     return t[...]
 
 
-def pack_z(f, b, s, d, lo, hi, own, fi, bi, sems):
+def fetch(f, b, s, d, fi, bi, sf, df, sems):
     copies = [
-        pltpu.make_async_copy(f, fi, sems.at[0]),
-        pltpu.make_async_copy(b, bi, sems.at[1]),
-        pltpu.make_async_copy(s, own.at[2], sems.at[2]),
-        pltpu.make_async_copy(d, own.at[3], sems.at[3]),
+        pltpu.make_async_copy(src, dst, sems.at[k])
+        for k, (src, dst) in enumerate(((f, fi), (b, bi), (s, sf), (d, df)))
     ]
     for copy in copies:
         copy.start()
-    for k, copy in enumerate(copies):
+    for copy in copies:
         copy.wait()
-        if k < 2:
-            own[k] = (fi, bi)[k][...].astype(F32)
-        lo[k] = own[k, 0:H]
-        hi[k] = own[k, 8 - H : 8]
+    return [fi[...].astype(F32), bi[...].astype(F32), sf[...], df[...]]
+
+
+def pack_z(f, b, s, d, lo, hi, *scratch):
+    for k, value in enumerate(fetch(f, b, s, d, *scratch)):
+        lo[k] = value[0:H]
+        hi[k] = value[8 - H : 8]
+
+
+def fetch_own(f, b, s, d, own, *scratch):
+    for k, value in enumerate(fetch(f, b, s, d, *scratch)):
+        own[k] = value
 
 
 FACIES, BOUNDARY, SOURCE, DENSITY = range(4)
@@ -221,92 +219,105 @@
             for tile, ref in enumerate((xl, xh, rl, rh)):
                 g, at, width = block_of(k, z, tile)
                 v = ref[k, z]
-                here = lane // width == at // width
-                a, b = turn(v, at), turn(v, at + width)
-                left[g] = a if at == 0 else jnp.where(here, a, left[g])
-                right[g] = b if at == 0 else jnp.where(here, b, right[g])
+                v = turn(v, at)
+                left[g] = v if at == 0 else jnp.where(lane // width == at // width, v, left[g])
+                before = (at // width - 1) % (128 // width)
+                right[g] = v if at == 0 else jnp.where(lane // width == before, v, right[g])
     for g in range(YTILES):
         lo[g] = left[g]
         hi[g] = right[g]
 
 
-def level0(pos, tables, xl, xh, rl, rh, yl, yh, a, packed, raw, hs, vs, dd, res, sk, t, m):
-    gx, gy, gz = pos[0], pos[1], pos[2]
+PART = PUX, PUZ, PSINK, PB, PH = range(5)
+
+
+def tile0(pos, tables, raw, first_lane, part, vs):
+    row, lane = iota((32, 128), 0), iota((32, 128), 1)
+    x = pos[0] * 16 + jnp.where(row < 24, row, row - 32)
+    y = pos[1] * 128 + first_lane + (lane if first_lane == 0 else jnp.where(lane < 64, lane, lane - 256))
+    inside = (x >= 0) & (x < 256) & (y >= 0) & (y < 512)
+    for z in range(Z0):
+        zg = pos[2] * 8 + z - H
+        here = inside & ((zg >= 0) & (zg < 32))
+        kind = raw(FACIES, z)
+        h = jnp.full((32, 128), tables[0], F32)
+        v = jnp.full((32, 128), tables[8], F32)
+        for n in range(1, 8):
+            is_n = kind == float(n)
+            h = jnp.where(is_n, tables[n], h)
+            v = jnp.where(is_n, tables[8 + n], v)
+        part[PH, z] = jnp.where(here, h, 0.0)
+        vs[z] = jnp.where(here, v, 0.0)
+    for z in range(Z0 - 1):
+        h, v = part[PH, z], vs[z]
+        hn, vn = up(h, 0), vs[z + 1]
+        hsum, vsum = h + hn, v + vn
+        hsum = jnp.where(hsum > 0.0, hsum, 1.0)
+        vsum = jnp.where(vsum > 0.0, vsum, 1.0)
+        twice = 2.0 / (hsum * vsum)
+        part[PUX, z] = (h * hn) * (twice * vsum)
+        part[PUZ, z] = (v * vn) * (twice * hsum)
+    for z in range(1, Z0 - 1):
+        kind = raw(BOUNDARY, z)
+        part[PSINK, z] = jnp.where(
+            kind == 1.0, 2.0 * vs[z], jnp.where(kind == 2.0, 0.5 * part[PH, z], 0.0)
+        )
+        dens = raw(DENSITY, z)
+        part[PB, z] = (
+            raw(SOURCE, z)
+            + 0.5 * part[PUZ, z] * (dens + raw(DENSITY, z + 1))
+            - 0.5 * part[PUZ, z - 1] * (raw(DENSITY, z - 1) + dens)
+        )
+
+
+def main0(pos, tables, xl, xh, rl, rh, part, vs):
+    def raw(k, z):
+        return jnp.concatenate([ref[k, z] for ref in (xl, xh, rl, rh)], axis=0)
+
+    tile0(pos, tables, raw, 0, part, vs)
+
+
+def level0(pos, tables, main, yl, yh, a, packed, raw, side, vs, hs, dd, res, t, m):
     lane8 = iota((8, 128), 1)
     for k in range(4):
         for z in range(Z0):
             for tile in range(4):
                 g, at, width = block_of(k, z, tile)
-                raw[k, z, 8 * tile : 8 * tile + 8, 128:256] = jnp.where(
-                    lane8 < width,
-                    turn(yl[g], -at),
-                    jnp.where(lane8 >= 128 - width, turn(yh[g], -at - width), 0.0),
-                )
-    for row, ref in ((0, xl), (8, xh), (16, rl), (24, rh)):
-        raw[:, :, row : row + 8, 0:128] = ref[...]
+                both = jnp.where(lane8 // width == at // width, yl[g], yh[g])
+                raw[k, z, 8 * tile : 8 * tile + 8] = turn(both, -at)
+    tile0(pos, tables, lambda k, z: raw[k, z], 128, side, vs)
+
+    def both(k, z):
+        return jnp.concatenate([main[k, z], side[k, z]], axis=1)
 
     row, lane = iota((32, 256), 0), iota((32, 256), 1)
-    x = gx * 16 + jnp.where(row < 24, row, row - 32)
-    y = gy * 128 + jnp.where(lane < 192, lane, lane - 256)
-    inside = (x >= 0) & (x < 256) & (y >= 0) & (y < 512)
-
-    def materials(z):
-        zg = gz * 8 + z - H
-        here = inside & ((zg >= 0) & (zg < 32))
-        kind = raw[0, z]
-        h = jnp.full((32, 256), tables[0], F32)
-        v = jnp.full((32, 256), tables[8], F32)
-        for n in range(1, 8):
-            is_n = kind == float(n)
-            h = jnp.where(is_n, tables[n], h)
-            v = jnp.where(is_n, tables[8 + n], v)
-        hs[z] = jnp.where(here, h, 0.0)
-        vs[z] = jnp.where(here, v, 0.0)
-
-    each(0, Z0, materials, 2)
-
-    def harmonic(c, n):
-        s = c + n
-        return 2.0 * c * n / jnp.where(s > 0.0, s, 1.0)
-
-    def couple(z):
-        h = hs[z]
-        a[UX, z] = harmonic(h, up(h, 0))
-        a[UY, z] = harmonic(h, up(h, 1))
-        a[UZ, z] = harmonic(vs[z], vs[z + 1])
-
-    each(0, Z0 - 1, couple, 2)
-
     odd_row, odd_lane = row % 2 == 1, lane % 2 == 1
-
-    def setup(z):
-        h, v = hs[z], vs[z]
-        sink = jnp.where(raw[1, z] == 1.0, 2.0 * v, jnp.where(raw[1, z] == 2.0, 0.5 * h, 0.0))
-        ux, uy, uz, lz = a[UX, z], a[UY, z], a[UZ, z], a[UZ, z - 1]
+    a[UZ, 0] = both(PUZ, 0)
+    for z in range(1, Z0 - 1):
+        h, sink, ux, uz, lz = both(PH, z), both(PSINK, z), both(PUX, z), both(PUZ, z), a[UZ, z - 1]
+        hn = up(h, 1)
+        hsum = h + hn
+        uy = 2.0 * h * hn / jnp.where(hsum > 0.0, hsum, 1.0)
+        a[UX, z], a[UY, z], a[UZ, z] = ux, uy, uz
         lx, ly = down(ux, 0), down(uy, 1)
         diag = sink + lz + uz + lx + ux + ly + uy
-        dens = raw[3, z]
-        b = raw[2, z] + 0.5 * uz * (dens + raw[3, z + 1]) - 0.5 * lz * (raw[3, z - 1] + dens)
         rd = jnp.where(diag > 0.0, W / jnp.where(diag > 0.0, diag, 1.0), 0.0)
         a[RD, z] = rd
-        a[C, z] = rd * b
+        a[C, z] = rd * both(PB, z)
         dd[z] = diag
-        sk[z] = sink
         outer = sink + jnp.where(odd_row, ux, lx) + jnp.where(odd_lane, uy, ly)
-        hs[z] = outer + jnp.where((z - H) % 2 == 1, uz, lz)
-
-    each(1, Z0 - 1, setup, 2)
+        hs[z] = (outer + (uz if (z - H) % 2 == 1 else lz))[0:16, 0:128]
 
     def first(z):
         a[V, z] = smoothed(a, lambda k: a[C, k], z, z - 1, z + 1)
 
-    each(2, Z0 - 2, first, 2)
+    each(2, Z0 - 2, first)
 
     def residual(z):
         v, beside = around(a, lambda k: a[V, k], z, z - 1, z + 1)
         res[z - H] = (dd[z] * (1.5 * a[C, z] - v) + beside)[0:16, 0:128]
 
-    each(H, H + 8, residual, 2)
+    each(H, H + 8, residual)
 
     o_row = iota((16, 128), 0) % 2 == 1
     o_lane = iota((16, 128), 1) % 2 == 1
@@ -314,23 +325,23 @@
     def coarsen(z):
         lo, hi = H + 2 * z, H + 2 * z + 1
 
-        def both(ref):
+        def pair(ref):
             return ref[lo, 0:16, 0:128] + ref[hi, 0:16, 0:128]
 
         parts = (
-            jnp.where(o_row, both(a.at[UX]), 0.0),
-            jnp.where(o_lane, both(a.at[UY]), 0.0),
+            jnp.where(o_row, pair(a.at[UX]), 0.0),
+            jnp.where(o_lane, pair(a.at[UY]), 0.0),
             a[UZ, hi, 0:16, 0:128],
-            both(sk),
+            pair(main.at[PSINK]),
             res[2 * z] + res[2 * z + 1],
-            both(hs),
+            hs[lo] + hs[hi],
         )
         for k, part in enumerate(parts):
             t[k, z] = part
         for k in range(6):
             m[k, z] = fold_rows(t.at[k, z], 8)
 
-    each(0, 4, coarsen, 4)
+    each(0, 4, coarsen)
     lower = lane8 < 64
     for s in range(2):
         parts = [jnp.where(lower, fold_lanes(m[k, s]), fold_lanes(m[k, 2 + s])) for k in range(6)]
@@ -355,15 +366,16 @@
         for s in range(2):
             part = slice(4 * s, 4 * s + 4)
             whole[:, 2 * n + s, 16:24] = jnp.concatenate([r2[:, n, part], l2[:, n, part]], axis=1)
-    block = (iota((8, 128), 1) % 64) // 12
+    lane = iota((8, 128), 1)
+    block, last = (lane % 64) // 12, ((lane + 12) % 64) // 12
     for g in range(32):
         left = right = None
         for at in range(5):
             layer, tile = divmod(5 * g + at, 4)
             v = whole[layer // 8, layer % 8, 8 * tile : 8 * tile + 8]
-            a, b = turn(v, 12 * at), turn(v, 12 * at - 52)
-            left = a if at == 0 else jnp.where(block == at, a, left)
-            right = b if at == 0 else jnp.where(block == at, b, right)
+            v = turn(v, 12 * at)
+            left = v if at == 0 else jnp.where(block == at, v, left)
+            right = v if at == 0 else jnp.where(last == at, v, right)
         lo[g] = left
         hi[g] = right
 
@@ -380,20 +392,17 @@
         for k in range(5):
             for n in range(8):
                 g, at = divmod(4 * (8 * k + n) + tile, 5)
-                v, right, left = whole[k, n, rows], yl[g], yh[g]
+                v = whole[k, n, rows]
+                near = jnp.where((lane % 64) // 12 == at, yl[g], yh[g])
                 for part in range(2):
                     own = turn(v, 64 * part)
-                    beyond = jnp.where(
-                        lane < 76,
-                        turn(right, 64 - 64 * part - 12 * at),
-                        jnp.where(lane >= 116, turn(left, 116 - 64 * part - 12 * at), 0.0),
-                    )
+                    beyond = turn(near, 64 - 64 * part - 12 * at)
                     value = jnp.where(inside, jnp.where(lane < 64, own, beyond), 0.0)
                     z = 4 * (n // 2) + 2 * part + n % 2
                     a[k, z, rows] = value
                     if k == SINK:
                         s1[z, rows] = value
-    pre(a, d1, None, r1, 16, 4)
+    pre(a, d1, None, r1, 16)
 
     def keep1(k, z, value):
         value = fold_lanes(value)
@@ -405,7 +414,7 @@
             q2[z] = value
 
     halve(a, s1, r1, t1, keep1, 16, 32)
-    pre(b, d2, q2, r2, 8, 8)
+    pre(b, d2, q2, r2, 8)
 
     def keep2(k, z, value):
         m1[z, 0, k : k + 1] = value[0:1]
@@ -424,13 +433,9 @@
         sent[:, :, 128 * k : 128 * k + 128] = jnp.broadcast_to(total[k : k + 1][None], (64, 1, 128))
 
 
-def sweep(a, src, dst, n, unroll):
-    c3 = circ(n)
-
-    def body(z):
-        dst[z] = smoothed(a, lambda k: src[k], *c3(z))
-
-    each(0, n, body, unroll)
+def sweep(a, src, dst, n, layers=None):
+    for z in layers or range(n):
+        dst[z % n] = smoothed(a, lambda k: src[k], z % n, (z - 1) % n, (z + 1) % n)
 
 
 def solve(
@@ -453,7 +458,7 @@
                 else:
                     r3[z, pl.ds(s, 16, stride=2), :] = value
     s3[...] = a3[SINK]
-    pre(a3, d3, r3, e3, 4, 4)
+    pre(a3, d3, r3, e3, 4)
 
     def keep3(k, z, value):
         value = fold_lanes(value)
@@ -465,7 +470,7 @@
             r4[z] = value
 
     halve(a3, s3, e3, t3, keep3, 4, 32)
-    pre(a4, d4, r4, e4, 2, 2)
+    pre(a4, d4, r4, e4, 2)
 
     def keep4(k, z, value):
         q5[k] = fold_lanes(value)
@@ -485,14 +490,14 @@
     e = spread_rows(g4, spread_lanes(v))
     for z in range(2):
         a4[V, z] = a4[V, z] + e
-    sweep(a4, a4.at[V], e4, 2, 2)
-    sweep(a4, e4, r4, 2, 2)
+    sweep(a4, a4.at[V], e4, 2)
+    sweep(a4, e4, r4, 2)
     for z in range(2):
         e = spread_rows(g3.at[z], spread_lanes(r4[z]))
         a3[V, 2 * z] = a3[V, 2 * z] + e
         a3[V, 2 * z + 1] = a3[V, 2 * z + 1] + e
-    sweep(a3, a3.at[V], e3, 4, 4)
-    sweep(a3, e3, r3, 4, 4)
+    sweep(a3, a3.at[V], e3, 4)
+    sweep(a3, e3, r3, 4)
     b3[:, 8:40] = r3[...]
     b3[:, 0:8] = r3[:, 24:32]
     b3[:, 40:48] = r3[:, 0:8]
@@ -505,14 +510,14 @@
         e = spread_rows(g2.at[z], e)
         e2[2 * z] = a2[V, 2 * z] + e
         e2[2 * z + 1] = a2[V, 2 * z + 1] + e
-    sweep(a2, e2, f2, 8, 8)
-    sweep(a2, f2, e2, 8, 8)
-    for z in range(8):
-        e = spread_rows(g1.at[z], spread_lanes(e2[z]))
-        e1[0, 2 * z] = a1[V, 2 * z] + e
-        e1[0, 2 * z + 1] = a1[V, 2 * z + 1] + e
-    sweep(a1, e1.at[0], e1.at[1], 16, 4)
-    sweep(a1, e1.at[1], e1.at[0], 16, 4)
+    sweep(a2, e2, f2, 8)
+    sweep(a2, f2, e2, 8, range(-2, 4))
+    for z in range(-2, 4):
+        e = spread_rows(g1.at[z % 8], spread_lanes(e2[z % 8]))
+        for zf in (2 * z % 16, 2 * z % 16 + 1):
+            e1[0, zf] = a1[V, zf] + e
+    sweep(a1, e1.at[0], e1.at[1], 16, range(-3, 7))
+    sweep(a1, e1.at[1], e1.at[0], 16, range(-2, 6))
     upper = iota((8, 128), 0) < 4
     for zc in range(-2, 6):
         v = e1[0, zc % 16]
@@ -530,8 +535,8 @@
 
         return body
 
-    each(3, Z0 - 3, sweep0(0, 1), 2)
-    each(4, Z0 - 4, sweep0(1, 0), 2)
+    each(3, Z0 - 3, sweep0(0, 1))
+    each(4, Z0 - 4, sweep0(1, 0))
 
     def last(z):
         v, beside = around(a0, lambda k: w0[0, k], z, z - 1, z + 1)
@@ -539,7 +544,7 @@
         pressure[z - H] = v[0:16, 0:128]
         left[z - H] = r[0:16, 0:128]
 
-    each(H, H + 8, last, 2)
+    each(H, H + 8, last)
 
 
 def shift(value, axis, by):
@@ -550,18 +555,15 @@
 def local(facies, boundary, hc, vc, source, density):
     pos = jnp.stack([lax.axis_index(n) for n in ("gx", "gy", "gz")]).astype(jnp.int32)
     tables = jnp.concatenate([hc, vc])
-    lo, hi, own = call(
-        pack_z,
-        [(4, H, 16, 128)] * 2 + [(4, 8, 16, 128)],
-        facies, boundary, source, density,
-        spaces=[HBM] * 4,
-        limit=60,
-        scratch=[
-            pltpu.VMEM((8, 16, 128), jnp.int32), pltpu.VMEM((8, 16, 128), jnp.int32),
-            pltpu.SemaphoreType.DMA((4,)),
-        ],
-    )
+    raw = (facies, boundary, source, density)
+    landing = [
+        pltpu.VMEM((8, 16, 128), jnp.int32), pltpu.VMEM((8, 16, 128), jnp.int32),
+        (8, 16, 128), (8, 16, 128), pltpu.SemaphoreType.DMA((4,)),
+    ]
+    plan = dict(spaces=[HBM] * 4, scratch=landing, limit=60)
+    lo, hi = call(pack_z, [(4, H, 16, 128)] * 2, *raw, **plan)
     above, below = shift(lo, "gz", 1), shift(hi, "gz", -1)
+    (own,) = call(fetch_own, [(4, 8, 16, 128)], *raw, **plan)
     xl, xh, lo, hi = call(
         pack_x, [(4, Z0, 8, 128)] * 2 + [(XTILES, 8, 128)] * 2, own, above, below
     )
@@ -570,14 +572,18 @@
         pack_y, [(4, Z0, 8, 128)] * 2 + [(YTILES, 8, 128)] * 2, xl, xh, ml, mh
     )
     yl, yh = shift(lo, "gy", 1), shift(hi, "gy", -1)
+    (main,) = call(
+        main0, [(5, Z0, 32, 128)], pos, tables, xl, xh, rl, rh,
+        spaces=[SMEM] * 2 + [VMEM] * 4, scratch=[(Z0, 32, 128)],
+    )
     a0, packed = call(
         level0,
         [(6, Z0, 32, 256), (5, 2, 8, 128)],
-        pos, tables, xl, xh, rl, rh, yl, yh,
-        spaces=[SMEM] * 2 + [VMEM] * 6,
+        pos, tables, main, yl, yh,
+        spaces=[SMEM] * 2 + [VMEM] * 3,
         scratch=[
-            (4, Z0, 32, 256), (Z0, 32, 256), (Z0, 32, 256), (Z0, 32, 256), (8, 16, 128),
-            (Z0, 32, 256), (6, 4, 16, 128), (6, 4, 8, 128),
+            (4, Z0, 32, 128), (5, Z0, 32, 128), (Z0, 32, 128), (Z0, 16, 128), (Z0, 32, 256),
+            (8, 16, 128), (6, 4, 16, 128), (6, 4, 8, 128),
         ],
     )
     blocks = [shift(packed, "gz", n) for n in (1, 2, 3)]

time: 86.9 us -> 82.3 us (0.947)
  waiting for transfers between devices: 24 us -> 21.3 us
  Pallas kernels: 18.1 us -> 16.1 us
    ppermute x15, waiting for transfers between devices: 24 us -> 21.3 us  [shift(): lax.ppermute(value, axis, [((i + by) % count, i) for i in range(count)])]
    pallas_call x8 -> x10, Pallas kernels: 18.1 us -> 16.1 us  [call(): pl.pallas_call(kernel, out_shape=[jax.ShapeDtypeStruct(s, F32) for s in o...]
  transfers between devices with their start and end apart: 15 -> 15, of which waited for: 13 -> 13; matrix products, arithmetic and copies ran while one was open for 1% -> 1% of each run, Pallas kernels for 0% -> 3%
where the time goes in v4:
time: 82.3 us; the launch traced here: 82 us
  starting transfers between devices  24.4 us (30%)
  waiting for transfers between devices  21.3 us (26%)
  blocking collectives  17.7 us (22%)
  Pallas kernels  16.1 us (20%)
  local copies, waits for them, and re-layouts  0.95 us (1%)
    ppermute x15, starting transfers between devices, shift(): lax.ppermute(value, axis, [((i + by) % count, i) for i in range(count)])  24.4 us
    ppermute x15, waiting for transfers between devices, shift(): lax.ppermute(value, axis, [((i + by) % count, i) for i in range(count)])  21.3 us
    all_to_all x1, blocking collectives, local(): got = lax.all_to_all(sent, ('gy', 'gx'), 0, 0)  17.7 us
    pallas_call x10, Pallas kernels, call(): pl.pallas_call(kernel, out_shape=[jax.ShapeDtypeStruct(s, F32) for s in o...  16.1 us
  transfers between devices with their start and end apart: 15, of which 13 were waited for; matrix products, arithmetic and copies ran while one was open for 1% of the time, Pallas kernels for 3%

profile of v4, /device:TPU:1, one launch (start us, length us, event | category | flops | bytes accessed | tf_op | source)
XLA Modules:
  0.0 82.0 jit_solution(104709604448921549)
XLA Ops:
  0.6 1.7 %shard_map.78 = (f32[4,5,16,128]{3,2,1,0:T(8,128)}, f32[4,5,16,128]{3,2,1,0:T(8,128)}) custom-call(s32[8,16,128]{2,1,0:T(8,128)} %f.3, s32[8,16,128]{2,1,0:T(8,128)} %b.3, f32[8,16,128]{2,1,0:T(8,128)} %s.3, f32[8,16,128]{2,1,0:T(8,128)} %d.3), custom_call_target="tpu_custom_call" | custom-call | tf_op jit(solution)/shard_map/pallas_call | solution.py:22
  2.3 3.4 %collective-permute-start = (f32[4,5,16,128]{3,2,1,0:T(8,128)}, f32[4,5,16,128]{3,2,1,0:T(8,128)S(1)}, u32[]{:S(2)}, u32[]{:S(2)}) collective-permute-start(f32[4,5,16,128]{3,2,1,0:T(8,128)} %get-tuple-element.23), channel_id=1, source_target_pairs={{1,0},{2,1},{3,2},{0,3},{5,4},{6,5},{7,6},{4,7},{9,8},{10,9},{11,1... | collective-permute-start | bytes 491528 | tf_op jit(solution)/shard_map/ppermute | solution.py:552
  5.7 1.7 %shard_map.77.own = f32[4,8,16,128]{3,2,1,0:T(8,128)} custom-call(s32[8,16,128]{2,1,0:T(8,128)} %f.3, s32[8,16,128]{2,1,0:T(8,128)} %b.3, f32[8,16,128]{2,1,0:T(8,128)} %s.3, f32[8,16,128]{2,1,0:T(8,128)} %d.3), custom_call_target="tpu_custom_call" | custom-call | tf_op jit(solution)/shard_map/pallas_call | solution.py:22
  7.4 1.5 %collective-permute-done.above = f32[4,5,16,128]{3,2,1,0:T(8,128)S(1)} collective-permute-done((f32[4,5,16,128]{3,2,1,0:T(8,128)}, f32[4,5,16,128]{3,2,1,0:T(8,128)S(1)}, u32[]{:S(2)}, u32[]{:S(2)}) %collective-permute-start) | collective-permute-done | bytes 163872 | tf_op jit(solution)/shard_map/ppermute | solution.py:552
  8.9 3.0 %collective-permute-done.1.below = f32[4,5,16,128]{3,2,1,0:T(8,128)S(1)} collective-permute-done((f32[4,5,16,128]{3,2,1,0:T(8,128)}, f32[4,5,16,128]{3,2,1,0:T(8,128)S(1)}, u32[]{:S(2)}, u32[]{:S(2)}) %collective-permute-start.1) | collective-permute-done | bytes 163872 | tf_op jit(solution)/shard_map/ppermute | solution.py:552
  11.9 0.9 %copy-done = f32[4,8,16,128]{3,2,1,0:T(8,128)S(1)} copy-done((f32[4,8,16,128]{3,2,1,0:T(8,128)S(1)}, f32[4,8,16,128]{3,2,1,0:T(8,128)}, u32[]{:S(2)}) %copy-start) | copy-done | bytes 262168
  12.9 1.9 %collective-permute-start.2 = (f32[39,8,128]{2,1,0:T(8,128)S(1)}, f32[39,8,128]{2,1,0:T(8,128)S(1)}, u32[]{:S(2)}, u32[]{:S(2)}) collective-permute-start(f32[39,8,128]{2,1,0:T(8,128)S(1)} %get-tuple-element.27), channel_id=1, source_target_pairs={{16,0},{32,16},{48,32},{64,48},{80,64},{96,80},{112,96},{128,112},... | collective-permute-start | bytes 479240 | tf_op jit(solution)/shard_map/ppermute | solution.py:552
  14.8 1.5 %collective-permute-start.3 = (f32[39,8,128]{2,1,0:T(8,128)S(1)}, f32[39,8,128]{2,1,0:T(8,128)S(1)}, u32[]{:S(2)}, u32[]{:S(2)}) collective-permute-start(f32[39,8,128]{2,1,0:T(8,128)S(1)} %get-tuple-element.28), channel_id=1, source_target_pairs={{240,0},{0,16},{16,32},{32,48},{48,64},{64,80},{80,96},{96,112},{1... | collective-permute-start | bytes 479240 | tf_op jit(solution)/shard_map/ppermute | solution.py:552
  16.4 0.7 pad_maximum_fusion.tables
  17.1 2.2 %collective-permute-done.2.ml = f32[39,8,128]{2,1,0:T(8,128)S(1)} collective-permute-done((f32[39,8,128]{2,1,0:T(8,128)S(1)}, f32[39,8,128]{2,1,0:T(8,128)S(1)}, u32[]{:S(2)}, u32[]{:S(2)}) %collective-permute-start.2) | collective-permute-done | bytes 159776 | tf_op jit(solution)/shard_map/ppermute | solution.py:552
  19.3 0.5 collective-permute-done.3.mh
  19.8 0.4 shard_map.80
  20.2 2.8 %collective-permute-start.4 = (f32[12,8,128]{2,1,0:T(8,128)S(1)}, f32[12,8,128]{2,1,0:T(8,128)S(1)}, u32[]{:S(2)}, u32[]{:S(2)}) collective-permute-start(f32[12,8,128]{2,1,0:T(8,128)S(1)} %get-tuple-element.31), channel_id=1, source_target_pairs={{4,0},{8,4},{12,8},{0,12},{5,1},{9,5},{13,9},{1,13},{6,2},{10,6},{... | collective-permute-start | bytes 147464 | tf_op jit(solution)/shard_map/ppermute | solution.py:552
  23.0 1.0 %shard_map.81.main = f32[5,18,32,128]{3,2,1,0:T(8,128)S(1)} custom-call(s32[3]{0:T(128)S(1)} %pad_add_fusion.pos, f32[16]{0:T(128)S(1)} %pad_maximum_fusion.tables, f32[4,18,8,128]{3,2,1,0:T(8,128)S(1)} %get-tuple-element.25.xl, f32[4,18,8,128]{3,2,1,0:T(8,128)S(1)} %get-tuple-element.26.xh, f32[4,18,8,128]{3,2,1,0:T(8,128)S(1)} %get-tuple-element.29.rl, ...), custom_call_target="tpu_custom_call" | custom-call | tf_op jit(solution)/shard_map/pallas_call | solution.py:22
  24.1 3.0 %collective-permute-done.5.yh = f32[12,8,128]{2,1,0:T(8,128)S(1)} collective-permute-done((f32[12,8,128]{2,1,0:T(8,128)S(1)}, f32[12,8,128]{2,1,0:T(8,128)S(1)}, u32[]{:S(2)}, u32[]{:S(2)}) %collective-permute-start.5) | collective-permute-done | bytes 49184 | tf_op jit(solution)/shard_map/ppermute | solution.py:552
  27.1 3.3 %shard_map.82 = (f32[6,18,32,256]{3,2,1,0:T(8,128)S(1)}, f32[5,2,8,128]{3,2,1,0:T(8,128)S(1)}) custom-call(s32[3]{0:T(128)S(1)} %pad_add_fusion.pos, f32[16]{0:T(128)S(1)} %pad_maximum_fusion.tables, f32[5,18,32,128]{3,2,1,0:T(8,128)S(1)} %shard_map.81.main, f32[12,8,128]{2,1,0:T(8,128)S(1)} %collective-permute-done.4.yl, ...), custom_call_target="tpu_custom_call" | custom-call | tf_op jit(solution)/shard_map/pallas_call | solution.py:22
  30.5 1.5 %collective-permute-start.7 = (f32[5,2,8,128]{3,2,1,0:T(8,128)S(1)}, f32[5,2,8,128]{3,2,1,0:T(8,128)S(1)}, u32[]{:S(2)}, u32[]{:S(2)}) collective-permute-start(f32[5,2,8,128]{3,2,1,0:T(8,128)S(1)} %get-tuple-element.33.own), channel_id=1, source_target_pairs={{2,0},{3,1},{0,2},{1,3},{6,4},{7,5},{4,6},{5,7},{10,8},{11,9},{8,1... | collective-permute-start | bytes 122888 | tf_op jit(solution)/shard_map/ppermute | solution.py:552
  32.0 1.2 %collective-permute-start.6 = (f32[5,2,8,128]{3,2,1,0:T(8,128)S(1)}, f32[5,2,8,128]{3,2,1,0:T(8,128)S(1)}, u32[]{:S(2)}, u32[]{:S(2)}) collective-permute-start(f32[5,2,8,128]{3,2,1,0:T(8,128)S(1)} %get-tuple-element.33.own), channel_id=1, source_target_pairs={{1,0},{2,1},{3,2},{0,3},{5,4},{6,5},{7,6},{4,7},{9,8},{10,9},{11,1... | collective-permute-start | bytes 122888 | tf_op jit(solution)/shard_map/ppermute | solution.py:552
  33.1 1.4 %collective-permute-done.8.b3 = f32[5,2,8,128]{3,2,1,0:T(8,128)S(1)} collective-permute-done((f32[5,2,8,128]{3,2,1,0:T(8,128)S(1)}, f32[5,2,8,128]{3,2,1,0:T(8,128)S(1)}, u32[]{:S(2)}, u32[]{:S(2)}) %collective-permute-start.8) | collective-permute-done | bytes 40992 | tf_op jit(solution)/shard_map/ppermute | solution.py:552
  34.5 0.4 collective-permute-done.7.b2
  35.0 0.6 collective-permute-done.6.b1
  35.6 4.1 %collective-permute-start.10 = (f32[5,8,8,128]{3,2,1,0:T(8,128)S(1)}, f32[5,8,8,128]{3,2,1,0:T(8,128)S(1)}, u32[]{:S(2)}, u32[]{:S(2)}) collective-permute-start(f32[5,8,8,128]{3,2,1,0:T(8,128)S(1)} %get-tuple-element.34.own), channel_id=1, source_target_pairs={{240,0},{0,16},{16,32},{32,48},{48,64},{64,80},{80,96},{96,112},{1... | collective-permute-start | bytes 491528 | tf_op jit(solution)/shard_map/ppermute | solution.py:552
  39.7 3.8 %collective-permute-start.9 = (f32[5,8,8,128]{3,2,1,0:T(8,128)S(1)}, f32[5,8,8,128]{3,2,1,0:T(8,128)S(1)}, u32[]{:S(2)}, u32[]{:S(2)}) collective-permute-start(f32[5,8,8,128]{3,2,1,0:T(8,128)S(1)} %get-tuple-element.34.own), channel_id=1, source_target_pairs={{16,0},{32,16},{48,32},{64,48},{80,64},{96,80},{112,96},{128,112},... | collective-permute-start | bytes 491528 | tf_op jit(solution)/shard_map/ppermute | solution.py:552
  43.5 2.6 %collective-permute-start.11 = (f32[5,4,8,128]{3,2,1,0:T(8,128)S(1)}, f32[5,4,8,128]{3,2,1,0:T(8,128)S(1)}, u32[]{:S(2)}, u32[]{:S(2)}) collective-permute-start(f32[5,4,8,128]{3,2,1,0:T(8,128)S(1)} %get-tuple-element.35), channel_id=1, source_target_pairs={{32,0},{48,16},{64,32},{80,48},{96,64},{112,80},{128,96},{144,112}... | collective-permute-start | bytes 245768 | tf_op jit(solution)/shard_map/ppermute | solution.py:552
  46.1 1.8 %collective-permute-done.11.r2 = f32[5,4,8,128]{3,2,1,0:T(8,128)S(1)} collective-permute-done((f32[5,4,8,128]{3,2,1,0:T(8,128)S(1)}, f32[5,4,8,128]{3,2,1,0:T(8,128)S(1)}, u32[]{:S(2)}, u32[]{:S(2)}) %collective-permute-start.11) | collective-permute-done | bytes 81952 | tf_op jit(solution)/shard_map/ppermute | solution.py:552
  47.9 3.1 %collective-permute-done.12.l2 = f32[5,4,8,128]{3,2,1,0:T(8,128)S(1)} collective-permute-done((f32[5,4,8,128]{3,2,1,0:T(8,128)S(1)}, f32[5,4,8,128]{3,2,1,0:T(8,128)S(1)}, u32[]{:S(2)}, u32[]{:S(2)}) %collective-permute-start.12) | collective-permute-done | bytes 81952 | tf_op jit(solution)/shard_map/ppermute | solution.py:552
  51.3 1.5 %collective-permute-start.14 = (f32[32,8,128]{2,1,0:T(8,128)S(1)}, f32[32,8,128]{2,1,0:T(8,128)S(1)}, u32[]{:S(2)}, u32[]{:S(2)}) collective-permute-start(f32[32,8,128]{2,1,0:T(8,128)S(1)} %get-tuple-element.39), channel_id=1, source_target_pairs={{12,0},{0,4},{4,8},{8,12},{13,1},{1,5},{5,9},{9,13},{14,2},{2,6},{... | collective-permute-start | bytes 393224 | tf_op jit(solution)/shard_map/ppermute | solution.py:552
  52.7 2.4 %collective-permute-done.13.yl = f32[32,8,128]{2,1,0:T(8,128)S(1)} collective-permute-done((f32[32,8,128]{2,1,0:T(8,128)S(1)}, f32[32,8,128]{2,1,0:T(8,128)S(1)}, u32[]{:S(2)}, u32[]{:S(2)}) %collective-permute-start.13) | collective-permute-done | bytes 131104 | tf_op jit(solution)/shard_map/ppermute | solution.py:552
  55.1 1.5 %collective-permute-done.14.yh = f32[32,8,128]{2,1,0:T(8,128)S(1)} collective-permute-done((f32[32,8,128]{2,1,0:T(8,128)S(1)}, f32[32,8,128]{2,1,0:T(8,128)S(1)}, u32[]{:S(2)}, u32[]{:S(2)}) %collective-permute-start.14) | collective-permute-done | bytes 131104 | tf_op jit(solution)/shard_map/ppermute | solution.py:552
  56.5 3.2 %shard_map.85 = (f32[6,16,32,128]{3,2,1,0:T(8,128)S(1)}, f32[6,8,16,128]{3,2,1,0:T(8,128)S(1)}, f32[64,1,640]{2,1,0:T(1,128)S(1)}) custom-call(s32[3]{0:T(128)S(1)} %pad_add_fusion.pos, f32[5,8,32,128]{3,2,1,0:T(8,128)S(1)} %get-tuple-element.37.whole, f32[32,8,128]{2,1,0:T(8,128)S(1)} %collective-permute-done.13.yl, ...), custom_call_target="tpu_custom_call" | custom-call | tf_op jit(solution)/shard_map/pallas_call | solution.py:22
  59.7 17.7 %all_to_all.5.got = f32[64,1,640]{2,1,0:T(1,128)S(1)} all-to-all(f32[64,1,640]{2,1,0:T(1,128)S(1)} %get-tuple-element.40), channel_id=1, replica_groups=mesh['gx'=16,'gy'=4,'gz'=4] {'gy','gx'}, dimensions={0} | all-to-all | bytes 327680 | tf_op jit(solution)/shard_map/all_to_all | solution.py:609
  77.4 4.6 %shard_map.86 = (f32[8,16,128]{2,1,0:T(8,128)}, f32[8,16,128]{2,1,0:T(8,128)}) custom-call(s32[3]{0:T(128)S(1)} %pad_add_fusion.pos, f32[64,1,640]{2,1,0:T(1,128)S(1)} %all_to_all.5.got, f32[6,18,32,256]{3,2,1,0:T(8,128)S(1)} %get-tuple-element.41.a0, f32[6,16,32,128]{3,2,1,0:T(8,128)S(1)} %get-tuple-element.42.a1, f32[6,8,16,128]{3,2,1,0:T(8,128)S(1)} %get-tuple-element.43.a2), custom_call_target="tpu_custom_call" | custom-call | tf_op jit(solution)/shard_map/pallas_call | solution.py:22
  (13 shorter events, 0.6 us)
Async XLA Ops:
  2.3 6.6 %collective-permute-start = (f32[4,5,16,128]{3,2,1,0:T(8,128)}, f32[4,5,16,128]{3,2,1,0:T(8,128)S(1)}, u32[]{:S(2)}, u32[]{:S(2)}) collective-permute-start(f32[4,5,16,128]{3,2,1,0:T(8,128)} %get-tuple-element.23), channel_id=1, source_target_pairs={{1,0},{2,1},{3,2},{0,3},{5,4},{6,5},{7,6},{4,7},{9,8},{10,9},{11,1... | collective-permute-start | bytes 491528 | tf_op jit(solution)/shard_map/ppermute | solution.py:552
  5.7 6.2 %collective-permute-start.1 = (f32[4,5,16,128]{3,2,1,0:T(8,128)}, f32[4,5,16,128]{3,2,1,0:T(8,128)S(1)}, u32[]{:S(2)}, u32[]{:S(2)}) collective-permute-start(f32[4,5,16,128]{3,2,1,0:T(8,128)} %get-tuple-element.24), channel_id=1, source_target_pairs={{3,0},{0,1},{1,2},{2,3},{7,4},{4,5},{5,6},{6,7},{11,8},{8,9},{9,10... | collective-permute-start | bytes 491528 | tf_op jit(solution)/shard_map/ppermute | solution.py:552
  11.9 1.0 %copy-start = (f32[4,8,16,128]{3,2,1,0:T(8,128)S(1)}, f32[4,8,16,128]{3,2,1,0:T(8,128)}, u32[]{:S(2)}) copy-start(f32[4,8,16,128]{3,2,1,0:T(8,128)} %shard_map.77.own) | copy-start | bytes 786436
  12.9 6.4 %collective-permute-start.2 = (f32[39,8,128]{2,1,0:T(8,128)S(1)}, f32[39,8,128]{2,1,0:T(8,128)S(1)}, u32[]{:S(2)}, u32[]{:S(2)}) collective-permute-start(f32[39,8,128]{2,1,0:T(8,128)S(1)} %get-tuple-element.27), channel_id=1, source_target_pairs={{16,0},{32,16},{48,32},{64,48},{80,64},{96,80},{112,96},{128,112},... | collective-permute-start | bytes 479240 | tf_op jit(solution)/shard_map/ppermute | solution.py:552
  14.8 5.0 %collective-permute-start.3 = (f32[39,8,128]{2,1,0:T(8,128)S(1)}, f32[39,8,128]{2,1,0:T(8,128)S(1)}, u32[]{:S(2)}, u32[]{:S(2)}) collective-permute-start(f32[39,8,128]{2,1,0:T(8,128)S(1)} %get-tuple-element.28), channel_id=1, source_target_pairs={{240,0},{0,16},{16,32},{32,48},{48,64},{64,80},{80,96},{96,112},{1... | collective-permute-start | bytes 479240 | tf_op jit(solution)/shard_map/ppermute | solution.py:552
  20.2 4.0 %collective-permute-start.4 = (f32[12,8,128]{2,1,0:T(8,128)S(1)}, f32[12,8,128]{2,1,0:T(8,128)S(1)}, u32[]{:S(2)}, u32[]{:S(2)}) collective-permute-start(f32[12,8,128]{2,1,0:T(8,128)S(1)} %get-tuple-element.31), channel_id=1, source_target_pairs={{4,0},{8,4},{12,8},{0,12},{5,1},{9,5},{13,9},{1,13},{6,2},{10,6},{... | collective-permute-start | bytes 147464 | tf_op jit(solution)/shard_map/ppermute | solution.py:552
  23.0 4.2 %collective-permute-start.5 = (f32[12,8,128]{2,1,0:T(8,128)S(1)}, f32[12,8,128]{2,1,0:T(8,128)S(1)}, u32[]{:S(2)}, u32[]{:S(2)}) collective-permute-start(f32[12,8,128]{2,1,0:T(8,128)S(1)} %get-tuple-element.32), channel_id=1, source_target_pairs={{12,0},{0,4},{4,8},{8,12},{13,1},{1,5},{5,9},{9,13},{14,2},{2,6},{... | collective-permute-start | bytes 147464 | tf_op jit(solution)/shard_map/ppermute | solution.py:552
  30.4 4.2 %collective-permute-start.8 = (f32[5,2,8,128]{3,2,1,0:T(8,128)S(1)}, f32[5,2,8,128]{3,2,1,0:T(8,128)S(1)}, u32[]{:S(2)}, u32[]{:S(2)}) collective-permute-start(f32[5,2,8,128]{3,2,1,0:T(8,128)S(1)} %get-tuple-element.33.own), channel_id=1, source_target_pairs={{3,0},{0,1},{1,2},{2,3},{7,4},{4,5},{5,6},{6,7},{11,8},{8,9},{9,10... | collective-permute-start | bytes 122888 | tf_op jit(solution)/shard_map/ppermute | solution.py:552
  30.5 4.5 %collective-permute-start.7 = (f32[5,2,8,128]{3,2,1,0:T(8,128)S(1)}, f32[5,2,8,128]{3,2,1,0:T(8,128)S(1)}, u32[]{:S(2)}, u32[]{:S(2)}) collective-permute-start(f32[5,2,8,128]{3,2,1,0:T(8,128)S(1)} %get-tuple-element.33.own), channel_id=1, source_target_pairs={{2,0},{3,1},{0,2},{1,3},{6,4},{7,5},{4,6},{5,7},{10,8},{11,9},{8,1... | collective-permute-start | bytes 122888 | tf_op jit(solution)/shard_map/ppermute | solution.py:552
  32.0 3.6 %collective-permute-start.6 = (f32[5,2,8,128]{3,2,1,0:T(8,128)S(1)}, f32[5,2,8,128]{3,2,1,0:T(8,128)S(1)}, u32[]{:S(2)}, u32[]{:S(2)}) collective-permute-start(f32[5,2,8,128]{3,2,1,0:T(8,128)S(1)} %get-tuple-element.33.own), channel_id=1, source_target_pairs={{1,0},{2,1},{3,2},{0,3},{5,4},{6,5},{7,6},{4,7},{9,8},{10,9},{11,1... | collective-permute-start | bytes 122888 | tf_op jit(solution)/shard_map/ppermute | solution.py:552
  35.6 15.4 %collective-permute-start.10 = (f32[5,8,8,128]{3,2,1,0:T(8,128)S(1)}, f32[5,8,8,128]{3,2,1,0:T(8,128)S(1)}, u32[]{:S(2)}, u32[]{:S(2)}) collective-permute-start(f32[5,8,8,128]{3,2,1,0:T(8,128)S(1)} %get-tuple-element.34.own), channel_id=1, source_target_pairs={{240,0},{0,16},{16,32},{32,48},{48,64},{64,80},{80,96},{96,112},{1... | collective-permute-start | bytes 491528 | tf_op jit(solution)/shard_map/ppermute | solution.py:552
  39.7 11.2 %collective-permute-start.9 = (f32[5,8,8,128]{3,2,1,0:T(8,128)S(1)}, f32[5,8,8,128]{3,2,1,0:T(8,128)S(1)}, u32[]{:S(2)}, u32[]{:S(2)}) collective-permute-start(f32[5,8,8,128]{3,2,1,0:T(8,128)S(1)} %get-tuple-element.34.own), channel_id=1, source_target_pairs={{16,0},{32,16},{48,32},{64,48},{80,64},{96,80},{112,96},{128,112},... | collective-permute-start | bytes 491528 | tf_op jit(solution)/shard_map/ppermute | solution.py:552
  43.5 4.4 %collective-permute-start.11 = (f32[5,4,8,128]{3,2,1,0:T(8,128)S(1)}, f32[5,4,8,128]{3,2,1,0:T(8,128)S(1)}, u32[]{:S(2)}, u32[]{:S(2)}) collective-permute-start(f32[5,4,8,128]{3,2,1,0:T(8,128)S(1)} %get-tuple-element.35), channel_id=1, source_target_pairs={{32,0},{48,16},{64,32},{80,48},{96,64},{112,80},{128,96},{144,112}... | collective-permute-start | bytes 245768 | tf_op jit(solution)/shard_map/ppermute | solution.py:552
  46.1 4.9 %collective-permute-start.12 = (f32[5,4,8,128]{3,2,1,0:T(8,128)S(1)}, f32[5,4,8,128]{3,2,1,0:T(8,128)S(1)}, u32[]{:S(2)}, u32[]{:S(2)}) collective-permute-start(f32[5,4,8,128]{3,2,1,0:T(8,128)S(1)} %get-tuple-element.36), channel_id=1, source_target_pairs={{224,0},{240,16},{0,32},{16,48},{32,64},{48,80},{64,96},{80,112},{... | collective-permute-start | bytes 245768 | tf_op jit(solution)/shard_map/ppermute | solution.py:552
  51.2 3.9 %collective-permute-start.13 = (f32[32,8,128]{2,1,0:T(8,128)S(1)}, f32[32,8,128]{2,1,0:T(8,128)S(1)}, u32[]{:S(2)}, u32[]{:S(2)}) collective-permute-start(f32[32,8,128]{2,1,0:T(8,128)S(1)} %get-tuple-element.38), channel_id=1, source_target_pairs={{4,0},{8,4},{12,8},{0,12},{5,1},{9,5},{13,9},{1,13},{6,2},{10,6},{... | collective-permute-start | bytes 393224 | tf_op jit(solution)/shard_map/ppermute | solution.py:552
  51.3 5.3 %collective-permute-start.14 = (f32[32,8,128]{2,1,0:T(8,128)S(1)}, f32[32,8,128]{2,1,0:T(8,128)S(1)}, u32[]{:S(2)}, u32[]{:S(2)}) collective-permute-start(f32[32,8,128]{2,1,0:T(8,128)S(1)} %get-tuple-element.39), channel_id=1, source_target_pairs={{12,0},{0,4},{4,8},{8,12},{13,1},{1,5},{5,9},{9,13},{14,2},{2,6},{... | collective-permute-start | bytes 393224 | tf_op jit(solution)/shard_map/ppermute | solution.py:552

commit v5 on v4

--- a/solution.py
+++ b/solution.py
@@ -155,9 +155,10 @@
 
 
 def pack_z(f, b, s, d, lo, hi, *scratch):
-    for k, value in enumerate(fetch(f, b, s, d, *scratch)):
-        lo[k] = value[0:H]
-        hi[k] = value[8 - H : 8]
+    f, b, s, d = fetch(f, b, s, d, *scratch)
+    for value, at, n in ((f, 0, H), (d, H, H), (b, 2 * H, H - 1), (s, 3 * H - 1, H - 1)):
+        lo[at : at + n] = value[0:n]
+        hi[at : at + n] = value[8 - n : 8]
 
 
 def fetch_own(f, b, s, d, own, *scratch):
@@ -171,9 +172,15 @@
 
 def pack_x(own, above, below, xl, xh, lo, hi):
     for out, row in ((xl, 0), (xh, 8)):
-        out[:, 0:H] = below[:, :, row : row + 8]
-        out[:, H : H + 8] = own[:, :, row : row + 8]
-        out[:, H + 8 : Z0] = above[:, :, row : row + 8]
+        rows = slice(row, row + 8)
+        out[:, H : H + 8] = own[:, :, rows]
+        for k, at in ((FACIES, 0), (DENSITY, H)):
+            out[k, 0:H] = below[at : at + H, rows]
+            out[k, H + 8 : Z0] = above[at : at + H, rows]
+        for k, at in ((BOUNDARY, 2 * H), (SOURCE, 3 * H - 1)):
+            out[k, 1:H] = below[at : at + H - 1, rows]
+            out[k, H + 8 : Z0 - 1] = above[at : at + H - 1, rows]
+            out[k, 0] = out[k, Z0 - 1] = jnp.zeros((8, 128), F32)
     first = iota((8, 128), 0) < 4
     lo[XTILES - 1] = hi[XTILES - 1] = jnp.zeros((8, 128), F32)
     for z in range(Z0):
@@ -350,29 +357,16 @@
         packed[4, s] = W * parts[4] / parts[5]
 
 
-def pack_x1(own, b1, b2, b3, full, lo, hi):
-    for n, ref in enumerate((own, b1, b2, b3)):
-        full[:, 2 * n : 2 * n + 2] = ref[...]
-        first, second = ref[:, 0], ref[:, 1]
-        lo[:, n] = jnp.concatenate([first[:, 0:4], second[:, 0:4]], axis=1)
-        hi[:, n] = jnp.concatenate([first[:, 4:8], second[:, 4:8]], axis=1)
-
-
-def pack_y1(own, r1, l1, r2, l2, whole, lo, hi):
-    whole[:, :, 0:8] = own[...]
-    whole[:, :, 8:16] = r1[...]
-    whole[:, :, 24:32] = l1[...]
-    for n in range(4):
-        for s in range(2):
-            part = slice(4 * s, 4 * s + 4)
-            whole[:, 2 * n + s, 16:24] = jnp.concatenate([r2[:, n, part], l2[:, n, part]], axis=1)
+def pack_y1(own, b1, b2, b3, stack, lo, hi):
     lane = iota((8, 128), 1)
     block, last = (lane % 64) // 12, ((lane + 12) % 64) // 12
-    for g in range(32):
+    blocks = (own, b1, b2, b3)
+    for g in range(8):
         left = right = None
         for at in range(5):
-            layer, tile = divmod(5 * g + at, 4)
-            v = whole[layer // 8, layer % 8, 8 * tile : 8 * tile + 8]
+            k, n = divmod(5 * g + at, 8)
+            v = blocks[n // 2][k, n % 2]
+            stack[5 * g + at] = v
             v = turn(v, 12 * at)
             left = v if at == 0 else jnp.where(block == at, v, left)
             right = v if at == 0 else jnp.where(last == at, v, right)
@@ -380,20 +374,41 @@
         hi[g] = right
 
 
-def level12(pos, whole, yl, yh, a, b, sent, d1, r1, t1, m1, d2, r2, s1, s2, q2):
+def pack_x1(stack, right, left, full, lo, hi):
+    first = iota((8, 128), 0) < 4
+    full[0:40] = stack[...]
+    full[40:48] = right[...]
+    full[48:56] = left[...]
+    for n in range(28):
+        a, b = full[2 * n], pltpu.roll(full[2 * n + 1], 4, 0)
+        lo[n] = jnp.where(first, a, b)
+        hi[n] = jnp.where(first, b, a)
+
+
+def level12(pos, full, xr, xl, xr2, xl2, a, b, sent, d1, r1, t1, m1, d2, r2, s1, s2, q2):
     gx, gy, gz = pos[0], pos[1], pos[2]
     row, lane = iota((8, 128), 0), iota((8, 128), 1)
     y = gy * 64 + jnp.where(lane < 96, lane, lane - 128)
     in_y = (y >= 0) & (y < 256)
-    for tile in range(4):
+    first = row < 4
+
+    def middle(i):
+        near, far = xr2[i // 2], xl2[i // 2]
+        if i % 2 == 0:
+            return jnp.where(first, near, far)
+        return pltpu.roll(jnp.where(first, far, near), 4, 0)
+
+    for tile, tiles in enumerate((full, xr, None, xl)):
+        of = middle if tiles is None else lambda i, tiles=tiles: tiles[i]
+        edges = [(of(40 + g), of(48 + g)) for g in range(8)]
         x = gx * 8 + jnp.where(8 * tile + row < 20, 8 * tile + row, 8 * tile + row - 32)
         inside = in_y & (x >= 0) & (x < 128)
         rows = slice(8 * tile, 8 * tile + 8)
         for k in range(5):
             for n in range(8):
-                g, at = divmod(4 * (8 * k + n) + tile, 5)
-                v = whole[k, n, rows]
-                near = jnp.where((lane % 64) // 12 == at, yl[g], yh[g])
+                g, at = divmod(8 * k + n, 5)
+                v = of(8 * k + n)
+                near = jnp.where((lane % 64) // 12 == at, *edges[g])
                 for part in range(2):
                     own = turn(v, 64 * part)
                     beyond = turn(near, 64 - 64 * part - 12 * at)
@@ -561,9 +576,9 @@
         (8, 16, 128), (8, 16, 128), pltpu.SemaphoreType.DMA((4,)),
     ]
     plan = dict(spaces=[HBM] * 4, scratch=landing, limit=60)
-    lo, hi = call(pack_z, [(4, H, 16, 128)] * 2, *raw, **plan)
+    lo, hi = call(pack_z, [(4 * H - 2, 16, 128)] * 2, *raw, **plan)
     above, below = shift(lo, "gz", 1), shift(hi, "gz", -1)
-    (own,) = call(fetch_own, [(4, 8, 16, 128)], *raw, **plan)
+    (own,) = call(fetch_own, [(4, 8, 16, 128)], *raw, **{**plan, "limit": 24})
     xl, xh, lo, hi = call(
         pack_x, [(4, Z0, 8, 128)] * 2 + [(XTILES, 8, 128)] * 2, own, above, below
     )
@@ -587,20 +602,15 @@
         ],
     )
     blocks = [shift(packed, "gz", n) for n in (1, 2, 3)]
-    full, lo, hi = call(
-        pack_x1, [(5, 8, 8, 128), (5, 4, 8, 128), (5, 4, 8, 128)], packed, *blocks
-    )
-    r1, l1 = shift(full, "gx", 1), shift(full, "gx", -1)
-    r2, l2 = shift(lo, "gx", 2), shift(hi, "gx", -2)
-    whole, lo, hi = call(
-        pack_y1, [(5, 8, 32, 128), (32, 8, 128), (32, 8, 128)], full, r1, l1, r2, l2
-    )
-    yl, yh = shift(lo, "gy", 1), shift(hi, "gy", -1)
+    stack, lo, hi = call(pack_y1, [(40, 8, 128)] + [(8, 8, 128)] * 2, packed, *blocks)
+    right, left = shift(lo, "gy", 1), shift(hi, "gy", -1)
+    full, lo, hi = call(pack_x1, [(56, 8, 128)] + [(28, 8, 128)] * 2, stack, right, left)
+    near = (shift(full, "gx", 1), shift(full, "gx", -1), shift(lo, "gx", 2), shift(hi, "gx", -2))
     a1, a2, sent = call(
         level12,
         [(6, 16, 32, 128), (6, 8, 16, 128), (64, 1, 640)],
-        pos, whole, yl, yh,
-        spaces=[SMEM] + [VMEM] * 3,
+        pos, full, *near,
+        spaces=[SMEM] + [VMEM] * 5,
         scratch=[
             (16, 32, 128), (16, 32, 128), (5, 8, 32, 128), (4, 2, 8, 128),
             (8, 16, 128), (8, 16, 128), (16, 32, 128), (8, 16, 128), (8, 16, 128),

time: 82.3 us -> 80.7 us (0.981)
  waiting for transfers between devices: 21.3 us -> 18.4 us
  local copies, waits for them, and re-layouts: 0.95 us -> 3.36 us
  Pallas kernels: 16.1 us -> 14.7 us
  starting transfers between devices: 24.4 us -> 25.6 us
  blocking collectives: 17.7 us -> 16.8 us
    ppermute x15, waiting for transfers between devices: 21.3 us -> 18.4 us  [shift(): lax.ppermute(value, axis, [((i + by) % count, i) for i in range(count)])]
    unnamed x2 -> x8, local copies, waits for them, and re-layouts: 0.95 us -> 3.36 us
    pallas_call x10, Pallas kernels: 16.1 us -> 14.7 us  [call(): pl.pallas_call(kernel, out_shape=[jax.ShapeDtypeStruct(s, F32) for s in o...]
    ppermute x15, starting transfers between devices: 24.4 us -> 25.6 us  [shift(): lax.ppermute(value, axis, [((i + by) % count, i) for i in range(count)])]
    all_to_all x1, blocking collectives: 17.7 us -> 16.8 us  [local(): got = lax.all_to_all(sent, ('gy', 'gx'), 0, 0)]
  transfers between devices with their start and end apart: 15 -> 15, of which waited for: 13 -> 12; matrix products, arithmetic and copies ran while one was open for 1% -> 1% of each run, Pallas kernels for 3% -> 2%
where the time goes in v5:
time: 80.7 us; the launch traced here: 80.3 us
  starting transfers between devices  25.6 us (32%)
  waiting for transfers between devices  18.4 us (23%)
  blocking collectives  16.8 us (21%)
  Pallas kernels  14.7 us (18%)
  local copies, waits for them, and re-layouts  3.36 us (4%)
  other arithmetic  0.82 us (1%)
    ppermute x15, starting transfers between devices, shift(): lax.ppermute(value, axis, [((i + by) % count, i) for i in range(count)])  25.6 us
    ppermute x15, waiting for transfers between devices, shift(): lax.ppermute(value, axis, [((i + by) % count, i) for i in range(count)])  18.4 us
    all_to_all x1, blocking collectives, local(): got = lax.all_to_all(sent, ('gy', 'gx'), 0, 0)  16.8 us
    pallas_call x10, Pallas kernels, call(): pl.pallas_call(kernel, out_shape=[jax.ShapeDtypeStruct(s, F32) for s in o...  14.7 us
    unnamed x8, local copies, waits for them, and re-layouts  3.36 us
  transfers between devices with their start and end apart: 15, of which 12 were waited for; matrix products, arithmetic and copies ran while one was open for 1% of the time, Pallas kernels for 2%

profile of v5, /device:TPU:1, one launch (start us, length us, event | category | flops | bytes accessed | tf_op | source)
XLA Modules:
  0.0 80.3 jit_solution(11338135476879415343)
XLA Ops:
  0.6 1.7 %shard_map.78 = (f32[18,16,128]{2,1,0:T(8,128)}, f32[18,16,128]{2,1,0:T(8,128)}) custom-call(s32[8,16,128]{2,1,0:T(8,128)} %f.3, s32[8,16,128]{2,1,0:T(8,128)} %b.3, f32[8,16,128]{2,1,0:T(8,128)} %s.3, f32[8,16,128]{2,1,0:T(8,128)} %d.3), custom_call_target="tpu_custom_call" | custom-call | tf_op jit(solution)/shard_map/pallas_call | solution.py:22
  2.3 3.4 %collective-permute-start = (f32[18,16,128]{2,1,0:T(8,128)}, f32[18,16,128]{2,1,0:T(8,128)S(1)}, u32[]{:S(2)}, u32[]{:S(2)}) collective-permute-start(f32[18,16,128]{2,1,0:T(8,128)} %get-tuple-element.23), channel_id=1, source_target_pairs={{1,0},{2,1},{3,2},{0,3},{5,4},{6,5},{7,6},{4,7},{9,8},{10,9},{11,1... | collective-permute-start | bytes 442376 | tf_op jit(solution)/shard_map/ppermute | solution.py:567
  5.7 0.8 %copy-done = s32[8,16,128]{2,1,0:T(8,128)S(1)} copy-done((s32[8,16,128]{2,1,0:T(8,128)S(1)}, s32[8,16,128]{2,1,0:T(8,128)}, u32[]{:S(2)}) %copy-start) | copy-done | bytes 65560
  6.6 0.8 %copy-done.1 = s32[8,16,128]{2,1,0:T(8,128)S(1)} copy-done((s32[8,16,128]{2,1,0:T(8,128)S(1)}, s32[8,16,128]{2,1,0:T(8,128)}, u32[]{:S(2)}) %copy-start.1) | copy-done | bytes 65560
  7.4 0.8 %copy-done.2 = f32[8,16,128]{2,1,0:T(8,128)S(1)} copy-done((f32[8,16,128]{2,1,0:T(8,128)S(1)}, f32[8,16,128]{2,1,0:T(8,128)}, u32[]{:S(2)}) %copy-start.2) | copy-done | bytes 65560
  8.2 0.8 %copy-done.3 = f32[8,16,128]{2,1,0:T(8,128)S(1)} copy-done((f32[8,16,128]{2,1,0:T(8,128)S(1)}, f32[8,16,128]{2,1,0:T(8,128)}, u32[]{:S(2)}) %copy-start.3) | copy-done | bytes 65560
  9.5 2.1 %collective-permute-done.1.below = f32[18,16,128]{2,1,0:T(8,128)S(1)} collective-permute-done((f32[18,16,128]{2,1,0:T(8,128)}, f32[18,16,128]{2,1,0:T(8,128)S(1)}, u32[]{:S(2)}, u32[]{:S(2)}) %collective-permute-start.1) | collective-permute-done | bytes 147488 | tf_op jit(solution)/shard_map/ppermute | solution.py:567
  11.6 1.9 %collective-permute-start.2 = (f32[39,8,128]{2,1,0:T(8,128)S(1)}, f32[39,8,128]{2,1,0:T(8,128)S(1)}, u32[]{:S(2)}, u32[]{:S(2)}) collective-permute-start(f32[39,8,128]{2,1,0:T(8,128)S(1)} %get-tuple-element.27), channel_id=1, source_target_pairs={{16,0},{32,16},{48,32},{64,48},{80,64},{96,80},{112,96},{128,112},... | collective-permute-start | bytes 479240 | tf_op jit(solution)/shard_map/ppermute | solution.py:567
  13.5 1.5 %collective-permute-start.3 = (f32[39,8,128]{2,1,0:T(8,128)S(1)}, f32[39,8,128]{2,1,0:T(8,128)S(1)}, u32[]{:S(2)}, u32[]{:S(2)}) collective-permute-start(f32[39,8,128]{2,1,0:T(8,128)S(1)} %get-tuple-element.28), channel_id=1, source_target_pairs={{240,0},{0,16},{16,32},{32,48},{48,64},{64,80},{80,96},{96,112},{1... | collective-permute-start | bytes 479240 | tf_op jit(solution)/shard_map/ppermute | solution.py:567
  15.0 0.7 pad_maximum_fusion.tables
  15.8 2.2 %collective-permute-done.2.ml = f32[39,8,128]{2,1,0:T(8,128)S(1)} collective-permute-done((f32[39,8,128]{2,1,0:T(8,128)S(1)}, f32[39,8,128]{2,1,0:T(8,128)S(1)}, u32[]{:S(2)}, u32[]{:S(2)}) %collective-permute-start.2) | collective-permute-done | bytes 159776 | tf_op jit(solution)/shard_map/ppermute | solution.py:567
  18.0 0.5 collective-permute-done.3.mh
  18.8 2.8 %collective-permute-start.4 = (f32[12,8,128]{2,1,0:T(8,128)S(1)}, f32[12,8,128]{2,1,0:T(8,128)S(1)}, u32[]{:S(2)}, u32[]{:S(2)}) collective-permute-start(f32[12,8,128]{2,1,0:T(8,128)S(1)} %get-tuple-element.31), channel_id=1, source_target_pairs={{4,0},{8,4},{12,8},{0,12},{5,1},{9,5},{13,9},{1,13},{6,2},{10,6},{... | collective-permute-start | bytes 147464 | tf_op jit(solution)/shard_map/ppermute | solution.py:567
  21.7 1.0 %shard_map.81.main = f32[5,18,32,128]{3,2,1,0:T(8,128)S(1)} custom-call(s32[3]{0:T(128)S(1)} %pad_add_fusion.pos, f32[16]{0:T(128)S(1)} %pad_maximum_fusion.tables, f32[4,18,8,128]{3,2,1,0:T(8,128)S(1)} %get-tuple-element.25.xl, f32[4,18,8,128]{3,2,1,0:T(8,128)S(1)} %get-tuple-element.26.xh, f32[4,18,8,128]{3,2,1,0:T(8,128)S(1)} %get-tuple-element.29.rl, ...), custom_call_target="tpu_custom_call" | custom-call | tf_op jit(solution)/shard_map/pallas_call | solution.py:22
  22.8 3.0 %collective-permute-done.5.yh = f32[12,8,128]{2,1,0:T(8,128)S(1)} collective-permute-done((f32[12,8,128]{2,1,0:T(8,128)S(1)}, f32[12,8,128]{2,1,0:T(8,128)S(1)}, u32[]{:S(2)}, u32[]{:S(2)}) %collective-permute-start.5) | collective-permute-done | bytes 49184 | tf_op jit(solution)/shard_map/ppermute | solution.py:567
  25.8 3.3 %shard_map.82 = (f32[6,18,32,256]{3,2,1,0:T(8,128)S(1)}, f32[5,2,8,128]{3,2,1,0:T(8,128)S(1)}) custom-call(s32[3]{0:T(128)S(1)} %pad_add_fusion.pos, f32[16]{0:T(128)S(1)} %pad_maximum_fusion.tables, f32[5,18,32,128]{3,2,1,0:T(8,128)S(1)} %shard_map.81.main, f32[12,8,128]{2,1,0:T(8,128)S(1)} %collective-permute-done.4.yl, ...), custom_call_target="tpu_custom_call" | custom-call | tf_op jit(solution)/shard_map/pallas_call | solution.py:22
  29.2 1.8 %collective-permute-start.7 = (f32[5,2,8,128]{3,2,1,0:T(8,128)S(1)}, f32[5,2,8,128]{3,2,1,0:T(8,128)S(1)}, u32[]{:S(2)}, u32[]{:S(2)}) collective-permute-start(f32[5,2,8,128]{3,2,1,0:T(8,128)S(1)} %get-tuple-element.33.own), channel_id=1, source_target_pairs={{2,0},{3,1},{0,2},{1,3},{6,4},{7,5},{4,6},{5,7},{10,8},{11,9},{8,1... | collective-permute-start | bytes 122888 | tf_op jit(solution)/shard_map/ppermute | solution.py:567
  30.9 0.9 %collective-permute-start.6 = (f32[5,2,8,128]{3,2,1,0:T(8,128)S(1)}, f32[5,2,8,128]{3,2,1,0:T(8,128)S(1)}, u32[]{:S(2)}, u32[]{:S(2)}) collective-permute-start(f32[5,2,8,128]{3,2,1,0:T(8,128)S(1)} %get-tuple-element.33.own), channel_id=1, source_target_pairs={{1,0},{2,1},{3,2},{0,3},{5,4},{6,5},{7,6},{4,7},{9,8},{10,9},{11,1... | collective-permute-start | bytes 122888 | tf_op jit(solution)/shard_map/ppermute | solution.py:567
  31.8 1.4 %collective-permute-done.8.b3 = f32[5,2,8,128]{3,2,1,0:T(8,128)S(1)} collective-permute-done((f32[5,2,8,128]{3,2,1,0:T(8,128)S(1)}, f32[5,2,8,128]{3,2,1,0:T(8,128)S(1)}, u32[]{:S(2)}, u32[]{:S(2)}) %collective-permute-start.8) | collective-permute-done | bytes 40992 | tf_op jit(solution)/shard_map/ppermute | solution.py:567
  33.2 0.4 collective-permute-done.7.b2
  33.6 0.6 collective-permute-done.6.b1
  34.5 1.4 %collective-permute-start.10 = (f32[8,8,128]{2,1,0:T(8,128)S(1)}, f32[8,8,128]{2,1,0:T(8,128)S(1)}, u32[]{:S(2)}, u32[]{:S(2)}) collective-permute-start(f32[8,8,128]{2,1,0:T(8,128)S(1)} %get-tuple-element.36), channel_id=1, source_target_pairs={{12,0},{0,4},{4,8},{8,12},{13,1},{1,5},{5,9},{9,13},{14,2},{2,6},{... | collective-permute-start | bytes 98312 | tf_op jit(solution)/shard_map/ppermute | solution.py:567
  35.9 1.3 %collective-permute-done.9.right = f32[8,8,128]{2,1,0:T(8,128)S(1)} collective-permute-done((f32[8,8,128]{2,1,0:T(8,128)S(1)}, f32[8,8,128]{2,1,0:T(8,128)S(1)}, u32[]{:S(2)}, u32[]{:S(2)}) %collective-permute-start.9) | collective-permute-done | bytes 32800 | tf_op jit(solution)/shard_map/ppermute | solution.py:567
  37.2 1.3 %collective-permute-done.10.left = f32[8,8,128]{2,1,0:T(8,128)S(1)} collective-permute-done((f32[8,8,128]{2,1,0:T(8,128)S(1)}, f32[8,8,128]{2,1,0:T(8,128)S(1)}, u32[]{:S(2)}, u32[]{:S(2)}) %collective-permute-start.10) | collective-permute-done | bytes 32800 | tf_op jit(solution)/shard_map/ppermute | solution.py:567
  38.5 5.3 %collective-permute-start.12 = (f32[56,8,128]{2,1,0:T(8,128)S(1)}, f32[56,8,128]{2,1,0:T(8,128)S(1)}, u32[]{:S(2)}, u32[]{:S(2)}) collective-permute-start(f32[56,8,128]{2,1,0:T(8,128)S(1)} %get-tuple-element.37.full), channel_id=1, source_target_pairs={{240,0},{0,16},{16,32},{32,48},{48,64},{64,80},{80,96},{96,112},{1... | collective-permute-start | bytes 688136 | tf_op jit(solution)/shard_map/ppermute | solution.py:567
  43.8 3.8 %collective-permute-start.11 = (f32[56,8,128]{2,1,0:T(8,128)S(1)}, f32[56,8,128]{2,1,0:T(8,128)S(1)}, u32[]{:S(2)}, u32[]{:S(2)}) collective-permute-start(f32[56,8,128]{2,1,0:T(8,128)S(1)} %get-tuple-element.37.full), channel_id=1, source_target_pairs={{16,0},{32,16},{48,32},{64,48},{80,64},{96,80},{112,96},{128,112},... | collective-permute-start | bytes 688136 | tf_op jit(solution)/shard_map/ppermute | solution.py:567
  47.6 2.6 %collective-permute-start.13 = (f32[28,8,128]{2,1,0:T(8,128)S(1)}, f32[28,8,128]{2,1,0:T(8,128)S(1)}, u32[]{:S(2)}, u32[]{:S(2)}) collective-permute-start(f32[28,8,128]{2,1,0:T(8,128)S(1)} %get-tuple-element.38), channel_id=1, source_target_pairs={{32,0},{48,16},{64,32},{80,48},{96,64},{112,80},{128,96},{144,112}... | collective-permute-start | bytes 344072 | tf_op jit(solution)/shard_map/ppermute | solution.py:567
  50.2 2.5 %collective-permute-done.13.xr2 = f32[28,8,128]{2,1,0:T(8,128)S(1)} collective-permute-done((f32[28,8,128]{2,1,0:T(8,128)S(1)}, f32[28,8,128]{2,1,0:T(8,128)S(1)}, u32[]{:S(2)}, u32[]{:S(2)}) %collective-permute-start.13) | collective-permute-done | bytes 114720 | tf_op jit(solution)/shard_map/ppermute | solution.py:567
  52.6 3.1 %collective-permute-done.14.xl2 = f32[28,8,128]{2,1,0:T(8,128)S(1)} collective-permute-done((f32[28,8,128]{2,1,0:T(8,128)S(1)}, f32[28,8,128]{2,1,0:T(8,128)S(1)}, u32[]{:S(2)}, u32[]{:S(2)}) %collective-permute-start.14) | collective-permute-done | bytes 114720 | tf_op jit(solution)/shard_map/ppermute | solution.py:567
  55.7 3.2 %shard_map.85 = (f32[6,16,32,128]{3,2,1,0:T(8,128)S(1)}, f32[6,8,16,128]{3,2,1,0:T(8,128)S(1)}, f32[64,1,640]{2,1,0:T(1,128)S(1)}) custom-call(s32[3]{0:T(128)S(1)} %pad_add_fusion.pos, f32[56,8,128]{2,1,0:T(8,128)S(1)} %get-tuple-element.37.full, f32[56,8,128]{2,1,0:T(8,128)S(1)} %collective-permute-done.11.xr, ...), custom_call_target="tpu_custom_call" | custom-call | tf_op jit(solution)/shard_map/pallas_call | solution.py:22
  58.9 16.8 %all_to_all.5.got = f32[64,1,640]{2,1,0:T(1,128)S(1)} all-to-all(f32[64,1,640]{2,1,0:T(1,128)S(1)} %get-tuple-element.40), channel_id=1, replica_groups=mesh['gx'=16,'gy'=4,'gz'=4] {'gy','gx'}, dimensions={0} | all-to-all | bytes 327680 | tf_op jit(solution)/shard_map/all_to_all | solution.py:619
  75.7 4.6 %shard_map.86 = (f32[8,16,128]{2,1,0:T(8,128)}, f32[8,16,128]{2,1,0:T(8,128)}) custom-call(s32[3]{0:T(128)S(1)} %pad_add_fusion.pos, f32[64,1,640]{2,1,0:T(1,128)S(1)} %all_to_all.5.got, f32[6,18,32,256]{3,2,1,0:T(8,128)S(1)} %get-tuple-element.41.a0, f32[6,16,32,128]{3,2,1,0:T(8,128)S(1)} %get-tuple-element.42.a1, f32[6,8,16,128]{3,2,1,0:T(8,128)S(1)} %get-tuple-element.43.a2), custom_call_target="tpu_custom_call" | custom-call | tf_op jit(solution)/shard_map/pallas_call | solution.py:22
  (19 shorter events, 1.3 us)
Async XLA Ops:
  2.3 7.1 %collective-permute-start = (f32[18,16,128]{2,1,0:T(8,128)}, f32[18,16,128]{2,1,0:T(8,128)S(1)}, u32[]{:S(2)}, u32[]{:S(2)}) collective-permute-start(f32[18,16,128]{2,1,0:T(8,128)} %get-tuple-element.23), channel_id=1, source_target_pairs={{1,0},{2,1},{3,2},{0,3},{5,4},{6,5},{7,6},{4,7},{9,8},{10,9},{11,1... | collective-permute-start | bytes 442376 | tf_op jit(solution)/shard_map/ppermute | solution.py:567
  5.7 5.8 %collective-permute-start.1 = (f32[18,16,128]{2,1,0:T(8,128)}, f32[18,16,128]{2,1,0:T(8,128)S(1)}, u32[]{:S(2)}, u32[]{:S(2)}) collective-permute-start(f32[18,16,128]{2,1,0:T(8,128)} %get-tuple-element.24), channel_id=1, source_target_pairs={{3,0},{0,1},{1,2},{2,3},{7,4},{4,5},{5,6},{6,7},{11,8},{8,9},{9,10... | collective-permute-start | bytes 442376 | tf_op jit(solution)/shard_map/ppermute | solution.py:567
  5.7 0.8 %copy-start = (s32[8,16,128]{2,1,0:T(8,128)S(1)}, s32[8,16,128]{2,1,0:T(8,128)}, u32[]{:S(2)}) copy-start(s32[8,16,128]{2,1,0:T(8,128)} %f.3) | copy-start | bytes 196612
  6.6 0.8 %copy-start.1 = (s32[8,16,128]{2,1,0:T(8,128)S(1)}, s32[8,16,128]{2,1,0:T(8,128)}, u32[]{:S(2)}) copy-start(s32[8,16,128]{2,1,0:T(8,128)} %b.3) | copy-start | bytes 196612
  7.4 0.8 %copy-start.2 = (f32[8,16,128]{2,1,0:T(8,128)S(1)}, f32[8,16,128]{2,1,0:T(8,128)}, u32[]{:S(2)}) copy-start(f32[8,16,128]{2,1,0:T(8,128)} %s.3) | copy-start | bytes 196612
  8.2 0.8 %copy-start.3 = (f32[8,16,128]{2,1,0:T(8,128)S(1)}, f32[8,16,128]{2,1,0:T(8,128)}, u32[]{:S(2)}) copy-start(f32[8,16,128]{2,1,0:T(8,128)} %d.3) | copy-start | bytes 196612
  11.6 6.4 %collective-permute-start.2 = (f32[39,8,128]{2,1,0:T(8,128)S(1)}, f32[39,8,128]{2,1,0:T(8,128)S(1)}, u32[]{:S(2)}, u32[]{:S(2)}) collective-permute-start(f32[39,8,128]{2,1,0:T(8,128)S(1)} %get-tuple-element.27), channel_id=1, source_target_pairs={{16,0},{32,16},{48,32},{64,48},{80,64},{96,80},{112,96},{128,112},... | collective-permute-start | bytes 479240 | tf_op jit(solution)/shard_map/ppermute | solution.py:567
  13.5 5.0 %collective-permute-start.3 = (f32[39,8,128]{2,1,0:T(8,128)S(1)}, f32[39,8,128]{2,1,0:T(8,128)S(1)}, u32[]{:S(2)}, u32[]{:S(2)}) collective-permute-start(f32[39,8,128]{2,1,0:T(8,128)S(1)} %get-tuple-element.28), channel_id=1, source_target_pairs={{240,0},{0,16},{16,32},{32,48},{48,64},{64,80},{80,96},{96,112},{1... | collective-permute-start | bytes 479240 | tf_op jit(solution)/shard_map/ppermute | solution.py:567
  18.8 4.0 %collective-permute-start.4 = (f32[12,8,128]{2,1,0:T(8,128)S(1)}, f32[12,8,128]{2,1,0:T(8,128)S(1)}, u32[]{:S(2)}, u32[]{:S(2)}) collective-permute-start(f32[12,8,128]{2,1,0:T(8,128)S(1)} %get-tuple-element.31), channel_id=1, source_target_pairs={{4,0},{8,4},{12,8},{0,12},{5,1},{9,5},{13,9},{1,13},{6,2},{10,6},{... | collective-permute-start | bytes 147464 | tf_op jit(solution)/shard_map/ppermute | solution.py:567
  21.7 4.2 %collective-permute-start.5 = (f32[12,8,128]{2,1,0:T(8,128)S(1)}, f32[12,8,128]{2,1,0:T(8,128)S(1)}, u32[]{:S(2)}, u32[]{:S(2)}) collective-permute-start(f32[12,8,128]{2,1,0:T(8,128)S(1)} %get-tuple-element.32), channel_id=1, source_target_pairs={{12,0},{0,4},{4,8},{8,12},{13,1},{1,5},{5,9},{9,13},{14,2},{2,6},{... | collective-permute-start | bytes 147464 | tf_op jit(solution)/shard_map/ppermute | solution.py:567
  29.1 4.2 %collective-permute-start.8 = (f32[5,2,8,128]{3,2,1,0:T(8,128)S(1)}, f32[5,2,8,128]{3,2,1,0:T(8,128)S(1)}, u32[]{:S(2)}, u32[]{:S(2)}) collective-permute-start(f32[5,2,8,128]{3,2,1,0:T(8,128)S(1)} %get-tuple-element.33.own), channel_id=1, source_target_pairs={{3,0},{0,1},{1,2},{2,3},{7,4},{4,5},{5,6},{6,7},{11,8},{8,9},{9,10... | collective-permute-start | bytes 122888 | tf_op jit(solution)/shard_map/ppermute | solution.py:567
  29.2 4.5 %collective-permute-start.7 = (f32[5,2,8,128]{3,2,1,0:T(8,128)S(1)}, f32[5,2,8,128]{3,2,1,0:T(8,128)S(1)}, u32[]{:S(2)}, u32[]{:S(2)}) collective-permute-start(f32[5,2,8,128]{3,2,1,0:T(8,128)S(1)} %get-tuple-element.33.own), channel_id=1, source_target_pairs={{2,0},{3,1},{0,2},{1,3},{6,4},{7,5},{4,6},{5,7},{10,8},{11,9},{8,1... | collective-permute-start | bytes 122888 | tf_op jit(solution)/shard_map/ppermute | solution.py:567
  30.9 3.3 %collective-permute-start.6 = (f32[5,2,8,128]{3,2,1,0:T(8,128)S(1)}, f32[5,2,8,128]{3,2,1,0:T(8,128)S(1)}, u32[]{:S(2)}, u32[]{:S(2)}) collective-permute-start(f32[5,2,8,128]{3,2,1,0:T(8,128)S(1)} %get-tuple-element.33.own), channel_id=1, source_target_pairs={{1,0},{2,1},{3,2},{0,3},{5,4},{6,5},{7,6},{4,7},{9,8},{10,9},{11,1... | collective-permute-start | bytes 122888 | tf_op jit(solution)/shard_map/ppermute | solution.py:567
  34.3 2.8 %collective-permute-start.9 = (f32[8,8,128]{2,1,0:T(8,128)S(1)}, f32[8,8,128]{2,1,0:T(8,128)S(1)}, u32[]{:S(2)}, u32[]{:S(2)}) collective-permute-start(f32[8,8,128]{2,1,0:T(8,128)S(1)} %get-tuple-element.35), channel_id=1, source_target_pairs={{4,0},{8,4},{12,8},{0,12},{5,1},{9,5},{13,9},{1,13},{6,2},{10,6},{... | collective-permute-start | bytes 98312 | tf_op jit(solution)/shard_map/ppermute | solution.py:567
  34.5 4.0 %collective-permute-start.10 = (f32[8,8,128]{2,1,0:T(8,128)S(1)}, f32[8,8,128]{2,1,0:T(8,128)S(1)}, u32[]{:S(2)}, u32[]{:S(2)}) collective-permute-start(f32[8,8,128]{2,1,0:T(8,128)S(1)} %get-tuple-element.36), channel_id=1, source_target_pairs={{12,0},{0,4},{4,8},{8,12},{13,1},{1,5},{5,9},{9,13},{14,2},{2,6},{... | collective-permute-start | bytes 98312 | tf_op jit(solution)/shard_map/ppermute | solution.py:567
  38.5 17.2 %collective-permute-start.12 = (f32[56,8,128]{2,1,0:T(8,128)S(1)}, f32[56,8,128]{2,1,0:T(8,128)S(1)}, u32[]{:S(2)}, u32[]{:S(2)}) collective-permute-start(f32[56,8,128]{2,1,0:T(8,128)S(1)} %get-tuple-element.37.full), channel_id=1, source_target_pairs={{240,0},{0,16},{16,32},{32,48},{48,64},{64,80},{80,96},{96,112},{1... | collective-permute-start | bytes 688136 | tf_op jit(solution)/shard_map/ppermute | solution.py:567
  43.8 11.9 %collective-permute-start.11 = (f32[56,8,128]{2,1,0:T(8,128)S(1)}, f32[56,8,128]{2,1,0:T(8,128)S(1)}, u32[]{:S(2)}, u32[]{:S(2)}) collective-permute-start(f32[56,8,128]{2,1,0:T(8,128)S(1)} %get-tuple-element.37.full), channel_id=1, source_target_pairs={{16,0},{32,16},{48,32},{64,48},{80,64},{96,80},{112,96},{128,112},... | collective-permute-start | bytes 688136 | tf_op jit(solution)/shard_map/ppermute | solution.py:567
  47.6 5.1 %collective-permute-start.13 = (f32[28,8,128]{2,1,0:T(8,128)S(1)}, f32[28,8,128]{2,1,0:T(8,128)S(1)}, u32[]{:S(2)}, u32[]{:S(2)}) collective-permute-start(f32[28,8,128]{2,1,0:T(8,128)S(1)} %get-tuple-element.38), channel_id=1, source_target_pairs={{32,0},{48,16},{64,32},{80,48},{96,64},{112,80},{128,96},{144,112}... | collective-permute-start | bytes 344072 | tf_op jit(solution)/shard_map/ppermute | solution.py:567
  50.2 5.6 %collective-permute-start.14 = (f32[28,8,128]{2,1,0:T(8,128)S(1)}, f32[28,8,128]{2,1,0:T(8,128)S(1)}, u32[]{:S(2)}, u32[]{:S(2)}) collective-permute-start(f32[28,8,128]{2,1,0:T(8,128)S(1)} %get-tuple-element.39), channel_id=1, source_target_pairs={{224,0},{240,16},{0,32},{16,48},{32,64},{48,80},{64,96},{80,112},{... | collective-permute-start | bytes 344072 | tf_op jit(solution)/shard_map/ppermute | solution.py:567

commit v6 on v5

--- a/solution.py
+++ b/solution.py
@@ -238,12 +238,12 @@
 PART = PUX, PUZ, PSINK, PB, PH = range(5)
 
 
-def tile0(pos, tables, raw, first_lane, part, vs):
+def tile0(pos, tables, raw, first_lane, part, vs, start=0, stop=Z0):
     row, lane = iota((32, 128), 0), iota((32, 128), 1)
     x = pos[0] * 16 + jnp.where(row < 24, row, row - 32)
     y = pos[1] * 128 + first_lane + (lane if first_lane == 0 else jnp.where(lane < 64, lane, lane - 256))
     inside = (x >= 0) & (x < 256) & (y >= 0) & (y < 512)
-    for z in range(Z0):
+    for z in range(start, stop):
         zg = pos[2] * 8 + z - H
         here = inside & ((zg >= 0) & (zg < 32))
         kind = raw(FACIES, z)
@@ -255,7 +255,7 @@
             v = jnp.where(is_n, tables[8 + n], v)
         part[PH, z] = jnp.where(here, h, 0.0)
         vs[z] = jnp.where(here, v, 0.0)
-    for z in range(Z0 - 1):
+    for z in range(start, stop - 1):
         h, v = part[PH, z], vs[z]
         hn, vn = up(h, 0), vs[z + 1]
         hsum, vsum = h + hn, v + vn
@@ -264,7 +264,7 @@
         twice = 2.0 / (hsum * vsum)
         part[PUX, z] = (h * hn) * (twice * vsum)
         part[PUZ, z] = (v * vn) * (twice * hsum)
-    for z in range(1, Z0 - 1):
+    for z in range(start + 1, stop - 1):
         kind = raw(BOUNDARY, z)
         part[PSINK, z] = jnp.where(
             kind == 1.0, 2.0 * vs[z], jnp.where(kind == 2.0, 0.5 * part[PH, z], 0.0)
@@ -284,45 +284,55 @@
     tile0(pos, tables, raw, 0, part, vs)
 
 
+def y_sides(yl, yh, raw, layers):
+    lane = iota((8, 128), 1)
+    for k in range(4):
+        for z in layers:
+            for tile in range(4):
+                g, at, width = block_of(k, z, tile)
+                both = jnp.where(lane // width == at // width, yl[g], yh[g])
+                raw[k, z, 8 * tile : 8 * tile + 8] = turn(both, -at)
+
+
+def setup0(a, main, side, z):
+    def both(k):
+        return jnp.concatenate([main[k, z], side[k, z]], axis=1)
+
+    h, sink, ux, uz, lz = both(PH), both(PSINK), both(PUX), both(PUZ), a[UZ, z - 1]
+    hn = up(h, 1)
+    hsum = h + hn
+    uy = 2.0 * h * hn / jnp.where(hsum > 0.0, hsum, 1.0)
+    a[UX, z], a[UY, z], a[UZ, z] = ux, uy, uz
+    lx, ly = down(ux, 0), down(uy, 1)
+    diag = sink + lz + uz + lx + ux + ly + uy
+    rd = jnp.where(diag > 0.0, W / jnp.where(diag > 0.0, diag, 1.0), 0.0)
+    a[RD, z] = rd
+    a[C, z] = rd * both(PB)
+    return diag, sink, ux, uy, uz, lx, ly, lz
+
+
 def level0(pos, tables, main, yl, yh, a, packed, raw, side, vs, hs, dd, res, t, m):
     lane8 = iota((8, 128), 1)
-    for k in range(4):
-        for z in range(Z0):
-            for tile in range(4):
-                g, at, width = block_of(k, z, tile)
-                both = jnp.where(lane8 // width == at // width, yl[g], yh[g])
-                raw[k, z, 8 * tile : 8 * tile + 8] = turn(both, -at)
-    tile0(pos, tables, lambda k, z: raw[k, z], 128, side, vs)
-
-    def both(k, z):
-        return jnp.concatenate([main[k, z], side[k, z]], axis=1)
-
+    y_sides(yl, yh, raw, range(2, Z0 - 2))
+    tile0(pos, tables, lambda k, z: raw[k, z], 128, side, vs, 2, Z0 - 2)
     row, lane = iota((32, 256), 0), iota((32, 256), 1)
     odd_row, odd_lane = row % 2 == 1, lane % 2 == 1
-    a[UZ, 0] = both(PUZ, 0)
-    for z in range(1, Z0 - 1):
-        h, sink, ux, uz, lz = both(PH, z), both(PSINK, z), both(PUX, z), both(PUZ, z), a[UZ, z - 1]
-        hn = up(h, 1)
-        hsum = h + hn
-        uy = 2.0 * h * hn / jnp.where(hsum > 0.0, hsum, 1.0)
-        a[UX, z], a[UY, z], a[UZ, z] = ux, uy, uz
-        lx, ly = down(ux, 0), down(uy, 1)
-        diag = sink + lz + uz + lx + ux + ly + uy
-        rd = jnp.where(diag > 0.0, W / jnp.where(diag > 0.0, diag, 1.0), 0.0)
-        a[RD, z] = rd
-        a[C, z] = rd * both(PB, z)
-        dd[z] = diag
-        outer = sink + jnp.where(odd_row, ux, lx) + jnp.where(odd_lane, uy, ly)
-        hs[z] = (outer + (uz if (z - H) % 2 == 1 else lz))[0:16, 0:128]
+    a[UZ, 2] = jnp.concatenate([main[PUZ, 2], side[PUZ, 2]], axis=1)
+    for z in range(3, Z0 - 3):
+        diag, sink, ux, uy, uz, lx, ly, lz = setup0(a, main, side, z)
+        if H <= z < H + 8:
+            dd[z - H] = diag[0:16, 0:128]
+            outer = sink + jnp.where(odd_row, ux, lx) + jnp.where(odd_lane, uy, ly)
+            hs[z - H] = (outer + (uz if (z - H) % 2 == 1 else lz))[0:16, 0:128]
 
     def first(z):
         a[V, z] = smoothed(a, lambda k: a[C, k], z, z - 1, z + 1)
 
-    each(2, Z0 - 2, first)
+    each(4, Z0 - 4, first)
 
     def residual(z):
         v, beside = around(a, lambda k: a[V, k], z, z - 1, z + 1)
-        res[z - H] = (dd[z] * (1.5 * a[C, z] - v) + beside)[0:16, 0:128]
+        res[z - H] = dd[z - H] * (1.5 * a[C, z] - v)[0:16, 0:128] + beside[0:16, 0:128]
 
     each(H, H + 8, residual)
 
@@ -341,7 +351,7 @@
             a[UZ, hi, 0:16, 0:128],
             pair(main.at[PSINK]),
             res[2 * z] + res[2 * z + 1],
-            hs[lo] + hs[hi],
+            hs[2 * z] + hs[2 * z + 1],
         )
         for k, part in enumerate(parts):
             t[k, z] = part
@@ -355,6 +365,23 @@
         for k in range(4):
             packed[k, s] = parts[k]
         packed[4, s] = W * parts[4] / parts[5]
+
+
+OUTER = (2, 3, Z0 - 4, Z0 - 3)
+
+
+def outer0(pos, tables, main, yl, yh, a0, field, raw, side, vs, a):
+    for start, stop in ((0, 4), (Z0 - 4, Z0)):
+        y_sides(yl, yh, raw, range(start, stop))
+        tile0(pos, tables, lambda k, z: raw[k, z], 128, side, vs, start, stop)
+        a[UZ, start] = jnp.concatenate([main[PUZ, start], side[PUZ, start]], axis=1)
+        for z in range(start + 1, stop - 1):
+            setup0(a, main, side, z)
+    for z in (3, 4, Z0 - 5, Z0 - 4):
+        for k in (UX, UY, UZ, RD, C):
+            a[k, z] = a0[k, z]
+    for n, z in enumerate(OUTER):
+        field[n] = smoothed(a, lambda k: a[C, k], z, z - 1, z + 1)
 
 
 def pack_y1(own, b1, b2, b3, stack, lo, hi):
@@ -443,9 +470,13 @@
         for s in range(2):
             v = m1[z, s]
             v = pick(v + up(v, 1), 2 * (lane % 16))
-            total = jnp.where(lane // 16 == 2 * zg + s, v, total)
-    for k in range(5):
-        sent[:, :, 128 * k : 128 * k + 128] = jnp.broadcast_to(total[k : k + 1][None], (64, 1, 128))
+            total = jnp.where(lane // 16 == lax.rem(2 * zg + s + gy, 8), v, total)
+    for tile in range(5):
+        value = total
+        for i in range(8):
+            value = jnp.where(row == i, total[(8 * tile + i) % 5 : (8 * tile + i) % 5 + 1], value)
+        for i in range(8):
+            sent[40 * i + 8 * tile : 40 * i + 8 * tile + 8] = value
 
 
 def sweep(a, src, dst, n, layers=None):
@@ -454,20 +485,21 @@
 
 
 def solve(
-    pos, got, a0, a1, a2, pressure, left,
+    pos, got, a0, v0, a1, a2, pressure, left,
     a3, a4, d3, d4, r3, r4, s3, s4, t3, q5, e1, e2, e3, e4, f2, g4, g3, g2, g1, g0, b3, w0,
 ):
     gx, gy, gz = pos[0], pos[1], pos[2]
     lane = iota((16, 128), 1)
     for k in range(5):
-        rows = [got[16 * g : 16 * g + 16, 0, 128 * k : 128 * k + 128] for g in range(4)]
+        rows = [got[pl.ds(80 * g + k, 16, stride=5), :] for g in range(4)]
+        rows = rows + [turn(value, 64) for value in rows]
         for z in range(4):
             for s in range(2):
-                at = (z * 2 + s) * 16
-                value = turn(rows[0], -at)
-                for g in range(1, 4):
-                    value = jnp.where(lane // 16 == g, turn(rows[g], 16 * g - at), value)
-                value = jnp.where(lane < 64, value, turn(value, 64))
+                at = 2 * z + s
+                value = rows[0]
+                for g in range(1, 8):
+                    value = jnp.where(lane // 16 == (at + g) % 8, rows[g], value)
+                value = turn(value, -16 * at)
                 if k < 4:
                     a3[k, z, pl.ds(s, 16, stride=2), :] = value
                 else:
@@ -542,7 +574,8 @@
             lanes = slice(128 * half, 128 * half + 128)
             for z in (2 * zc, 2 * zc + 1):
                 if -3 <= z <= 10:
-                    w0[0, z + H, :, lanes] = a0[V, z + H, :, lanes] + e
+                    old = v0.at[OUTER.index(z + H)] if z + H in OUTER else a0.at[V, z + H]
+                    w0[0, z + H, :, lanes] = old[:, lanes] + e
 
     def sweep0(src, dst):
         def body(z):
@@ -597,9 +630,14 @@
         pos, tables, main, yl, yh,
         spaces=[SMEM] * 2 + [VMEM] * 3,
         scratch=[
-            (4, Z0, 32, 128), (5, Z0, 32, 128), (Z0, 32, 128), (Z0, 16, 128), (Z0, 32, 256),
+            (4, Z0, 32, 128), (5, Z0, 32, 128), (Z0, 32, 128), (8, 16, 128), (8, 16, 128),
             (8, 16, 128), (6, 4, 16, 128), (6, 4, 8, 128),
         ],
+    )
+    (v0,) = call(
+        outer0, [(4, 32, 256)], pos, tables, main, yl, yh, a0,
+        spaces=[SMEM] * 2 + [VMEM] * 4,
+        scratch=[(4, Z0, 32, 128), (5, Z0, 32, 128), (Z0, 32, 128), (6, Z0, 32, 256)],
     )
     blocks = [shift(packed, "gz", n) for n in (1, 2, 3)]
     stack, lo, hi = call(pack_y1, [(40, 8, 128)] + [(8, 8, 128)] * 2, packed, *blocks)
@@ -608,7 +646,7 @@
     near = (shift(full, "gx", 1), shift(full, "gx", -1), shift(lo, "gx", 2), shift(hi, "gx", -2))
     a1, a2, sent = call(
         level12,
-        [(6, 16, 32, 128), (6, 8, 16, 128), (64, 1, 640)],
+        [(6, 16, 32, 128), (6, 8, 16, 128), (320, 128)],
         pos, full, *near,
         spaces=[SMEM] + [VMEM] * 5,
         scratch=[
@@ -616,13 +654,13 @@
             (8, 16, 128), (8, 16, 128), (16, 32, 128), (8, 16, 128), (8, 16, 128),
         ],
     )
-    got = lax.all_to_all(sent, ("gy", "gx"), 0, 0)
+    got = lax.all_to_all(sent.reshape(64, 1, 640), ("gy", "gx"), 0, 0).reshape(320, 128)
     return tuple(
         call(
             solve,
             [(8, 16, 128), (8, 16, 128)],
-            pos, got, a0, a1, a2,
-            spaces=[SMEM] + [VMEM] * 4,
+            pos, got, a0, v0, a1, a2,
+            spaces=[SMEM] + [VMEM] * 5,
             scratch=[
                 (6, 4, 32, 128), (6, 2, 16, 128),
                 (4, 32, 128), (2, 16, 128),

time: 80.7 us -> 87.7 us (1.087)
  blocking collectives: 16.8 us -> 0 us
  local copies, waits for them, and re-layouts: 3.36 us -> 14 us
  starting transfers between devices: 25.6 us -> 32.1 us
  waiting for transfers between devices: 18.4 us -> 24.2 us
    all_to_all x1 -> x0, blocking collectives: 16.8 us -> none  [local(): got = lax.all_to_all(sent, ('gy', 'gx'), 0, 0)]
    unnamed x8 -> x34, local copies, waits for them, and re-layouts: 3.36 us -> 14 us
    all_to_all x0 -> x1, starting transfers between devices: none -> 6.58 us  [local(): lax.all_to_all(sent.reshape(64, 1, 640), ('gy', 'gx'), 0, 0)]
    all_to_all x0 -> x1, waiting for transfers between devices: none -> 5.86 us  [local(): lax.all_to_all(sent.reshape(64, 1, 640), ('gy', 'gx'), 0, 0)]
    pallas_call x10 -> x11, Pallas kernels: 14.7 us -> 15.2 us  [call(): pl.pallas_call(kernel, out_shape=[jax.ShapeDtypeStruct(s, F32) for s in o...]
  transfers between devices with their start and end apart: 15 -> 16, of which waited for: 12 -> 11; matrix products, arithmetic and copies ran while one was open for 1% -> 1% of each run, Pallas kernels for 2% -> 3%
where the time goes in v6:
time: 87.7 us; the launch traced here: 87 us
  starting transfers between devices  32.1 us (37%)
  waiting for transfers between devices  24.2 us (28%)
  Pallas kernels  15.2 us (17%)
  local copies, waits for them, and re-layouts  14 us (16%)
    ppermute x15, starting transfers between devices, shift(): lax.ppermute(value, axis, [((i + by) % count, i) for i in range(count)])  25.5 us
    ppermute x15, waiting for transfers between devices, shift(): lax.ppermute(value, axis, [((i + by) % count, i) for i in range(count)])  18.4 us
    pallas_call x11, Pallas kernels, call(): pl.pallas_call(kernel, out_shape=[jax.ShapeDtypeStruct(s, F32) for s in o...  15.2 us
    unnamed x34, local copies, waits for them, and re-layouts  14 us
    all_to_all x1, starting transfers between devices, local(): lax.all_to_all(sent.reshape(64, 1, 640), ('gy', 'gx'), 0, 0)  6.58 us
    all_to_all x1, waiting for transfers between devices, local(): lax.all_to_all(sent.reshape(64, 1, 640), ('gy', 'gx'), 0, 0)  5.86 us
  transfers between devices with their start and end apart: 16, of which 11 were waited for; matrix products, arithmetic and copies ran while one was open for 1% of the time, Pallas kernels for 3%

profile of v6, /device:TPU:1, one launch (start us, length us, event | category | flops | bytes accessed | tf_op | source)
XLA Modules:
  0.0 87.0 jit_solution(15720916855725049230)
XLA Ops:
  0.6 1.7 %shard_map.78 = (f32[18,16,128]{2,1,0:T(8,128)}, f32[18,16,128]{2,1,0:T(8,128)}) custom-call(s32[8,16,128]{2,1,0:T(8,128)} %f.3, s32[8,16,128]{2,1,0:T(8,128)} %b.3, f32[8,16,128]{2,1,0:T(8,128)} %s.3, f32[8,16,128]{2,1,0:T(8,128)} %d.3), custom_call_target="tpu_custom_call" | custom-call | tf_op jit(solution)/shard_map/pallas_call | solution.py:22
  2.3 3.4 %collective-permute-start = (f32[18,16,128]{2,1,0:T(8,128)}, f32[18,16,128]{2,1,0:T(8,128)S(1)}, u32[]{:S(2)}, u32[]{:S(2)}) collective-permute-start(f32[18,16,128]{2,1,0:T(8,128)} %get-tuple-element.23), channel_id=1, source_target_pairs={{1,0},{2,1},{3,2},{0,3},{5,4},{6,5},{7,6},{4,7},{9,8},{10,9},{11,1... | collective-permute-start | bytes 442376 | tf_op jit(solution)/shard_map/ppermute | solution.py:600
  9.5 2.1 %collective-permute-done.1.below = f32[18,16,128]{2,1,0:T(8,128)S(1)} collective-permute-done((f32[18,16,128]{2,1,0:T(8,128)}, f32[18,16,128]{2,1,0:T(8,128)S(1)}, u32[]{:S(2)}, u32[]{:S(2)}) %collective-permute-start.1) | collective-permute-done | bytes 147488 | tf_op jit(solution)/shard_map/ppermute | solution.py:600
  11.6 1.9 %collective-permute-start.2 = (f32[39,8,128]{2,1,0:T(8,128)S(1)}, f32[39,8,128]{2,1,0:T(8,128)S(1)}, u32[]{:S(2)}, u32[]{:S(2)}) collective-permute-start(f32[39,8,128]{2,1,0:T(8,128)S(1)} %get-tuple-element.27), channel_id=1, source_target_pairs={{16,0},{32,16},{48,32},{64,48},{80,64},{96,80},{112,96},{128,112},... | collective-permute-start | bytes 479240 | tf_op jit(solution)/shard_map/ppermute | solution.py:600
  13.5 1.5 %collective-permute-start.3 = (f32[39,8,128]{2,1,0:T(8,128)S(1)}, f32[39,8,128]{2,1,0:T(8,128)S(1)}, u32[]{:S(2)}, u32[]{:S(2)}) collective-permute-start(f32[39,8,128]{2,1,0:T(8,128)S(1)} %get-tuple-element.28), channel_id=1, source_target_pairs={{240,0},{0,16},{16,32},{32,48},{48,64},{64,80},{80,96},{96,112},{1... | collective-permute-start | bytes 479240 | tf_op jit(solution)/shard_map/ppermute | solution.py:600
  15.8 2.2 %collective-permute-done.2.ml = f32[39,8,128]{2,1,0:T(8,128)S(1)} collective-permute-done((f32[39,8,128]{2,1,0:T(8,128)S(1)}, f32[39,8,128]{2,1,0:T(8,128)S(1)}, u32[]{:S(2)}, u32[]{:S(2)}) %collective-permute-start.2) | collective-permute-done | bytes 159776 | tf_op jit(solution)/shard_map/ppermute | solution.py:600
  18.8 2.8 %collective-permute-start.4 = (f32[12,8,128]{2,1,0:T(8,128)S(1)}, f32[12,8,128]{2,1,0:T(8,128)S(1)}, u32[]{:S(2)}, u32[]{:S(2)}) collective-permute-start(f32[12,8,128]{2,1,0:T(8,128)S(1)} %get-tuple-element.31), channel_id=1, source_target_pairs={{4,0},{8,4},{12,8},{0,12},{5,1},{9,5},{13,9},{1,13},{6,2},{10,6},{... | collective-permute-start | bytes 147464 | tf_op jit(solution)/shard_map/ppermute | solution.py:600
  21.7 1.1 %shard_map.81.main = f32[5,18,32,128]{3,2,1,0:T(8,128)S(1)} custom-call(s32[3]{0:T(128)S(1)} %pad_add_fusion.pos, f32[16]{0:T(128)S(1)} %pad_maximum_fusion.tables, f32[4,18,8,128]{3,2,1,0:T(8,128)S(1)} %get-tuple-element.25.xl, f32[4,18,8,128]{3,2,1,0:T(8,128)S(1)} %get-tuple-element.26.xh, f32[4,18,8,128]{3,2,1,0:T(8,128)S(1)} %get-tuple-element.29.rl, ...), custom_call_target="tpu_custom_call" | custom-call | tf_op jit(solution)/shard_map/pallas_call | solution.py:22
  22.8 3.0 %collective-permute-done.5.yh = f32[12,8,128]{2,1,0:T(8,128)S(1)} collective-permute-done((f32[12,8,128]{2,1,0:T(8,128)S(1)}, f32[12,8,128]{2,1,0:T(8,128)S(1)}, u32[]{:S(2)}, u32[]{:S(2)}) %collective-permute-start.5) | collective-permute-done | bytes 49184 | tf_op jit(solution)/shard_map/ppermute | solution.py:600
  25.8 2.7 %shard_map.82 = (f32[6,18,32,256]{3,2,1,0:T(8,128)S(1)}, f32[5,2,8,128]{3,2,1,0:T(8,128)S(1)}) custom-call(s32[3]{0:T(128)S(1)} %pad_add_fusion.pos, f32[16]{0:T(128)S(1)} %pad_maximum_fusion.tables, f32[5,18,32,128]{3,2,1,0:T(8,128)S(1)} %shard_map.81.main, f32[12,8,128]{2,1,0:T(8,128)S(1)} %collective-permute-done.4.yl, ...), custom_call_target="tpu_custom_call" | custom-call | tf_op jit(solution)/shard_map/pallas_call | solution.py:22
  28.5 1.1 %copy-done = f32[5,18,32,128]{3,2,1,0:T(8,128)} copy-done((f32[5,18,32,128]{3,2,1,0:T(8,128)}, f32[5,18,32,128]{3,2,1,0:T(8,128)S(1)}, u32[]{:S(2)}) %copy-start) | copy-done | bytes 1474584
  29.6 1.8 %collective-permute-start.7 = (f32[5,2,8,128]{3,2,1,0:T(8,128)S(1)}, f32[5,2,8,128]{3,2,1,0:T(8,128)S(1)}, u32[]{:S(2)}, u32[]{:S(2)}) collective-permute-start(f32[5,2,8,128]{3,2,1,0:T(8,128)S(1)} %get-tuple-element.33.own), channel_id=1, source_target_pairs={{2,0},{3,1},{0,2},{1,3},{6,4},{7,5},{4,6},{5,7},{10,8},{11,9},{8,1... | collective-permute-start | bytes 122888 | tf_op jit(solution)/shard_map/ppermute | solution.py:600
  31.4 0.9 %collective-permute-start.6 = (f32[5,2,8,128]{3,2,1,0:T(8,128)S(1)}, f32[5,2,8,128]{3,2,1,0:T(8,128)S(1)}, u32[]{:S(2)}, u32[]{:S(2)}) collective-permute-start(f32[5,2,8,128]{3,2,1,0:T(8,128)S(1)} %get-tuple-element.33.own), channel_id=1, source_target_pairs={{1,0},{2,1},{3,2},{0,3},{5,4},{6,5},{7,6},{4,7},{9,8},{10,9},{11,1... | collective-permute-start | bytes 122888 | tf_op jit(solution)/shard_map/ppermute | solution.py:600
  32.3 1.8 %collective-permute-done.8.b3 = f32[5,2,8,128]{3,2,1,0:T(8,128)S(1)} collective-permute-done((f32[5,2,8,128]{3,2,1,0:T(8,128)S(1)}, f32[5,2,8,128]{3,2,1,0:T(8,128)S(1)}, u32[]{:S(2)}, u32[]{:S(2)}) %collective-permute-start.8) | collective-permute-done | bytes 40992 | tf_op jit(solution)/shard_map/ppermute | solution.py:600
  34.9 1.4 %collective-permute-start.10 = (f32[8,8,128]{2,1,0:T(8,128)S(1)}, f32[8,8,128]{2,1,0:T(8,128)S(1)}, u32[]{:S(2)}, u32[]{:S(2)}) collective-permute-start(f32[8,8,128]{2,1,0:T(8,128)S(1)} %get-tuple-element.36), channel_id=1, source_target_pairs={{12,0},{0,4},{4,8},{8,12},{13,1},{1,5},{5,9},{9,13},{14,2},{2,6},{... | collective-permute-start | bytes 98312 | tf_op jit(solution)/shard_map/ppermute | solution.py:600
  36.4 1.3 %collective-permute-done.9.right = f32[8,8,128]{2,1,0:T(8,128)S(1)} collective-permute-done((f32[8,8,128]{2,1,0:T(8,128)S(1)}, f32[8,8,128]{2,1,0:T(8,128)S(1)}, u32[]{:S(2)}, u32[]{:S(2)}) %collective-permute-start.9) | collective-permute-done | bytes 32800 | tf_op jit(solution)/shard_map/ppermute | solution.py:600
  37.7 1.3 %collective-permute-done.10.left = f32[8,8,128]{2,1,0:T(8,128)S(1)} collective-permute-done((f32[8,8,128]{2,1,0:T(8,128)S(1)}, f32[8,8,128]{2,1,0:T(8,128)S(1)}, u32[]{:S(2)}, u32[]{:S(2)}) %collective-permute-start.10) | collective-permute-done | bytes 32800 | tf_op jit(solution)/shard_map/ppermute | solution.py:600
  39.0 5.3 %collective-permute-start.12 = (f32[56,8,128]{2,1,0:T(8,128)S(1)}, f32[56,8,128]{2,1,0:T(8,128)S(1)}, u32[]{:S(2)}, u32[]{:S(2)}) collective-permute-start(f32[56,8,128]{2,1,0:T(8,128)S(1)} %get-tuple-element.37.full), channel_id=1, source_target_pairs={{240,0},{0,16},{16,32},{32,48},{48,64},{64,80},{80,96},{96,112},{1... | collective-permute-start | bytes 688136 | tf_op jit(solution)/shard_map/ppermute | solution.py:600
  44.3 3.8 %collective-permute-start.11 = (f32[56,8,128]{2,1,0:T(8,128)S(1)}, f32[56,8,128]{2,1,0:T(8,128)S(1)}, u32[]{:S(2)}, u32[]{:S(2)}) collective-permute-start(f32[56,8,128]{2,1,0:T(8,128)S(1)} %get-tuple-element.37.full), channel_id=1, source_target_pairs={{16,0},{32,16},{48,32},{64,48},{80,64},{96,80},{112,96},{128,112},... | collective-permute-start | bytes 688136 | tf_op jit(solution)/shard_map/ppermute | solution.py:600
  48.1 2.6 %collective-permute-start.13 = (f32[28,8,128]{2,1,0:T(8,128)S(1)}, f32[28,8,128]{2,1,0:T(8,128)S(1)}, u32[]{:S(2)}, u32[]{:S(2)}) collective-permute-start(f32[28,8,128]{2,1,0:T(8,128)S(1)} %get-tuple-element.38), channel_id=1, source_target_pairs={{32,0},{48,16},{64,32},{80,48},{96,64},{112,80},{128,96},{144,112}... | collective-permute-start | bytes 344072 | tf_op jit(solution)/shard_map/ppermute | solution.py:600
  50.6 2.5 %collective-permute-done.13.xr2 = f32[28,8,128]{2,1,0:T(8,128)S(1)} collective-permute-done((f32[28,8,128]{2,1,0:T(8,128)S(1)}, f32[28,8,128]{2,1,0:T(8,128)S(1)}, u32[]{:S(2)}, u32[]{:S(2)}) %collective-permute-start.13) | collective-permute-done | bytes 114720 | tf_op jit(solution)/shard_map/ppermute | solution.py:600
  53.1 3.1 %collective-permute-done.14.xl2 = f32[28,8,128]{2,1,0:T(8,128)S(1)} collective-permute-done((f32[28,8,128]{2,1,0:T(8,128)S(1)}, f32[28,8,128]{2,1,0:T(8,128)S(1)}, u32[]{:S(2)}, u32[]{:S(2)}) %collective-permute-start.14) | collective-permute-done | bytes 114720 | tf_op jit(solution)/shard_map/ppermute | solution.py:600
  56.2 3.1 %shard_map.85 = (f32[6,16,32,128]{3,2,1,0:T(8,128)S(1)}, f32[6,8,16,128]{3,2,1,0:T(8,128)S(1)}, f32[320,128]{1,0:T(8,128)S(1)}) custom-call(s32[3]{0:T(128)S(1)} %pad_add_fusion.pos, f32[56,8,128]{2,1,0:T(8,128)S(1)} %get-tuple-element.37.full, f32[56,8,128]{2,1,0:T(8,128)S(1)} %collective-permute-done.11.xr, f32[56,8,128]{2,1,0:T(8,128)S(1)} %collective-permute-done.12.xl, ...), custom_call_target="tpu_custom_call" | custom-call | tf_op jit(solution)/shard_map/pallas_call | solution.py:22
  59.3 1.2 %copy-done.2 = f32[6,16,32,128]{3,2,1,0:T(8,128)} copy-done((f32[6,16,32,128]{3,2,1,0:T(8,128)}, f32[6,16,32,128]{3,2,1,0:T(8,128)S(1)}, u32[]{:S(2)}) %copy-start.2) | copy-done | bytes 1572888
  61.9 6.6 %all-to-all-start = ((f32[64,1,640]{2,1,0:T(1,128)}), f32[64,1,640]{2,1,0:T(1,128)}, u32[]{:S(2)}, u32[]{:S(2)}) async-start(f32[64,1,640]{2,1,0:T(1,128)} %bitcast.5), calls=%async_computation | async-start | bytes 327680 | tf_op jit(solution)/shard_map/all_to_all | solution.py:657
  68.5 1.4 %copy-done.1 = f32[5,18,32,128]{3,2,1,0:T(8,128)S(1)} copy-done((f32[5,18,32,128]{3,2,1,0:T(8,128)S(1)}, f32[5,18,32,128]{3,2,1,0:T(8,128)}, u32[]{:S(2)}) %copy-start.1) | copy-done | bytes 1474584
  71.5 1.0 %shard_map.86.v0 = f32[4,32,256]{2,1,0:T(8,128)S(1)} custom-call(s32[3]{0:T(128)S(1)} %pad_add_fusion.pos, f32[16]{0:T(128)S(1)} %pad_maximum_fusion.tables, f32[5,18,32,128]{3,2,1,0:T(8,128)S(1)} %copy-done.1, f32[12,8,128]{2,1,0:T(8,128)S(1)} %copy-done.13, f32[12,8,128]{2,1,0:T(8,128)S(1)} %copy-done.15, f32[6,18,32,256]{3,2,1,0:T(8,128)S(1)} %get-tuple-element.41.a0), custom_call_target="tpu_custom_call" | custom-call | tf_op jit(solution)/shard_map/pallas_call | solution.py:22
  73.2 5.9 %all-to-all-done = f32[64,1,640]{2,1,0:T(1,128)} async-done(((f32[64,1,640]{2,1,0:T(1,128)}), f32[64,1,640]{2,1,0:T(1,128)}, u32[]{:S(2)}, u32[]{:S(2)}) %all-to-all-start) | async-done | bytes 163872 | tf_op jit(solution)/shard_map/all_to_all | solution.py:657
  79.0 1.4 %copy-done.3 = f32[6,16,32,128]{3,2,1,0:T(8,128)S(1)} copy-done((f32[6,16,32,128]{3,2,1,0:T(8,128)S(1)}, f32[6,16,32,128]{3,2,1,0:T(8,128)}, u32[]{:S(2)}) %copy-start.3) | copy-done | bytes 1572888
  80.4 0.9 %copy-done.5 = f32[4,32,256]{2,1,0:T(8,128)S(1)} copy-done((f32[4,32,256]{2,1,0:T(8,128)S(1)}, f32[4,32,256]{2,1,0:T(8,128)}, u32[]{:S(2)}) %copy-start.5) | copy-done | bytes 131096
  81.3 1.0 %copy-done.7 = f32[6,8,16,128]{3,2,1,0:T(8,128)S(1)} copy-done((f32[6,8,16,128]{3,2,1,0:T(8,128)S(1)}, f32[6,8,16,128]{3,2,1,0:T(8,128)}, u32[]{:S(2)}) %copy-start.7) | copy-done | bytes 393240
  82.3 4.7 %shard_map.87 = (f32[8,16,128]{2,1,0:T(8,128)}, f32[8,16,128]{2,1,0:T(8,128)}) custom-call(s32[3]{0:T(128)S(1)} %pad_add_fusion.pos, f32[320,128]{1,0:T(8,128)} %bitcast.4.got, f32[6,18,32,256]{3,2,1,0:T(8,128)S(1)} %get-tuple-element.41.a0, f32[4,32,256]{2,1,0:T(8,128)S(1)} %copy-done.5, f32[6,16,32,128]{3,2,1,0:T(8,128)S(1)} %copy-done.3, ...), custom_call_target="tpu_custom_call" | custom-call | tf_op jit(solution)/shard_map/pallas_call | solution.py:22
  (47 shorter events, 10.0 us)
Async XLA Ops:
  2.3 7.1 %collective-permute-start = (f32[18,16,128]{2,1,0:T(8,128)}, f32[18,16,128]{2,1,0:T(8,128)S(1)}, u32[]{:S(2)}, u32[]{:S(2)}) collective-permute-start(f32[18,16,128]{2,1,0:T(8,128)} %get-tuple-element.23), channel_id=1, source_target_pairs={{1,0},{2,1},{3,2},{0,3},{5,4},{6,5},{7,6},{4,7},{9,8},{10,9},{11,1... | collective-permute-start | bytes 442376 | tf_op jit(solution)/shard_map/ppermute | solution.py:600
  5.7 5.8 %collective-permute-start.1 = (f32[18,16,128]{2,1,0:T(8,128)}, f32[18,16,128]{2,1,0:T(8,128)S(1)}, u32[]{:S(2)}, u32[]{:S(2)}) collective-permute-start(f32[18,16,128]{2,1,0:T(8,128)} %get-tuple-element.24), channel_id=1, source_target_pairs={{3,0},{0,1},{1,2},{2,3},{7,4},{4,5},{5,6},{6,7},{11,8},{8,9},{9,10... | collective-permute-start | bytes 442376 | tf_op jit(solution)/shard_map/ppermute | solution.py:600
  5.7 0.8 copy-start.8
  6.6 0.8 copy-start.9
  7.4 0.8 copy-start.10
  8.2 0.8 copy-start.11
  11.6 6.4 %collective-permute-start.2 = (f32[39,8,128]{2,1,0:T(8,128)S(1)}, f32[39,8,128]{2,1,0:T(8,128)S(1)}, u32[]{:S(2)}, u32[]{:S(2)}) collective-permute-start(f32[39,8,128]{2,1,0:T(8,128)S(1)} %get-tuple-element.27), channel_id=1, source_target_pairs={{16,0},{32,16},{48,32},{64,48},{80,64},{96,80},{112,96},{128,112},... | collective-permute-start | bytes 479240 | tf_op jit(solution)/shard_map/ppermute | solution.py:600
  13.5 5.0 %collective-permute-start.3 = (f32[39,8,128]{2,1,0:T(8,128)S(1)}, f32[39,8,128]{2,1,0:T(8,128)S(1)}, u32[]{:S(2)}, u32[]{:S(2)}) collective-permute-start(f32[39,8,128]{2,1,0:T(8,128)S(1)} %get-tuple-element.28), channel_id=1, source_target_pairs={{240,0},{0,16},{16,32},{32,48},{48,64},{64,80},{80,96},{96,112},{1... | collective-permute-start | bytes 479240 | tf_op jit(solution)/shard_map/ppermute | solution.py:600
  18.8 4.0 %collective-permute-start.4 = (f32[12,8,128]{2,1,0:T(8,128)S(1)}, f32[12,8,128]{2,1,0:T(8,128)S(1)}, u32[]{:S(2)}, u32[]{:S(2)}) collective-permute-start(f32[12,8,128]{2,1,0:T(8,128)S(1)} %get-tuple-element.31), channel_id=1, source_target_pairs={{4,0},{8,4},{12,8},{0,12},{5,1},{9,5},{13,9},{1,13},{6,2},{10,6},{... | collective-permute-start | bytes 147464 | tf_op jit(solution)/shard_map/ppermute | solution.py:600
  21.7 4.2 %collective-permute-start.5 = (f32[12,8,128]{2,1,0:T(8,128)S(1)}, f32[12,8,128]{2,1,0:T(8,128)S(1)}, u32[]{:S(2)}, u32[]{:S(2)}) collective-permute-start(f32[12,8,128]{2,1,0:T(8,128)S(1)} %get-tuple-element.32), channel_id=1, source_target_pairs={{12,0},{0,4},{4,8},{8,12},{13,1},{1,5},{5,9},{9,13},{14,2},{2,6},{... | collective-permute-start | bytes 147464 | tf_op jit(solution)/shard_map/ppermute | solution.py:600
  22.8 33.4 %copy-start.12 = (f32[12,8,128]{2,1,0:T(8,128)}, f32[12,8,128]{2,1,0:T(8,128)S(1)}, u32[]{:S(2)}) copy-start(f32[12,8,128]{2,1,0:T(8,128)S(1)} %collective-permute-done.4.yl) | copy-start | bytes 147460
  25.8 30.4 %copy-start.14 = (f32[12,8,128]{2,1,0:T(8,128)}, f32[12,8,128]{2,1,0:T(8,128)S(1)}, u32[]{:S(2)}) copy-start(f32[12,8,128]{2,1,0:T(8,128)S(1)} %collective-permute-done.5.yh) | copy-start | bytes 147460
  28.5 1.1 %copy-start = (f32[5,18,32,128]{3,2,1,0:T(8,128)}, f32[5,18,32,128]{3,2,1,0:T(8,128)S(1)}, u32[]{:S(2)}) copy-start(f32[5,18,32,128]{3,2,1,0:T(8,128)S(1)} %shard_map.81.main) | copy-start | bytes 4423684
  29.6 4.5 %collective-permute-start.8 = (f32[5,2,8,128]{3,2,1,0:T(8,128)S(1)}, f32[5,2,8,128]{3,2,1,0:T(8,128)S(1)}, u32[]{:S(2)}, u32[]{:S(2)}) collective-permute-start(f32[5,2,8,128]{3,2,1,0:T(8,128)S(1)} %get-tuple-element.33.own), channel_id=1, source_target_pairs={{3,0},{0,1},{1,2},{2,3},{7,4},{4,5},{5,6},{6,7},{11,8},{8,9},{9,10... | collective-permute-start | bytes 122888 | tf_op jit(solution)/shard_map/ppermute | solution.py:600
  29.6 4.5 %collective-permute-start.7 = (f32[5,2,8,128]{3,2,1,0:T(8,128)S(1)}, f32[5,2,8,128]{3,2,1,0:T(8,128)S(1)}, u32[]{:S(2)}, u32[]{:S(2)}) collective-permute-start(f32[5,2,8,128]{3,2,1,0:T(8,128)S(1)} %get-tuple-element.33.own), channel_id=1, source_target_pairs={{2,0},{3,1},{0,2},{1,3},{6,4},{7,5},{4,6},{5,7},{10,8},{11,9},{8,1... | collective-permute-start | bytes 122888 | tf_op jit(solution)/shard_map/ppermute | solution.py:600
  31.4 3.3 %collective-permute-start.6 = (f32[5,2,8,128]{3,2,1,0:T(8,128)S(1)}, f32[5,2,8,128]{3,2,1,0:T(8,128)S(1)}, u32[]{:S(2)}, u32[]{:S(2)}) collective-permute-start(f32[5,2,8,128]{3,2,1,0:T(8,128)S(1)} %get-tuple-element.33.own), channel_id=1, source_target_pairs={{1,0},{2,1},{3,2},{0,3},{5,4},{6,5},{7,6},{4,7},{9,8},{10,9},{11,1... | collective-permute-start | bytes 122888 | tf_op jit(solution)/shard_map/ppermute | solution.py:600
  34.8 2.8 %collective-permute-start.9 = (f32[8,8,128]{2,1,0:T(8,128)S(1)}, f32[8,8,128]{2,1,0:T(8,128)S(1)}, u32[]{:S(2)}, u32[]{:S(2)}) collective-permute-start(f32[8,8,128]{2,1,0:T(8,128)S(1)} %get-tuple-element.35), channel_id=1, source_target_pairs={{4,0},{8,4},{12,8},{0,12},{5,1},{9,5},{13,9},{1,13},{6,2},{10,6},{... | collective-permute-start | bytes 98312 | tf_op jit(solution)/shard_map/ppermute | solution.py:600
  34.9 4.0 %collective-permute-start.10 = (f32[8,8,128]{2,1,0:T(8,128)S(1)}, f32[8,8,128]{2,1,0:T(8,128)S(1)}, u32[]{:S(2)}, u32[]{:S(2)}) collective-permute-start(f32[8,8,128]{2,1,0:T(8,128)S(1)} %get-tuple-element.36), channel_id=1, source_target_pairs={{12,0},{0,4},{4,8},{8,12},{13,1},{1,5},{5,9},{9,13},{14,2},{2,6},{... | collective-permute-start | bytes 98312 | tf_op jit(solution)/shard_map/ppermute | solution.py:600
  39.0 17.2 %collective-permute-start.12 = (f32[56,8,128]{2,1,0:T(8,128)S(1)}, f32[56,8,128]{2,1,0:T(8,128)S(1)}, u32[]{:S(2)}, u32[]{:S(2)}) collective-permute-start(f32[56,8,128]{2,1,0:T(8,128)S(1)} %get-tuple-element.37.full), channel_id=1, source_target_pairs={{240,0},{0,16},{16,32},{32,48},{48,64},{64,80},{80,96},{96,112},{1... | collective-permute-start | bytes 688136 | tf_op jit(solution)/shard_map/ppermute | solution.py:600
  44.3 12.0 %collective-permute-start.11 = (f32[56,8,128]{2,1,0:T(8,128)S(1)}, f32[56,8,128]{2,1,0:T(8,128)S(1)}, u32[]{:S(2)}, u32[]{:S(2)}) collective-permute-start(f32[56,8,128]{2,1,0:T(8,128)S(1)} %get-tuple-element.37.full), channel_id=1, source_target_pairs={{16,0},{32,16},{48,32},{64,48},{80,64},{96,80},{112,96},{128,112},... | collective-permute-start | bytes 688136 | tf_op jit(solution)/shard_map/ppermute | solution.py:600
  48.1 5.1 %collective-permute-start.13 = (f32[28,8,128]{2,1,0:T(8,128)S(1)}, f32[28,8,128]{2,1,0:T(8,128)S(1)}, u32[]{:S(2)}, u32[]{:S(2)}) collective-permute-start(f32[28,8,128]{2,1,0:T(8,128)S(1)} %get-tuple-element.38), channel_id=1, source_target_pairs={{32,0},{48,16},{64,32},{80,48},{96,64},{112,80},{128,96},{144,112}... | collective-permute-start | bytes 344072 | tf_op jit(solution)/shard_map/ppermute | solution.py:600
  50.6 5.6 %collective-permute-start.14 = (f32[28,8,128]{2,1,0:T(8,128)S(1)}, f32[28,8,128]{2,1,0:T(8,128)S(1)}, u32[]{:S(2)}, u32[]{:S(2)}) collective-permute-start(f32[28,8,128]{2,1,0:T(8,128)S(1)} %get-tuple-element.39), channel_id=1, source_target_pairs={{224,0},{240,16},{0,32},{16,48},{32,64},{48,80},{64,96},{80,112},{... | collective-permute-start | bytes 344072 | tf_op jit(solution)/shard_map/ppermute | solution.py:600
  59.3 1.2 %copy-start.2 = (f32[6,16,32,128]{3,2,1,0:T(8,128)}, f32[6,16,32,128]{3,2,1,0:T(8,128)S(1)}, u32[]{:S(2)}) copy-start(f32[6,16,32,128]{3,2,1,0:T(8,128)S(1)} %get-tuple-element.42.a1) | copy-start | bytes 4718596
  60.5 0.8 copy-start.6
  61.9 17.1 %all-to-all-start = ((f32[64,1,640]{2,1,0:T(1,128)}), f32[64,1,640]{2,1,0:T(1,128)}, u32[]{:S(2)}, u32[]{:S(2)}) async-start(f32[64,1,640]{2,1,0:T(1,128)} %bitcast.5), calls=%async_computation | async-start | bytes 327680 | tf_op jit(solution)/shard_map/all_to_all | solution.py:657
  68.5 1.4 %copy-start.1 = (f32[5,18,32,128]{3,2,1,0:T(8,128)S(1)}, f32[5,18,32,128]{3,2,1,0:T(8,128)}, u32[]{:S(2)}) copy-start(f32[5,18,32,128]{3,2,1,0:T(8,128)} %copy-done) | copy-start | bytes 4423684
  69.9 0.8 copy-start.13
  70.7 0.8 copy-start.15
  72.5 0.7 copy-start.4
  79.0 1.4 %copy-start.3 = (f32[6,16,32,128]{3,2,1,0:T(8,128)S(1)}, f32[6,16,32,128]{3,2,1,0:T(8,128)}, u32[]{:S(2)}) copy-start(f32[6,16,32,128]{3,2,1,0:T(8,128)} %copy-done.2) | copy-start | bytes 4718596
  80.4 0.9 %copy-start.5 = (f32[4,32,256]{2,1,0:T(8,128)S(1)}, f32[4,32,256]{2,1,0:T(8,128)}, u32[]{:S(2)}) copy-start(f32[4,32,256]{2,1,0:T(8,128)} %copy-done.4) | copy-start | bytes 393220
  81.3 1.0 %copy-start.7 = (f32[6,8,16,128]{3,2,1,0:T(8,128)S(1)}, f32[6,8,16,128]{3,2,1,0:T(8,128)}, u32[]{:S(2)}) copy-start(f32[6,8,16,128]{3,2,1,0:T(8,128)} %copy-done.6) | copy-start | bytes 1179652
  (1 other events, 0.7 us)

commit v7 on v6

--- a/solution.py
+++ b/solution.py
@@ -412,7 +412,7 @@
         hi[n] = jnp.where(first, b, a)
 
 
-def level12(pos, full, xr, xl, xr2, xl2, a, b, sent, d1, r1, t1, m1, d2, r2, s1, s2, q2):
+def level12(pos, full, xr, xl, xr2, xl2, before, a, b, sent, d1, r1, t1, m1, d2, r2, s1, s2, q2):
     gx, gy, gz = pos[0], pos[1], pos[2]
     row, lane = iota((8, 128), 0), iota((8, 128), 1)
     y = gy * 64 + jnp.where(lane < 96, lane, lane - 128)
@@ -647,8 +647,8 @@
     a1, a2, sent = call(
         level12,
         [(6, 16, 32, 128), (6, 8, 16, 128), (320, 128)],
-        pos, full, *near,
-        spaces=[SMEM] + [VMEM] * 5,
+        pos, full, *near, v0,
+        spaces=[SMEM] + [VMEM] * 6,
         scratch=[
             (16, 32, 128), (16, 32, 128), (5, 8, 32, 128), (4, 2, 8, 128),
             (8, 16, 128), (8, 16, 128), (16, 32, 128), (8, 16, 128), (8, 16, 128),

time: 87.7 us -> 79.9 us (0.911)
  blocking collectives: 0 us -> 16.8 us
  local copies, waits for them, and re-layouts: 14 us -> 3.36 us
  waiting for transfers between devices: 24.2 us -> 17.3 us
  starting transfers between devices: 32.1 us -> 25.6 us
    all_to_all x0 -> x1, blocking collectives: none -> 16.8 us  [local(): lax.all_to_all(sent.reshape(64, 1, 640), ('gy', 'gx'), 0, 0)]
    unnamed x34 -> x8, local copies, waits for them, and re-layouts: 14 us -> 3.36 us
    all_to_all x1 -> x0, starting transfers between devices: 6.58 us -> none  [local(): lax.all_to_all(sent.reshape(64, 1, 640), ('gy', 'gx'), 0, 0)]
    all_to_all x1 -> x0, waiting for transfers between devices: 5.86 us -> none  [local(): lax.all_to_all(sent.reshape(64, 1, 640), ('gy', 'gx'), 0, 0)]
    ppermute x15, waiting for transfers between devices: 18.4 us -> 17.3 us  [shift(): lax.ppermute(value, axis, [((i + by) % count, i) for i in range(count)])]
  transfers between devices with their start and end apart: 16 -> 15, of which waited for: 11 -> 11; matrix products, arithmetic and copies ran while one was open for 1% -> 1% of each run, Pallas kernels for 3% -> 3%
where the time goes in v7:
time: 79.9 us; the launch traced here: 79.5 us
  starting transfers between devices  25.6 us (32%)
  waiting for transfers between devices  17.3 us (22%)
  blocking collectives  16.8 us (21%)
  Pallas kernels  15 us (19%)
  local copies, waits for them, and re-layouts  3.36 us (4%)
  other arithmetic  0.82 us (1%)
    ppermute x15, starting transfers between devices, shift(): lax.ppermute(value, axis, [((i + by) % count, i) for i in range(count)])  25.6 us
    ppermute x15, waiting for transfers between devices, shift(): lax.ppermute(value, axis, [((i + by) % count, i) for i in range(count)])  17.3 us
    all_to_all x1, blocking collectives, local(): lax.all_to_all(sent.reshape(64, 1, 640), ('gy', 'gx'), 0, 0)  16.8 us
    pallas_call x11, Pallas kernels, call(): pl.pallas_call(kernel, out_shape=[jax.ShapeDtypeStruct(s, F32) for s in o...  15 us
    unnamed x8, local copies, waits for them, and re-layouts  3.36 us
  transfers between devices with their start and end apart: 15, of which 11 were waited for; matrix products, arithmetic and copies ran while one was open for 1% of the time, Pallas kernels for 3%

profile of v7, /device:TPU:1, one launch (start us, length us, event | category | flops | bytes accessed | tf_op | source)
XLA Modules:
  0.0 79.5 jit_solution(4467378573503937554)
XLA Ops:
  0.6 1.7 %shard_map.78 = (f32[18,16,128]{2,1,0:T(8,128)}, f32[18,16,128]{2,1,0:T(8,128)}) custom-call(s32[8,16,128]{2,1,0:T(8,128)} %f.3, s32[8,16,128]{2,1,0:T(8,128)} %b.3, f32[8,16,128]{2,1,0:T(8,128)} %s.3, f32[8,16,128]{2,1,0:T(8,128)} %d.3), custom_call_target="tpu_custom_call" | custom-call | tf_op jit(solution)/shard_map/pallas_call | solution.py:22
  2.3 3.4 %collective-permute-start = (f32[18,16,128]{2,1,0:T(8,128)}, f32[18,16,128]{2,1,0:T(8,128)S(1)}, u32[]{:S(2)}, u32[]{:S(2)}) collective-permute-start(f32[18,16,128]{2,1,0:T(8,128)} %get-tuple-element.23), channel_id=1, source_target_pairs={{1,0},{2,1},{3,2},{0,3},{5,4},{6,5},{7,6},{4,7},{9,8},{10,9},{11,1... | collective-permute-start | bytes 442376 | tf_op jit(solution)/shard_map/ppermute | solution.py:600
  5.7 0.8 %copy-done = s32[8,16,128]{2,1,0:T(8,128)S(1)} copy-done((s32[8,16,128]{2,1,0:T(8,128)S(1)}, s32[8,16,128]{2,1,0:T(8,128)}, u32[]{:S(2)}) %copy-start) | copy-done | bytes 65560
  6.6 0.8 %copy-done.1 = s32[8,16,128]{2,1,0:T(8,128)S(1)} copy-done((s32[8,16,128]{2,1,0:T(8,128)S(1)}, s32[8,16,128]{2,1,0:T(8,128)}, u32[]{:S(2)}) %copy-start.1) | copy-done | bytes 65560
  7.4 0.8 %copy-done.2 = f32[8,16,128]{2,1,0:T(8,128)S(1)} copy-done((f32[8,16,128]{2,1,0:T(8,128)S(1)}, f32[8,16,128]{2,1,0:T(8,128)}, u32[]{:S(2)}) %copy-start.2) | copy-done | bytes 65560
  8.2 0.8 %copy-done.3 = f32[8,16,128]{2,1,0:T(8,128)S(1)} copy-done((f32[8,16,128]{2,1,0:T(8,128)S(1)}, f32[8,16,128]{2,1,0:T(8,128)}, u32[]{:S(2)}) %copy-start.3) | copy-done | bytes 65560
  9.5 2.1 %collective-permute-done.1.below = f32[18,16,128]{2,1,0:T(8,128)S(1)} collective-permute-done((f32[18,16,128]{2,1,0:T(8,128)}, f32[18,16,128]{2,1,0:T(8,128)S(1)}, u32[]{:S(2)}, u32[]{:S(2)}) %collective-permute-start.1) | collective-permute-done | bytes 147488 | tf_op jit(solution)/shard_map/ppermute | solution.py:600
  11.6 1.9 %collective-permute-start.2 = (f32[39,8,128]{2,1,0:T(8,128)S(1)}, f32[39,8,128]{2,1,0:T(8,128)S(1)}, u32[]{:S(2)}, u32[]{:S(2)}) collective-permute-start(f32[39,8,128]{2,1,0:T(8,128)S(1)} %get-tuple-element.27), channel_id=1, source_target_pairs={{16,0},{32,16},{48,32},{64,48},{80,64},{96,80},{112,96},{128,112},... | collective-permute-start | bytes 479240 | tf_op jit(solution)/shard_map/ppermute | solution.py:600
  13.5 1.5 %collective-permute-start.3 = (f32[39,8,128]{2,1,0:T(8,128)S(1)}, f32[39,8,128]{2,1,0:T(8,128)S(1)}, u32[]{:S(2)}, u32[]{:S(2)}) collective-permute-start(f32[39,8,128]{2,1,0:T(8,128)S(1)} %get-tuple-element.28), channel_id=1, source_target_pairs={{240,0},{0,16},{16,32},{32,48},{48,64},{64,80},{80,96},{96,112},{1... | collective-permute-start | bytes 479240 | tf_op jit(solution)/shard_map/ppermute | solution.py:600
  15.0 0.7 pad_maximum_fusion.tables
  15.8 2.2 %collective-permute-done.2.ml = f32[39,8,128]{2,1,0:T(8,128)S(1)} collective-permute-done((f32[39,8,128]{2,1,0:T(8,128)S(1)}, f32[39,8,128]{2,1,0:T(8,128)S(1)}, u32[]{:S(2)}, u32[]{:S(2)}) %collective-permute-start.2) | collective-permute-done | bytes 159776 | tf_op jit(solution)/shard_map/ppermute | solution.py:600
  18.0 0.5 collective-permute-done.3.mh
  18.8 2.8 %collective-permute-start.4 = (f32[12,8,128]{2,1,0:T(8,128)S(1)}, f32[12,8,128]{2,1,0:T(8,128)S(1)}, u32[]{:S(2)}, u32[]{:S(2)}) collective-permute-start(f32[12,8,128]{2,1,0:T(8,128)S(1)} %get-tuple-element.31), channel_id=1, source_target_pairs={{4,0},{8,4},{12,8},{0,12},{5,1},{9,5},{13,9},{1,13},{6,2},{10,6},{... | collective-permute-start | bytes 147464 | tf_op jit(solution)/shard_map/ppermute | solution.py:600
  21.7 1.1 %shard_map.81.main = f32[5,18,32,128]{3,2,1,0:T(8,128)S(1)} custom-call(s32[3]{0:T(128)S(1)} %pad_add_fusion.pos, f32[16]{0:T(128)S(1)} %pad_maximum_fusion.tables, f32[4,18,8,128]{3,2,1,0:T(8,128)S(1)} %get-tuple-element.25.xl, f32[4,18,8,128]{3,2,1,0:T(8,128)S(1)} %get-tuple-element.26.xh, f32[4,18,8,128]{3,2,1,0:T(8,128)S(1)} %get-tuple-element.29.rl, ...), custom_call_target="tpu_custom_call" | custom-call | tf_op jit(solution)/shard_map/pallas_call | solution.py:22
  22.8 3.0 %collective-permute-done.5.yh = f32[12,8,128]{2,1,0:T(8,128)S(1)} collective-permute-done((f32[12,8,128]{2,1,0:T(8,128)S(1)}, f32[12,8,128]{2,1,0:T(8,128)S(1)}, u32[]{:S(2)}, u32[]{:S(2)}) %collective-permute-start.5) | collective-permute-done | bytes 49184 | tf_op jit(solution)/shard_map/ppermute | solution.py:600
  25.8 2.7 %shard_map.82 = (f32[6,18,32,256]{3,2,1,0:T(8,128)S(1)}, f32[5,2,8,128]{3,2,1,0:T(8,128)S(1)}) custom-call(s32[3]{0:T(128)S(1)} %pad_add_fusion.pos, f32[16]{0:T(128)S(1)} %pad_maximum_fusion.tables, f32[5,18,32,128]{3,2,1,0:T(8,128)S(1)} %shard_map.81.main, f32[12,8,128]{2,1,0:T(8,128)S(1)} %collective-permute-done.4.yl, ...), custom_call_target="tpu_custom_call" | custom-call | tf_op jit(solution)/shard_map/pallas_call | solution.py:22
  28.6 1.8 %collective-permute-start.7 = (f32[5,2,8,128]{3,2,1,0:T(8,128)S(1)}, f32[5,2,8,128]{3,2,1,0:T(8,128)S(1)}, u32[]{:S(2)}, u32[]{:S(2)}) collective-permute-start(f32[5,2,8,128]{3,2,1,0:T(8,128)S(1)} %get-tuple-element.33.own), channel_id=1, source_target_pairs={{2,0},{3,1},{0,2},{1,3},{6,4},{7,5},{4,6},{5,7},{10,8},{11,9},{8,1... | collective-permute-start | bytes 122888 | tf_op jit(solution)/shard_map/ppermute | solution.py:600
  30.4 0.9 %collective-permute-start.6 = (f32[5,2,8,128]{3,2,1,0:T(8,128)S(1)}, f32[5,2,8,128]{3,2,1,0:T(8,128)S(1)}, u32[]{:S(2)}, u32[]{:S(2)}) collective-permute-start(f32[5,2,8,128]{3,2,1,0:T(8,128)S(1)} %get-tuple-element.33.own), channel_id=1, source_target_pairs={{1,0},{2,1},{3,2},{0,3},{5,4},{6,5},{7,6},{4,7},{9,8},{10,9},{11,1... | collective-permute-start | bytes 122888 | tf_op jit(solution)/shard_map/ppermute | solution.py:600
  31.3 1.4 %collective-permute-done.8.b3 = f32[5,2,8,128]{3,2,1,0:T(8,128)S(1)} collective-permute-done((f32[5,2,8,128]{3,2,1,0:T(8,128)S(1)}, f32[5,2,8,128]{3,2,1,0:T(8,128)S(1)}, u32[]{:S(2)}, u32[]{:S(2)}) %collective-permute-start.8) | collective-permute-done | bytes 40992 | tf_op jit(solution)/shard_map/ppermute | solution.py:600
  33.1 0.6 collective-permute-done.6.b1
  33.9 1.4 %collective-permute-start.10 = (f32[8,8,128]{2,1,0:T(8,128)S(1)}, f32[8,8,128]{2,1,0:T(8,128)S(1)}, u32[]{:S(2)}, u32[]{:S(2)}) collective-permute-start(f32[8,8,128]{2,1,0:T(8,128)S(1)} %get-tuple-element.36), channel_id=1, source_target_pairs={{12,0},{0,4},{4,8},{8,12},{13,1},{1,5},{5,9},{9,13},{14,2},{2,6},{... | collective-permute-start | bytes 98312 | tf_op jit(solution)/shard_map/ppermute | solution.py:600
  35.4 1.3 %collective-permute-done.9.right = f32[8,8,128]{2,1,0:T(8,128)S(1)} collective-permute-done((f32[8,8,128]{2,1,0:T(8,128)S(1)}, f32[8,8,128]{2,1,0:T(8,128)S(1)}, u32[]{:S(2)}, u32[]{:S(2)}) %collective-permute-start.9) | collective-permute-done | bytes 32800 | tf_op jit(solution)/shard_map/ppermute | solution.py:600
  36.7 1.3 %collective-permute-done.10.left = f32[8,8,128]{2,1,0:T(8,128)S(1)} collective-permute-done((f32[8,8,128]{2,1,0:T(8,128)S(1)}, f32[8,8,128]{2,1,0:T(8,128)S(1)}, u32[]{:S(2)}, u32[]{:S(2)}) %collective-permute-start.10) | collective-permute-done | bytes 32800 | tf_op jit(solution)/shard_map/ppermute | solution.py:600
  38.0 5.3 %collective-permute-start.12 = (f32[56,8,128]{2,1,0:T(8,128)S(1)}, f32[56,8,128]{2,1,0:T(8,128)S(1)}, u32[]{:S(2)}, u32[]{:S(2)}) collective-permute-start(f32[56,8,128]{2,1,0:T(8,128)S(1)} %get-tuple-element.37.full), channel_id=1, source_target_pairs={{240,0},{0,16},{16,32},{32,48},{48,64},{64,80},{80,96},{96,112},{1... | collective-permute-start | bytes 688136 | tf_op jit(solution)/shard_map/ppermute | solution.py:600
  43.3 3.8 %collective-permute-start.11 = (f32[56,8,128]{2,1,0:T(8,128)S(1)}, f32[56,8,128]{2,1,0:T(8,128)S(1)}, u32[]{:S(2)}, u32[]{:S(2)}) collective-permute-start(f32[56,8,128]{2,1,0:T(8,128)S(1)} %get-tuple-element.37.full), channel_id=1, source_target_pairs={{16,0},{32,16},{48,32},{64,48},{80,64},{96,80},{112,96},{128,112},... | collective-permute-start | bytes 688136 | tf_op jit(solution)/shard_map/ppermute | solution.py:600
  47.1 2.6 %collective-permute-start.13 = (f32[28,8,128]{2,1,0:T(8,128)S(1)}, f32[28,8,128]{2,1,0:T(8,128)S(1)}, u32[]{:S(2)}, u32[]{:S(2)}) collective-permute-start(f32[28,8,128]{2,1,0:T(8,128)S(1)} %get-tuple-element.38), channel_id=1, source_target_pairs={{32,0},{48,16},{64,32},{80,48},{96,64},{112,80},{128,96},{144,112}... | collective-permute-start | bytes 344072 | tf_op jit(solution)/shard_map/ppermute | solution.py:600
  49.6 1.0 %shard_map.85.before.v0 = f32[4,32,256]{2,1,0:T(8,128)S(1)} custom-call(s32[3]{0:T(128)S(1)} %pad_add_fusion.pos, f32[16]{0:T(128)S(1)} %pad_maximum_fusion.tables, f32[5,18,32,128]{3,2,1,0:T(8,128)S(1)} %shard_map.81.main, f32[12,8,128]{2,1,0:T(8,128)S(1)} %collective-permute-done.4.yl, f32[12,8,128]{2,1,0:T(8,128)S(1)} %collective-permute-done.5.yh, ...), custom_call_target="tpu_custom_call" | custom-call | tf_op jit(solution)/shard_map/pallas_call | solution.py:22
  50.7 1.4 %collective-permute-done.13.xr2 = f32[28,8,128]{2,1,0:T(8,128)S(1)} collective-permute-done((f32[28,8,128]{2,1,0:T(8,128)S(1)}, f32[28,8,128]{2,1,0:T(8,128)S(1)}, u32[]{:S(2)}, u32[]{:S(2)}) %collective-permute-start.13) | collective-permute-done | bytes 114720 | tf_op jit(solution)/shard_map/ppermute | solution.py:600
  52.1 3.1 %collective-permute-done.14.xl2 = f32[28,8,128]{2,1,0:T(8,128)S(1)} collective-permute-done((f32[28,8,128]{2,1,0:T(8,128)S(1)}, f32[28,8,128]{2,1,0:T(8,128)S(1)}, u32[]{:S(2)}, u32[]{:S(2)}) %collective-permute-start.14) | collective-permute-done | bytes 114720 | tf_op jit(solution)/shard_map/ppermute | solution.py:600
  55.2 3.1 %shard_map.86 = (f32[6,16,32,128]{3,2,1,0:T(8,128)S(1)}, f32[6,8,16,128]{3,2,1,0:T(8,128)S(1)}, f32[320,128]{1,0:T(8,128)S(1)}) custom-call(s32[3]{0:T(128)S(1)} %pad_add_fusion.pos, f32[56,8,128]{2,1,0:T(8,128)S(1)} %get-tuple-element.37.full, f32[56,8,128]{2,1,0:T(8,128)S(1)} %collective-permute-done.11.xr, f32[56,8,128]{2,1,0:T(8,128)S(1)} %collective-permute-done.12.xl, ...), custom_call_target="tpu_custom_call" | custom-call | tf_op jit(solution)/shard_map/pallas_call | solution.py:22
  58.3 16.8 %all_to_all.5 = f32[64,1,640]{2,1,0:T(1,128)S(1)} all-to-all(f32[64,1,640]{2,1,0:T(1,128)S(1)} %bitcast.6), channel_id=1, replica_groups=mesh['gx'=16,'gy'=4,'gz'=4] {'gy','gx'}, dimensions={0} | all-to-all | bytes 327680 | tf_op jit(solution)/shard_map/all_to_all | solution.py:657
  75.1 4.4 %shard_map.87 = (f32[8,16,128]{2,1,0:T(8,128)}, f32[8,16,128]{2,1,0:T(8,128)}) custom-call(s32[3]{0:T(128)S(1)} %pad_add_fusion.pos, f32[320,128]{1,0:T(8,128)S(1)} %bitcast.5, f32[6,18,32,256]{3,2,1,0:T(8,128)S(1)} %get-tuple-element.40.a0, f32[4,32,256]{2,1,0:T(8,128)S(1)} %shard_map.85.before.v0, f32[6,16,32,128]{3,2,1,0:T(8,128)S(1)} %get-tuple-element.42.a1, ...), custom_call_target="tpu_custom_call" | custom-call | tf_op jit(solution)/shard_map/pallas_call | solution.py:22
  (20 shorter events, 1.7 us)
Async XLA Ops:
  2.3 7.1 %collective-permute-start = (f32[18,16,128]{2,1,0:T(8,128)}, f32[18,16,128]{2,1,0:T(8,128)S(1)}, u32[]{:S(2)}, u32[]{:S(2)}) collective-permute-start(f32[18,16,128]{2,1,0:T(8,128)} %get-tuple-element.23), channel_id=1, source_target_pairs={{1,0},{2,1},{3,2},{0,3},{5,4},{6,5},{7,6},{4,7},{9,8},{10,9},{11,1... | collective-permute-start | bytes 442376 | tf_op jit(solution)/shard_map/ppermute | solution.py:600
  5.7 5.8 %collective-permute-start.1 = (f32[18,16,128]{2,1,0:T(8,128)}, f32[18,16,128]{2,1,0:T(8,128)S(1)}, u32[]{:S(2)}, u32[]{:S(2)}) collective-permute-start(f32[18,16,128]{2,1,0:T(8,128)} %get-tuple-element.24), channel_id=1, source_target_pairs={{3,0},{0,1},{1,2},{2,3},{7,4},{4,5},{5,6},{6,7},{11,8},{8,9},{9,10... | collective-permute-start | bytes 442376 | tf_op jit(solution)/shard_map/ppermute | solution.py:600
  5.7 0.8 %copy-start = (s32[8,16,128]{2,1,0:T(8,128)S(1)}, s32[8,16,128]{2,1,0:T(8,128)}, u32[]{:S(2)}) copy-start(s32[8,16,128]{2,1,0:T(8,128)} %f.3) | copy-start | bytes 196612
  6.6 0.8 %copy-start.1 = (s32[8,16,128]{2,1,0:T(8,128)S(1)}, s32[8,16,128]{2,1,0:T(8,128)}, u32[]{:S(2)}) copy-start(s32[8,16,128]{2,1,0:T(8,128)} %b.3) | copy-start | bytes 196612
  7.4 0.8 %copy-start.2 = (f32[8,16,128]{2,1,0:T(8,128)S(1)}, f32[8,16,128]{2,1,0:T(8,128)}, u32[]{:S(2)}) copy-start(f32[8,16,128]{2,1,0:T(8,128)} %s.3) | copy-start | bytes 196612
  8.2 0.8 %copy-start.3 = (f32[8,16,128]{2,1,0:T(8,128)S(1)}, f32[8,16,128]{2,1,0:T(8,128)}, u32[]{:S(2)}) copy-start(f32[8,16,128]{2,1,0:T(8,128)} %d.3) | copy-start | bytes 196612
  11.6 6.4 %collective-permute-start.2 = (f32[39,8,128]{2,1,0:T(8,128)S(1)}, f32[39,8,128]{2,1,0:T(8,128)S(1)}, u32[]{:S(2)}, u32[]{:S(2)}) collective-permute-start(f32[39,8,128]{2,1,0:T(8,128)S(1)} %get-tuple-element.27), channel_id=1, source_target_pairs={{16,0},{32,16},{48,32},{64,48},{80,64},{96,80},{112,96},{128,112},... | collective-permute-start | bytes 479240 | tf_op jit(solution)/shard_map/ppermute | solution.py:600
  13.5 5.0 %collective-permute-start.3 = (f32[39,8,128]{2,1,0:T(8,128)S(1)}, f32[39,8,128]{2,1,0:T(8,128)S(1)}, u32[]{:S(2)}, u32[]{:S(2)}) collective-permute-start(f32[39,8,128]{2,1,0:T(8,128)S(1)} %get-tuple-element.28), channel_id=1, source_target_pairs={{240,0},{0,16},{16,32},{32,48},{48,64},{64,80},{80,96},{96,112},{1... | collective-permute-start | bytes 479240 | tf_op jit(solution)/shard_map/ppermute | solution.py:600
  18.8 4.0 %collective-permute-start.4 = (f32[12,8,128]{2,1,0:T(8,128)S(1)}, f32[12,8,128]{2,1,0:T(8,128)S(1)}, u32[]{:S(2)}, u32[]{:S(2)}) collective-permute-start(f32[12,8,128]{2,1,0:T(8,128)S(1)} %get-tuple-element.31), channel_id=1, source_target_pairs={{4,0},{8,4},{12,8},{0,12},{5,1},{9,5},{13,9},{1,13},{6,2},{10,6},{... | collective-permute-start | bytes 147464 | tf_op jit(solution)/shard_map/ppermute | solution.py:600
  21.7 4.2 %collective-permute-start.5 = (f32[12,8,128]{2,1,0:T(8,128)S(1)}, f32[12,8,128]{2,1,0:T(8,128)S(1)}, u32[]{:S(2)}, u32[]{:S(2)}) collective-permute-start(f32[12,8,128]{2,1,0:T(8,128)S(1)} %get-tuple-element.32), channel_id=1, source_target_pairs={{12,0},{0,4},{4,8},{8,12},{13,1},{1,5},{5,9},{9,13},{14,2},{2,6},{... | collective-permute-start | bytes 147464 | tf_op jit(solution)/shard_map/ppermute | solution.py:600
  28.5 4.2 %collective-permute-start.8 = (f32[5,2,8,128]{3,2,1,0:T(8,128)S(1)}, f32[5,2,8,128]{3,2,1,0:T(8,128)S(1)}, u32[]{:S(2)}, u32[]{:S(2)}) collective-permute-start(f32[5,2,8,128]{3,2,1,0:T(8,128)S(1)} %get-tuple-element.33.own), channel_id=1, source_target_pairs={{3,0},{0,1},{1,2},{2,3},{7,4},{4,5},{5,6},{6,7},{11,8},{8,9},{9,10... | collective-permute-start | bytes 122888 | tf_op jit(solution)/shard_map/ppermute | solution.py:600
  28.6 4.5 %collective-permute-start.7 = (f32[5,2,8,128]{3,2,1,0:T(8,128)S(1)}, f32[5,2,8,128]{3,2,1,0:T(8,128)S(1)}, u32[]{:S(2)}, u32[]{:S(2)}) collective-permute-start(f32[5,2,8,128]{3,2,1,0:T(8,128)S(1)} %get-tuple-element.33.own), channel_id=1, source_target_pairs={{2,0},{3,1},{0,2},{1,3},{6,4},{7,5},{4,6},{5,7},{10,8},{11,9},{8,1... | collective-permute-start | bytes 122888 | tf_op jit(solution)/shard_map/ppermute | solution.py:600
  30.4 3.3 %collective-permute-start.6 = (f32[5,2,8,128]{3,2,1,0:T(8,128)S(1)}, f32[5,2,8,128]{3,2,1,0:T(8,128)S(1)}, u32[]{:S(2)}, u32[]{:S(2)}) collective-permute-start(f32[5,2,8,128]{3,2,1,0:T(8,128)S(1)} %get-tuple-element.33.own), channel_id=1, source_target_pairs={{1,0},{2,1},{3,2},{0,3},{5,4},{6,5},{7,6},{4,7},{9,8},{10,9},{11,1... | collective-permute-start | bytes 122888 | tf_op jit(solution)/shard_map/ppermute | solution.py:600
  33.8 2.8 %collective-permute-start.9 = (f32[8,8,128]{2,1,0:T(8,128)S(1)}, f32[8,8,128]{2,1,0:T(8,128)S(1)}, u32[]{:S(2)}, u32[]{:S(2)}) collective-permute-start(f32[8,8,128]{2,1,0:T(8,128)S(1)} %get-tuple-element.35), channel_id=1, source_target_pairs={{4,0},{8,4},{12,8},{0,12},{5,1},{9,5},{13,9},{1,13},{6,2},{10,6},{... | collective-permute-start | bytes 98312 | tf_op jit(solution)/shard_map/ppermute | solution.py:600
  33.9 4.0 %collective-permute-start.10 = (f32[8,8,128]{2,1,0:T(8,128)S(1)}, f32[8,8,128]{2,1,0:T(8,128)S(1)}, u32[]{:S(2)}, u32[]{:S(2)}) collective-permute-start(f32[8,8,128]{2,1,0:T(8,128)S(1)} %get-tuple-element.36), channel_id=1, source_target_pairs={{12,0},{0,4},{4,8},{8,12},{13,1},{1,5},{5,9},{9,13},{14,2},{2,6},{... | collective-permute-start | bytes 98312 | tf_op jit(solution)/shard_map/ppermute | solution.py:600
  38.0 17.2 %collective-permute-start.12 = (f32[56,8,128]{2,1,0:T(8,128)S(1)}, f32[56,8,128]{2,1,0:T(8,128)S(1)}, u32[]{:S(2)}, u32[]{:S(2)}) collective-permute-start(f32[56,8,128]{2,1,0:T(8,128)S(1)} %get-tuple-element.37.full), channel_id=1, source_target_pairs={{240,0},{0,16},{16,32},{32,48},{48,64},{64,80},{80,96},{96,112},{1... | collective-permute-start | bytes 688136 | tf_op jit(solution)/shard_map/ppermute | solution.py:600
  43.3 11.9 %collective-permute-start.11 = (f32[56,8,128]{2,1,0:T(8,128)S(1)}, f32[56,8,128]{2,1,0:T(8,128)S(1)}, u32[]{:S(2)}, u32[]{:S(2)}) collective-permute-start(f32[56,8,128]{2,1,0:T(8,128)S(1)} %get-tuple-element.37.full), channel_id=1, source_target_pairs={{16,0},{32,16},{48,32},{64,48},{80,64},{96,80},{112,96},{128,112},... | collective-permute-start | bytes 688136 | tf_op jit(solution)/shard_map/ppermute | solution.py:600
  47.1 5.1 %collective-permute-start.13 = (f32[28,8,128]{2,1,0:T(8,128)S(1)}, f32[28,8,128]{2,1,0:T(8,128)S(1)}, u32[]{:S(2)}, u32[]{:S(2)}) collective-permute-start(f32[28,8,128]{2,1,0:T(8,128)S(1)} %get-tuple-element.38), channel_id=1, source_target_pairs={{32,0},{48,16},{64,32},{80,48},{96,64},{112,80},{128,96},{144,112}... | collective-permute-start | bytes 344072 | tf_op jit(solution)/shard_map/ppermute | solution.py:600
  49.6 5.6 %collective-permute-start.14 = (f32[28,8,128]{2,1,0:T(8,128)S(1)}, f32[28,8,128]{2,1,0:T(8,128)S(1)}, u32[]{:S(2)}, u32[]{:S(2)}) collective-permute-start(f32[28,8,128]{2,1,0:T(8,128)S(1)} %get-tuple-element.39), channel_id=1, source_target_pairs={{224,0},{240,16},{0,32},{16,48},{32,64},{48,80},{64,96},{80,112},{... | collective-permute-start | bytes 344072 | tf_op jit(solution)/shard_map/ppermute | solution.py:600

commit v8 on v7

--- a/solution.py
+++ b/solution.py
@@ -18,10 +18,10 @@
 HBM = pl.BlockSpec(memory_space=pltpu.HBM)
 
 
-def call(kernel, outs, *args, scratch=(), spaces=None, limit=24):
+def call(kernel, outs, *args, scratch=(), spaces=None, limit=24, pin=False):
     return pl.pallas_call(
         kernel,
-        out_shape=[jax.ShapeDtypeStruct(s, F32) for s in outs],
+        out_shape=[(pltpu.VMEM if pin else jax.ShapeDtypeStruct)(s, F32) for s in outs],
         in_specs=spaces or [VMEM] * len(args),
         out_specs=[VMEM] * len(outs),
         scratch_shapes=[pltpu.VMEM(s, F32) if isinstance(s, tuple) else s for s in scratch],
@@ -142,28 +142,19 @@
     return t[...]
 
 
-def fetch(f, b, s, d, fi, bi, sf, df, sems):
+def pack_z(f, b, s, d, lo, hi, own, fi, bi, sems):
     copies = [
         pltpu.make_async_copy(src, dst, sems.at[k])
-        for k, (src, dst) in enumerate(((f, fi), (b, bi), (s, sf), (d, df)))
+        for k, (src, dst) in enumerate(((f, fi), (b, bi), (s, own.at[2]), (d, own.at[3])))
     ]
     for copy in copies:
         copy.start()
-    for copy in copies:
-        copy.wait()
-    return [fi[...].astype(F32), bi[...].astype(F32), sf[...], df[...]]
-
-
-def pack_z(f, b, s, d, lo, hi, *scratch):
-    f, b, s, d = fetch(f, b, s, d, *scratch)
-    for value, at, n in ((f, 0, H), (d, H, H), (b, 2 * H, H - 1), (s, 3 * H - 1, H - 1)):
-        lo[at : at + n] = value[0:n]
-        hi[at : at + n] = value[8 - n : 8]
-
-
-def fetch_own(f, b, s, d, own, *scratch):
-    for k, value in enumerate(fetch(f, b, s, d, *scratch)):
-        own[k] = value
+    for k, (at, n) in enumerate(((0, H), (2 * H, H - 1), (3 * H - 1, H - 1), (H, H))):
+        copies[k].wait()
+        if k < 2:
+            own[k] = (fi, bi)[k][...].astype(F32)
+        lo[at : at + n] = own[k, 0:n]
+        hi[at : at + n] = own[k, 8 - n : 8]
 
 
 FACIES, BOUNDARY, SOURCE, DENSITY = range(4)
@@ -479,6 +470,18 @@
             sent[40 * i + 8 * tile : 40 * i + 8 * tile + 8] = value
 
 
+def cut(v):
+    return jnp.concatenate([v[0:16], v[24:32]], axis=0)
+
+
+class Cut:
+    def __init__(self, ref):
+        self.ref = ref
+
+    def __getitem__(self, at):
+        return cut(self.ref[at])
+
+
 def sweep(a, src, dst, n, layers=None):
     for z in layers or range(n):
         dst[z % n] = smoothed(a, lambda k: src[k], z % n, (z - 1) % n, (z + 1) % n)
@@ -560,15 +563,15 @@
     sweep(a2, e2, f2, 8)
     sweep(a2, f2, e2, 8, range(-2, 4))
     for z in range(-2, 4):
-        e = spread_rows(g1.at[z % 8], spread_lanes(e2[z % 8]))
+        e = cut(spread_rows(g1.at[z % 8], spread_lanes(e2[z % 8])))
         for zf in (2 * z % 16, 2 * z % 16 + 1):
-            e1[0, zf] = a1[V, zf] + e
-    sweep(a1, e1.at[0], e1.at[1], 16, range(-3, 7))
-    sweep(a1, e1.at[1], e1.at[0], 16, range(-2, 6))
+            e1[0, zf] = cut(a1[V, zf]) + e
+    sweep(Cut(a1), e1.at[0], e1.at[1], 16, range(-3, 7))
+    sweep(Cut(a1), e1.at[1], e1.at[0], 16, range(-2, 6))
     upper = iota((8, 128), 0) < 4
     for zc in range(-2, 6):
         v = e1[0, zc % 16]
-        v = jnp.concatenate([v[0:8], jnp.where(upper, v[8:16], v[24:32])], axis=0)
+        v = jnp.concatenate([v[0:8], jnp.where(upper, v[8:16], v[16:24])], axis=0)
         for half in range(2):
             e = spread_rows(g0.at[half, zc + 2], spread_lanes(v, 64 * half))
             lanes = slice(128 * half, 128 * half + 128)
@@ -603,15 +606,19 @@
 def local(facies, boundary, hc, vc, source, density):
     pos = jnp.stack([lax.axis_index(n) for n in ("gx", "gy", "gz")]).astype(jnp.int32)
     tables = jnp.concatenate([hc, vc])
-    raw = (facies, boundary, source, density)
-    landing = [
-        pltpu.VMEM((8, 16, 128), jnp.int32), pltpu.VMEM((8, 16, 128), jnp.int32),
-        (8, 16, 128), (8, 16, 128), pltpu.SemaphoreType.DMA((4,)),
-    ]
-    plan = dict(spaces=[HBM] * 4, scratch=landing, limit=60)
-    lo, hi = call(pack_z, [(4 * H - 2, 16, 128)] * 2, *raw, **plan)
+    lo, hi, own = call(
+        pack_z,
+        [(4 * H - 2, 16, 128)] * 2 + [(4, 8, 16, 128)],
+        facies, boundary, source, density,
+        spaces=[HBM] * 4,
+        scratch=[
+            pltpu.VMEM((8, 16, 128), jnp.int32), pltpu.VMEM((8, 16, 128), jnp.int32),
+            pltpu.SemaphoreType.DMA((4,)),
+        ],
+        limit=60,
+        pin=True,
+    )
     above, below = shift(lo, "gz", 1), shift(hi, "gz", -1)
-    (own,) = call(fetch_own, [(4, 8, 16, 128)], *raw, **{**plan, "limit": 24})
     xl, xh, lo, hi = call(
         pack_x, [(4, Z0, 8, 128)] * 2 + [(XTILES, 8, 128)] * 2, own, above, below
     )
@@ -666,7 +673,7 @@
                 (4, 32, 128), (2, 16, 128),
                 (4, 32, 128), (2, 16, 128), (4, 32, 128), (2, 16, 128),
                 (5, 2, 32, 128), (5, 8, 128),
-                (2, 16, 32, 128), (8, 16, 128), (4, 32, 128), (2, 16, 128), (8, 16, 128),
+                (2, 16, 24, 128), (8, 16, 128), (4, 32, 128), (2, 16, 128), (8, 16, 128),
                 (16, 128), (2, 32, 128), (4, 16, 128), (8, 32, 128), (2, 8, 32, 128),
                 (4, 48, 128), (2, Z0, 32, 256),
             ],

time: 79.9 us -> 78.8 us (0.986)
  waiting for transfers between devices: 17.3 us -> 20.8 us
  local copies, waits for them, and re-layouts: 3.36 us -> 0 us
  Pallas kernels: 15 us -> 13.9 us
    ppermute x15, waiting for transfers between devices: 17.3 us -> 20.8 us  [shift(): lax.ppermute(value, axis, [((i + by) % count, i) for i in range(count)])]
    unnamed x8 -> x0, local copies, waits for them, and re-layouts: 3.36 us -> none
    pallas_call x11 -> x10, Pallas kernels: 15 us -> 13.9 us  [call(): pl.pallas_call(kernel, out_shape=[(pltpu.VMEM if pin else jax.ShapeDtypeS...]
  transfers between devices with their start and end apart: 15 -> 15, of which waited for: 11 -> 12; matrix products, arithmetic and copies ran while one was open for 1% -> 1% of each run, Pallas kernels for 3% -> 3%
where the time goes in v8:
time: 78.8 us; the launch traced here: 78.6 us
  starting transfers between devices  25.6 us (32%)
  waiting for transfers between devices  20.8 us (26%)
  blocking collectives  16.8 us (21%)
  Pallas kernels  13.9 us (18%)
  other arithmetic  0.82 us (1%)
    ppermute x15, starting transfers between devices, shift(): lax.ppermute(value, axis, [((i + by) % count, i) for i in range(count)])  25.6 us
    ppermute x15, waiting for transfers between devices, shift(): lax.ppermute(value, axis, [((i + by) % count, i) for i in range(count)])  20.8 us
    all_to_all x1, blocking collectives, local(): lax.all_to_all(sent.reshape(64, 1, 640), ('gy', 'gx'), 0, 0)  16.8 us
    pallas_call x10, Pallas kernels, call(): pl.pallas_call(kernel, out_shape=[(pltpu.VMEM if pin else jax.ShapeDtypeS...  13.9 us
  transfers between devices with their start and end apart: 15, of which 12 were waited for; matrix products, arithmetic and copies ran while one was open for 1% of the time, Pallas kernels for 3%

profile of v8, /device:TPU:1, one launch (start us, length us, event | category | flops | bytes accessed | tf_op | source)
XLA Modules:
  0.0 78.6 jit_solution(7163664135363766835)
XLA Ops:
  0.6 1.0 %shard_map.77 = (f32[18,16,128]{2,1,0:T(8,128)S(1)}, f32[18,16,128]{2,1,0:T(8,128)S(1)}, f32[4,8,16,128]{3,2,1,0:T(8,128)S(1)}) custom-call(s32[8,16,128]{2,1,0:T(8,128)} %f.1, s32[8,16,128]{2,1,0:T(8,128)} %b.1, f32[8,16,128]{2,1,0:T(8,128)} %s.1, f32[8,16,128]{2,1,0:T(8,128)} %d.1), custom_call_target="tpu_custom_call" | custom-call | tf_op jit(solution)/shard_map/pallas_call | solution.py:22
  1.6 3.4 %collective-permute-start = (f32[18,16,128]{2,1,0:T(8,128)S(1)}, f32[18,16,128]{2,1,0:T(8,128)S(1)}, u32[]{:S(2)}, u32[]{:S(2)}) collective-permute-start(f32[18,16,128]{2,1,0:T(8,128)S(1)} %get-tuple-element.25), channel_id=1, source_target_pairs={{1,0},{2,1},{3,2},{0,3},{5,4},{6,5},{7,6},{4,7},{9,8},{10,9},{11,1... | collective-permute-start | bytes 442376 | tf_op jit(solution)/shard_map/ppermute | solution.py:603
  5.0 2.5 %collective-permute-done.above = f32[18,16,128]{2,1,0:T(8,128)S(1)} collective-permute-done((f32[18,16,128]{2,1,0:T(8,128)S(1)}, f32[18,16,128]{2,1,0:T(8,128)S(1)}, u32[]{:S(2)}, u32[]{:S(2)}) %collective-permute-start) | collective-permute-done | bytes 147488 | tf_op jit(solution)/shard_map/ppermute | solution.py:603
  7.5 3.1 %collective-permute-done.1.below = f32[18,16,128]{2,1,0:T(8,128)S(1)} collective-permute-done((f32[18,16,128]{2,1,0:T(8,128)S(1)}, f32[18,16,128]{2,1,0:T(8,128)S(1)}, u32[]{:S(2)}, u32[]{:S(2)}) %collective-permute-start.1) | collective-permute-done | bytes 147488 | tf_op jit(solution)/shard_map/ppermute | solution.py:603
  10.7 1.9 %collective-permute-start.2 = (f32[39,8,128]{2,1,0:T(8,128)S(1)}, f32[39,8,128]{2,1,0:T(8,128)S(1)}, u32[]{:S(2)}, u32[]{:S(2)}) collective-permute-start(f32[39,8,128]{2,1,0:T(8,128)S(1)} %get-tuple-element.29), channel_id=1, source_target_pairs={{16,0},{32,16},{48,32},{64,48},{80,64},{96,80},{112,96},{128,112},... | collective-permute-start | bytes 479240 | tf_op jit(solution)/shard_map/ppermute | solution.py:603
  12.6 1.5 %collective-permute-start.3 = (f32[39,8,128]{2,1,0:T(8,128)S(1)}, f32[39,8,128]{2,1,0:T(8,128)S(1)}, u32[]{:S(2)}, u32[]{:S(2)}) collective-permute-start(f32[39,8,128]{2,1,0:T(8,128)S(1)} %get-tuple-element.30), channel_id=1, source_target_pairs={{240,0},{0,16},{16,32},{32,48},{48,64},{64,80},{80,96},{96,112},{1... | collective-permute-start | bytes 479240 | tf_op jit(solution)/shard_map/ppermute | solution.py:603
  14.1 0.7 pad_maximum_fusion.tables
  14.9 2.2 %collective-permute-done.2.ml = f32[39,8,128]{2,1,0:T(8,128)S(1)} collective-permute-done((f32[39,8,128]{2,1,0:T(8,128)S(1)}, f32[39,8,128]{2,1,0:T(8,128)S(1)}, u32[]{:S(2)}, u32[]{:S(2)}) %collective-permute-start.2) | collective-permute-done | bytes 159776 | tf_op jit(solution)/shard_map/ppermute | solution.py:603
  17.0 0.5 collective-permute-done.3.mh
  17.5 0.4 shard_map.79
  17.9 2.8 %collective-permute-start.4 = (f32[12,8,128]{2,1,0:T(8,128)S(1)}, f32[12,8,128]{2,1,0:T(8,128)S(1)}, u32[]{:S(2)}, u32[]{:S(2)}) collective-permute-start(f32[12,8,128]{2,1,0:T(8,128)S(1)} %get-tuple-element.33), channel_id=1, source_target_pairs={{4,0},{8,4},{12,8},{0,12},{5,1},{9,5},{13,9},{1,13},{6,2},{10,6},{... | collective-permute-start | bytes 147464 | tf_op jit(solution)/shard_map/ppermute | solution.py:603
  20.8 1.1 %shard_map.80.main = f32[5,18,32,128]{3,2,1,0:T(8,128)S(1)} custom-call(s32[3]{0:T(128)S(1)} %pad_add_fusion.pos, f32[16]{0:T(128)S(1)} %pad_maximum_fusion.tables, f32[4,18,8,128]{3,2,1,0:T(8,128)S(1)} %get-tuple-element.27.xl, f32[4,18,8,128]{3,2,1,0:T(8,128)S(1)} %get-tuple-element.28.xh, f32[4,18,8,128]{3,2,1,0:T(8,128)S(1)} %get-tuple-element.31.rl, ...), custom_call_target="tpu_custom_call" | custom-call | tf_op jit(solution)/shard_map/pallas_call | solution.py:22
  21.9 3.0 %collective-permute-done.5.yh = f32[12,8,128]{2,1,0:T(8,128)S(1)} collective-permute-done((f32[12,8,128]{2,1,0:T(8,128)S(1)}, f32[12,8,128]{2,1,0:T(8,128)S(1)}, u32[]{:S(2)}, u32[]{:S(2)}) %collective-permute-start.5) | collective-permute-done | bytes 49184 | tf_op jit(solution)/shard_map/ppermute | solution.py:603
  24.9 2.7 %shard_map.81 = (f32[6,18,32,256]{3,2,1,0:T(8,128)S(1)}, f32[5,2,8,128]{3,2,1,0:T(8,128)S(1)}) custom-call(s32[3]{0:T(128)S(1)} %pad_add_fusion.pos, f32[16]{0:T(128)S(1)} %pad_maximum_fusion.tables, f32[5,18,32,128]{3,2,1,0:T(8,128)S(1)} %shard_map.80.main, f32[12,8,128]{2,1,0:T(8,128)S(1)} %collective-permute-done.4.yl, ...), custom_call_target="tpu_custom_call" | custom-call | tf_op jit(solution)/shard_map/pallas_call | solution.py:22
  27.7 1.5 %collective-permute-start.7 = (f32[5,2,8,128]{3,2,1,0:T(8,128)S(1)}, f32[5,2,8,128]{3,2,1,0:T(8,128)S(1)}, u32[]{:S(2)}, u32[]{:S(2)}) collective-permute-start(f32[5,2,8,128]{3,2,1,0:T(8,128)S(1)} %get-tuple-element.35.own), channel_id=1, source_target_pairs={{2,0},{3,1},{0,2},{1,3},{6,4},{7,5},{4,6},{5,7},{10,8},{11,9},{8,1... | collective-permute-start | bytes 122888 | tf_op jit(solution)/shard_map/ppermute | solution.py:603
  29.2 1.2 %collective-permute-start.6 = (f32[5,2,8,128]{3,2,1,0:T(8,128)S(1)}, f32[5,2,8,128]{3,2,1,0:T(8,128)S(1)}, u32[]{:S(2)}, u32[]{:S(2)}) collective-permute-start(f32[5,2,8,128]{3,2,1,0:T(8,128)S(1)} %get-tuple-element.35.own), channel_id=1, source_target_pairs={{1,0},{2,1},{3,2},{0,3},{5,4},{6,5},{7,6},{4,7},{9,8},{10,9},{11,1... | collective-permute-start | bytes 122888 | tf_op jit(solution)/shard_map/ppermute | solution.py:603
  30.4 1.4 %collective-permute-done.8.b3 = f32[5,2,8,128]{3,2,1,0:T(8,128)S(1)} collective-permute-done((f32[5,2,8,128]{3,2,1,0:T(8,128)S(1)}, f32[5,2,8,128]{3,2,1,0:T(8,128)S(1)}, u32[]{:S(2)}, u32[]{:S(2)}) %collective-permute-start.8) | collective-permute-done | bytes 40992 | tf_op jit(solution)/shard_map/ppermute | solution.py:603
  31.8 0.4 collective-permute-done.7.b2
  32.2 0.6 collective-permute-done.6.b1
  32.9 0.1 collective-permute-start.9
  33.0 1.4 %collective-permute-start.10 = (f32[8,8,128]{2,1,0:T(8,128)S(1)}, f32[8,8,128]{2,1,0:T(8,128)S(1)}, u32[]{:S(2)}, u32[]{:S(2)}) collective-permute-start(f32[8,8,128]{2,1,0:T(8,128)S(1)} %get-tuple-element.38), channel_id=1, source_target_pairs={{12,0},{0,4},{4,8},{8,12},{13,1},{1,5},{5,9},{9,13},{14,2},{2,6},{... | collective-permute-start | bytes 98312 | tf_op jit(solution)/shard_map/ppermute | solution.py:603
  34.4 1.3 %collective-permute-done.9.right = f32[8,8,128]{2,1,0:T(8,128)S(1)} collective-permute-done((f32[8,8,128]{2,1,0:T(8,128)S(1)}, f32[8,8,128]{2,1,0:T(8,128)S(1)}, u32[]{:S(2)}, u32[]{:S(2)}) %collective-permute-start.9) | collective-permute-done | bytes 32800 | tf_op jit(solution)/shard_map/ppermute | solution.py:603
  35.7 1.3 %collective-permute-done.10.left = f32[8,8,128]{2,1,0:T(8,128)S(1)} collective-permute-done((f32[8,8,128]{2,1,0:T(8,128)S(1)}, f32[8,8,128]{2,1,0:T(8,128)S(1)}, u32[]{:S(2)}, u32[]{:S(2)}) %collective-permute-start.10) | collective-permute-done | bytes 32800 | tf_op jit(solution)/shard_map/ppermute | solution.py:603
  37.1 5.3 %collective-permute-start.12 = (f32[56,8,128]{2,1,0:T(8,128)S(1)}, f32[56,8,128]{2,1,0:T(8,128)S(1)}, u32[]{:S(2)}, u32[]{:S(2)}) collective-permute-start(f32[56,8,128]{2,1,0:T(8,128)S(1)} %get-tuple-element.39.full), channel_id=1, source_target_pairs={{240,0},{0,16},{16,32},{32,48},{48,64},{64,80},{80,96},{96,112},{1... | collective-permute-start | bytes 688136 | tf_op jit(solution)/shard_map/ppermute | solution.py:603
  42.3 3.8 %collective-permute-start.11 = (f32[56,8,128]{2,1,0:T(8,128)S(1)}, f32[56,8,128]{2,1,0:T(8,128)S(1)}, u32[]{:S(2)}, u32[]{:S(2)}) collective-permute-start(f32[56,8,128]{2,1,0:T(8,128)S(1)} %get-tuple-element.39.full), channel_id=1, source_target_pairs={{16,0},{32,16},{48,32},{64,48},{80,64},{96,80},{112,96},{128,112},... | collective-permute-start | bytes 688136 | tf_op jit(solution)/shard_map/ppermute | solution.py:603
  46.1 2.6 %collective-permute-start.13 = (f32[28,8,128]{2,1,0:T(8,128)S(1)}, f32[28,8,128]{2,1,0:T(8,128)S(1)}, u32[]{:S(2)}, u32[]{:S(2)}) collective-permute-start(f32[28,8,128]{2,1,0:T(8,128)S(1)} %get-tuple-element.40), channel_id=1, source_target_pairs={{32,0},{48,16},{64,32},{80,48},{96,64},{112,80},{128,96},{144,112}... | collective-permute-start | bytes 344072 | tf_op jit(solution)/shard_map/ppermute | solution.py:603
  48.7 1.0 %shard_map.84.before.v0 = f32[4,32,256]{2,1,0:T(8,128)S(1)} custom-call(s32[3]{0:T(128)S(1)} %pad_add_fusion.pos, f32[16]{0:T(128)S(1)} %pad_maximum_fusion.tables, f32[5,18,32,128]{3,2,1,0:T(8,128)S(1)} %shard_map.80.main, f32[12,8,128]{2,1,0:T(8,128)S(1)} %collective-permute-done.4.yl, f32[12,8,128]{2,1,0:T(8,128)S(1)} %collective-permute-done.5.yh, ...), custom_call_target="tpu_custom_call" | custom-call | tf_op jit(solution)/shard_map/pallas_call | solution.py:22
  49.8 1.4 %collective-permute-done.13.xr2 = f32[28,8,128]{2,1,0:T(8,128)S(1)} collective-permute-done((f32[28,8,128]{2,1,0:T(8,128)S(1)}, f32[28,8,128]{2,1,0:T(8,128)S(1)}, u32[]{:S(2)}, u32[]{:S(2)}) %collective-permute-start.13) | collective-permute-done | bytes 114720 | tf_op jit(solution)/shard_map/ppermute | solution.py:603
  51.2 3.1 %collective-permute-done.14.xl2 = f32[28,8,128]{2,1,0:T(8,128)S(1)} collective-permute-done((f32[28,8,128]{2,1,0:T(8,128)S(1)}, f32[28,8,128]{2,1,0:T(8,128)S(1)}, u32[]{:S(2)}, u32[]{:S(2)}) %collective-permute-start.14) | collective-permute-done | bytes 114720 | tf_op jit(solution)/shard_map/ppermute | solution.py:603
  54.3 3.1 %shard_map.85 = (f32[6,16,32,128]{3,2,1,0:T(8,128)S(1)}, f32[6,8,16,128]{3,2,1,0:T(8,128)S(1)}, f32[320,128]{1,0:T(8,128)S(1)}) custom-call(s32[3]{0:T(128)S(1)} %pad_add_fusion.pos, f32[56,8,128]{2,1,0:T(8,128)S(1)} %get-tuple-element.39.full, f32[56,8,128]{2,1,0:T(8,128)S(1)} %collective-permute-done.11.xr, f32[56,8,128]{2,1,0:T(8,128)S(1)} %collective-permute-done.12.xl, ...), custom_call_target="tpu_custom_call" | custom-call | tf_op jit(solution)/shard_map/pallas_call | solution.py:22
  57.4 16.8 %all_to_all.5 = f32[64,1,640]{2,1,0:T(1,128)S(1)} all-to-all(f32[64,1,640]{2,1,0:T(1,128)S(1)} %bitcast.6), channel_id=1, replica_groups=mesh['gx'=16,'gy'=4,'gz'=4] {'gy','gx'}, dimensions={0} | all-to-all | bytes 327680 | tf_op jit(solution)/shard_map/all_to_all | solution.py:664
  74.2 4.4 %shard_map.86 = (f32[8,16,128]{2,1,0:T(8,128)}, f32[8,16,128]{2,1,0:T(8,128)}) custom-call(s32[3]{0:T(128)S(1)} %pad_add_fusion.pos, f32[320,128]{1,0:T(8,128)S(1)} %bitcast.5, f32[6,18,32,256]{3,2,1,0:T(8,128)S(1)} %get-tuple-element.42.a0, f32[4,32,256]{2,1,0:T(8,128)S(1)} %shard_map.84.before.v0, f32[6,16,32,128]{3,2,1,0:T(8,128)S(1)} %get-tuple-element.44.a1, ...), custom_call_target="tpu_custom_call" | custom-call | tf_op jit(solution)/shard_map/pallas_call | solution.py:22
  (11 shorter events, 0.4 us)
Async XLA Ops:
  1.6 5.9 %collective-permute-start = (f32[18,16,128]{2,1,0:T(8,128)S(1)}, f32[18,16,128]{2,1,0:T(8,128)S(1)}, u32[]{:S(2)}, u32[]{:S(2)}) collective-permute-start(f32[18,16,128]{2,1,0:T(8,128)S(1)} %get-tuple-element.25), channel_id=1, source_target_pairs={{1,0},{2,1},{3,2},{0,3},{5,4},{6,5},{7,6},{4,7},{9,8},{10,9},{11,1... | collective-permute-start | bytes 442376 | tf_op jit(solution)/shard_map/ppermute | solution.py:603
  5.0 5.6 %collective-permute-start.1 = (f32[18,16,128]{2,1,0:T(8,128)S(1)}, f32[18,16,128]{2,1,0:T(8,128)S(1)}, u32[]{:S(2)}, u32[]{:S(2)}) collective-permute-start(f32[18,16,128]{2,1,0:T(8,128)S(1)} %get-tuple-element.26), channel_id=1, source_target_pairs={{3,0},{0,1},{1,2},{2,3},{7,4},{4,5},{5,6},{6,7},{11,8},{8,9},{9,10... | collective-permute-start | bytes 442376 | tf_op jit(solution)/shard_map/ppermute | solution.py:603
  10.7 6.4 %collective-permute-start.2 = (f32[39,8,128]{2,1,0:T(8,128)S(1)}, f32[39,8,128]{2,1,0:T(8,128)S(1)}, u32[]{:S(2)}, u32[]{:S(2)}) collective-permute-start(f32[39,8,128]{2,1,0:T(8,128)S(1)} %get-tuple-element.29), channel_id=1, source_target_pairs={{16,0},{32,16},{48,32},{64,48},{80,64},{96,80},{112,96},{128,112},... | collective-permute-start | bytes 479240 | tf_op jit(solution)/shard_map/ppermute | solution.py:603
  12.6 5.0 %collective-permute-start.3 = (f32[39,8,128]{2,1,0:T(8,128)S(1)}, f32[39,8,128]{2,1,0:T(8,128)S(1)}, u32[]{:S(2)}, u32[]{:S(2)}) collective-permute-start(f32[39,8,128]{2,1,0:T(8,128)S(1)} %get-tuple-element.30), channel_id=1, source_target_pairs={{240,0},{0,16},{16,32},{32,48},{48,64},{64,80},{80,96},{96,112},{1... | collective-permute-start | bytes 479240 | tf_op jit(solution)/shard_map/ppermute | solution.py:603
  17.9 4.0 %collective-permute-start.4 = (f32[12,8,128]{2,1,0:T(8,128)S(1)}, f32[12,8,128]{2,1,0:T(8,128)S(1)}, u32[]{:S(2)}, u32[]{:S(2)}) collective-permute-start(f32[12,8,128]{2,1,0:T(8,128)S(1)} %get-tuple-element.33), channel_id=1, source_target_pairs={{4,0},{8,4},{12,8},{0,12},{5,1},{9,5},{13,9},{1,13},{6,2},{10,6},{... | collective-permute-start | bytes 147464 | tf_op jit(solution)/shard_map/ppermute | solution.py:603
  20.7 4.2 %collective-permute-start.5 = (f32[12,8,128]{2,1,0:T(8,128)S(1)}, f32[12,8,128]{2,1,0:T(8,128)S(1)}, u32[]{:S(2)}, u32[]{:S(2)}) collective-permute-start(f32[12,8,128]{2,1,0:T(8,128)S(1)} %get-tuple-element.34), channel_id=1, source_target_pairs={{12,0},{0,4},{4,8},{8,12},{13,1},{1,5},{5,9},{9,13},{14,2},{2,6},{... | collective-permute-start | bytes 147464 | tf_op jit(solution)/shard_map/ppermute | solution.py:603
  27.6 4.2 %collective-permute-start.8 = (f32[5,2,8,128]{3,2,1,0:T(8,128)S(1)}, f32[5,2,8,128]{3,2,1,0:T(8,128)S(1)}, u32[]{:S(2)}, u32[]{:S(2)}) collective-permute-start(f32[5,2,8,128]{3,2,1,0:T(8,128)S(1)} %get-tuple-element.35.own), channel_id=1, source_target_pairs={{3,0},{0,1},{1,2},{2,3},{7,4},{4,5},{5,6},{6,7},{11,8},{8,9},{9,10... | collective-permute-start | bytes 122888 | tf_op jit(solution)/shard_map/ppermute | solution.py:603
  27.7 4.5 %collective-permute-start.7 = (f32[5,2,8,128]{3,2,1,0:T(8,128)S(1)}, f32[5,2,8,128]{3,2,1,0:T(8,128)S(1)}, u32[]{:S(2)}, u32[]{:S(2)}) collective-permute-start(f32[5,2,8,128]{3,2,1,0:T(8,128)S(1)} %get-tuple-element.35.own), channel_id=1, source_target_pairs={{2,0},{3,1},{0,2},{1,3},{6,4},{7,5},{4,6},{5,7},{10,8},{11,9},{8,1... | collective-permute-start | bytes 122888 | tf_op jit(solution)/shard_map/ppermute | solution.py:603
  29.2 3.6 %collective-permute-start.6 = (f32[5,2,8,128]{3,2,1,0:T(8,128)S(1)}, f32[5,2,8,128]{3,2,1,0:T(8,128)S(1)}, u32[]{:S(2)}, u32[]{:S(2)}) collective-permute-start(f32[5,2,8,128]{3,2,1,0:T(8,128)S(1)} %get-tuple-element.35.own), channel_id=1, source_target_pairs={{1,0},{2,1},{3,2},{0,3},{5,4},{6,5},{7,6},{4,7},{9,8},{10,9},{11,1... | collective-permute-start | bytes 122888 | tf_op jit(solution)/shard_map/ppermute | solution.py:603
  32.9 2.8 %collective-permute-start.9 = (f32[8,8,128]{2,1,0:T(8,128)S(1)}, f32[8,8,128]{2,1,0:T(8,128)S(1)}, u32[]{:S(2)}, u32[]{:S(2)}) collective-permute-start(f32[8,8,128]{2,1,0:T(8,128)S(1)} %get-tuple-element.37), channel_id=1, source_target_pairs={{4,0},{8,4},{12,8},{0,12},{5,1},{9,5},{13,9},{1,13},{6,2},{10,6},{... | collective-permute-start | bytes 98312 | tf_op jit(solution)/shard_map/ppermute | solution.py:603
  33.0 4.0 %collective-permute-start.10 = (f32[8,8,128]{2,1,0:T(8,128)S(1)}, f32[8,8,128]{2,1,0:T(8,128)S(1)}, u32[]{:S(2)}, u32[]{:S(2)}) collective-permute-start(f32[8,8,128]{2,1,0:T(8,128)S(1)} %get-tuple-element.38), channel_id=1, source_target_pairs={{12,0},{0,4},{4,8},{8,12},{13,1},{1,5},{5,9},{9,13},{14,2},{2,6},{... | collective-permute-start | bytes 98312 | tf_op jit(solution)/shard_map/ppermute | solution.py:603
  37.1 17.2 %collective-permute-start.12 = (f32[56,8,128]{2,1,0:T(8,128)S(1)}, f32[56,8,128]{2,1,0:T(8,128)S(1)}, u32[]{:S(2)}, u32[]{:S(2)}) collective-permute-start(f32[56,8,128]{2,1,0:T(8,128)S(1)} %get-tuple-element.39.full), channel_id=1, source_target_pairs={{240,0},{0,16},{16,32},{32,48},{48,64},{64,80},{80,96},{96,112},{1... | collective-permute-start | bytes 688136 | tf_op jit(solution)/shard_map/ppermute | solution.py:603
  42.3 11.9 %collective-permute-start.11 = (f32[56,8,128]{2,1,0:T(8,128)S(1)}, f32[56,8,128]{2,1,0:T(8,128)S(1)}, u32[]{:S(2)}, u32[]{:S(2)}) collective-permute-start(f32[56,8,128]{2,1,0:T(8,128)S(1)} %get-tuple-element.39.full), channel_id=1, source_target_pairs={{16,0},{32,16},{48,32},{64,48},{80,64},{96,80},{112,96},{128,112},... | collective-permute-start | bytes 688136 | tf_op jit(solution)/shard_map/ppermute | solution.py:603
  46.1 5.1 %collective-permute-start.13 = (f32[28,8,128]{2,1,0:T(8,128)S(1)}, f32[28,8,128]{2,1,0:T(8,128)S(1)}, u32[]{:S(2)}, u32[]{:S(2)}) collective-permute-start(f32[28,8,128]{2,1,0:T(8,128)S(1)} %get-tuple-element.40), channel_id=1, source_target_pairs={{32,0},{48,16},{64,32},{80,48},{96,64},{112,80},{128,96},{144,112}... | collective-permute-start | bytes 344072 | tf_op jit(solution)/shard_map/ppermute | solution.py:603
  48.7 5.6 %collective-permute-start.14 = (f32[28,8,128]{2,1,0:T(8,128)S(1)}, f32[28,8,128]{2,1,0:T(8,128)S(1)}, u32[]{:S(2)}, u32[]{:S(2)}) collective-permute-start(f32[28,8,128]{2,1,0:T(8,128)S(1)} %get-tuple-element.41), channel_id=1, source_target_pairs={{224,0},{240,16},{0,32},{16,48},{32,64},{48,80},{64,96},{80,112},{... | collective-permute-start | bytes 344072 | tf_op jit(solution)/shard_map/ppermute | solution.py:603

commit v9 on v8

--- a/solution.py
+++ b/solution.py
@@ -65,6 +65,27 @@
 
 def wrap(z, n):
     return z % n
+
+
+class Held:
+    def __init__(self, ref=None):
+        self.values, self.ref = {}, ref
+
+    def __getitem__(self, at):
+        return self.values[at]
+
+    def __setitem__(self, at, value):
+        self.values[at] = value
+        if self.ref is not None:
+            self.ref[at] = value
+
+
+class Field:
+    def __init__(self, held, k):
+        self.held, self.k = held, k
+
+    def __getitem__(self, z):
+        return self.held[self.k, z]
 
 
 def around(a, field, z, zm, zp):
@@ -403,7 +424,8 @@
         hi[n] = jnp.where(first, b, a)
 
 
-def level12(pos, full, xr, xl, xr2, xl2, before, a, b, sent, d1, r1, t1, m1, d2, r2, s1, s2, q2):
+def level12(pos, full, xr, xl, xr2, xl2, before, a, b2, sent, d1, r1, t1, m1, s1):
+    b, d2, r2, s2, q2 = Held(b2), Held(), Held(), Held(), Held()
     gx, gy, gz = pos[0], pos[1], pos[2]
     row, lane = iota((8, 128), 0), iota((8, 128), 1)
     y = gy * 64 + jnp.where(lane < 96, lane, lane - 128)
@@ -489,8 +511,9 @@
 
 def solve(
     pos, got, a0, v0, a1, a2, pressure, left,
-    a3, a4, d3, d4, r3, r4, s3, s4, t3, q5, e1, e2, e3, e4, f2, g4, g3, g2, g1, g0, b3, w0,
+    got3, t3, e1, g4, g3, g2, g1, g0, b3, w0,
 ):
+    a3, a4, d3, d4, r3, r4, s3, s4, e2, e3, e4, f2, q5 = (Held() for _ in range(13))
     gx, gy, gz = pos[0], pos[1], pos[2]
     lane = iota((16, 128), 1)
     for k in range(5):
@@ -503,11 +526,11 @@
                 for g in range(1, 8):
                     value = jnp.where(lane // 16 == (at + g) % 8, rows[g], value)
                 value = turn(value, -16 * at)
-                if k < 4:
-                    a3[k, z, pl.ds(s, 16, stride=2), :] = value
-                else:
-                    r3[z, pl.ds(s, 16, stride=2), :] = value
-    s3[...] = a3[SINK]
+                got3[k, z, pl.ds(s, 16, stride=2), :] = value
+    for z in range(4):
+        for k in range(4):
+            a3[k, z] = got3[k, z]
+        s3[z], r3[z] = got3[SINK, z], got3[4, z]
     pre(a3, d3, r3, e3, 4)
 
     def keep3(k, z, value):
@@ -540,17 +563,18 @@
     e = spread_rows(g4, spread_lanes(v))
     for z in range(2):
         a4[V, z] = a4[V, z] + e
-    sweep(a4, a4.at[V], e4, 2)
+    sweep(a4, Field(a4, V), e4, 2)
     sweep(a4, e4, r4, 2)
     for z in range(2):
         e = spread_rows(g3.at[z], spread_lanes(r4[z]))
         a3[V, 2 * z] = a3[V, 2 * z] + e
         a3[V, 2 * z + 1] = a3[V, 2 * z + 1] + e
-    sweep(a3, a3.at[V], e3, 4)
+    sweep(a3, Field(a3, V), e3, 4)
     sweep(a3, e3, r3, 4)
-    b3[:, 8:40] = r3[...]
-    b3[:, 0:8] = r3[:, 24:32]
-    b3[:, 40:48] = r3[:, 0:8]
+    for z in range(4):
+        b3[z, 8:40] = r3[z]
+        b3[z, 0:8] = r3[z][24:32]
+        b3[z, 40:48] = r3[z][0:8]
     lane = iota((8, 128), 1) % 64
     index = jnp.where(lane < 40, lane // 2, lane // 2 - 32) + 16 * gy
     index = lax.rem(index + 64, 64)
@@ -657,8 +681,7 @@
         pos, full, *near, v0,
         spaces=[SMEM] + [VMEM] * 6,
         scratch=[
-            (16, 32, 128), (16, 32, 128), (5, 8, 32, 128), (4, 2, 8, 128),
-            (8, 16, 128), (8, 16, 128), (16, 32, 128), (8, 16, 128), (8, 16, 128),
+            (16, 32, 128), (16, 32, 128), (5, 8, 32, 128), (4, 2, 8, 128), (16, 32, 128),
         ],
     )
     got = lax.all_to_all(sent.reshape(64, 1, 640), ("gy", "gx"), 0, 0).reshape(320, 128)
@@ -669,11 +692,7 @@
             pos, got, a0, v0, a1, a2,
             spaces=[SMEM] + [VMEM] * 5,
             scratch=[
-                (6, 4, 32, 128), (6, 2, 16, 128),
-                (4, 32, 128), (2, 16, 128),
-                (4, 32, 128), (2, 16, 128), (4, 32, 128), (2, 16, 128),
-                (5, 2, 32, 128), (5, 8, 128),
-                (2, 16, 24, 128), (8, 16, 128), (4, 32, 128), (2, 16, 128), (8, 16, 128),
+                (5, 4, 32, 128), (5, 2, 32, 128), (2, 16, 24, 128),
                 (16, 128), (2, 32, 128), (4, 16, 128), (8, 32, 128), (2, 8, 32, 128),
                 (4, 48, 128), (2, Z0, 32, 256),
             ],

time: 78.8 us -> 79 us (level)
  no operation moved by 1% of the time
where the time goes in v9:
time: 79 us; the launch traced here: 78.8 us
  starting transfers between devices  25.6 us (32%)
  waiting for transfers between devices  20.8 us (26%)
  blocking collectives  16.8 us (21%)
  Pallas kernels  14.1 us (18%)
  other arithmetic  0.82 us (1%)
    ppermute x15, starting transfers between devices, shift(): lax.ppermute(value, axis, [((i + by) % count, i) for i in range(count)])  25.6 us
    ppermute x15, waiting for transfers between devices, shift(): lax.ppermute(value, axis, [((i + by) % count, i) for i in range(count)])  20.8 us
    all_to_all x1, blocking collectives, local(): lax.all_to_all(sent.reshape(64, 1, 640), ('gy', 'gx'), 0, 0)  16.8 us
    pallas_call x10, Pallas kernels, call(): pl.pallas_call(kernel, out_shape=[(pltpu.VMEM if pin else jax.ShapeDtypeS...  14.1 us
  transfers between devices with their start and end apart: 15, of which 12 were waited for; matrix products, arithmetic and copies ran while one was open for 1% of the time, Pallas kernels for 3%

profile of v9, /device:TPU:1, one launch (start us, length us, event | category | flops | bytes accessed | tf_op | source)
XLA Modules:
  0.0 78.8 jit_solution(15149386686323954462)
XLA Ops:
  0.6 1.0 %shard_map.77 = (f32[18,16,128]{2,1,0:T(8,128)S(1)}, f32[18,16,128]{2,1,0:T(8,128)S(1)}, f32[4,8,16,128]{3,2,1,0:T(8,128)S(1)}) custom-call(s32[8,16,128]{2,1,0:T(8,128)} %f.1, s32[8,16,128]{2,1,0:T(8,128)} %b.1, f32[8,16,128]{2,1,0:T(8,128)} %s.1, f32[8,16,128]{2,1,0:T(8,128)} %d.1), custom_call_target="tpu_custom_call" | custom-call | tf_op jit(solution)/shard_map/pallas_call | solution.py:22
  1.6 3.4 %collective-permute-start = (f32[18,16,128]{2,1,0:T(8,128)S(1)}, f32[18,16,128]{2,1,0:T(8,128)S(1)}, u32[]{:S(2)}, u32[]{:S(2)}) collective-permute-start(f32[18,16,128]{2,1,0:T(8,128)S(1)} %get-tuple-element.25), channel_id=1, source_target_pairs={{1,0},{2,1},{3,2},{0,3},{5,4},{6,5},{7,6},{4,7},{9,8},{10,9},{11,1... | collective-permute-start | bytes 442376 | tf_op jit(solution)/shard_map/ppermute | solution.py:627
  5.0 2.5 %collective-permute-done.above = f32[18,16,128]{2,1,0:T(8,128)S(1)} collective-permute-done((f32[18,16,128]{2,1,0:T(8,128)S(1)}, f32[18,16,128]{2,1,0:T(8,128)S(1)}, u32[]{:S(2)}, u32[]{:S(2)}) %collective-permute-start) | collective-permute-done | bytes 147488 | tf_op jit(solution)/shard_map/ppermute | solution.py:627
  7.5 3.1 %collective-permute-done.1.below = f32[18,16,128]{2,1,0:T(8,128)S(1)} collective-permute-done((f32[18,16,128]{2,1,0:T(8,128)S(1)}, f32[18,16,128]{2,1,0:T(8,128)S(1)}, u32[]{:S(2)}, u32[]{:S(2)}) %collective-permute-start.1) | collective-permute-done | bytes 147488 | tf_op jit(solution)/shard_map/ppermute | solution.py:627
  10.7 1.9 %collective-permute-start.2 = (f32[39,8,128]{2,1,0:T(8,128)S(1)}, f32[39,8,128]{2,1,0:T(8,128)S(1)}, u32[]{:S(2)}, u32[]{:S(2)}) collective-permute-start(f32[39,8,128]{2,1,0:T(8,128)S(1)} %get-tuple-element.29), channel_id=1, source_target_pairs={{16,0},{32,16},{48,32},{64,48},{80,64},{96,80},{112,96},{128,112},... | collective-permute-start | bytes 479240 | tf_op jit(solution)/shard_map/ppermute | solution.py:627
  12.6 1.5 %collective-permute-start.3 = (f32[39,8,128]{2,1,0:T(8,128)S(1)}, f32[39,8,128]{2,1,0:T(8,128)S(1)}, u32[]{:S(2)}, u32[]{:S(2)}) collective-permute-start(f32[39,8,128]{2,1,0:T(8,128)S(1)} %get-tuple-element.30), channel_id=1, source_target_pairs={{240,0},{0,16},{16,32},{32,48},{48,64},{64,80},{80,96},{96,112},{1... | collective-permute-start | bytes 479240 | tf_op jit(solution)/shard_map/ppermute | solution.py:627
  14.1 0.7 pad_maximum_fusion.tables
  14.9 2.2 %collective-permute-done.2.ml = f32[39,8,128]{2,1,0:T(8,128)S(1)} collective-permute-done((f32[39,8,128]{2,1,0:T(8,128)S(1)}, f32[39,8,128]{2,1,0:T(8,128)S(1)}, u32[]{:S(2)}, u32[]{:S(2)}) %collective-permute-start.2) | collective-permute-done | bytes 159776 | tf_op jit(solution)/shard_map/ppermute | solution.py:627
  17.0 0.5 collective-permute-done.3.mh
  17.5 0.4 shard_map.79
  17.9 2.8 %collective-permute-start.4 = (f32[12,8,128]{2,1,0:T(8,128)S(1)}, f32[12,8,128]{2,1,0:T(8,128)S(1)}, u32[]{:S(2)}, u32[]{:S(2)}) collective-permute-start(f32[12,8,128]{2,1,0:T(8,128)S(1)} %get-tuple-element.33), channel_id=1, source_target_pairs={{4,0},{8,4},{12,8},{0,12},{5,1},{9,5},{13,9},{1,13},{6,2},{10,6},{... | collective-permute-start | bytes 147464 | tf_op jit(solution)/shard_map/ppermute | solution.py:627
  20.8 1.1 %shard_map.80.main = f32[5,18,32,128]{3,2,1,0:T(8,128)S(1)} custom-call(s32[3]{0:T(128)S(1)} %pad_add_fusion.pos, f32[16]{0:T(128)S(1)} %pad_maximum_fusion.tables, f32[4,18,8,128]{3,2,1,0:T(8,128)S(1)} %get-tuple-element.27.xl, f32[4,18,8,128]{3,2,1,0:T(8,128)S(1)} %get-tuple-element.28.xh, f32[4,18,8,128]{3,2,1,0:T(8,128)S(1)} %get-tuple-element.31.rl, ...), custom_call_target="tpu_custom_call" | custom-call | tf_op jit(solution)/shard_map/pallas_call | solution.py:22
  21.9 3.0 %collective-permute-done.5.yh = f32[12,8,128]{2,1,0:T(8,128)S(1)} collective-permute-done((f32[12,8,128]{2,1,0:T(8,128)S(1)}, f32[12,8,128]{2,1,0:T(8,128)S(1)}, u32[]{:S(2)}, u32[]{:S(2)}) %collective-permute-start.5) | collective-permute-done | bytes 49184 | tf_op jit(solution)/shard_map/ppermute | solution.py:627
  24.9 2.7 %shard_map.81 = (f32[6,18,32,256]{3,2,1,0:T(8,128)S(1)}, f32[5,2,8,128]{3,2,1,0:T(8,128)S(1)}) custom-call(s32[3]{0:T(128)S(1)} %pad_add_fusion.pos, f32[16]{0:T(128)S(1)} %pad_maximum_fusion.tables, f32[5,18,32,128]{3,2,1,0:T(8,128)S(1)} %shard_map.80.main, f32[12,8,128]{2,1,0:T(8,128)S(1)} %collective-permute-done.4.yl, ...), custom_call_target="tpu_custom_call" | custom-call | tf_op jit(solution)/shard_map/pallas_call | solution.py:22
  27.7 1.5 %collective-permute-start.7 = (f32[5,2,8,128]{3,2,1,0:T(8,128)S(1)}, f32[5,2,8,128]{3,2,1,0:T(8,128)S(1)}, u32[]{:S(2)}, u32[]{:S(2)}) collective-permute-start(f32[5,2,8,128]{3,2,1,0:T(8,128)S(1)} %get-tuple-element.35.own), channel_id=1, source_target_pairs={{2,0},{3,1},{0,2},{1,3},{6,4},{7,5},{4,6},{5,7},{10,8},{11,9},{8,1... | collective-permute-start | bytes 122888 | tf_op jit(solution)/shard_map/ppermute | solution.py:627
  29.2 1.2 %collective-permute-start.6 = (f32[5,2,8,128]{3,2,1,0:T(8,128)S(1)}, f32[5,2,8,128]{3,2,1,0:T(8,128)S(1)}, u32[]{:S(2)}, u32[]{:S(2)}) collective-permute-start(f32[5,2,8,128]{3,2,1,0:T(8,128)S(1)} %get-tuple-element.35.own), channel_id=1, source_target_pairs={{1,0},{2,1},{3,2},{0,3},{5,4},{6,5},{7,6},{4,7},{9,8},{10,9},{11,1... | collective-permute-start | bytes 122888 | tf_op jit(solution)/shard_map/ppermute | solution.py:627
  30.4 1.4 %collective-permute-done.8.b3 = f32[5,2,8,128]{3,2,1,0:T(8,128)S(1)} collective-permute-done((f32[5,2,8,128]{3,2,1,0:T(8,128)S(1)}, f32[5,2,8,128]{3,2,1,0:T(8,128)S(1)}, u32[]{:S(2)}, u32[]{:S(2)}) %collective-permute-start.8) | collective-permute-done | bytes 40992 | tf_op jit(solution)/shard_map/ppermute | solution.py:627
  31.8 0.4 collective-permute-done.7.b2
  32.2 0.6 collective-permute-done.6.b1
  32.9 0.1 collective-permute-start.9
  33.0 1.4 %collective-permute-start.10 = (f32[8,8,128]{2,1,0:T(8,128)S(1)}, f32[8,8,128]{2,1,0:T(8,128)S(1)}, u32[]{:S(2)}, u32[]{:S(2)}) collective-permute-start(f32[8,8,128]{2,1,0:T(8,128)S(1)} %get-tuple-element.38), channel_id=1, source_target_pairs={{12,0},{0,4},{4,8},{8,12},{13,1},{1,5},{5,9},{9,13},{14,2},{2,6},{... | collective-permute-start | bytes 98312 | tf_op jit(solution)/shard_map/ppermute | solution.py:627
  34.4 1.3 %collective-permute-done.9.right = f32[8,8,128]{2,1,0:T(8,128)S(1)} collective-permute-done((f32[8,8,128]{2,1,0:T(8,128)S(1)}, f32[8,8,128]{2,1,0:T(8,128)S(1)}, u32[]{:S(2)}, u32[]{:S(2)}) %collective-permute-start.9) | collective-permute-done | bytes 32800 | tf_op jit(solution)/shard_map/ppermute | solution.py:627
  35.7 1.3 %collective-permute-done.10.left = f32[8,8,128]{2,1,0:T(8,128)S(1)} collective-permute-done((f32[8,8,128]{2,1,0:T(8,128)S(1)}, f32[8,8,128]{2,1,0:T(8,128)S(1)}, u32[]{:S(2)}, u32[]{:S(2)}) %collective-permute-start.10) | collective-permute-done | bytes 32800 | tf_op jit(solution)/shard_map/ppermute | solution.py:627
  37.1 5.3 %collective-permute-start.12 = (f32[56,8,128]{2,1,0:T(8,128)S(1)}, f32[56,8,128]{2,1,0:T(8,128)S(1)}, u32[]{:S(2)}, u32[]{:S(2)}) collective-permute-start(f32[56,8,128]{2,1,0:T(8,128)S(1)} %get-tuple-element.39.full), channel_id=1, source_target_pairs={{240,0},{0,16},{16,32},{32,48},{48,64},{64,80},{80,96},{96,112},{1... | collective-permute-start | bytes 688136 | tf_op jit(solution)/shard_map/ppermute | solution.py:627
  42.3 3.8 %collective-permute-start.11 = (f32[56,8,128]{2,1,0:T(8,128)S(1)}, f32[56,8,128]{2,1,0:T(8,128)S(1)}, u32[]{:S(2)}, u32[]{:S(2)}) collective-permute-start(f32[56,8,128]{2,1,0:T(8,128)S(1)} %get-tuple-element.39.full), channel_id=1, source_target_pairs={{16,0},{32,16},{48,32},{64,48},{80,64},{96,80},{112,96},{128,112},... | collective-permute-start | bytes 688136 | tf_op jit(solution)/shard_map/ppermute | solution.py:627
  46.1 2.6 %collective-permute-start.13 = (f32[28,8,128]{2,1,0:T(8,128)S(1)}, f32[28,8,128]{2,1,0:T(8,128)S(1)}, u32[]{:S(2)}, u32[]{:S(2)}) collective-permute-start(f32[28,8,128]{2,1,0:T(8,128)S(1)} %get-tuple-element.40), channel_id=1, source_target_pairs={{32,0},{48,16},{64,32},{80,48},{96,64},{112,80},{128,96},{144,112}... | collective-permute-start | bytes 344072 | tf_op jit(solution)/shard_map/ppermute | solution.py:627
  48.7 1.0 %shard_map.84.before.v0 = f32[4,32,256]{2,1,0:T(8,128)S(1)} custom-call(s32[3]{0:T(128)S(1)} %pad_add_fusion.pos, f32[16]{0:T(128)S(1)} %pad_maximum_fusion.tables, f32[5,18,32,128]{3,2,1,0:T(8,128)S(1)} %shard_map.80.main, f32[12,8,128]{2,1,0:T(8,128)S(1)} %collective-permute-done.4.yl, f32[12,8,128]{2,1,0:T(8,128)S(1)} %collective-permute-done.5.yh, ...), custom_call_target="tpu_custom_call" | custom-call | tf_op jit(solution)/shard_map/pallas_call | solution.py:22
  49.8 1.4 %collective-permute-done.13.xr2 = f32[28,8,128]{2,1,0:T(8,128)S(1)} collective-permute-done((f32[28,8,128]{2,1,0:T(8,128)S(1)}, f32[28,8,128]{2,1,0:T(8,128)S(1)}, u32[]{:S(2)}, u32[]{:S(2)}) %collective-permute-start.13) | collective-permute-done | bytes 114720 | tf_op jit(solution)/shard_map/ppermute | solution.py:627
  51.2 3.1 %collective-permute-done.14.xl2 = f32[28,8,128]{2,1,0:T(8,128)S(1)} collective-permute-done((f32[28,8,128]{2,1,0:T(8,128)S(1)}, f32[28,8,128]{2,1,0:T(8,128)S(1)}, u32[]{:S(2)}, u32[]{:S(2)}) %collective-permute-start.14) | collective-permute-done | bytes 114720 | tf_op jit(solution)/shard_map/ppermute | solution.py:627
  54.3 3.3 %shard_map.85 = (f32[6,16,32,128]{3,2,1,0:T(8,128)S(1)}, f32[6,8,16,128]{3,2,1,0:T(8,128)S(1)}, f32[320,128]{1,0:T(8,128)S(1)}) custom-call(s32[3]{0:T(128)S(1)} %pad_add_fusion.pos, f32[56,8,128]{2,1,0:T(8,128)S(1)} %get-tuple-element.39.full, f32[56,8,128]{2,1,0:T(8,128)S(1)} %collective-permute-done.11.xr, f32[56,8,128]{2,1,0:T(8,128)S(1)} %collective-permute-done.12.xl, ...), custom_call_target="tpu_custom_call" | custom-call | tf_op jit(solution)/shard_map/pallas_call | solution.py:22
  57.6 16.8 %all_to_all.5 = f32[64,1,640]{2,1,0:T(1,128)S(1)} all-to-all(f32[64,1,640]{2,1,0:T(1,128)S(1)} %bitcast.6), channel_id=1, replica_groups=mesh['gx'=16,'gy'=4,'gz'=4] {'gy','gx'}, dimensions={0} | all-to-all | bytes 327680 | tf_op jit(solution)/shard_map/all_to_all | solution.py:687
  74.4 4.4 %shard_map.86 = (f32[8,16,128]{2,1,0:T(8,128)}, f32[8,16,128]{2,1,0:T(8,128)}) custom-call(s32[3]{0:T(128)S(1)} %pad_add_fusion.pos, f32[320,128]{1,0:T(8,128)S(1)} %bitcast.5, f32[6,18,32,256]{3,2,1,0:T(8,128)S(1)} %get-tuple-element.42.a0, f32[4,32,256]{2,1,0:T(8,128)S(1)} %shard_map.84.before.v0, f32[6,16,32,128]{3,2,1,0:T(8,128)S(1)} %get-tuple-element.44.a1, ...), custom_call_target="tpu_custom_call" | custom-call | tf_op jit(solution)/shard_map/pallas_call | solution.py:22
  (11 shorter events, 0.4 us)
Async XLA Ops:
  1.6 5.9 %collective-permute-start = (f32[18,16,128]{2,1,0:T(8,128)S(1)}, f32[18,16,128]{2,1,0:T(8,128)S(1)}, u32[]{:S(2)}, u32[]{:S(2)}) collective-permute-start(f32[18,16,128]{2,1,0:T(8,128)S(1)} %get-tuple-element.25), channel_id=1, source_target_pairs={{1,0},{2,1},{3,2},{0,3},{5,4},{6,5},{7,6},{4,7},{9,8},{10,9},{11,1... | collective-permute-start | bytes 442376 | tf_op jit(solution)/shard_map/ppermute | solution.py:627
  5.0 5.6 %collective-permute-start.1 = (f32[18,16,128]{2,1,0:T(8,128)S(1)}, f32[18,16,128]{2,1,0:T(8,128)S(1)}, u32[]{:S(2)}, u32[]{:S(2)}) collective-permute-start(f32[18,16,128]{2,1,0:T(8,128)S(1)} %get-tuple-element.26), channel_id=1, source_target_pairs={{3,0},{0,1},{1,2},{2,3},{7,4},{4,5},{5,6},{6,7},{11,8},{8,9},{9,10... | collective-permute-start | bytes 442376 | tf_op jit(solution)/shard_map/ppermute | solution.py:627
  10.7 6.4 %collective-permute-start.2 = (f32[39,8,128]{2,1,0:T(8,128)S(1)}, f32[39,8,128]{2,1,0:T(8,128)S(1)}, u32[]{:S(2)}, u32[]{:S(2)}) collective-permute-start(f32[39,8,128]{2,1,0:T(8,128)S(1)} %get-tuple-element.29), channel_id=1, source_target_pairs={{16,0},{32,16},{48,32},{64,48},{80,64},{96,80},{112,96},{128,112},... | collective-permute-start | bytes 479240 | tf_op jit(solution)/shard_map/ppermute | solution.py:627
  12.6 5.0 %collective-permute-start.3 = (f32[39,8,128]{2,1,0:T(8,128)S(1)}, f32[39,8,128]{2,1,0:T(8,128)S(1)}, u32[]{:S(2)}, u32[]{:S(2)}) collective-permute-start(f32[39,8,128]{2,1,0:T(8,128)S(1)} %get-tuple-element.30), channel_id=1, source_target_pairs={{240,0},{0,16},{16,32},{32,48},{48,64},{64,80},{80,96},{96,112},{1... | collective-permute-start | bytes 479240 | tf_op jit(solution)/shard_map/ppermute | solution.py:627
  17.9 4.0 %collective-permute-start.4 = (f32[12,8,128]{2,1,0:T(8,128)S(1)}, f32[12,8,128]{2,1,0:T(8,128)S(1)}, u32[]{:S(2)}, u32[]{:S(2)}) collective-permute-start(f32[12,8,128]{2,1,0:T(8,128)S(1)} %get-tuple-element.33), channel_id=1, source_target_pairs={{4,0},{8,4},{12,8},{0,12},{5,1},{9,5},{13,9},{1,13},{6,2},{10,6},{... | collective-permute-start | bytes 147464 | tf_op jit(solution)/shard_map/ppermute | solution.py:627
  20.7 4.2 %collective-permute-start.5 = (f32[12,8,128]{2,1,0:T(8,128)S(1)}, f32[12,8,128]{2,1,0:T(8,128)S(1)}, u32[]{:S(2)}, u32[]{:S(2)}) collective-permute-start(f32[12,8,128]{2,1,0:T(8,128)S(1)} %get-tuple-element.34), channel_id=1, source_target_pairs={{12,0},{0,4},{4,8},{8,12},{13,1},{1,5},{5,9},{9,13},{14,2},{2,6},{... | collective-permute-start | bytes 147464 | tf_op jit(solution)/shard_map/ppermute | solution.py:627
  27.6 4.2 %collective-permute-start.8 = (f32[5,2,8,128]{3,2,1,0:T(8,128)S(1)}, f32[5,2,8,128]{3,2,1,0:T(8,128)S(1)}, u32[]{:S(2)}, u32[]{:S(2)}) collective-permute-start(f32[5,2,8,128]{3,2,1,0:T(8,128)S(1)} %get-tuple-element.35.own), channel_id=1, source_target_pairs={{3,0},{0,1},{1,2},{2,3},{7,4},{4,5},{5,6},{6,7},{11,8},{8,9},{9,10... | collective-permute-start | bytes 122888 | tf_op jit(solution)/shard_map/ppermute | solution.py:627
  27.7 4.5 %collective-permute-start.7 = (f32[5,2,8,128]{3,2,1,0:T(8,128)S(1)}, f32[5,2,8,128]{3,2,1,0:T(8,128)S(1)}, u32[]{:S(2)}, u32[]{:S(2)}) collective-permute-start(f32[5,2,8,128]{3,2,1,0:T(8,128)S(1)} %get-tuple-element.35.own), channel_id=1, source_target_pairs={{2,0},{3,1},{0,2},{1,3},{6,4},{7,5},{4,6},{5,7},{10,8},{11,9},{8,1... | collective-permute-start | bytes 122888 | tf_op jit(solution)/shard_map/ppermute | solution.py:627
  29.2 3.6 %collective-permute-start.6 = (f32[5,2,8,128]{3,2,1,0:T(8,128)S(1)}, f32[5,2,8,128]{3,2,1,0:T(8,128)S(1)}, u32[]{:S(2)}, u32[]{:S(2)}) collective-permute-start(f32[5,2,8,128]{3,2,1,0:T(8,128)S(1)} %get-tuple-element.35.own), channel_id=1, source_target_pairs={{1,0},{2,1},{3,2},{0,3},{5,4},{6,5},{7,6},{4,7},{9,8},{10,9},{11,1... | collective-permute-start | bytes 122888 | tf_op jit(solution)/shard_map/ppermute | solution.py:627
  32.9 2.8 %collective-permute-start.9 = (f32[8,8,128]{2,1,0:T(8,128)S(1)}, f32[8,8,128]{2,1,0:T(8,128)S(1)}, u32[]{:S(2)}, u32[]{:S(2)}) collective-permute-start(f32[8,8,128]{2,1,0:T(8,128)S(1)} %get-tuple-element.37), channel_id=1, source_target_pairs={{4,0},{8,4},{12,8},{0,12},{5,1},{9,5},{13,9},{1,13},{6,2},{10,6},{... | collective-permute-start | bytes 98312 | tf_op jit(solution)/shard_map/ppermute | solution.py:627
  33.0 4.0 %collective-permute-start.10 = (f32[8,8,128]{2,1,0:T(8,128)S(1)}, f32[8,8,128]{2,1,0:T(8,128)S(1)}, u32[]{:S(2)}, u32[]{:S(2)}) collective-permute-start(f32[8,8,128]{2,1,0:T(8,128)S(1)} %get-tuple-element.38), channel_id=1, source_target_pairs={{12,0},{0,4},{4,8},{8,12},{13,1},{1,5},{5,9},{9,13},{14,2},{2,6},{... | collective-permute-start | bytes 98312 | tf_op jit(solution)/shard_map/ppermute | solution.py:627
  37.1 17.2 %collective-permute-start.12 = (f32[56,8,128]{2,1,0:T(8,128)S(1)}, f32[56,8,128]{2,1,0:T(8,128)S(1)}, u32[]{:S(2)}, u32[]{:S(2)}) collective-permute-start(f32[56,8,128]{2,1,0:T(8,128)S(1)} %get-tuple-element.39.full), channel_id=1, source_target_pairs={{240,0},{0,16},{16,32},{32,48},{48,64},{64,80},{80,96},{96,112},{1... | collective-permute-start | bytes 688136 | tf_op jit(solution)/shard_map/ppermute | solution.py:627
  42.3 11.9 %collective-permute-start.11 = (f32[56,8,128]{2,1,0:T(8,128)S(1)}, f32[56,8,128]{2,1,0:T(8,128)S(1)}, u32[]{:S(2)}, u32[]{:S(2)}) collective-permute-start(f32[56,8,128]{2,1,0:T(8,128)S(1)} %get-tuple-element.39.full), channel_id=1, source_target_pairs={{16,0},{32,16},{48,32},{64,48},{80,64},{96,80},{112,96},{128,112},... | collective-permute-start | bytes 688136 | tf_op jit(solution)/shard_map/ppermute | solution.py:627
  46.1 5.1 %collective-permute-start.13 = (f32[28,8,128]{2,1,0:T(8,128)S(1)}, f32[28,8,128]{2,1,0:T(8,128)S(1)}, u32[]{:S(2)}, u32[]{:S(2)}) collective-permute-start(f32[28,8,128]{2,1,0:T(8,128)S(1)} %get-tuple-element.40), channel_id=1, source_target_pairs={{32,0},{48,16},{64,32},{80,48},{96,64},{112,80},{128,96},{144,112}... | collective-permute-start | bytes 344072 | tf_op jit(solution)/shard_map/ppermute | solution.py:627
  48.7 5.6 %collective-permute-start.14 = (f32[28,8,128]{2,1,0:T(8,128)S(1)}, f32[28,8,128]{2,1,0:T(8,128)S(1)}, u32[]{:S(2)}, u32[]{:S(2)}) collective-permute-start(f32[28,8,128]{2,1,0:T(8,128)S(1)} %get-tuple-element.41), channel_id=1, source_target_pairs={{224,0},{240,16},{0,32},{16,48},{32,64},{48,80},{64,96},{80,112},{... | collective-permute-start | bytes 344072 | tf_op jit(solution)/shard_map/ppermute | solution.py:627

commit v10 on v9

--- a/solution.py
+++ b/solution.py
@@ -14,7 +14,6 @@
 Z0 = 8 + 2 * H
 
 VMEM = pl.BlockSpec(memory_space=pltpu.VMEM)
-SMEM = pl.BlockSpec(memory_space=pltpu.SMEM)
 HBM = pl.BlockSpec(memory_space=pltpu.HBM)
 
 
@@ -29,6 +28,10 @@
     )(*args)
 
 
+def position():
+    return [lax.axis_index(name) for name in ("gx", "gy", "gz")]
+
+
 def iota(shape, dim):
     return lax.broadcasted_iota(jnp.int32, shape, dim)
 
@@ -68,16 +71,14 @@
 
 
 class Held:
-    def __init__(self, ref=None):
-        self.values, self.ref = {}, ref
+    def __init__(self):
+        self.values = {}
 
     def __getitem__(self, at):
         return self.values[at]
 
     def __setitem__(self, at, value):
         self.values[at] = value
-        if self.ref is not None:
-            self.ref[at] = value
 
 
 class Field:
@@ -250,7 +251,9 @@
 PART = PUX, PUZ, PSINK, PB, PH = range(5)
 
 
-def tile0(pos, tables, raw, first_lane, part, vs, start=0, stop=Z0):
+def tile0(tables, raw, first_lane, part, vs, start=0, stop=Z0):
+    pos = position()
+    table = [jnp.broadcast_to(tables[n : n + 1], (32, 128)) for n in range(16)]
     row, lane = iota((32, 128), 0), iota((32, 128), 1)
     x = pos[0] * 16 + jnp.where(row < 24, row, row - 32)
     y = pos[1] * 128 + first_lane + (lane if first_lane == 0 else jnp.where(lane < 64, lane, lane - 256))
@@ -259,12 +262,12 @@
         zg = pos[2] * 8 + z - H
         here = inside & ((zg >= 0) & (zg < 32))
         kind = raw(FACIES, z)
-        h = jnp.full((32, 128), tables[0], F32)
-        v = jnp.full((32, 128), tables[8], F32)
+        h = table[0]
+        v = table[8]
         for n in range(1, 8):
             is_n = kind == float(n)
-            h = jnp.where(is_n, tables[n], h)
-            v = jnp.where(is_n, tables[8 + n], v)
+            h = jnp.where(is_n, table[n], h)
+            v = jnp.where(is_n, table[8 + n], v)
         part[PH, z] = jnp.where(here, h, 0.0)
         vs[z] = jnp.where(here, v, 0.0)
     for z in range(start, stop - 1):
@@ -289,11 +292,11 @@
         )
 
 
-def main0(pos, tables, xl, xh, rl, rh, part, vs):
+def main0(tables, xl, xh, rl, rh, part, vs):
     def raw(k, z):
         return jnp.concatenate([ref[k, z] for ref in (xl, xh, rl, rh)], axis=0)
 
-    tile0(pos, tables, raw, 0, part, vs)
+    tile0(tables, raw, 0, part, vs)
 
 
 def y_sides(yl, yh, raw, layers):
@@ -323,10 +326,10 @@
     return diag, sink, ux, uy, uz, lx, ly, lz
 
 
-def level0(pos, tables, main, yl, yh, a, packed, raw, side, vs, hs, dd, res, t, m):
+def level0(tables, main, yl, yh, a, packed, raw, side, vs, hs, dd, res, t, m):
     lane8 = iota((8, 128), 1)
     y_sides(yl, yh, raw, range(2, Z0 - 2))
-    tile0(pos, tables, lambda k, z: raw[k, z], 128, side, vs, 2, Z0 - 2)
+    tile0(tables, lambda k, z: raw[k, z], 128, side, vs, 2, Z0 - 2)
     row, lane = iota((32, 256), 0), iota((32, 256), 1)
     odd_row, odd_lane = row % 2 == 1, lane % 2 == 1
     a[UZ, 2] = jnp.concatenate([main[PUZ, 2], side[PUZ, 2]], axis=1)
@@ -382,10 +385,10 @@
 OUTER = (2, 3, Z0 - 4, Z0 - 3)
 
 
-def outer0(pos, tables, main, yl, yh, a0, field, raw, side, vs, a):
+def outer0(tables, main, yl, yh, a0, field, raw, side, vs, a):
     for start, stop in ((0, 4), (Z0 - 4, Z0)):
         y_sides(yl, yh, raw, range(start, stop))
-        tile0(pos, tables, lambda k, z: raw[k, z], 128, side, vs, start, stop)
+        tile0(tables, lambda k, z: raw[k, z], 128, side, vs, start, stop)
         a[UZ, start] = jnp.concatenate([main[PUZ, start], side[PUZ, start]], axis=1)
         for z in range(start + 1, stop - 1):
             setup0(a, main, side, z)
@@ -424,9 +427,8 @@
         hi[n] = jnp.where(first, b, a)
 
 
-def level12(pos, full, xr, xl, xr2, xl2, before, a, b2, sent, d1, r1, t1, m1, s1):
-    b, d2, r2, s2, q2 = Held(b2), Held(), Held(), Held(), Held()
-    gx, gy, gz = pos[0], pos[1], pos[2]
+def level12(full, xr, xl, xr2, xl2, before, a, b, sent, d1, r1, t1, m1, d2, r2, s1, s2, q2):
+    gx, gy, gz = position()
     row, lane = iota((8, 128), 0), iota((8, 128), 1)
     y = gy * 64 + jnp.where(lane < 96, lane, lane - 128)
     in_y = (y >= 0) & (y < 256)
@@ -510,11 +512,11 @@
 
 
 def solve(
-    pos, got, a0, v0, a1, a2, pressure, left,
+    got, a0, v0, a1, a2, pressure, left,
     got3, t3, e1, g4, g3, g2, g1, g0, b3, w0,
 ):
     a3, a4, d3, d4, r3, r4, s3, s4, e2, e3, e4, f2, q5 = (Held() for _ in range(13))
-    gx, gy, gz = pos[0], pos[1], pos[2]
+    gx, gy, gz = position()
     lane = iota((16, 128), 1)
     for k in range(5):
         rows = [got[pl.ds(80 * g + k, 16, stride=5), :] for g in range(4)]
@@ -628,8 +630,7 @@
 
 
 def local(facies, boundary, hc, vc, source, density):
-    pos = jnp.stack([lax.axis_index(n) for n in ("gx", "gy", "gz")]).astype(jnp.int32)
-    tables = jnp.concatenate([hc, vc])
+    tables = jnp.broadcast_to(jnp.concatenate([hc, vc])[:, None], (16, 128))
     lo, hi, own = call(
         pack_z,
         [(4 * H - 2, 16, 128)] * 2 + [(4, 8, 16, 128)],
@@ -652,22 +653,19 @@
     )
     yl, yh = shift(lo, "gy", 1), shift(hi, "gy", -1)
     (main,) = call(
-        main0, [(5, Z0, 32, 128)], pos, tables, xl, xh, rl, rh,
-        spaces=[SMEM] * 2 + [VMEM] * 4, scratch=[(Z0, 32, 128)],
+        main0, [(5, Z0, 32, 128)], tables, xl, xh, rl, rh, scratch=[(Z0, 32, 128)],
     )
     a0, packed = call(
         level0,
         [(6, Z0, 32, 256), (5, 2, 8, 128)],
-        pos, tables, main, yl, yh,
-        spaces=[SMEM] * 2 + [VMEM] * 3,
+        tables, main, yl, yh,
         scratch=[
             (4, Z0, 32, 128), (5, Z0, 32, 128), (Z0, 32, 128), (8, 16, 128), (8, 16, 128),
             (8, 16, 128), (6, 4, 16, 128), (6, 4, 8, 128),
         ],
     )
     (v0,) = call(
-        outer0, [(4, 32, 256)], pos, tables, main, yl, yh, a0,
-        spaces=[SMEM] * 2 + [VMEM] * 4,
+        outer0, [(4, 32, 256)], tables, main, yl, yh, a0,
         scratch=[(4, Z0, 32, 128), (5, Z0, 32, 128), (Z0, 32, 128), (6, Z0, 32, 256)],
     )
     blocks = [shift(packed, "gz", n) for n in (1, 2, 3)]
@@ -678,10 +676,10 @@
     a1, a2, sent = call(
         level12,
         [(6, 16, 32, 128), (6, 8, 16, 128), (320, 128)],
-        pos, full, *near, v0,
-        spaces=[SMEM] + [VMEM] * 6,
+        full, *near, v0,
         scratch=[
-            (16, 32, 128), (16, 32, 128), (5, 8, 32, 128), (4, 2, 8, 128), (16, 32, 128),
+            (16, 32, 128), (16, 32, 128), (5, 8, 32, 128), (4, 2, 8, 128),
+            (8, 16, 128), (8, 16, 128), (16, 32, 128), (8, 16, 128), (8, 16, 128),
         ],
     )
     got = lax.all_to_all(sent.reshape(64, 1, 640), ("gy", "gx"), 0, 0).reshape(320, 128)
@@ -689,8 +687,7 @@
         call(
             solve,
             [(8, 16, 128), (8, 16, 128)],
-            pos, got, a0, v0, a1, a2,
-            spaces=[SMEM] + [VMEM] * 5,
+            got, a0, v0, a1, a2,
             scratch=[
                 (5, 4, 32, 128), (5, 2, 32, 128), (2, 16, 24, 128),
                 (16, 128), (2, 32, 128), (4, 16, 128), (8, 32, 128), (2, 8, 32, 128),

time: 79 us -> 76.9 us (0.973)
  Pallas kernels: 14.1 us -> 10.8 us
  waiting for transfers between devices: 20.8 us -> 22.6 us
    pallas_call x10, Pallas kernels: 14.1 us -> 10.8 us  [call(): pl.pallas_call(kernel, out_shape=[(pltpu.VMEM if pin else jax.ShapeDtypeS...]
    ppermute x15, waiting for transfers between devices: 20.8 us -> 22.6 us  [shift(): lax.ppermute(value, axis, [((i + by) % count, i) for i in range(count)])]
  transfers between devices with their start and end apart: 15 -> 15, of which waited for: 12 -> 13; matrix products, arithmetic and copies ran while one was open for 1% -> 0% of each run, Pallas kernels for 3% -> 1%
where the time goes in v10:
time: 76.9 us; the launch traced here: 76.7 us
  starting transfers between devices  25.6 us (33%)
  waiting for transfers between devices  22.6 us (29%)
  blocking collectives  16.8 us (22%)
  Pallas kernels  10.8 us (14%)
    ppermute x15, starting transfers between devices, shift(): lax.ppermute(value, axis, [((i + by) % count, i) for i in range(count)])  25.6 us
    ppermute x15, waiting for transfers between devices, shift(): lax.ppermute(value, axis, [((i + by) % count, i) for i in range(count)])  22.6 us
    all_to_all x1, blocking collectives, local(): lax.all_to_all(sent.reshape(64, 1, 640), ('gy', 'gx'), 0, 0)  16.8 us
    pallas_call x10, Pallas kernels, call(): pl.pallas_call(kernel, out_shape=[(pltpu.VMEM if pin else jax.ShapeDtypeS...  10.8 us
  transfers between devices with their start and end apart: 15, of which 13 were waited for; matrix products, arithmetic and copies ran while one was open for 0% of the time, Pallas kernels for 1%

profile of v10, /device:TPU:1, one launch (start us, length us, event | category | flops | bytes accessed | tf_op | source)
XLA Modules:
  0.0 76.7 jit_solution(18440238523405027376)
XLA Ops:
  0.7 1.0 %shard_map.77 = (f32[18,16,128]{2,1,0:T(8,128)S(1)}, f32[18,16,128]{2,1,0:T(8,128)S(1)}, f32[4,8,16,128]{3,2,1,0:T(8,128)S(1)}) custom-call(s32[8,16,128]{2,1,0:T(8,128)} %f.1, s32[8,16,128]{2,1,0:T(8,128)} %b.1, f32[8,16,128]{2,1,0:T(8,128)} %s.1, f32[8,16,128]{2,1,0:T(8,128)} %d.1), custom_call_target="tpu_custom_call" | custom-call | tf_op jit(solution)/shard_map/pallas_call | solution.py:21
  1.6 3.4 %collective-permute-start = (f32[18,16,128]{2,1,0:T(8,128)S(1)}, f32[18,16,128]{2,1,0:T(8,128)S(1)}, u32[]{:S(2)}, u32[]{:S(2)}) collective-permute-start(f32[18,16,128]{2,1,0:T(8,128)S(1)} %get-tuple-element.25), channel_id=1, source_target_pairs={{1,0},{2,1},{3,2},{0,3},{5,4},{6,5},{7,6},{4,7},{9,8},{10,9},{11,1... | collective-permute-start | bytes 442376 | tf_op jit(solution)/shard_map/ppermute | solution.py:629
  5.0 2.5 %collective-permute-done.above = f32[18,16,128]{2,1,0:T(8,128)S(1)} collective-permute-done((f32[18,16,128]{2,1,0:T(8,128)S(1)}, f32[18,16,128]{2,1,0:T(8,128)S(1)}, u32[]{:S(2)}, u32[]{:S(2)}) %collective-permute-start) | collective-permute-done | bytes 147488 | tf_op jit(solution)/shard_map/ppermute | solution.py:629
  7.5 3.1 %collective-permute-done.1.below = f32[18,16,128]{2,1,0:T(8,128)S(1)} collective-permute-done((f32[18,16,128]{2,1,0:T(8,128)S(1)}, f32[18,16,128]{2,1,0:T(8,128)S(1)}, u32[]{:S(2)}, u32[]{:S(2)}) %collective-permute-start.1) | collective-permute-done | bytes 147488 | tf_op jit(solution)/shard_map/ppermute | solution.py:629
  10.7 1.9 %collective-permute-start.2 = (f32[39,8,128]{2,1,0:T(8,128)S(1)}, f32[39,8,128]{2,1,0:T(8,128)S(1)}, u32[]{:S(2)}, u32[]{:S(2)}) collective-permute-start(f32[39,8,128]{2,1,0:T(8,128)S(1)} %get-tuple-element.29), channel_id=1, source_target_pairs={{16,0},{32,16},{48,32},{64,48},{80,64},{96,80},{112,96},{128,112},... | collective-permute-start | bytes 479240 | tf_op jit(solution)/shard_map/ppermute | solution.py:629
  12.6 1.5 %collective-permute-start.3 = (f32[39,8,128]{2,1,0:T(8,128)S(1)}, f32[39,8,128]{2,1,0:T(8,128)S(1)}, u32[]{:S(2)}, u32[]{:S(2)}) collective-permute-start(f32[39,8,128]{2,1,0:T(8,128)S(1)} %get-tuple-element.30), channel_id=1, source_target_pairs={{240,0},{0,16},{16,32},{32,48},{48,64},{64,80},{80,96},{96,112},{1... | collective-permute-start | bytes 479240 | tf_op jit(solution)/shard_map/ppermute | solution.py:629
  14.1 2.9 %collective-permute-done.2.ml = f32[39,8,128]{2,1,0:T(8,128)S(1)} collective-permute-done((f32[39,8,128]{2,1,0:T(8,128)S(1)}, f32[39,8,128]{2,1,0:T(8,128)S(1)}, u32[]{:S(2)}, u32[]{:S(2)}) %collective-permute-start.2) | collective-permute-done | bytes 159776 | tf_op jit(solution)/shard_map/ppermute | solution.py:629
  17.1 0.5 collective-permute-done.3.mh
  17.6 0.4 shard_map.79
  17.9 2.8 %collective-permute-start.4 = (f32[12,8,128]{2,1,0:T(8,128)S(1)}, f32[12,8,128]{2,1,0:T(8,128)S(1)}, u32[]{:S(2)}, u32[]{:S(2)}) collective-permute-start(f32[12,8,128]{2,1,0:T(8,128)S(1)} %get-tuple-element.33), channel_id=1, source_target_pairs={{4,0},{8,4},{12,8},{0,12},{5,1},{9,5},{13,9},{1,13},{6,2},{10,6},{... | collective-permute-start | bytes 147464 | tf_op jit(solution)/shard_map/ppermute | solution.py:629
  20.9 0.5 shard_map.80.main
  21.4 0.5 collective-permute-done.4.yl
  21.9 3.0 %collective-permute-done.5.yh = f32[12,8,128]{2,1,0:T(8,128)S(1)} collective-permute-done((f32[12,8,128]{2,1,0:T(8,128)S(1)}, f32[12,8,128]{2,1,0:T(8,128)S(1)}, u32[]{:S(2)}, u32[]{:S(2)}) %collective-permute-start.5) | collective-permute-done | bytes 49184 | tf_op jit(solution)/shard_map/ppermute | solution.py:629
  24.9 2.1 %shard_map.81 = (f32[6,18,32,256]{3,2,1,0:T(8,128)S(1)}, f32[5,2,8,128]{3,2,1,0:T(8,128)S(1)}) custom-call(f32[16,128]{1,0:T(8,128)S(1)} %broadcast_in_dim.2.tables, f32[5,18,32,128]{3,2,1,0:T(8,128)S(1)} %shard_map.80.main, f32[12,8,128]{2,1,0:T(8,128)S(1)} %collective-permute-done.4.yl, f32[12,8,128]{2,1,0:T(8,128)S(1)} %collective-permute-done.5.yh), custom_call_target="tpu_custom_call" | custom-call | tf_op jit(solution)/shard_map/pallas_call | solution.py:21
  27.1 1.5 %collective-permute-start.7 = (f32[5,2,8,128]{3,2,1,0:T(8,128)S(1)}, f32[5,2,8,128]{3,2,1,0:T(8,128)S(1)}, u32[]{:S(2)}, u32[]{:S(2)}) collective-permute-start(f32[5,2,8,128]{3,2,1,0:T(8,128)S(1)} %get-tuple-element.35.own), channel_id=1, source_target_pairs={{2,0},{3,1},{0,2},{1,3},{6,4},{7,5},{4,6},{5,7},{10,8},{11,9},{8,1... | collective-permute-start | bytes 122888 | tf_op jit(solution)/shard_map/ppermute | solution.py:629
  28.6 1.2 %collective-permute-start.6 = (f32[5,2,8,128]{3,2,1,0:T(8,128)S(1)}, f32[5,2,8,128]{3,2,1,0:T(8,128)S(1)}, u32[]{:S(2)}, u32[]{:S(2)}) collective-permute-start(f32[5,2,8,128]{3,2,1,0:T(8,128)S(1)} %get-tuple-element.35.own), channel_id=1, source_target_pairs={{1,0},{2,1},{3,2},{0,3},{5,4},{6,5},{7,6},{4,7},{9,8},{10,9},{11,1... | collective-permute-start | bytes 122888 | tf_op jit(solution)/shard_map/ppermute | solution.py:629
  29.8 1.4 %collective-permute-done.8.b3 = f32[5,2,8,128]{3,2,1,0:T(8,128)S(1)} collective-permute-done((f32[5,2,8,128]{3,2,1,0:T(8,128)S(1)}, f32[5,2,8,128]{3,2,1,0:T(8,128)S(1)}, u32[]{:S(2)}, u32[]{:S(2)}) %collective-permute-start.8) | collective-permute-done | bytes 40992 | tf_op jit(solution)/shard_map/ppermute | solution.py:629
  31.2 0.4 collective-permute-done.7.b2
  31.6 0.6 collective-permute-done.6.b1
  32.3 0.1 collective-permute-start.9
  32.4 1.4 %collective-permute-start.10 = (f32[8,8,128]{2,1,0:T(8,128)S(1)}, f32[8,8,128]{2,1,0:T(8,128)S(1)}, u32[]{:S(2)}, u32[]{:S(2)}) collective-permute-start(f32[8,8,128]{2,1,0:T(8,128)S(1)} %get-tuple-element.38), channel_id=1, source_target_pairs={{12,0},{0,4},{4,8},{8,12},{13,1},{1,5},{5,9},{9,13},{14,2},{2,6},{... | collective-permute-start | bytes 98312 | tf_op jit(solution)/shard_map/ppermute | solution.py:629
  33.9 1.3 %collective-permute-done.9.right = f32[8,8,128]{2,1,0:T(8,128)S(1)} collective-permute-done((f32[8,8,128]{2,1,0:T(8,128)S(1)}, f32[8,8,128]{2,1,0:T(8,128)S(1)}, u32[]{:S(2)}, u32[]{:S(2)}) %collective-permute-start.9) | collective-permute-done | bytes 32800 | tf_op jit(solution)/shard_map/ppermute | solution.py:629
  35.2 1.3 %collective-permute-done.10.left = f32[8,8,128]{2,1,0:T(8,128)S(1)} collective-permute-done((f32[8,8,128]{2,1,0:T(8,128)S(1)}, f32[8,8,128]{2,1,0:T(8,128)S(1)}, u32[]{:S(2)}, u32[]{:S(2)}) %collective-permute-start.10) | collective-permute-done | bytes 32800 | tf_op jit(solution)/shard_map/ppermute | solution.py:629
  36.5 5.3 %collective-permute-start.12 = (f32[56,8,128]{2,1,0:T(8,128)S(1)}, f32[56,8,128]{2,1,0:T(8,128)S(1)}, u32[]{:S(2)}, u32[]{:S(2)}) collective-permute-start(f32[56,8,128]{2,1,0:T(8,128)S(1)} %get-tuple-element.39.full), channel_id=1, source_target_pairs={{240,0},{0,16},{16,32},{32,48},{48,64},{64,80},{80,96},{96,112},{1... | collective-permute-start | bytes 688136 | tf_op jit(solution)/shard_map/ppermute | solution.py:629
  41.8 3.8 %collective-permute-start.11 = (f32[56,8,128]{2,1,0:T(8,128)S(1)}, f32[56,8,128]{2,1,0:T(8,128)S(1)}, u32[]{:S(2)}, u32[]{:S(2)}) collective-permute-start(f32[56,8,128]{2,1,0:T(8,128)S(1)} %get-tuple-element.39.full), channel_id=1, source_target_pairs={{16,0},{32,16},{48,32},{64,48},{80,64},{96,80},{112,96},{128,112},... | collective-permute-start | bytes 688136 | tf_op jit(solution)/shard_map/ppermute | solution.py:629
  45.6 2.6 %collective-permute-start.13 = (f32[28,8,128]{2,1,0:T(8,128)S(1)}, f32[28,8,128]{2,1,0:T(8,128)S(1)}, u32[]{:S(2)}, u32[]{:S(2)}) collective-permute-start(f32[28,8,128]{2,1,0:T(8,128)S(1)} %get-tuple-element.40), channel_id=1, source_target_pairs={{32,0},{48,16},{64,32},{80,48},{96,64},{112,80},{128,96},{144,112}... | collective-permute-start | bytes 344072 | tf_op jit(solution)/shard_map/ppermute | solution.py:629
  48.2 0.5 shard_map.84.before.v0
  48.6 2.0 %collective-permute-done.13.xr2 = f32[28,8,128]{2,1,0:T(8,128)S(1)} collective-permute-done((f32[28,8,128]{2,1,0:T(8,128)S(1)}, f32[28,8,128]{2,1,0:T(8,128)S(1)}, u32[]{:S(2)}, u32[]{:S(2)}) %collective-permute-start.13) | collective-permute-done | bytes 114720 | tf_op jit(solution)/shard_map/ppermute | solution.py:629
  50.6 3.1 %collective-permute-done.14.xl2 = f32[28,8,128]{2,1,0:T(8,128)S(1)} collective-permute-done((f32[28,8,128]{2,1,0:T(8,128)S(1)}, f32[28,8,128]{2,1,0:T(8,128)S(1)}, u32[]{:S(2)}, u32[]{:S(2)}) %collective-permute-start.14) | collective-permute-done | bytes 114720 | tf_op jit(solution)/shard_map/ppermute | solution.py:629
  53.7 2.4 %shard_map.85 = (f32[6,16,32,128]{3,2,1,0:T(8,128)S(1)}, f32[6,8,16,128]{3,2,1,0:T(8,128)S(1)}, f32[320,128]{1,0:T(8,128)S(1)}) custom-call(f32[56,8,128]{2,1,0:T(8,128)S(1)} %get-tuple-element.39.full, f32[56,8,128]{2,1,0:T(8,128)S(1)} %collective-permute-done.11.xr, f32[56,8,128]{2,1,0:T(8,128)S(1)} %collective-permute-done.12.xl, ...), custom_call_target="tpu_custom_call" | custom-call | tf_op jit(solution)/shard_map/pallas_call | solution.py:21
  56.2 16.8 %all_to_all.5 = f32[64,1,640]{2,1,0:T(1,128)S(1)} all-to-all(f32[64,1,640]{2,1,0:T(1,128)S(1)} %bitcast.3), channel_id=1, replica_groups=mesh['gx'=16,'gy'=4,'gz'=4] {'gy','gx'}, dimensions={0} | all-to-all | bytes 327680 | tf_op jit(solution)/shard_map/all_to_all | solution.py:685
  73.0 3.7 %shard_map.86 = (f32[8,16,128]{2,1,0:T(8,128)}, f32[8,16,128]{2,1,0:T(8,128)}) custom-call(f32[320,128]{1,0:T(8,128)S(1)} %bitcast.2, f32[6,18,32,256]{3,2,1,0:T(8,128)S(1)} %get-tuple-element.42.a0, f32[4,32,256]{2,1,0:T(8,128)S(1)} %shard_map.84.before.v0, f32[6,16,32,128]{3,2,1,0:T(8,128)S(1)} %get-tuple-element.44.a1, ...), custom_call_target="tpu_custom_call" | custom-call | tf_op jit(solution)/shard_map/pallas_call | solution.py:21
  (15 shorter events, 0.5 us)
Async XLA Ops:
  0.6 20.1 %copy-start = (f32[8]{0:T(128)S(1)}, f32[8]{0:T(128)}, u32[]{:S(2)}) copy-start(f32[8]{0:T(128)} %param.9) | copy-start | bytes 100
  0.6 20.1 %copy-start.1 = (f32[8]{0:T(128)S(1)}, f32[8]{0:T(128)}, u32[]{:S(2)}) copy-start(f32[8]{0:T(128)} %param.8) | copy-start | bytes 100
  1.6 5.9 %collective-permute-start = (f32[18,16,128]{2,1,0:T(8,128)S(1)}, f32[18,16,128]{2,1,0:T(8,128)S(1)}, u32[]{:S(2)}, u32[]{:S(2)}) collective-permute-start(f32[18,16,128]{2,1,0:T(8,128)S(1)} %get-tuple-element.25), channel_id=1, source_target_pairs={{1,0},{2,1},{3,2},{0,3},{5,4},{6,5},{7,6},{4,7},{9,8},{10,9},{11,1... | collective-permute-start | bytes 442376 | tf_op jit(solution)/shard_map/ppermute | solution.py:629
  5.0 5.6 %collective-permute-start.1 = (f32[18,16,128]{2,1,0:T(8,128)S(1)}, f32[18,16,128]{2,1,0:T(8,128)S(1)}, u32[]{:S(2)}, u32[]{:S(2)}) collective-permute-start(f32[18,16,128]{2,1,0:T(8,128)S(1)} %get-tuple-element.26), channel_id=1, source_target_pairs={{3,0},{0,1},{1,2},{2,3},{7,4},{4,5},{5,6},{6,7},{11,8},{8,9},{9,10... | collective-permute-start | bytes 442376 | tf_op jit(solution)/shard_map/ppermute | solution.py:629
  10.7 6.4 %collective-permute-start.2 = (f32[39,8,128]{2,1,0:T(8,128)S(1)}, f32[39,8,128]{2,1,0:T(8,128)S(1)}, u32[]{:S(2)}, u32[]{:S(2)}) collective-permute-start(f32[39,8,128]{2,1,0:T(8,128)S(1)} %get-tuple-element.29), channel_id=1, source_target_pairs={{16,0},{32,16},{48,32},{64,48},{80,64},{96,80},{112,96},{128,112},... | collective-permute-start | bytes 479240 | tf_op jit(solution)/shard_map/ppermute | solution.py:629
  12.6 5.0 %collective-permute-start.3 = (f32[39,8,128]{2,1,0:T(8,128)S(1)}, f32[39,8,128]{2,1,0:T(8,128)S(1)}, u32[]{:S(2)}, u32[]{:S(2)}) collective-permute-start(f32[39,8,128]{2,1,0:T(8,128)S(1)} %get-tuple-element.30), channel_id=1, source_target_pairs={{240,0},{0,16},{16,32},{32,48},{48,64},{64,80},{80,96},{96,112},{1... | collective-permute-start | bytes 479240 | tf_op jit(solution)/shard_map/ppermute | solution.py:629
  17.9 4.0 %collective-permute-start.4 = (f32[12,8,128]{2,1,0:T(8,128)S(1)}, f32[12,8,128]{2,1,0:T(8,128)S(1)}, u32[]{:S(2)}, u32[]{:S(2)}) collective-permute-start(f32[12,8,128]{2,1,0:T(8,128)S(1)} %get-tuple-element.33), channel_id=1, source_target_pairs={{4,0},{8,4},{12,8},{0,12},{5,1},{9,5},{13,9},{1,13},{6,2},{10,6},{... | collective-permute-start | bytes 147464 | tf_op jit(solution)/shard_map/ppermute | solution.py:629
  20.8 4.2 %collective-permute-start.5 = (f32[12,8,128]{2,1,0:T(8,128)S(1)}, f32[12,8,128]{2,1,0:T(8,128)S(1)}, u32[]{:S(2)}, u32[]{:S(2)}) collective-permute-start(f32[12,8,128]{2,1,0:T(8,128)S(1)} %get-tuple-element.34), channel_id=1, source_target_pairs={{12,0},{0,4},{4,8},{8,12},{13,1},{1,5},{5,9},{9,13},{14,2},{2,6},{... | collective-permute-start | bytes 147464 | tf_op jit(solution)/shard_map/ppermute | solution.py:629
  27.1 4.2 %collective-permute-start.8 = (f32[5,2,8,128]{3,2,1,0:T(8,128)S(1)}, f32[5,2,8,128]{3,2,1,0:T(8,128)S(1)}, u32[]{:S(2)}, u32[]{:S(2)}) collective-permute-start(f32[5,2,8,128]{3,2,1,0:T(8,128)S(1)} %get-tuple-element.35.own), channel_id=1, source_target_pairs={{3,0},{0,1},{1,2},{2,3},{7,4},{4,5},{5,6},{6,7},{11,8},{8,9},{9,10... | collective-permute-start | bytes 122888 | tf_op jit(solution)/shard_map/ppermute | solution.py:629
  27.1 4.5 %collective-permute-start.7 = (f32[5,2,8,128]{3,2,1,0:T(8,128)S(1)}, f32[5,2,8,128]{3,2,1,0:T(8,128)S(1)}, u32[]{:S(2)}, u32[]{:S(2)}) collective-permute-start(f32[5,2,8,128]{3,2,1,0:T(8,128)S(1)} %get-tuple-element.35.own), channel_id=1, source_target_pairs={{2,0},{3,1},{0,2},{1,3},{6,4},{7,5},{4,6},{5,7},{10,8},{11,9},{8,1... | collective-permute-start | bytes 122888 | tf_op jit(solution)/shard_map/ppermute | solution.py:629
  28.6 3.6 %collective-permute-start.6 = (f32[5,2,8,128]{3,2,1,0:T(8,128)S(1)}, f32[5,2,8,128]{3,2,1,0:T(8,128)S(1)}, u32[]{:S(2)}, u32[]{:S(2)}) collective-permute-start(f32[5,2,8,128]{3,2,1,0:T(8,128)S(1)} %get-tuple-element.35.own), channel_id=1, source_target_pairs={{1,0},{2,1},{3,2},{0,3},{5,4},{6,5},{7,6},{4,7},{9,8},{10,9},{11,1... | collective-permute-start | bytes 122888 | tf_op jit(solution)/shard_map/ppermute | solution.py:629
  32.3 2.8 %collective-permute-start.9 = (f32[8,8,128]{2,1,0:T(8,128)S(1)}, f32[8,8,128]{2,1,0:T(8,128)S(1)}, u32[]{:S(2)}, u32[]{:S(2)}) collective-permute-start(f32[8,8,128]{2,1,0:T(8,128)S(1)} %get-tuple-element.37), channel_id=1, source_target_pairs={{4,0},{8,4},{12,8},{0,12},{5,1},{9,5},{13,9},{1,13},{6,2},{10,6},{... | collective-permute-start | bytes 98312 | tf_op jit(solution)/shard_map/ppermute | solution.py:629
  32.4 4.0 %collective-permute-start.10 = (f32[8,8,128]{2,1,0:T(8,128)S(1)}, f32[8,8,128]{2,1,0:T(8,128)S(1)}, u32[]{:S(2)}, u32[]{:S(2)}) collective-permute-start(f32[8,8,128]{2,1,0:T(8,128)S(1)} %get-tuple-element.38), channel_id=1, source_target_pairs={{12,0},{0,4},{4,8},{8,12},{13,1},{1,5},{5,9},{9,13},{14,2},{2,6},{... | collective-permute-start | bytes 98312 | tf_op jit(solution)/shard_map/ppermute | solution.py:629
  36.5 17.2 %collective-permute-start.12 = (f32[56,8,128]{2,1,0:T(8,128)S(1)}, f32[56,8,128]{2,1,0:T(8,128)S(1)}, u32[]{:S(2)}, u32[]{:S(2)}) collective-permute-start(f32[56,8,128]{2,1,0:T(8,128)S(1)} %get-tuple-element.39.full), channel_id=1, source_target_pairs={{240,0},{0,16},{16,32},{32,48},{48,64},{64,80},{80,96},{96,112},{1... | collective-permute-start | bytes 688136 | tf_op jit(solution)/shard_map/ppermute | solution.py:629
  41.8 11.9 %collective-permute-start.11 = (f32[56,8,128]{2,1,0:T(8,128)S(1)}, f32[56,8,128]{2,1,0:T(8,128)S(1)}, u32[]{:S(2)}, u32[]{:S(2)}) collective-permute-start(f32[56,8,128]{2,1,0:T(8,128)S(1)} %get-tuple-element.39.full), channel_id=1, source_target_pairs={{16,0},{32,16},{48,32},{64,48},{80,64},{96,80},{112,96},{128,112},... | collective-permute-start | bytes 688136 | tf_op jit(solution)/shard_map/ppermute | solution.py:629
  45.6 5.1 %collective-permute-start.13 = (f32[28,8,128]{2,1,0:T(8,128)S(1)}, f32[28,8,128]{2,1,0:T(8,128)S(1)}, u32[]{:S(2)}, u32[]{:S(2)}) collective-permute-start(f32[28,8,128]{2,1,0:T(8,128)S(1)} %get-tuple-element.40), channel_id=1, source_target_pairs={{32,0},{48,16},{64,32},{80,48},{96,64},{112,80},{128,96},{144,112}... | collective-permute-start | bytes 344072 | tf_op jit(solution)/shard_map/ppermute | solution.py:629
  48.1 5.6 %collective-permute-start.14 = (f32[28,8,128]{2,1,0:T(8,128)S(1)}, f32[28,8,128]{2,1,0:T(8,128)S(1)}, u32[]{:S(2)}, u32[]{:S(2)}) collective-permute-start(f32[28,8,128]{2,1,0:T(8,128)S(1)} %get-tuple-element.41), channel_id=1, source_target_pairs={{224,0},{240,16},{0,32},{16,48},{32,64},{48,80},{64,96},{80,112},{... | collective-permute-start | bytes 344072 | tf_op jit(solution)/shard_map/ppermute | solution.py:629

commit v11 on v10

--- a/solution.py
+++ b/solution.py
@@ -17,12 +17,12 @@
 HBM = pl.BlockSpec(memory_space=pltpu.HBM)
 
 
-def call(kernel, outs, *args, scratch=(), spaces=None, limit=24, pin=False):
+def call(kernel, outs, *args, scratch=(), spaces=None, limit=24, pin=False, out_space=VMEM):
     return pl.pallas_call(
         kernel,
         out_shape=[(pltpu.VMEM if pin else jax.ShapeDtypeStruct)(s, F32) for s in outs],
         in_specs=spaces or [VMEM] * len(args),
-        out_specs=[VMEM] * len(outs),
+        out_specs=[out_space] * len(outs),
         scratch_shapes=[pltpu.VMEM(s, F32) if isinstance(s, tuple) else s for s in scratch],
         compiler_params=pltpu.CompilerParams(vmem_limit_bytes=limit * 2**20),
     )(*args)
@@ -513,7 +513,7 @@
 
 def solve(
     got, a0, v0, a1, a2, pressure, left,
-    got3, t3, e1, g4, g3, g2, g1, g0, b3, w0,
+    got3, t3, e1, g4, g3, g2, g1, g0, b3, w0, final, rest, sems,
 ):
     a3, a4, d3, d4, r3, r4, s3, s4, e2, e3, e4, f2, q5 = (Held() for _ in range(13))
     gx, gy, gz = position()
@@ -615,13 +615,22 @@
     each(3, Z0 - 3, sweep0(0, 1))
     each(4, Z0 - 4, sweep0(1, 0))
 
-    def last(z):
-        v, beside = around(a0, lambda k: w0[0, k], z, z - 1, z + 1)
-        r = W / a0[RD, z] * (1.5 * a0[C, z] - v) + beside
-        pressure[z - H] = v[0:16, 0:128]
-        left[z - H] = r[0:16, 0:128]
-
-    each(H, H + 8, last)
+    for z in range(8):
+        final[z] = w0[0, z + H, 0:16, 0:128]
+    copies = [
+        pltpu.make_async_copy(final, pressure, sems.at[0]),
+        pltpu.make_async_copy(rest.at[0:4], left.at[0:4], sems.at[1]),
+        pltpu.make_async_copy(rest.at[4:8], left.at[4:8], sems.at[2]),
+    ]
+    copies[0].start()
+    for z in range(8):
+        v, beside = around(a0, lambda k: w0[0, k], z + H, z + H - 1, z + H + 1)
+        r = W / a0[RD, z + H] * (1.5 * a0[C, z + H] - v) + beside
+        rest[z] = r[0:16, 0:128]
+        if z % 4 == 3:
+            copies[1 + z // 4].start()
+    for copy in copies:
+        copy.wait()
 
 
 def shift(value, axis, by):
@@ -692,7 +701,9 @@
                 (5, 4, 32, 128), (5, 2, 32, 128), (2, 16, 24, 128),
                 (16, 128), (2, 32, 128), (4, 16, 128), (8, 32, 128), (2, 8, 32, 128),
                 (4, 48, 128), (2, Z0, 32, 256),
+                (8, 16, 128), (8, 16, 128), pltpu.SemaphoreType.DMA((3,)),
             ],
+            out_space=HBM,
         )
     )
 

time: 76.9 us -> 77 us (level)
  no operation moved by 1% of the time
where the time goes in v11:
time: 77 us; the launch traced here: 76.9 us
  starting transfers between devices  25.6 us (33%)
  waiting for transfers between devices  22.6 us (29%)
  blocking collectives  16.8 us (22%)
  Pallas kernels  10.8 us (14%)
  between operations  0.89 us (1%)
    ppermute x15, starting transfers between devices, shift(): lax.ppermute(value, axis, [((i + by) % count, i) for i in range(count)])  25.6 us
    ppermute x15, waiting for transfers between devices, shift(): lax.ppermute(value, axis, [((i + by) % count, i) for i in range(count)])  22.6 us
    all_to_all x1, blocking collectives, local(): lax.all_to_all(sent.reshape(64, 1, 640), ('gy', 'gx'), 0, 0)  16.8 us
    pallas_call x10, Pallas kernels, call(): pl.pallas_call(kernel, out_shape=[(pltpu.VMEM if pin else jax.ShapeDtypeS...  10.8 us
  transfers between devices with their start and end apart: 15, of which 13 were waited for; matrix products, arithmetic and copies ran while one was open for 0% of the time, Pallas kernels for 1%

profile of v11, /device:TPU:1, one launch (start us, length us, event | category | flops | bytes accessed | tf_op | source)
XLA Modules:
  0.0 76.9 jit_solution(5938837562789773341)
XLA Ops:
  0.7 1.0 %shard_map.77 = (f32[18,16,128]{2,1,0:T(8,128)S(1)}, f32[18,16,128]{2,1,0:T(8,128)S(1)}, f32[4,8,16,128]{3,2,1,0:T(8,128)S(1)}) custom-call(s32[8,16,128]{2,1,0:T(8,128)} %f.1, s32[8,16,128]{2,1,0:T(8,128)} %b.1, f32[8,16,128]{2,1,0:T(8,128)} %s.1, f32[8,16,128]{2,1,0:T(8,128)} %d.1), custom_call_target="tpu_custom_call" | custom-call | tf_op jit(solution)/shard_map/pallas_call | solution.py:21
  1.6 3.4 %collective-permute-start = (f32[18,16,128]{2,1,0:T(8,128)S(1)}, f32[18,16,128]{2,1,0:T(8,128)S(1)}, u32[]{:S(2)}, u32[]{:S(2)}) collective-permute-start(f32[18,16,128]{2,1,0:T(8,128)S(1)} %get-tuple-element.25), channel_id=1, source_target_pairs={{1,0},{2,1},{3,2},{0,3},{5,4},{6,5},{7,6},{4,7},{9,8},{10,9},{11,1... | collective-permute-start | bytes 442376 | tf_op jit(solution)/shard_map/ppermute | solution.py:638
  5.0 2.5 %collective-permute-done.above = f32[18,16,128]{2,1,0:T(8,128)S(1)} collective-permute-done((f32[18,16,128]{2,1,0:T(8,128)S(1)}, f32[18,16,128]{2,1,0:T(8,128)S(1)}, u32[]{:S(2)}, u32[]{:S(2)}) %collective-permute-start) | collective-permute-done | bytes 147488 | tf_op jit(solution)/shard_map/ppermute | solution.py:638
  7.5 3.1 %collective-permute-done.1.below = f32[18,16,128]{2,1,0:T(8,128)S(1)} collective-permute-done((f32[18,16,128]{2,1,0:T(8,128)S(1)}, f32[18,16,128]{2,1,0:T(8,128)S(1)}, u32[]{:S(2)}, u32[]{:S(2)}) %collective-permute-start.1) | collective-permute-done | bytes 147488 | tf_op jit(solution)/shard_map/ppermute | solution.py:638
  10.7 1.9 %collective-permute-start.2 = (f32[39,8,128]{2,1,0:T(8,128)S(1)}, f32[39,8,128]{2,1,0:T(8,128)S(1)}, u32[]{:S(2)}, u32[]{:S(2)}) collective-permute-start(f32[39,8,128]{2,1,0:T(8,128)S(1)} %get-tuple-element.29), channel_id=1, source_target_pairs={{16,0},{32,16},{48,32},{64,48},{80,64},{96,80},{112,96},{128,112},... | collective-permute-start | bytes 479240 | tf_op jit(solution)/shard_map/ppermute | solution.py:638
  12.6 1.5 %collective-permute-start.3 = (f32[39,8,128]{2,1,0:T(8,128)S(1)}, f32[39,8,128]{2,1,0:T(8,128)S(1)}, u32[]{:S(2)}, u32[]{:S(2)}) collective-permute-start(f32[39,8,128]{2,1,0:T(8,128)S(1)} %get-tuple-element.30), channel_id=1, source_target_pairs={{240,0},{0,16},{16,32},{32,48},{48,64},{64,80},{80,96},{96,112},{1... | collective-permute-start | bytes 479240 | tf_op jit(solution)/shard_map/ppermute | solution.py:638
  14.1 2.9 %collective-permute-done.2.ml = f32[39,8,128]{2,1,0:T(8,128)S(1)} collective-permute-done((f32[39,8,128]{2,1,0:T(8,128)S(1)}, f32[39,8,128]{2,1,0:T(8,128)S(1)}, u32[]{:S(2)}, u32[]{:S(2)}) %collective-permute-start.2) | collective-permute-done | bytes 159776 | tf_op jit(solution)/shard_map/ppermute | solution.py:638
  17.1 0.5 collective-permute-done.3.mh
  17.6 0.4 shard_map.79
  17.9 2.8 %collective-permute-start.4 = (f32[12,8,128]{2,1,0:T(8,128)S(1)}, f32[12,8,128]{2,1,0:T(8,128)S(1)}, u32[]{:S(2)}, u32[]{:S(2)}) collective-permute-start(f32[12,8,128]{2,1,0:T(8,128)S(1)} %get-tuple-element.33), channel_id=1, source_target_pairs={{4,0},{8,4},{12,8},{0,12},{5,1},{9,5},{13,9},{1,13},{6,2},{10,6},{... | collective-permute-start | bytes 147464 | tf_op jit(solution)/shard_map/ppermute | solution.py:638
  20.9 0.5 shard_map.80.main
  21.4 0.5 collective-permute-done.4.yl
  21.9 3.0 %collective-permute-done.5.yh = f32[12,8,128]{2,1,0:T(8,128)S(1)} collective-permute-done((f32[12,8,128]{2,1,0:T(8,128)S(1)}, f32[12,8,128]{2,1,0:T(8,128)S(1)}, u32[]{:S(2)}, u32[]{:S(2)}) %collective-permute-start.5) | collective-permute-done | bytes 49184 | tf_op jit(solution)/shard_map/ppermute | solution.py:638
  24.9 2.1 %shard_map.81 = (f32[6,18,32,256]{3,2,1,0:T(8,128)S(1)}, f32[5,2,8,128]{3,2,1,0:T(8,128)S(1)}) custom-call(f32[16,128]{1,0:T(8,128)S(1)} %broadcast_in_dim.2.tables, f32[5,18,32,128]{3,2,1,0:T(8,128)S(1)} %shard_map.80.main, f32[12,8,128]{2,1,0:T(8,128)S(1)} %collective-permute-done.4.yl, f32[12,8,128]{2,1,0:T(8,128)S(1)} %collective-permute-done.5.yh), custom_call_target="tpu_custom_call" | custom-call | tf_op jit(solution)/shard_map/pallas_call | solution.py:21
  27.1 1.5 %collective-permute-start.7 = (f32[5,2,8,128]{3,2,1,0:T(8,128)S(1)}, f32[5,2,8,128]{3,2,1,0:T(8,128)S(1)}, u32[]{:S(2)}, u32[]{:S(2)}) collective-permute-start(f32[5,2,8,128]{3,2,1,0:T(8,128)S(1)} %get-tuple-element.35.own), channel_id=1, source_target_pairs={{2,0},{3,1},{0,2},{1,3},{6,4},{7,5},{4,6},{5,7},{10,8},{11,9},{8,1... | collective-permute-start | bytes 122888 | tf_op jit(solution)/shard_map/ppermute | solution.py:638
  28.6 1.2 %collective-permute-start.6 = (f32[5,2,8,128]{3,2,1,0:T(8,128)S(1)}, f32[5,2,8,128]{3,2,1,0:T(8,128)S(1)}, u32[]{:S(2)}, u32[]{:S(2)}) collective-permute-start(f32[5,2,8,128]{3,2,1,0:T(8,128)S(1)} %get-tuple-element.35.own), channel_id=1, source_target_pairs={{1,0},{2,1},{3,2},{0,3},{5,4},{6,5},{7,6},{4,7},{9,8},{10,9},{11,1... | collective-permute-start | bytes 122888 | tf_op jit(solution)/shard_map/ppermute | solution.py:638
  29.8 1.4 %collective-permute-done.8.b3 = f32[5,2,8,128]{3,2,1,0:T(8,128)S(1)} collective-permute-done((f32[5,2,8,128]{3,2,1,0:T(8,128)S(1)}, f32[5,2,8,128]{3,2,1,0:T(8,128)S(1)}, u32[]{:S(2)}, u32[]{:S(2)}) %collective-permute-start.8) | collective-permute-done | bytes 40992 | tf_op jit(solution)/shard_map/ppermute | solution.py:638
  31.2 0.4 collective-permute-done.7.b2
  31.6 0.6 collective-permute-done.6.b1
  32.3 0.1 collective-permute-start.9
  32.4 1.4 %collective-permute-start.10 = (f32[8,8,128]{2,1,0:T(8,128)S(1)}, f32[8,8,128]{2,1,0:T(8,128)S(1)}, u32[]{:S(2)}, u32[]{:S(2)}) collective-permute-start(f32[8,8,128]{2,1,0:T(8,128)S(1)} %get-tuple-element.38), channel_id=1, source_target_pairs={{12,0},{0,4},{4,8},{8,12},{13,1},{1,5},{5,9},{9,13},{14,2},{2,6},{... | collective-permute-start | bytes 98312 | tf_op jit(solution)/shard_map/ppermute | solution.py:638
  33.9 1.3 %collective-permute-done.9.right = f32[8,8,128]{2,1,0:T(8,128)S(1)} collective-permute-done((f32[8,8,128]{2,1,0:T(8,128)S(1)}, f32[8,8,128]{2,1,0:T(8,128)S(1)}, u32[]{:S(2)}, u32[]{:S(2)}) %collective-permute-start.9) | collective-permute-done | bytes 32800 | tf_op jit(solution)/shard_map/ppermute | solution.py:638
  35.2 1.3 %collective-permute-done.10.left = f32[8,8,128]{2,1,0:T(8,128)S(1)} collective-permute-done((f32[8,8,128]{2,1,0:T(8,128)S(1)}, f32[8,8,128]{2,1,0:T(8,128)S(1)}, u32[]{:S(2)}, u32[]{:S(2)}) %collective-permute-start.10) | collective-permute-done | bytes 32800 | tf_op jit(solution)/shard_map/ppermute | solution.py:638
  36.5 5.3 %collective-permute-start.12 = (f32[56,8,128]{2,1,0:T(8,128)S(1)}, f32[56,8,128]{2,1,0:T(8,128)S(1)}, u32[]{:S(2)}, u32[]{:S(2)}) collective-permute-start(f32[56,8,128]{2,1,0:T(8,128)S(1)} %get-tuple-element.39.full), channel_id=1, source_target_pairs={{240,0},{0,16},{16,32},{32,48},{48,64},{64,80},{80,96},{96,112},{1... | collective-permute-start | bytes 688136 | tf_op jit(solution)/shard_map/ppermute | solution.py:638
  41.8 3.8 %collective-permute-start.11 = (f32[56,8,128]{2,1,0:T(8,128)S(1)}, f32[56,8,128]{2,1,0:T(8,128)S(1)}, u32[]{:S(2)}, u32[]{:S(2)}) collective-permute-start(f32[56,8,128]{2,1,0:T(8,128)S(1)} %get-tuple-element.39.full), channel_id=1, source_target_pairs={{16,0},{32,16},{48,32},{64,48},{80,64},{96,80},{112,96},{128,112},... | collective-permute-start | bytes 688136 | tf_op jit(solution)/shard_map/ppermute | solution.py:638
  45.6 2.6 %collective-permute-start.13 = (f32[28,8,128]{2,1,0:T(8,128)S(1)}, f32[28,8,128]{2,1,0:T(8,128)S(1)}, u32[]{:S(2)}, u32[]{:S(2)}) collective-permute-start(f32[28,8,128]{2,1,0:T(8,128)S(1)} %get-tuple-element.40), channel_id=1, source_target_pairs={{32,0},{48,16},{64,32},{80,48},{96,64},{112,80},{128,96},{144,112}... | collective-permute-start | bytes 344072 | tf_op jit(solution)/shard_map/ppermute | solution.py:638
  48.2 0.5 shard_map.84.before.v0
  48.6 2.0 %collective-permute-done.13.xr2 = f32[28,8,128]{2,1,0:T(8,128)S(1)} collective-permute-done((f32[28,8,128]{2,1,0:T(8,128)S(1)}, f32[28,8,128]{2,1,0:T(8,128)S(1)}, u32[]{:S(2)}, u32[]{:S(2)}) %collective-permute-start.13) | collective-permute-done | bytes 114720 | tf_op jit(solution)/shard_map/ppermute | solution.py:638
  50.6 3.1 %collective-permute-done.14.xl2 = f32[28,8,128]{2,1,0:T(8,128)S(1)} collective-permute-done((f32[28,8,128]{2,1,0:T(8,128)S(1)}, f32[28,8,128]{2,1,0:T(8,128)S(1)}, u32[]{:S(2)}, u32[]{:S(2)}) %collective-permute-start.14) | collective-permute-done | bytes 114720 | tf_op jit(solution)/shard_map/ppermute | solution.py:638
  53.7 2.4 %shard_map.85 = (f32[6,16,32,128]{3,2,1,0:T(8,128)S(1)}, f32[6,8,16,128]{3,2,1,0:T(8,128)S(1)}, f32[320,128]{1,0:T(8,128)S(1)}) custom-call(f32[56,8,128]{2,1,0:T(8,128)S(1)} %get-tuple-element.39.full, f32[56,8,128]{2,1,0:T(8,128)S(1)} %collective-permute-done.11.xr, f32[56,8,128]{2,1,0:T(8,128)S(1)} %collective-permute-done.12.xl, ...), custom_call_target="tpu_custom_call" | custom-call | tf_op jit(solution)/shard_map/pallas_call | solution.py:21
  56.2 16.8 %all_to_all.5 = f32[64,1,640]{2,1,0:T(1,128)S(1)} all-to-all(f32[64,1,640]{2,1,0:T(1,128)S(1)} %bitcast.3), channel_id=1, replica_groups=mesh['gx'=16,'gy'=4,'gz'=4] {'gy','gx'}, dimensions={0} | all-to-all | bytes 327680 | tf_op jit(solution)/shard_map/all_to_all | solution.py:694
  73.0 3.8 %shard_map.86 = (f32[8,16,128]{2,1,0:T(8,128)}, f32[8,16,128]{2,1,0:T(8,128)}) custom-call(f32[320,128]{1,0:T(8,128)S(1)} %bitcast.2, f32[6,18,32,256]{3,2,1,0:T(8,128)S(1)} %get-tuple-element.42.a0, f32[4,32,256]{2,1,0:T(8,128)S(1)} %shard_map.84.before.v0, f32[6,16,32,128]{3,2,1,0:T(8,128)S(1)} %get-tuple-element.44.a1, ...), custom_call_target="tpu_custom_call" | custom-call | tf_op jit(solution)/shard_map/pallas_call | solution.py:21
  (15 shorter events, 0.5 us)
Async XLA Ops:
  0.6 20.1 %copy-start = (f32[8]{0:T(128)S(1)}, f32[8]{0:T(128)}, u32[]{:S(2)}) copy-start(f32[8]{0:T(128)} %param.9) | copy-start | bytes 100
  0.6 20.1 %copy-start.1 = (f32[8]{0:T(128)S(1)}, f32[8]{0:T(128)}, u32[]{:S(2)}) copy-start(f32[8]{0:T(128)} %param.8) | copy-start | bytes 100
  1.6 5.9 %collective-permute-start = (f32[18,16,128]{2,1,0:T(8,128)S(1)}, f32[18,16,128]{2,1,0:T(8,128)S(1)}, u32[]{:S(2)}, u32[]{:S(2)}) collective-permute-start(f32[18,16,128]{2,1,0:T(8,128)S(1)} %get-tuple-element.25), channel_id=1, source_target_pairs={{1,0},{2,1},{3,2},{0,3},{5,4},{6,5},{7,6},{4,7},{9,8},{10,9},{11,1... | collective-permute-start | bytes 442376 | tf_op jit(solution)/shard_map/ppermute | solution.py:638
  5.0 5.6 %collective-permute-start.1 = (f32[18,16,128]{2,1,0:T(8,128)S(1)}, f32[18,16,128]{2,1,0:T(8,128)S(1)}, u32[]{:S(2)}, u32[]{:S(2)}) collective-permute-start(f32[18,16,128]{2,1,0:T(8,128)S(1)} %get-tuple-element.26), channel_id=1, source_target_pairs={{3,0},{0,1},{1,2},{2,3},{7,4},{4,5},{5,6},{6,7},{11,8},{8,9},{9,10... | collective-permute-start | bytes 442376 | tf_op jit(solution)/shard_map/ppermute | solution.py:638
  10.7 6.4 %collective-permute-start.2 = (f32[39,8,128]{2,1,0:T(8,128)S(1)}, f32[39,8,128]{2,1,0:T(8,128)S(1)}, u32[]{:S(2)}, u32[]{:S(2)}) collective-permute-start(f32[39,8,128]{2,1,0:T(8,128)S(1)} %get-tuple-element.29), channel_id=1, source_target_pairs={{16,0},{32,16},{48,32},{64,48},{80,64},{96,80},{112,96},{128,112},... | collective-permute-start | bytes 479240 | tf_op jit(solution)/shard_map/ppermute | solution.py:638
  12.6 5.0 %collective-permute-start.3 = (f32[39,8,128]{2,1,0:T(8,128)S(1)}, f32[39,8,128]{2,1,0:T(8,128)S(1)}, u32[]{:S(2)}, u32[]{:S(2)}) collective-permute-start(f32[39,8,128]{2,1,0:T(8,128)S(1)} %get-tuple-element.30), channel_id=1, source_target_pairs={{240,0},{0,16},{16,32},{32,48},{48,64},{64,80},{80,96},{96,112},{1... | collective-permute-start | bytes 479240 | tf_op jit(solution)/shard_map/ppermute | solution.py:638
  17.9 4.0 %collective-permute-start.4 = (f32[12,8,128]{2,1,0:T(8,128)S(1)}, f32[12,8,128]{2,1,0:T(8,128)S(1)}, u32[]{:S(2)}, u32[]{:S(2)}) collective-permute-start(f32[12,8,128]{2,1,0:T(8,128)S(1)} %get-tuple-element.33), channel_id=1, source_target_pairs={{4,0},{8,4},{12,8},{0,12},{5,1},{9,5},{13,9},{1,13},{6,2},{10,6},{... | collective-permute-start | bytes 147464 | tf_op jit(solution)/shard_map/ppermute | solution.py:638
  20.8 4.2 %collective-permute-start.5 = (f32[12,8,128]{2,1,0:T(8,128)S(1)}, f32[12,8,128]{2,1,0:T(8,128)S(1)}, u32[]{:S(2)}, u32[]{:S(2)}) collective-permute-start(f32[12,8,128]{2,1,0:T(8,128)S(1)} %get-tuple-element.34), channel_id=1, source_target_pairs={{12,0},{0,4},{4,8},{8,12},{13,1},{1,5},{5,9},{9,13},{14,2},{2,6},{... | collective-permute-start | bytes 147464 | tf_op jit(solution)/shard_map/ppermute | solution.py:638
  27.1 4.2 %collective-permute-start.8 = (f32[5,2,8,128]{3,2,1,0:T(8,128)S(1)}, f32[5,2,8,128]{3,2,1,0:T(8,128)S(1)}, u32[]{:S(2)}, u32[]{:S(2)}) collective-permute-start(f32[5,2,8,128]{3,2,1,0:T(8,128)S(1)} %get-tuple-element.35.own), channel_id=1, source_target_pairs={{3,0},{0,1},{1,2},{2,3},{7,4},{4,5},{5,6},{6,7},{11,8},{8,9},{9,10... | collective-permute-start | bytes 122888 | tf_op jit(solution)/shard_map/ppermute | solution.py:638
  27.1 4.5 %collective-permute-start.7 = (f32[5,2,8,128]{3,2,1,0:T(8,128)S(1)}, f32[5,2,8,128]{3,2,1,0:T(8,128)S(1)}, u32[]{:S(2)}, u32[]{:S(2)}) collective-permute-start(f32[5,2,8,128]{3,2,1,0:T(8,128)S(1)} %get-tuple-element.35.own), channel_id=1, source_target_pairs={{2,0},{3,1},{0,2},{1,3},{6,4},{7,5},{4,6},{5,7},{10,8},{11,9},{8,1... | collective-permute-start | bytes 122888 | tf_op jit(solution)/shard_map/ppermute | solution.py:638
  28.6 3.6 %collective-permute-start.6 = (f32[5,2,8,128]{3,2,1,0:T(8,128)S(1)}, f32[5,2,8,128]{3,2,1,0:T(8,128)S(1)}, u32[]{:S(2)}, u32[]{:S(2)}) collective-permute-start(f32[5,2,8,128]{3,2,1,0:T(8,128)S(1)} %get-tuple-element.35.own), channel_id=1, source_target_pairs={{1,0},{2,1},{3,2},{0,3},{5,4},{6,5},{7,6},{4,7},{9,8},{10,9},{11,1... | collective-permute-start | bytes 122888 | tf_op jit(solution)/shard_map/ppermute | solution.py:638
  32.3 2.8 %collective-permute-start.9 = (f32[8,8,128]{2,1,0:T(8,128)S(1)}, f32[8,8,128]{2,1,0:T(8,128)S(1)}, u32[]{:S(2)}, u32[]{:S(2)}) collective-permute-start(f32[8,8,128]{2,1,0:T(8,128)S(1)} %get-tuple-element.37), channel_id=1, source_target_pairs={{4,0},{8,4},{12,8},{0,12},{5,1},{9,5},{13,9},{1,13},{6,2},{10,6},{... | collective-permute-start | bytes 98312 | tf_op jit(solution)/shard_map/ppermute | solution.py:638
  32.4 4.0 %collective-permute-start.10 = (f32[8,8,128]{2,1,0:T(8,128)S(1)}, f32[8,8,128]{2,1,0:T(8,128)S(1)}, u32[]{:S(2)}, u32[]{:S(2)}) collective-permute-start(f32[8,8,128]{2,1,0:T(8,128)S(1)} %get-tuple-element.38), channel_id=1, source_target_pairs={{12,0},{0,4},{4,8},{8,12},{13,1},{1,5},{5,9},{9,13},{14,2},{2,6},{... | collective-permute-start | bytes 98312 | tf_op jit(solution)/shard_map/ppermute | solution.py:638
  36.5 17.2 %collective-permute-start.12 = (f32[56,8,128]{2,1,0:T(8,128)S(1)}, f32[56,8,128]{2,1,0:T(8,128)S(1)}, u32[]{:S(2)}, u32[]{:S(2)}) collective-permute-start(f32[56,8,128]{2,1,0:T(8,128)S(1)} %get-tuple-element.39.full), channel_id=1, source_target_pairs={{240,0},{0,16},{16,32},{32,48},{48,64},{64,80},{80,96},{96,112},{1... | collective-permute-start | bytes 688136 | tf_op jit(solution)/shard_map/ppermute | solution.py:638
  41.8 11.9 %collective-permute-start.11 = (f32[56,8,128]{2,1,0:T(8,128)S(1)}, f32[56,8,128]{2,1,0:T(8,128)S(1)}, u32[]{:S(2)}, u32[]{:S(2)}) collective-permute-start(f32[56,8,128]{2,1,0:T(8,128)S(1)} %get-tuple-element.39.full), channel_id=1, source_target_pairs={{16,0},{32,16},{48,32},{64,48},{80,64},{96,80},{112,96},{128,112},... | collective-permute-start | bytes 688136 | tf_op jit(solution)/shard_map/ppermute | solution.py:638
  45.6 5.1 %collective-permute-start.13 = (f32[28,8,128]{2,1,0:T(8,128)S(1)}, f32[28,8,128]{2,1,0:T(8,128)S(1)}, u32[]{:S(2)}, u32[]{:S(2)}) collective-permute-start(f32[28,8,128]{2,1,0:T(8,128)S(1)} %get-tuple-element.40), channel_id=1, source_target_pairs={{32,0},{48,16},{64,32},{80,48},{96,64},{112,80},{128,96},{144,112}... | collective-permute-start | bytes 344072 | tf_op jit(solution)/shard_map/ppermute | solution.py:638
  48.1 5.6 %collective-permute-start.14 = (f32[28,8,128]{2,1,0:T(8,128)S(1)}, f32[28,8,128]{2,1,0:T(8,128)S(1)}, u32[]{:S(2)}, u32[]{:S(2)}) collective-permute-start(f32[28,8,128]{2,1,0:T(8,128)S(1)} %get-tuple-element.41), channel_id=1, source_target_pairs={{224,0},{240,16},{0,32},{16,48},{32,64},{48,80},{64,96},{80,112},{... | collective-permute-start | bytes 344072 | tf_op jit(solution)/shard_map/ppermute | solution.py:638

commit v12 on v10

--- a/solution.py
+++ b/solution.py
@@ -399,7 +399,7 @@
         field[n] = smoothed(a, lambda k: a[C, k], z, z - 1, z + 1)
 
 
-def pack_y1(own, b1, b2, b3, stack, lo, hi):
+def pack_y1(own, b1, b3, b2, stack, lo, hi):
     lane = iota((8, 128), 1)
     block, last = (lane % 64) // 12, ((lane + 12) % 64) // 12
     blocks = (own, b1, b2, b3)
@@ -668,7 +668,7 @@
         outer0, [(4, 32, 256)], tables, main, yl, yh, a0,
         scratch=[(4, Z0, 32, 128), (5, Z0, 32, 128), (Z0, 32, 128), (6, Z0, 32, 256)],
     )
-    blocks = [shift(packed, "gz", n) for n in (1, 2, 3)]
+    blocks = [shift(packed, "gz", n) for n in (1, 3, 2)]
     stack, lo, hi = call(pack_y1, [(40, 8, 128)] + [(8, 8, 128)] * 2, packed, *blocks)
     right, left = shift(lo, "gy", 1), shift(hi, "gy", -1)
     full, lo, hi = call(pack_x1, [(56, 8, 128)] + [(28, 8, 128)] * 2, stack, right, left)

time: 76.9 us -> 76.1 us (0.990)
  transfers between devices with their start and end apart: 15 -> 15, of which waited for: 13 -> 12; matrix products, arithmetic and copies ran while one was open for 0% -> 0% of each run, Pallas kernels for 1% -> 1%
where the time goes in v12:
time: 76.1 us; the launch traced here: 75.9 us
  starting transfers between devices  25.4 us (33%)
  waiting for transfers between devices  22 us (29%)
  blocking collectives  16.8 us (22%)
  Pallas kernels  10.8 us (14%)
    ppermute x15, starting transfers between devices, shift(): lax.ppermute(value, axis, [((i + by) % count, i) for i in range(count)])  25.4 us
    ppermute x15, waiting for transfers between devices, shift(): lax.ppermute(value, axis, [((i + by) % count, i) for i in range(count)])  22 us
    all_to_all x1, blocking collectives, local(): lax.all_to_all(sent.reshape(64, 1, 640), ('gy', 'gx'), 0, 0)  16.8 us
    pallas_call x10, Pallas kernels, call(): pl.pallas_call(kernel, out_shape=[(pltpu.VMEM if pin else jax.ShapeDtypeS...  10.8 us
  transfers between devices with their start and end apart: 15, of which 12 were waited for; matrix products, arithmetic and copies ran while one was open for 0% of the time, Pallas kernels for 1%

profile of v12, /device:TPU:1, one launch (start us, length us, event | category | flops | bytes accessed | tf_op | source)
XLA Modules:
  0.0 75.9 jit_solution(15281478660546225252)
XLA Ops:
  0.7 1.0 %shard_map.77 = (f32[18,16,128]{2,1,0:T(8,128)S(1)}, f32[18,16,128]{2,1,0:T(8,128)S(1)}, f32[4,8,16,128]{3,2,1,0:T(8,128)S(1)}) custom-call(s32[8,16,128]{2,1,0:T(8,128)} %f.1, s32[8,16,128]{2,1,0:T(8,128)} %b.1, f32[8,16,128]{2,1,0:T(8,128)} %s.1, f32[8,16,128]{2,1,0:T(8,128)} %d.1), custom_call_target="tpu_custom_call" | custom-call | tf_op jit(solution)/shard_map/pallas_call | solution.py:21
  1.6 3.4 %collective-permute-start = (f32[18,16,128]{2,1,0:T(8,128)S(1)}, f32[18,16,128]{2,1,0:T(8,128)S(1)}, u32[]{:S(2)}, u32[]{:S(2)}) collective-permute-start(f32[18,16,128]{2,1,0:T(8,128)S(1)} %get-tuple-element.25), channel_id=1, source_target_pairs={{1,0},{2,1},{3,2},{0,3},{5,4},{6,5},{7,6},{4,7},{9,8},{10,9},{11,1... | collective-permute-start | bytes 442376 | tf_op jit(solution)/shard_map/ppermute | solution.py:629
  5.0 2.5 %collective-permute-done.above = f32[18,16,128]{2,1,0:T(8,128)S(1)} collective-permute-done((f32[18,16,128]{2,1,0:T(8,128)S(1)}, f32[18,16,128]{2,1,0:T(8,128)S(1)}, u32[]{:S(2)}, u32[]{:S(2)}) %collective-permute-start) | collective-permute-done | bytes 147488 | tf_op jit(solution)/shard_map/ppermute | solution.py:629
  7.5 3.1 %collective-permute-done.1.below = f32[18,16,128]{2,1,0:T(8,128)S(1)} collective-permute-done((f32[18,16,128]{2,1,0:T(8,128)S(1)}, f32[18,16,128]{2,1,0:T(8,128)S(1)}, u32[]{:S(2)}, u32[]{:S(2)}) %collective-permute-start.1) | collective-permute-done | bytes 147488 | tf_op jit(solution)/shard_map/ppermute | solution.py:629
  10.7 1.9 %collective-permute-start.2 = (f32[39,8,128]{2,1,0:T(8,128)S(1)}, f32[39,8,128]{2,1,0:T(8,128)S(1)}, u32[]{:S(2)}, u32[]{:S(2)}) collective-permute-start(f32[39,8,128]{2,1,0:T(8,128)S(1)} %get-tuple-element.29), channel_id=1, source_target_pairs={{16,0},{32,16},{48,32},{64,48},{80,64},{96,80},{112,96},{128,112},... | collective-permute-start | bytes 479240 | tf_op jit(solution)/shard_map/ppermute | solution.py:629
  12.6 1.5 %collective-permute-start.3 = (f32[39,8,128]{2,1,0:T(8,128)S(1)}, f32[39,8,128]{2,1,0:T(8,128)S(1)}, u32[]{:S(2)}, u32[]{:S(2)}) collective-permute-start(f32[39,8,128]{2,1,0:T(8,128)S(1)} %get-tuple-element.30), channel_id=1, source_target_pairs={{240,0},{0,16},{16,32},{32,48},{48,64},{64,80},{80,96},{96,112},{1... | collective-permute-start | bytes 479240 | tf_op jit(solution)/shard_map/ppermute | solution.py:629
  14.1 2.9 %collective-permute-done.2.ml = f32[39,8,128]{2,1,0:T(8,128)S(1)} collective-permute-done((f32[39,8,128]{2,1,0:T(8,128)S(1)}, f32[39,8,128]{2,1,0:T(8,128)S(1)}, u32[]{:S(2)}, u32[]{:S(2)}) %collective-permute-start.2) | collective-permute-done | bytes 159776 | tf_op jit(solution)/shard_map/ppermute | solution.py:629
  17.1 0.5 collective-permute-done.3.mh
  17.6 0.4 shard_map.79
  17.9 2.8 %collective-permute-start.4 = (f32[12,8,128]{2,1,0:T(8,128)S(1)}, f32[12,8,128]{2,1,0:T(8,128)S(1)}, u32[]{:S(2)}, u32[]{:S(2)}) collective-permute-start(f32[12,8,128]{2,1,0:T(8,128)S(1)} %get-tuple-element.33), channel_id=1, source_target_pairs={{4,0},{8,4},{12,8},{0,12},{5,1},{9,5},{13,9},{1,13},{6,2},{10,6},{... | collective-permute-start | bytes 147464 | tf_op jit(solution)/shard_map/ppermute | solution.py:629
  20.9 0.5 shard_map.80.main
  21.4 0.5 collective-permute-done.4.yl
  21.9 3.0 %collective-permute-done.5.yh = f32[12,8,128]{2,1,0:T(8,128)S(1)} collective-permute-done((f32[12,8,128]{2,1,0:T(8,128)S(1)}, f32[12,8,128]{2,1,0:T(8,128)S(1)}, u32[]{:S(2)}, u32[]{:S(2)}) %collective-permute-start.5) | collective-permute-done | bytes 49184 | tf_op jit(solution)/shard_map/ppermute | solution.py:629
  24.9 2.1 %shard_map.81 = (f32[6,18,32,256]{3,2,1,0:T(8,128)S(1)}, f32[5,2,8,128]{3,2,1,0:T(8,128)S(1)}) custom-call(f32[16,128]{1,0:T(8,128)S(1)} %broadcast_in_dim.2.tables, f32[5,18,32,128]{3,2,1,0:T(8,128)S(1)} %shard_map.80.main, f32[12,8,128]{2,1,0:T(8,128)S(1)} %collective-permute-done.4.yl, f32[12,8,128]{2,1,0:T(8,128)S(1)} %collective-permute-done.5.yh), custom_call_target="tpu_custom_call" | custom-call | tf_op jit(solution)/shard_map/pallas_call | solution.py:21
  27.2 0.9 %collective-permute-start.7 = (f32[5,2,8,128]{3,2,1,0:T(8,128)S(1)}, f32[5,2,8,128]{3,2,1,0:T(8,128)S(1)}, u32[]{:S(2)}, u32[]{:S(2)}) collective-permute-start(f32[5,2,8,128]{3,2,1,0:T(8,128)S(1)} %get-tuple-element.35.own), channel_id=1, source_target_pairs={{3,0},{0,1},{1,2},{2,3},{7,4},{4,5},{5,6},{6,7},{11,8},{8,9},{9,10... | collective-permute-start | bytes 122888 | tf_op jit(solution)/shard_map/ppermute | solution.py:629
  28.0 1.9 %collective-permute-start.6 = (f32[5,2,8,128]{3,2,1,0:T(8,128)S(1)}, f32[5,2,8,128]{3,2,1,0:T(8,128)S(1)}, u32[]{:S(2)}, u32[]{:S(2)}) collective-permute-start(f32[5,2,8,128]{3,2,1,0:T(8,128)S(1)} %get-tuple-element.35.own), channel_id=1, source_target_pairs={{1,0},{2,1},{3,2},{0,3},{5,4},{6,5},{7,6},{4,7},{9,8},{10,9},{11,1... | collective-permute-start | bytes 122888 | tf_op jit(solution)/shard_map/ppermute | solution.py:629
  29.9 1.7 %collective-permute-done.8.b2 = f32[5,2,8,128]{3,2,1,0:T(8,128)S(1)} collective-permute-done((f32[5,2,8,128]{3,2,1,0:T(8,128)S(1)}, f32[5,2,8,128]{3,2,1,0:T(8,128)S(1)}, u32[]{:S(2)}, u32[]{:S(2)}) %collective-permute-start.8) | collective-permute-done | bytes 40992 | tf_op jit(solution)/shard_map/ppermute | solution.py:629
  31.6 0.1 collective-permute-done.7.b3
  31.7 0.1 shard_map.82
  31.8 0.1 collective-permute-start.9
  32.0 1.4 %collective-permute-start.10 = (f32[8,8,128]{2,1,0:T(8,128)S(1)}, f32[8,8,128]{2,1,0:T(8,128)S(1)}, u32[]{:S(2)}, u32[]{:S(2)}) collective-permute-start(f32[8,8,128]{2,1,0:T(8,128)S(1)} %get-tuple-element.38), channel_id=1, source_target_pairs={{12,0},{0,4},{4,8},{8,12},{13,1},{1,5},{5,9},{9,13},{14,2},{2,6},{... | collective-permute-start | bytes 98312 | tf_op jit(solution)/shard_map/ppermute | solution.py:629
  33.4 1.3 %collective-permute-done.9.right = f32[8,8,128]{2,1,0:T(8,128)S(1)} collective-permute-done((f32[8,8,128]{2,1,0:T(8,128)S(1)}, f32[8,8,128]{2,1,0:T(8,128)S(1)}, u32[]{:S(2)}, u32[]{:S(2)}) %collective-permute-start.9) | collective-permute-done | bytes 32800 | tf_op jit(solution)/shard_map/ppermute | solution.py:629
  34.7 1.3 %collective-permute-done.10.left = f32[8,8,128]{2,1,0:T(8,128)S(1)} collective-permute-done((f32[8,8,128]{2,1,0:T(8,128)S(1)}, f32[8,8,128]{2,1,0:T(8,128)S(1)}, u32[]{:S(2)}, u32[]{:S(2)}) %collective-permute-start.10) | collective-permute-done | bytes 32800 | tf_op jit(solution)/shard_map/ppermute | solution.py:629
  36.0 5.0 %collective-permute-start.12 = (f32[56,8,128]{2,1,0:T(8,128)S(1)}, f32[56,8,128]{2,1,0:T(8,128)S(1)}, u32[]{:S(2)}, u32[]{:S(2)}) collective-permute-start(f32[56,8,128]{2,1,0:T(8,128)S(1)} %get-tuple-element.39.full), channel_id=1, source_target_pairs={{240,0},{0,16},{16,32},{32,48},{48,64},{64,80},{80,96},{96,112},{1... | collective-permute-start | bytes 688136 | tf_op jit(solution)/shard_map/ppermute | solution.py:629
  41.0 3.8 %collective-permute-start.11 = (f32[56,8,128]{2,1,0:T(8,128)S(1)}, f32[56,8,128]{2,1,0:T(8,128)S(1)}, u32[]{:S(2)}, u32[]{:S(2)}) collective-permute-start(f32[56,8,128]{2,1,0:T(8,128)S(1)} %get-tuple-element.39.full), channel_id=1, source_target_pairs={{16,0},{32,16},{48,32},{64,48},{80,64},{96,80},{112,96},{128,112},... | collective-permute-start | bytes 688136 | tf_op jit(solution)/shard_map/ppermute | solution.py:629
  44.8 2.6 %collective-permute-start.13 = (f32[28,8,128]{2,1,0:T(8,128)S(1)}, f32[28,8,128]{2,1,0:T(8,128)S(1)}, u32[]{:S(2)}, u32[]{:S(2)}) collective-permute-start(f32[28,8,128]{2,1,0:T(8,128)S(1)} %get-tuple-element.40), channel_id=1, source_target_pairs={{32,0},{48,16},{64,32},{80,48},{96,64},{112,80},{128,96},{144,112}... | collective-permute-start | bytes 344072 | tf_op jit(solution)/shard_map/ppermute | solution.py:629
  47.4 0.5 shard_map.84.before.v0
  47.9 2.0 %collective-permute-done.13.xr2 = f32[28,8,128]{2,1,0:T(8,128)S(1)} collective-permute-done((f32[28,8,128]{2,1,0:T(8,128)S(1)}, f32[28,8,128]{2,1,0:T(8,128)S(1)}, u32[]{:S(2)}, u32[]{:S(2)}) %collective-permute-start.13) | collective-permute-done | bytes 114720 | tf_op jit(solution)/shard_map/ppermute | solution.py:629
  49.9 3.1 %collective-permute-done.14.xl2 = f32[28,8,128]{2,1,0:T(8,128)S(1)} collective-permute-done((f32[28,8,128]{2,1,0:T(8,128)S(1)}, f32[28,8,128]{2,1,0:T(8,128)S(1)}, u32[]{:S(2)}, u32[]{:S(2)}) %collective-permute-start.14) | collective-permute-done | bytes 114720 | tf_op jit(solution)/shard_map/ppermute | solution.py:629
  53.0 2.4 %shard_map.85 = (f32[6,16,32,128]{3,2,1,0:T(8,128)S(1)}, f32[6,8,16,128]{3,2,1,0:T(8,128)S(1)}, f32[320,128]{1,0:T(8,128)S(1)}) custom-call(f32[56,8,128]{2,1,0:T(8,128)S(1)} %get-tuple-element.39.full, f32[56,8,128]{2,1,0:T(8,128)S(1)} %collective-permute-done.11.xr, f32[56,8,128]{2,1,0:T(8,128)S(1)} %collective-permute-done.12.xl, ...), custom_call_target="tpu_custom_call" | custom-call | tf_op jit(solution)/shard_map/pallas_call | solution.py:21
  55.4 16.8 %all_to_all.5 = f32[64,1,640]{2,1,0:T(1,128)S(1)} all-to-all(f32[64,1,640]{2,1,0:T(1,128)S(1)} %bitcast.3), channel_id=1, replica_groups=mesh['gx'=16,'gy'=4,'gz'=4] {'gy','gx'}, dimensions={0} | all-to-all | bytes 327680 | tf_op jit(solution)/shard_map/all_to_all | solution.py:685
  72.2 3.7 %shard_map.86 = (f32[8,16,128]{2,1,0:T(8,128)}, f32[8,16,128]{2,1,0:T(8,128)}) custom-call(f32[320,128]{1,0:T(8,128)S(1)} %bitcast.2, f32[6,18,32,256]{3,2,1,0:T(8,128)S(1)} %get-tuple-element.42.a0, f32[4,32,256]{2,1,0:T(8,128)S(1)} %shard_map.84.before.v0, f32[6,16,32,128]{3,2,1,0:T(8,128)S(1)} %get-tuple-element.44.a1, ...), custom_call_target="tpu_custom_call" | custom-call | tf_op jit(solution)/shard_map/pallas_call | solution.py:21
  (15 shorter events, 0.4 us)
Async XLA Ops:
  0.6 20.1 %copy-start = (f32[8]{0:T(128)S(1)}, f32[8]{0:T(128)}, u32[]{:S(2)}) copy-start(f32[8]{0:T(128)} %param.9) | copy-start | bytes 100
  0.6 20.1 %copy-start.1 = (f32[8]{0:T(128)S(1)}, f32[8]{0:T(128)}, u32[]{:S(2)}) copy-start(f32[8]{0:T(128)} %param.8) | copy-start | bytes 100
  1.6 5.9 %collective-permute-start = (f32[18,16,128]{2,1,0:T(8,128)S(1)}, f32[18,16,128]{2,1,0:T(8,128)S(1)}, u32[]{:S(2)}, u32[]{:S(2)}) collective-permute-start(f32[18,16,128]{2,1,0:T(8,128)S(1)} %get-tuple-element.25), channel_id=1, source_target_pairs={{1,0},{2,1},{3,2},{0,3},{5,4},{6,5},{7,6},{4,7},{9,8},{10,9},{11,1... | collective-permute-start | bytes 442376 | tf_op jit(solution)/shard_map/ppermute | solution.py:629
  5.0 5.6 %collective-permute-start.1 = (f32[18,16,128]{2,1,0:T(8,128)S(1)}, f32[18,16,128]{2,1,0:T(8,128)S(1)}, u32[]{:S(2)}, u32[]{:S(2)}) collective-permute-start(f32[18,16,128]{2,1,0:T(8,128)S(1)} %get-tuple-element.26), channel_id=1, source_target_pairs={{3,0},{0,1},{1,2},{2,3},{7,4},{4,5},{5,6},{6,7},{11,8},{8,9},{9,10... | collective-permute-start | bytes 442376 | tf_op jit(solution)/shard_map/ppermute | solution.py:629
  10.7 6.4 %collective-permute-start.2 = (f32[39,8,128]{2,1,0:T(8,128)S(1)}, f32[39,8,128]{2,1,0:T(8,128)S(1)}, u32[]{:S(2)}, u32[]{:S(2)}) collective-permute-start(f32[39,8,128]{2,1,0:T(8,128)S(1)} %get-tuple-element.29), channel_id=1, source_target_pairs={{16,0},{32,16},{48,32},{64,48},{80,64},{96,80},{112,96},{128,112},... | collective-permute-start | bytes 479240 | tf_op jit(solution)/shard_map/ppermute | solution.py:629
  12.6 5.0 %collective-permute-start.3 = (f32[39,8,128]{2,1,0:T(8,128)S(1)}, f32[39,8,128]{2,1,0:T(8,128)S(1)}, u32[]{:S(2)}, u32[]{:S(2)}) collective-permute-start(f32[39,8,128]{2,1,0:T(8,128)S(1)} %get-tuple-element.30), channel_id=1, source_target_pairs={{240,0},{0,16},{16,32},{32,48},{48,64},{64,80},{80,96},{96,112},{1... | collective-permute-start | bytes 479240 | tf_op jit(solution)/shard_map/ppermute | solution.py:629
  17.9 4.0 %collective-permute-start.4 = (f32[12,8,128]{2,1,0:T(8,128)S(1)}, f32[12,8,128]{2,1,0:T(8,128)S(1)}, u32[]{:S(2)}, u32[]{:S(2)}) collective-permute-start(f32[12,8,128]{2,1,0:T(8,128)S(1)} %get-tuple-element.33), channel_id=1, source_target_pairs={{4,0},{8,4},{12,8},{0,12},{5,1},{9,5},{13,9},{1,13},{6,2},{10,6},{... | collective-permute-start | bytes 147464 | tf_op jit(solution)/shard_map/ppermute | solution.py:629
  20.8 4.2 %collective-permute-start.5 = (f32[12,8,128]{2,1,0:T(8,128)S(1)}, f32[12,8,128]{2,1,0:T(8,128)S(1)}, u32[]{:S(2)}, u32[]{:S(2)}) collective-permute-start(f32[12,8,128]{2,1,0:T(8,128)S(1)} %get-tuple-element.34), channel_id=1, source_target_pairs={{12,0},{0,4},{4,8},{8,12},{13,1},{1,5},{5,9},{9,13},{14,2},{2,6},{... | collective-permute-start | bytes 147464 | tf_op jit(solution)/shard_map/ppermute | solution.py:629
  27.1 4.5 %collective-permute-start.8 = (f32[5,2,8,128]{3,2,1,0:T(8,128)S(1)}, f32[5,2,8,128]{3,2,1,0:T(8,128)S(1)}, u32[]{:S(2)}, u32[]{:S(2)}) collective-permute-start(f32[5,2,8,128]{3,2,1,0:T(8,128)S(1)} %get-tuple-element.35.own), channel_id=1, source_target_pairs={{2,0},{3,1},{0,2},{1,3},{6,4},{7,5},{4,6},{5,7},{10,8},{11,9},{8,1... | collective-permute-start | bytes 122888 | tf_op jit(solution)/shard_map/ppermute | solution.py:629
  27.2 4.6 %collective-permute-start.7 = (f32[5,2,8,128]{3,2,1,0:T(8,128)S(1)}, f32[5,2,8,128]{3,2,1,0:T(8,128)S(1)}, u32[]{:S(2)}, u32[]{:S(2)}) collective-permute-start(f32[5,2,8,128]{3,2,1,0:T(8,128)S(1)} %get-tuple-element.35.own), channel_id=1, source_target_pairs={{3,0},{0,1},{1,2},{2,3},{7,4},{4,5},{5,6},{6,7},{11,8},{8,9},{9,10... | collective-permute-start | bytes 122888 | tf_op jit(solution)/shard_map/ppermute | solution.py:629
  28.0 3.7 %collective-permute-start.6 = (f32[5,2,8,128]{3,2,1,0:T(8,128)S(1)}, f32[5,2,8,128]{3,2,1,0:T(8,128)S(1)}, u32[]{:S(2)}, u32[]{:S(2)}) collective-permute-start(f32[5,2,8,128]{3,2,1,0:T(8,128)S(1)} %get-tuple-element.35.own), channel_id=1, source_target_pairs={{1,0},{2,1},{3,2},{0,3},{5,4},{6,5},{7,6},{4,7},{9,8},{10,9},{11,1... | collective-permute-start | bytes 122888 | tf_op jit(solution)/shard_map/ppermute | solution.py:629
  31.8 2.8 %collective-permute-start.9 = (f32[8,8,128]{2,1,0:T(8,128)S(1)}, f32[8,8,128]{2,1,0:T(8,128)S(1)}, u32[]{:S(2)}, u32[]{:S(2)}) collective-permute-start(f32[8,8,128]{2,1,0:T(8,128)S(1)} %get-tuple-element.37), channel_id=1, source_target_pairs={{4,0},{8,4},{12,8},{0,12},{5,1},{9,5},{13,9},{1,13},{6,2},{10,6},{... | collective-permute-start | bytes 98312 | tf_op jit(solution)/shard_map/ppermute | solution.py:629
  32.0 4.0 %collective-permute-start.10 = (f32[8,8,128]{2,1,0:T(8,128)S(1)}, f32[8,8,128]{2,1,0:T(8,128)S(1)}, u32[]{:S(2)}, u32[]{:S(2)}) collective-permute-start(f32[8,8,128]{2,1,0:T(8,128)S(1)} %get-tuple-element.38), channel_id=1, source_target_pairs={{12,0},{0,4},{4,8},{8,12},{13,1},{1,5},{5,9},{9,13},{14,2},{2,6},{... | collective-permute-start | bytes 98312 | tf_op jit(solution)/shard_map/ppermute | solution.py:629
  36.0 16.9 %collective-permute-start.12 = (f32[56,8,128]{2,1,0:T(8,128)S(1)}, f32[56,8,128]{2,1,0:T(8,128)S(1)}, u32[]{:S(2)}, u32[]{:S(2)}) collective-permute-start(f32[56,8,128]{2,1,0:T(8,128)S(1)} %get-tuple-element.39.full), channel_id=1, source_target_pairs={{240,0},{0,16},{16,32},{32,48},{48,64},{64,80},{80,96},{96,112},{1... | collective-permute-start | bytes 688136 | tf_op jit(solution)/shard_map/ppermute | solution.py:629
  41.0 11.9 %collective-permute-start.11 = (f32[56,8,128]{2,1,0:T(8,128)S(1)}, f32[56,8,128]{2,1,0:T(8,128)S(1)}, u32[]{:S(2)}, u32[]{:S(2)}) collective-permute-start(f32[56,8,128]{2,1,0:T(8,128)S(1)} %get-tuple-element.39.full), channel_id=1, source_target_pairs={{16,0},{32,16},{48,32},{64,48},{80,64},{96,80},{112,96},{128,112},... | collective-permute-start | bytes 688136 | tf_op jit(solution)/shard_map/ppermute | solution.py:629
  44.8 5.1 %collective-permute-start.13 = (f32[28,8,128]{2,1,0:T(8,128)S(1)}, f32[28,8,128]{2,1,0:T(8,128)S(1)}, u32[]{:S(2)}, u32[]{:S(2)}) collective-permute-start(f32[28,8,128]{2,1,0:T(8,128)S(1)} %get-tuple-element.40), channel_id=1, source_target_pairs={{32,0},{48,16},{64,32},{80,48},{96,64},{112,80},{128,96},{144,112}... | collective-permute-start | bytes 344072 | tf_op jit(solution)/shard_map/ppermute | solution.py:629
  47.4 5.6 %collective-permute-start.14 = (f32[28,8,128]{2,1,0:T(8,128)S(1)}, f32[28,8,128]{2,1,0:T(8,128)S(1)}, u32[]{:S(2)}, u32[]{:S(2)}) collective-permute-start(f32[28,8,128]{2,1,0:T(8,128)S(1)} %get-tuple-element.41), channel_id=1, source_target_pairs={{224,0},{240,16},{0,32},{16,48},{32,64},{48,80},{64,96},{80,112},{... | collective-permute-start | bytes 344072 | tf_op jit(solution)/shard_map/ppermute | solution.py:629
